TPU v7x, 32 devices: a whole 2x2x4 slice. The times are simulated.
32 devices in a mesh: ctx: 8 (over y, x, core), fsdp: 4 (over z).
Axes of the slice: x: 2, y: 2, z: 4, core: 2. Of those that a mesh axis runs over, the one named last changes fastest.
Arguments:
- inputs: bfloat16 [4096, 2048], P(('ctx', 'fsdp')), may hold values from -6 to 6
- attention_gain: float32 [2048], replicated, may hold values from 0.5 to 1.5
- qkv_weight: bfloat16 [2048, 3072], P('fsdp'), may hold values from -0.125 to 0.125
- query_gain: float32 [64], replicated, may hold values from 0.1 to 1.9
- key_gain: float32 [64], replicated, may hold values from 0.1 to 1.9
- out_weight: bfloat16 [2048, 2048], P('fsdp'), may hold values from -1.5 to 1.5
- mlp_gain: float32 [2048], replicated, may hold values from 0.5 to 1.5
- gate_up_weight: bfloat16 [2048, 16384], P('fsdp'), may hold values from -0.125 to 0.125
- down_weight: bfloat16 [8192, 2048], P('fsdp'), may hold values from -0.0625 to 0.0625
- cotangent: bfloat16 [4096, 2048], P(('ctx', 'fsdp')), may hold values from -6 to 6
Outputs:
- outputs: bfloat16 [4096, 2048], P(('ctx', 'fsdp'))
- grad_inputs: bfloat16 [4096, 2048], P(('ctx', 'fsdp'))
- grad_attention_gain: float32 [2048], replicated
- grad_qkv_weight: float32 [2048, 3072], P('fsdp')
- grad_query_gain: float32 [64], replicated
- grad_key_gain: float32 [64], replicated
- grad_out_weight: float32 [2048, 2048], P('fsdp')
- grad_mlp_gain: float32 [2048], replicated
- grad_gate_up_weight: float32 [2048, 16384], P('fsdp')
- grad_down_weight: float32 [8192, 2048], P('fsdp')
All inputs are finite; a program needn't handle non-finite values.
Results may differ from a plain program's by a relative error of at most 0.023.
Values may be sent and summed in bfloat16 or wider, within the bound.
No kernel may reach another device: no remote copies, remote signals or barrier semaphores. Data moves between devices by JAX's collectives and lax.ppermute only.
A program may use at most 640 MiB of HBM per device.

v0:
```python
import jax
import jax.numpy as jnp
from jax import lax
from jax.sharding import PartitionSpec as P

HEADS = 32
KV_HEADS = 8
HEAD_DIM = 64


epsilon = 1e-05
theta = 1000000.0
negative = -1e30
block_keys = 1024


def rms_scale(values, gain):
    return values * lax.rsqrt(jnp.mean(values * values, axis=-1, keepdims=True) + epsilon) * gain


def rotate(values, positions):
    half_dim = values.shape[-1] // 2
    frequency = theta ** (-jnp.arange(half_dim, dtype=jnp.float32) * 2.0 / values.shape[-1])
    angles = positions.astype(jnp.float32)[:, None] * frequency[None, :]
    cosine = jnp.cos(angles)[:, None, :]
    sine_part = jnp.sin(angles)[:, None, :]
    lower_half = values[..., :half_dim]
    upper_half = values[..., half_dim:]
    return jnp.concatenate(
        [
            lower_half * cosine - upper_half * sine_part,
            upper_half * cosine + lower_half * sine_part,
        ],
        axis=-1,
    )


def attention_inputs(qkv_rows, query_gain, key_gain, positions):
    row_count = qkv_rows.shape[0]
    query_width = HEADS * HEAD_DIM
    key_width = KV_HEADS * HEAD_DIM
    queries = qkv_rows[:, :query_width].reshape(row_count, HEADS, HEAD_DIM)
    key_rows = qkv_rows[:, query_width : query_width + key_width].reshape(
        row_count, KV_HEADS, HEAD_DIM
    )
    value_rows = qkv_rows[:, query_width + key_width :].reshape(row_count, KV_HEADS, HEAD_DIM)
    return (
        rotate(rms_scale(queries, query_gain), positions),
        rotate(rms_scale(key_rows, key_gain), positions),
        value_rows,
    )


def swiglu(gate_up):
    hidden_width = gate_up.shape[1] // 2
    return jax.nn.silu(gate_up[:, :hidden_width]) * gate_up[:, hidden_width:]


def weights_forward(left, shard):
    return (
        jnp.dot(
            left,
            lax.all_gather(shard, "fsdp", axis=0, tiled=True),
            preferred_element_type=jnp.float32,
        ),
        left,
    )


def weights_backward(gradient, shard, saved):
    left_grad = lax.dot_general(
        gradient,
        lax.all_gather(shard, "fsdp", axis=0, tiled=True),
        (((1,), (1,)), ((), ())),
        preferred_element_type=jnp.float32,
    )
    weight_grad = lax.psum_scatter(
        lax.dot_general(
            saved, gradient, (((0,), (0,)), ((), ())), preferred_element_type=jnp.float32
        ).astype(jnp.bfloat16),
        "fsdp",
        scatter_dimension=0,
        tiled=True,
    ).astype(jnp.float32)
    return (left_grad, weight_grad)


def body(
    inputs,
    attention_gain,
    qkv_weight,
    query_gain,
    key_gain,
    out_weight,
    mlp_gain,
    gate_up_weight,
    down_weight,
    cotangent,
):
    tokens_here = inputs.shape[0]
    fsdp_count = lax.axis_size("fsdp")
    ctx_here = lax.axis_index("ctx")
    fsdp_here = lax.axis_index("fsdp")

    def place_of(ctx_id, fsdp_id, row_id):
        return (ctx_id * fsdp_count + fsdp_id) * tokens_here + row_id

    def key_places(gathered_rows):
        block_size = fsdp_count * tokens_here
        return place_of(
            gathered_rows // block_size,
            gathered_rows // tokens_here % fsdp_count,
            gathered_rows % tokens_here,
        )

    group_size = HEADS // KV_HEADS
    group_rows = group_size * tokens_here
    score_scale = HEAD_DIM ** (-0.5)
    positions = place_of(ctx_here, fsdp_here, jnp.arange(tokens_here, dtype=jnp.int32))
    row_positions = jnp.tile(positions, group_size)
    last_position = jnp.max(positions)
    source = inputs.astype(jnp.float32)
    normed_attn_low = rms_scale(source, attention_gain).astype(jnp.bfloat16)
    qkv_rows, saved_qkv = weights_forward(normed_attn_low, qkv_weight)
    query_rot, key_rot, value_rows = attention_inputs(qkv_rows, query_gain, key_gain, positions)
    query_low = query_rot.astype(jnp.bfloat16)
    grouped = (
        query_low.reshape(tokens_here, KV_HEADS, group_size, HEAD_DIM)
        .transpose(1, 2, 0, 3)
        .reshape(KV_HEADS, group_rows, HEAD_DIM)
    )
    key_low = key_rot.astype(jnp.bfloat16).reshape(tokens_here, KV_HEADS * HEAD_DIM)
    value_low = value_rows.astype(jnp.bfloat16).reshape(tokens_here, KV_HEADS * HEAD_DIM)
    group_pair = (
        lax.all_gather(key_low, "fsdp", axis=0, tiled=True),
        lax.all_gather(value_low, "fsdp", axis=0, tiled=True),
    )

    def split_blocks(arrays):
        key_total = arrays[0].shape[0]
        block_count = key_total // block_keys
        pieces = tuple((entry.reshape(block_count, block_keys, entry.shape[1]) for entry in arrays))
        places = key_places(jnp.arange(key_total, dtype=jnp.int32)).reshape(block_count, block_keys)
        return (pieces, places)

    def scores_mask(key_block, key_positions):
        key_count = key_block.shape[0]
        key_heads = key_block.reshape(key_count, KV_HEADS, HEAD_DIM)
        scores = (
            jnp.einsum("hrd,nhd->hrn", grouped, key_heads, preferred_element_type=jnp.float32)
            * score_scale
        )
        visible = key_positions[None, None, :] <= row_positions[None, :, None]
        return (scores, visible)

    output_start = jnp.zeros((KV_HEADS, group_rows, HEAD_DIM), jnp.float32)
    online_start = (
        jnp.full((KV_HEADS, group_rows), negative, jnp.float32),
        jnp.zeros((KV_HEADS, group_rows), jnp.float32),
        output_start,
    )
    blocks, places = split_blocks(
        (
            lax.all_gather(group_pair[0], "ctx", axis=0, tiled=True),
            lax.all_gather(group_pair[1], "ctx", axis=0, tiled=True),
        )
    )

    def scan_step(running, block_item):
        key_block, value_block, key_positions = block_item

        def scan_compute(current):
            top_now, total_now, sum_now = current
            scores, visible = scores_mask(key_block, key_positions)
            masked = jnp.where(visible, scores, negative)
            top_new = jnp.maximum(top_now, jnp.max(masked, axis=-1))
            weights_now = jnp.where(visible, jnp.exp(masked - top_new[..., None]), 0.0)
            factor = jnp.exp(top_now - top_new)
            value_heads = value_block.reshape(value_block.shape[0], KV_HEADS, HEAD_DIM)
            added = jnp.einsum(
                "hrn,nhd->hrd",
                weights_now.astype(jnp.bfloat16),
                value_heads,
                preferred_element_type=jnp.float32,
            )
            return (
                top_new,
                total_now * factor + jnp.sum(weights_now, axis=-1),
                sum_now * factor[..., None] + added,
            )

        return (
            lax.cond(
                jnp.min(key_positions) <= last_position,
                scan_compute,
                lambda current: current,
                running,
            ),
            None,
        )

    top_value, total_value, summed_values = lax.scan(
        scan_step, online_start, (blocks[0], blocks[1], places)
    )[0]
    log_total = top_value + jnp.log(total_value)
    attended = summed_values / total_value[..., None]
    attended_rows = (
        attended.reshape(KV_HEADS, group_size, tokens_here, HEAD_DIM)
        .transpose(2, 0, 1, 3)
        .reshape(tokens_here, HEADS * HEAD_DIM)
    )
    attended_low = attended_rows.astype(jnp.bfloat16)
    attn_branch, saved_out = weights_forward(attended_low, out_weight)
    hidden_mid = source + attn_branch
    normed_mlp_low = rms_scale(hidden_mid, mlp_gain).astype(jnp.bfloat16)
    gate_up, saved_gate = weights_forward(normed_mlp_low, gate_up_weight)
    activated_low = swiglu(gate_up).astype(jnp.bfloat16)
    mlp_branch, saved_down = weights_forward(activated_low, down_weight)
    outputs = (hidden_mid + mlp_branch).astype(jnp.bfloat16)
    act_grad, grad_down = weights_backward(cotangent, down_weight, saved_down)
    gate_grad = jax.vjp(swiglu, gate_up)[1](act_grad)[0].astype(jnp.bfloat16)
    normed_grad, grad_gate_up = weights_backward(gate_grad, gate_up_weight, saved_gate)
    mid_part, mlp_gain_grad = jax.vjp(rms_scale, hidden_mid, mlp_gain)[1](normed_grad)
    hidden_grad = cotangent.astype(jnp.float32) + mid_part
    branch_grad = hidden_grad.astype(jnp.bfloat16)
    attended_grad, grad_out = weights_backward(branch_grad, out_weight, saved_out)
    out_grad_low = attended_grad.astype(jnp.bfloat16)
    grouped_grad = (
        out_grad_low.reshape(tokens_here, KV_HEADS, group_size, HEAD_DIM)
        .transpose(1, 2, 0, 3)
        .reshape(KV_HEADS, group_rows, HEAD_DIM)
    )
    row_delta = jnp.sum(grouped_grad.astype(jnp.float32) * attended, axis=-1)
    key_value_all = (
        lax.all_gather(group_pair[0], "ctx", axis=0, tiled=True),
        lax.all_gather(group_pair[1], "ctx", axis=0, tiled=True),
    )
    blocks, places = split_blocks(key_value_all)

    def grad_step(running, block_item):
        key_block, value_block, key_positions = block_item
        key_count = key_block.shape[0]

        def grad_compute(current):
            scores, visible = scores_mask(key_block, key_positions)
            probabilities = jnp.where(visible, jnp.exp(scores - log_total[..., None]), 0.0)
            key_heads = key_block.reshape(key_count, KV_HEADS, HEAD_DIM)
            value_heads = value_block.reshape(key_count, KV_HEADS, HEAD_DIM)
            prob_grad = jnp.einsum(
                "hrd,nhd->hrn", grouped_grad, value_heads, preferred_element_type=jnp.float32
            )
            score_grad = (probabilities * (prob_grad - row_delta[..., None])).astype(jnp.bfloat16)
            query_next = (
                current
                + jnp.einsum(
                    "hrn,nhd->hrd", score_grad, key_heads, preferred_element_type=jnp.float32
                )
                * score_scale
            )
            key_grad = (
                jnp.einsum("hrn,hrd->nhd", score_grad, grouped, preferred_element_type=jnp.float32)
                * score_scale
            )
            value_grad = jnp.einsum(
                "hrn,hrd->nhd",
                probabilities.astype(jnp.bfloat16),
                grouped_grad,
                preferred_element_type=jnp.float32,
            )
            return (
                query_next,
                (
                    key_grad.reshape(key_count, KV_HEADS * HEAD_DIM),
                    value_grad.reshape(key_count, KV_HEADS * HEAD_DIM),
                ),
            )

        def skip_block(current):
            empty_rows = jnp.zeros((key_count, KV_HEADS * HEAD_DIM), jnp.float32)
            return (current, (empty_rows, empty_rows))

        return lax.cond(jnp.min(key_positions) <= last_position, grad_compute, skip_block, running)

    query_grad, block_grads = lax.scan(grad_step, output_start, (blocks[0], blocks[1], places))
    key_terms = block_grads[0].reshape(-1, KV_HEADS * HEAD_DIM)
    value_terms = block_grads[1].reshape(-1, KV_HEADS * HEAD_DIM)
    group_terms = (
        lax.psum_scatter(
            key_terms.astype(jnp.bfloat16), "ctx", scatter_dimension=0, tiled=True
        ).astype(jnp.float32),
        lax.psum_scatter(
            value_terms.astype(jnp.bfloat16), "ctx", scatter_dimension=0, tiled=True
        ).astype(jnp.float32),
    )
    local_terms = (
        lax.psum_scatter(
            group_terms[0].astype(jnp.bfloat16), "fsdp", scatter_dimension=0, tiled=True
        ).astype(jnp.float32),
        lax.psum_scatter(
            group_terms[1].astype(jnp.bfloat16), "fsdp", scatter_dimension=0, tiled=True
        ).astype(jnp.float32),
    )
    query_rows_grad = (
        query_grad.reshape(KV_HEADS, group_size, tokens_here, HEAD_DIM)
        .transpose(2, 0, 1, 3)
        .reshape(tokens_here, HEADS, HEAD_DIM)
    )
    key_rows_grad = local_terms[0].reshape(tokens_here, KV_HEADS, HEAD_DIM)
    value_rows_grad = local_terms[1].reshape(tokens_here, KV_HEADS, HEAD_DIM)

    def local_inputs(rows_in, query_scale, key_scale):
        return attention_inputs(rows_in, query_scale, key_scale, positions)

    pull_back = jax.vjp(local_inputs, qkv_rows, query_gain, key_gain)[1]
    qkv_grad, query_gain_grad, key_gain_grad = pull_back(
        (query_rows_grad, key_rows_grad, value_rows_grad)
    )
    qkv_grad_low = qkv_grad.astype(jnp.bfloat16)
    attn_normed_grad, grad_qkv = weights_backward(qkv_grad_low, qkv_weight, saved_qkv)
    source_part, attention_gain_grad = jax.vjp(rms_scale, source, attention_gain)[1](
        attn_normed_grad
    )
    grad_inputs = (hidden_grad + source_part).astype(jnp.bfloat16)
    summed = (
        lax.psum(grad_qkv.astype(jnp.bfloat16), "ctx").astype(jnp.float32),
        lax.psum(grad_out.astype(jnp.bfloat16), "ctx").astype(jnp.float32),
        lax.psum(grad_gate_up.astype(jnp.bfloat16), "ctx").astype(jnp.float32),
        lax.psum(grad_down.astype(jnp.bfloat16), "ctx").astype(jnp.float32),
    )
    gain_sums = lax.psum(
        (attention_gain_grad, query_gain_grad, key_gain_grad, mlp_gain_grad), ("ctx", "fsdp")
    )
    return (
        outputs,
        grad_inputs,
        gain_sums[0],
        summed[0],
        gain_sums[1],
        gain_sums[2],
        summed[1],
        gain_sums[3],
        summed[2],
        summed[3],
    )


def solution(mesh):
    return jax.shard_map(
        body,
        mesh=mesh,
        in_specs=(
            P(("ctx", "fsdp"), None),
            P(),
            P("fsdp", None),
            P(),
            P(),
            P("fsdp", None),
            P(),
            P("fsdp", None),
            P("fsdp", None),
            P(("ctx", "fsdp"), None),
        ),
        out_specs=(
            P(("ctx", "fsdp"), None),
            P(("ctx", "fsdp"), None),
            P(),
            P("fsdp", None),
            P(),
            P(),
            P("fsdp", None),
            P(),
            P("fsdp", None),
            P("fsdp", None),
        ),
        check_vma=False,
    )
```

profile of v0, /device:TPU:0, one launch (start us, length us, event | category | flops | bytes accessed | tf_op | source)
XLA Modules:
  0.0 4961.9 jit_solution(10807863972853312027)
XLA Ops:
  10.0 220.5 %all-gather.7.cloned.1.call-done = bf16[2048,3072]{1,0:T(8,128)(2,1)} async-done(((bf16[512,3072]{1,0:T(8,128)(2,1)}), bf16[2048,3072]{1,0:T(8,128)(2,1)}) %all-gather.7.cloned.1.call-update) | async-done | bytes 12582928 | tf_op jit(solution)/shard_map/all_gather | solution.py:63
  238.1 16.0 all_gather.31
  254.3 15.5 all_gather.33
  274.1 16.1 all-gather.9.cloned.1.call-done
  303.0 25.8 all-gather.11.cloned.1.call-done
  335.2 22.4 while.33
  337.1 14.9 conditional.6
  358.1 121.9 %all-gather.13.cloned.1.call-done = bf16[2048,2048]{1,0:T(8,128)(2,1)} async-done(((bf16[512,2048]{1,0:T(8,128)(2,1)}), bf16[2048,2048]{1,0:T(8,128)(2,1)}) %all-gather.13.cloned.1.call-update) | async-done | bytes 8388624 | tf_op jit(solution)/shard_map/all_gather | solution.py:63
  484.8 1105.5 %all-gather.15.cloned.1.call-done = bf16[2048,16384]{1,0:T(8,128)(2,1)} async-done(((bf16[512,16384]{1,0:T(8,128)(2,1)}), bf16[2048,16384]{1,0:T(8,128)(2,1)}) %all-gather.15.cloned.1.call-update) | async-done | bytes 67108880 | tf_op jit(solution)/shard_map/all_gather | solution.py:63
  1590.3 34.1 fusion.62
  1624.4 526.9 %all-gather.17.cloned.1.call-done = bf16[8192,2048]{1,0:T(8,128)(2,1)} async-done(((bf16[2048,2048]{1,0:T(8,128)(2,1)}), bf16[8192,2048]{1,0:T(8,128)(2,1)}) %all-gather.17.cloned.1.call-update) | async-done | bytes 33554448 | tf_op jit(solution)/shard_map/all_gather | solution.py:63
  2151.3 22.7 fusion.38
  2174.1 31.8 multiply_reduce_fusion
  2217.0 54.9 %while.34 = (s32[]{:T(128)}, f32[8,512,64]{1,2,0:T(8,128)}, bf16[4,1024,512]{2,1,0:T(8,128)(2,1)}, bf16[4,1024,512]{2,1,0:T(8,128)(2,1)}, s32[4,1024]{1,0:T(4,12...) while((s32[]{:T(128)}, f32[8,512,64]{1,2,0:T(8,128)}, ...), condition=%wide.region_18.19_spmd.clone, body=%wide.region_14.18_spmd.clone.sunk | while | flops 2728395776 | bytes 101254440 | solution.py:284
  2219.2 36.0 conditional.7
  2221.0 9.6 fusion.65
  2272.7 156.1 %reduce-scatter.17.cloned.1.call-done = bf16[512,512]{1,0:T(8,128)(2,1)} async-done(((bf16[4096,512]{1,0:T(8,128)(2,1)}), bf16[512,512]{1,0:T(8,128)(2,1)}) %reduce-scatter.17.cloned.1.call-update) | async-done | bytes 524304 | tf_op jit(solution)/shard_map/reduce_scatter | solution.py:288
  2428.9 55.0 %reduce-scatter.13.cloned.1.call-done = bf16[512,512]{1,0:T(8,128)(2,1)} async-done(((bf16[4096,512]{1,0:T(8,128)(2,1)}), bf16[512,512]{1,0:T(8,128)(2,1)}) %reduce-scatter.13.cloned.1.call-update) | async-done | bytes 524304 | tf_op jit(solution)/shard_map/reduce_scatter | solution.py:291
  2494.9 12.9 reduce-scatter.19.cloned.1.call-done
  2509.3 20.6 reduce-scatter.15.cloned.1.call-done
  2538.6 15.9 convolution_convert_fusion.1
  2555.7 28.9 convolution_convert_fusion
  2584.8 90.0 %reduce-scatter.23.cloned.1.call-done = bf16[512,2048]{1,0:T(8,128)(2,1)} async-done(((bf16[2048,2048]{1,0:T(8,128)(2,1)}), bf16[512,2048]{1,0:T(8,128)(2,1)}) %reduce-scatter.23.cloned.1.call-update) | async-done | bytes 2097168 | tf_op jit(solution)/shard_map/reduce_scatter | solution.py:77
  2674.9 215.4 %reduce-scatter.21.cloned.1.call-done = bf16[512,3072]{1,0:T(8,128)(2,1)} async-done(((bf16[2048,3072]{1,0:T(8,128)(2,1)}), bf16[512,3072]{1,0:T(8,128)(2,1)}) %reduce-scatter.21.cloned.1.call-update) | async-done | bytes 3145744 | tf_op jit(solution)/shard_map/reduce_scatter | solution.py:77
  2890.3 556.1 %reduce-scatter.27.cloned.1.call-done = bf16[2048,2048]{1,0:T(8,128)(2,1)} async-done(((bf16[8192,2048]{1,0:T(8,128)(2,1)}), bf16[2048,2048]{1,0:T(8,128)(2,1)}) %reduce-scatter.27.cloned.1.call-update) | async-done | bytes 8388624
  3446.3 1097.8 %reduce-scatter.25.cloned.1.call-done = bf16[512,16384]{1,0:T(8,128)(2,1)} async-done(((bf16[2048,16384]{1,0:T(8,128)(2,1)}), bf16[512,16384]{1,0:T(8,128)(2,1)}) %reduce-scatter.25.cloned.1.call-update) | async-done | bytes 16777232
  4544.1 16.8 fusion.27
  4561.0 9.4 fusion.31
  4570.4 43.0 all-reduce.11
  4614.5 302.6 %all-reduce.15.cloned.1.call-done = (bf16[512,3072]{1,0:T(8,128)(2,1)}, bf16[512,2048]{1,0:T(8,128)(2,1)}, bf16[512,16384]{1,0:T(8,128)(2,1)}, bf16[2048,2048]{1,0:T(8,128)(2,1)}) async-done(((bf16[512,3072]{1,0:T(8,128)(2,1)}, bf16[512,2048]{1,0:T(8,128)(2,1)}, bf16[512,16384]{1,0:T(8,128)(2,1)}, bf16[2048,2048]{1,0:T(8,128)(2,1)}), (bf16[512,3072]{1,0:T(8,128)(2,1)}, bf16[512,2048]{1,0:T(8,128)(2,1)}, ...) | async-done | bytes 30408720 | tf_op jit(solution)/shard_map/psum | solution.py:325
  4925.2 18.3 convert_element_type.165
  4943.4 11.7 convert_element_type.167
  (230 shorter events, 140.5 us)
Async XLA Ops:
  7.2 223.3 %all-gather.7.cloned.1.call-start = ((), (), s32[]{:S(2)}) async-start(), calls=%async_computation.8 | async-start | bytes 15728640 | tf_op jit(solution)/shard_map/all_gather | solution.py:63
  7.9 282.3 %all-gather.9.cloned.1.call-start = ((), (), s32[]{:S(2)}) async-start(), calls=%async_computation.9 | async-start | bytes 4718592 | tf_op jit(solution)/shard_map/all_gather | solution.py:164
  9.8 227.4 %copy-start.37 = (f32[128]{0:T(128)}, f32[128]{0:T(128)S(1)}, u32[]{:S(2)}) copy-start(f32[128]{0:T(128)S(1)} %fusion.55) | copy-start | bytes 1540
  10.0 263.2 %copy-start.22 = (f32[128,32]{0,1:T(8,128)}, f32[128,32]{0,1:T(8,128)S(1)}, u32[]{:S(2)}) copy-start(f32[128,32]{0,1:T(8,128)S(1)} %get-tuple-element.550) | copy-start | bytes 49156
  10.0 263.2 %copy-start.24 = (f32[128,32]{0,1:T(8,128)}, f32[128,32]{0,1:T(8,128)S(1)}, u32[]{:S(2)}) copy-start(f32[128,32]{0,1:T(8,128)S(1)} %get-tuple-element.551) | copy-start | bytes 49156
  10.0 227.5 %copy-start.39 = (f32[64]{0:T(128)S(1)}, f32[64]{0:T(128)}, u32[]{:S(2)}) copy-start(f32[64]{0:T(128)} %param.22) | copy-start | bytes 772
  254.2 74.7 %all-gather.11.cloned.1.call-start = ((), (), s32[]{:S(2)}) async-start(), calls=%async_computation.10 | async-start | bytes 4718592 | tf_op jit(solution)/shard_map/all_gather | solution.py:165
  269.8 210.2 %all-gather.13.cloned.1.call-start = ((), (), s32[]{:S(2)}) async-start(), calls=%async_computation.11 | async-start | bytes 10485760 | tf_op jit(solution)/shard_map/all_gather | solution.py:63
  270.3 1320.0 %all-gather.15.cloned.1.call-start = ((), (), s32[]{:S(2)}) async-start(), calls=%async_computation.12 | async-start | bytes 83886080 | tf_op jit(solution)/shard_map/all_gather | solution.py:63
  270.9 1880.4 %all-gather.17.cloned.1.call-start = ((), (), s32[]{:S(2)}) async-start(), calls=%async_computation.13 | async-start | bytes 41943040 | tf_op jit(solution)/shard_map/all_gather | solution.py:63
  271.5 2157.3 %reduce-scatter.17.cloned.1.call-start = ((), (), s32[]{:S(2)}) async-start(), calls=%async_computation.16 | async-start | bytes 4718592 | tf_op jit(solution)/shard_map/reduce_scatter | solution.py:288
  335.2 144.8 %copy-start.4 = (bf16[128,2048]{1,0:T(8,128)(2,1)S(1)}, bf16[128,2048]{1,0:T(8,128)(2,1)}, u32[]{:S(2)}) copy-start(bf16[128,2048]{1,0:T(8,128)(2,1)} %param.18) | copy-start | bytes 1572868
  358.1 126.7 %copy-start.8 = (bf16[128,8,4,64]{0,3,2,1:T(8,128)(2,1)}, bf16[128,8,4,64]{0,3,2,1:T(8,128)(2,1)S(1)}, u32[]{:S(2)}) copy-start(bf16[128,8,4,64]{0,3,2,1:T(8,128)(2,1)S(1)} %copy.80) | copy-start | bytes 1572868
  480.0 1110.3 %copy-start.17 = (f32[2048]{0:T(1024)S(1)}, f32[2048]{0:T(1024)}, u32[]{:S(2)}) copy-start(f32[2048]{0:T(1024)} %param.24) | copy-start | bytes 24580
  484.7 1721.2 %copy-start = (f32[128,2048]{1,0:T(8,128)}, f32[128,2048]{1,0:T(8,128)S(1)}, u32[]{:S(2)}) copy-start(f32[128,2048]{1,0:T(8,128)S(1)} %get-tuple-element.553) | copy-start | bytes 3145732
  484.8 1721.2 %copy-start.26 = (f32[128]{0:T(128)}, f32[128]{0:T(128)S(1)}, u32[]{:S(2)}) copy-start(f32[128]{0:T(128)S(1)} %fusion.56) | copy-start | bytes 1540
  1590.3 561.0 %copy-start.15 = (bf16[128,2048]{1,0:T(8,128)(2,1)S(1)}, bf16[128,2048]{1,0:T(8,128)(2,1)}, u32[]{:S(2)}) copy-start(bf16[128,2048]{1,0:T(8,128)(2,1)} %param.27) | copy-start | bytes 1572868
  2271.9 212.3 %copy-start.7 = (f32[128,2048]{1,0:T(8,128)S(1)}, f32[128,2048]{1,0:T(8,128)}, u32[]{:S(2)}) copy-start(f32[128,2048]{1,0:T(8,128)} %copy-done.6) | copy-start | bytes 3145732
  2271.9 212.3 %copy-start.9 = (bf16[128,8,4,64]{0,3,2,1:T(8,128)(2,1)S(1)}, bf16[128,8,4,64]{0,3,2,1:T(8,128)(2,1)}, u32[]{:S(2)}) copy-start(bf16[128,8,4,64]{0,3,2,1:T(8,128)(2,1)} %copy-done.8) | copy-start | bytes 1572868
  2271.9 212.0 %reduce-scatter.13.cloned.1.call-start = ((), (), s32[]{:S(2)}) async-start(), calls=%async_computation.14 | async-start | bytes 4718592 | tf_op jit(solution)/shard_map/reduce_scatter | solution.py:291
  2272.7 235.1 %reduce-scatter.19.cloned.1.call-start = ((), (), s32[]{:S(2)}) async-start(), calls=%async_computation.17 | async-start | bytes 655360 | tf_op jit(solution)/shard_map/reduce_scatter | solution.py:296
  2428.8 101.1 %reduce-scatter.15.cloned.1.call-start = ((), (), s32[]{:S(2)}) async-start(), calls=%async_computation.15 | async-start | bytes 655360 | tf_op jit(solution)/shard_map/reduce_scatter | solution.py:299
  2483.9 191.0 %reduce-scatter.23.cloned.1.call-start = ((), (), s32[]{:S(2)}) async-start(), calls=%async_computation.19 | async-start | bytes 10485760 | tf_op jit(solution)/shard_map/reduce_scatter | solution.py:77
  2489.8 40.1 copy-start.5
  2489.8 40.1 copy-start.21
  2489.8 40.1 copy-start.38
  2489.8 400.4 %reduce-scatter.21.cloned.1.call-start = ((), (), s32[]{:S(2)}) async-start(), calls=%async_computation.18 | async-start | bytes 15728640 | tf_op jit(solution)/shard_map/reduce_scatter | solution.py:77
  2494.9 42.6 copy-start.12
  2537.6 908.8 %reduce-scatter.27.cloned.1.call-start = ((), (), s32[]{:S(2)}) async-start(), calls=%async_computation.21 | async-start | bytes 41943040
  2554.5 1989.6 %reduce-scatter.25.cloned.1.call-start = ((), (), s32[]{:S(2)}) async-start(), calls=%async_computation.20 | async-start | bytes 83886080
  2584.6 2332.5 %all-reduce.15.cloned.1.call-start = ((), (), s32[]{:S(2)}) async-start(), calls=%async_computation.22 | async-start | bytes 60817408 | tf_op jit(solution)/shard_map/psum | solution.py:325
  4561.0 52.4 %copy-start.44 = (f32[128]{0:T(128)S(1)}, f32[128]{0:T(128)}, u32[]{:S(2)}) copy-start(f32[128]{0:T(128)} %copy-done.43) | copy-start | bytes 1540
  (28 other events, 280.0 us)
Sparse Core Ops, SparseCore 0:
  9.6 220.8 all-gather.6
  254.3 35.8 all-gather.8
  292.1 36.7 all-gather.10
  330.3 149.6 all-gather.12
  481.4 1108.8 all-gather.14
  1591.7 559.5 all-gather.16
  2272.0 156.7 reduce-scatter.16
  2432.5 51.2 reduce-scatter.12
  2486.2 21.5 reduce-scatter.18
  2509.9 19.9 reduce-scatter.14
  2532.3 142.5 reduce-scatter.22
  2677.7 212.5 reduce-scatter.20
  2893.2 553.1 reduce-scatter.26
  3448.7 1095.3 reduce-scatter.24
  4548.2 368.8 all-reduce.14
where the time goes:
time: 4970 us; the launch traced here: 4960 us
  waiting for transfers between devices  4530 us (91%)
  matrix products  233 us (5%)
  blocking collectives  74.5 us (1%)
  other arithmetic  56.6 us (1%)
    all_gather x4, waiting for transfers between devices, weights_forward(): lax.all_gather(shard, 'fsdp', axis=0, tiled=True)  1970 us
    unnamed x17, waiting for transfers between devices  1660 us
    reduce_scatter x2, waiting for transfers between devices, weights_backward(): lax.psum_scatter(lax.dot_general(saved, gradient, (((0,), (0,)), ((), ())...  305 us
    psum x1, waiting for transfers between devices, body(): lax.psum(grad_qkv.astype(jnp.bfloat16), 'ctx').astype(jnp.float32)  303 us
    reduce_scatter x1, waiting for transfers between devices, body(): lax.psum_scatter(key_terms.astype(jnp.bfloat16), 'ctx', scatter_dimension...  156 us
  transfers between devices with their start and end apart: 15, of which 15 were waited for; matrix products, arithmetic and copies ran while one was open for 3% of the time, Pallas kernels for 0%

commit v1 on v0

v1 whole, which is shorter than its diff:
```python
import functools

import jax
import jax.numpy as jnp
from jax import lax
from jax.experimental import pallas as pl
from jax.experimental.pallas import tpu as pltpu
from jax.sharding import PartitionSpec as P

HEADS = 32
KV_HEADS = 8
HEAD_DIM = 64
GROUP = HEADS // KV_HEADS
GROUP_WIDTH = GROUP * HEAD_DIM

epsilon = 1e-05
theta = 1000000.0
score_scale = HEAD_DIM ** (-0.5)

f32 = jnp.float32
bf16 = jnp.bfloat16

CELL = KV_HEADS

NN = (((1,), (0,)), ((), ()))
NT = (((1,), (1,)), ((), ()))
TN = (((0,), (0,)), ((), ()))


def dot(left, right, dims=NN):
    return lax.dot_general(left, right, dims, preferred_element_type=f32)


def rms_scale(values, gain):
    return values * lax.rsqrt(jnp.mean(values * values, axis=-1, keepdims=True) + epsilon) * gain


def xor_send(values, distance):
    count = lax.axis_size("ctx")
    return lax.ppermute(values, "ctx", [(i, i ^ distance) for i in range(count)])


def cell_send(values, step):
    count = lax.axis_size("ctx")
    return lax.ppermute(values, "ctx", [(i, (i + step * CELL) % count) for i in range(count)])


def fsdp_send(values, step):
    count = lax.axis_size("fsdp")
    return lax.ppermute(values, "fsdp", [(i, (i + step) % count) for i in range(count)])


def pair_send(values, step, pair):
    count = lax.axis_size("fsdp")
    return lax.ppermute(
        values, "fsdp", [(i, i // pair * pair + (i % pair + step) % pair) for i in range(count)]
    )


def gather_cell(shard):
    half = shard.shape[0] // 2
    from_x = xor_send(shard, 2)
    from_y = xor_send(shard, 4)
    own_twin = xor_send(shard, 1)
    corner = jnp.concatenate([xor_send(from_y[:half], 2), xor_send(from_x[half:], 4)], axis=0)
    return [
        shard,
        own_twin,
        from_x,
        xor_send(from_x, 1),
        from_y,
        xor_send(from_y, 1),
        corner,
        xor_send(corner, 1),
    ]


def blank(shape, dtype):
    return pl.pallas_call(
        lambda ref: None,
        out_specs=pl.BlockSpec(memory_space=pl.ANY),
        out_shape=jax.ShapeDtypeStruct(shape, dtype),
        cost_estimate=pl.CostEstimate(flops=0, bytes_accessed=0, transcendentals=0),
    )()


def add_low(left, right):
    return (left.astype(f32) + right.astype(f32)).astype(bf16)


def reduce_cell(pieces):
    corner = add_low(pieces[6], xor_send(pieces[7], 1))
    at_x = add_low(pieces[2], xor_send(pieces[3], 1))
    at_y = add_low(pieces[4], xor_send(pieces[5], 1))
    own = add_low(pieces[0], xor_send(pieces[1], 1))
    half = corner.shape[0] // 2
    over_x = xor_send(corner[:half], 2)
    over_y = xor_send(corner[half:], 4)
    at_y = jnp.concatenate([add_low(at_y[:half], over_x), at_y[half:]], axis=0)
    at_x = jnp.concatenate([at_x[:half], add_low(at_x[half:], over_y)], axis=0)
    return (
        own.astype(f32) + xor_send(at_x, 2).astype(f32) + xor_send(at_y, 4).astype(f32)
    )


def stack_heads(block):
    return jnp.concatenate(
        [block[:, i * HEAD_DIM : (i + 1) * HEAD_DIM] for i in range(GROUP)], axis=0
    )


def unstack_heads(turned, rows):
    return jnp.concatenate([turned[:, i * rows : (i + 1) * rows].T for i in range(GROUP)], axis=1)


def fill_turned(place_ref, kv_ref, turned_ref, chunk):
    @pl.when(pl.program_id(0) == 0)
    def _():
        def turn(n, _):
            start = pl.multiple_of(n * chunk, chunk)
            turned_ref[:, pl.ds(start, chunk)] = kv_ref[pl.ds(start, chunk), :].T
            return 0

        lax.fori_loop(0, (place_ref[1] + 1) * CELL, turn, 0)


def visible_keys(place_ref, chunk, rows):
    key_at = lax.broadcasted_iota(jnp.int32, (chunk, GROUP * rows), 0)
    row_at = lax.broadcasted_iota(jnp.int32, (chunk, GROUP * rows), 1) % rows
    return key_at <= row_at + place_ref[0] * rows


def attention_kernel(chunk, place_ref, q_ref, kv_ref, out_ref, log_ref, turned_ref):
    rows = q_ref.shape[0]
    fill_turned(place_ref, kv_ref, turned_ref, chunk)
    queries = stack_heads(q_ref[...].astype(f32) * score_scale).astype(bf16)
    queries = jnp.concatenate([queries, jnp.zeros_like(queries)], axis=1)

    def step(n, running, masked):
        total, summed = running
        start = pl.multiple_of(n * chunk, chunk)
        weights = jnp.exp(dot(kv_ref[pl.ds(start, chunk), :], queries, NT))
        if masked:
            weights = jnp.where(visible_keys(place_ref, chunk, rows), weights, 0.0)
        return (
            total + jnp.sum(weights, axis=0, keepdims=True),
            summed + dot(turned_ref[:, pl.ds(start, chunk)], weights.astype(bf16)),
        )

    last = place_ref[1] * CELL + pl.program_id(0)
    running = (
        jnp.zeros((1, GROUP * rows), f32),
        jnp.zeros((2 * HEAD_DIM, GROUP * rows), f32),
    )
    running = lax.fori_loop(0, last, lambda n, r: step(n, r, False), running)
    total, summed = step(last, running, True)
    out_ref[...] = unstack_heads(summed[HEAD_DIM:] / total, rows)
    log_ref[...] = jnp.log(total)[None]


def attention(place, queries, keys_values, rows, chunk):
    count = queries.shape[0] // rows
    keys = keys_values.shape[0]
    return pl.pallas_call(
        functools.partial(attention_kernel, chunk),
        grid_spec=pltpu.PrefetchScalarGridSpec(
            num_scalar_prefetch=1,
            grid=(count,),
            in_specs=[
                pl.BlockSpec((rows, GROUP_WIDTH), lambda i, place: (i, 0)),
                pl.BlockSpec((keys, 2 * HEAD_DIM), lambda i, place: (0, 0)),
            ],
            out_specs=[
                pl.BlockSpec((rows, GROUP_WIDTH), lambda i, place: (i, 0)),
                pl.BlockSpec((1, 1, GROUP * rows), lambda i, place: (i, 0, 0)),
            ],
            scratch_shapes=[pltpu.VMEM((2 * HEAD_DIM, keys), bf16)],
        ),
        out_shape=[
            jax.ShapeDtypeStruct(queries.shape, f32),
            jax.ShapeDtypeStruct((count, 1, GROUP * rows), f32),
        ],
        compiler_params=pltpu.CompilerParams(vmem_limit_bytes=48 * 1024 * 1024),
        cost_estimate=pl.CostEstimate(
            flops=4 * HEADS * HEAD_DIM * rows * keys * 4,
            bytes_accessed=8 * 1024 * 1024,
            transcendentals=GROUP * rows * keys * 4,
        ),
    )(place, queries, keys_values)


def attention_grad_kernel(
    chunk, place_ref, q_ref, grad_ref, out_ref, log_ref, kv_ref, q_grad_ref, kv_grad_ref, turned_ref
):
    rows = q_ref.shape[0]
    fill_turned(place_ref, kv_ref, turned_ref, chunk)

    @pl.when(pl.program_id(0) == 0)
    def _():
        kv_grad_ref[...] = jnp.zeros_like(kv_grad_ref)

    queries = stack_heads(q_ref[...].astype(f32) * score_scale).astype(bf16)
    queries = jnp.concatenate([queries, jnp.zeros_like(queries)], axis=1)
    grads = stack_heads(grad_ref[...])
    row_delta = jnp.sum((grads.astype(f32) * stack_heads(out_ref[...])).T, axis=0, keepdims=True)
    grads = jnp.concatenate([jnp.zeros_like(grads), grads], axis=1)
    log_total = log_ref[0]

    def step(n, summed, masked):
        start = pl.multiple_of(n * chunk, chunk)
        block = kv_ref[pl.ds(start, chunk), :]
        weights = jnp.exp(dot(block, queries, NT) - log_total)
        if masked:
            weights = jnp.where(visible_keys(place_ref, chunk, rows), weights, 0.0)
        score_grad = (weights * (dot(block, grads, NT) - row_delta)).astype(bf16)
        kv_grad_ref[pl.ds(start, chunk), :] += dot(score_grad, queries) + dot(
            weights.astype(bf16), grads
        )
        return summed + dot(turned_ref[:, pl.ds(start, chunk)], score_grad)

    last = place_ref[1] * CELL + pl.program_id(0)
    summed = jnp.zeros((2 * HEAD_DIM, GROUP * rows), f32)
    summed = lax.fori_loop(0, last, lambda n, r: step(n, r, False), summed)
    summed = step(last, summed, True)
    q_grad_ref[...] = unstack_heads(summed[:HEAD_DIM] * score_scale, rows)


def attention_grad(place, queries, out_grad, attended, log_total, keys_values, rows, chunk):
    count = queries.shape[0] // rows
    keys = keys_values.shape[0]
    row_spec = pl.BlockSpec((rows, GROUP_WIDTH), lambda i, place: (i, 0))
    whole_spec = pl.BlockSpec((keys, 2 * HEAD_DIM), lambda i, place: (0, 0))
    return pl.pallas_call(
        functools.partial(attention_grad_kernel, chunk),
        grid_spec=pltpu.PrefetchScalarGridSpec(
            num_scalar_prefetch=1,
            grid=(count,),
            in_specs=[
                row_spec,
                row_spec,
                row_spec,
                pl.BlockSpec((1, 1, GROUP * rows), lambda i, place: (i, 0, 0)),
                whole_spec,
            ],
            out_specs=[row_spec, whole_spec],
            scratch_shapes=[pltpu.VMEM((2 * HEAD_DIM, keys), bf16)],
        ),
        out_shape=[
            jax.ShapeDtypeStruct(queries.shape, f32),
            jax.ShapeDtypeStruct(keys_values.shape, f32),
        ],
        compiler_params=pltpu.CompilerParams(vmem_limit_bytes=56 * 1024 * 1024),
        cost_estimate=pl.CostEstimate(
            flops=10 * HEADS * HEAD_DIM * rows * keys * 4,
            bytes_accessed=8 * 1024 * 1024,
            transcendentals=GROUP * rows * keys * 4,
        ),
    )(place, queries, out_grad, attended, log_total, keys_values)


def place_kernel(block_at, place_ref, shard_ref, *refs):
    refs[-1][...] = shard_ref[...].astype(f32)


def place_columns(whole, shape, shard, unit, place, block_at):
    rows, columns = shard.shape
    in_specs = [pl.BlockSpec((rows, unit), lambda g, place: (0, g))]
    operands = [place, shard]
    aliases = {}
    if whole is not None:
        in_specs.append(pl.BlockSpec(memory_space=pl.ANY))
        operands.append(whole)
        aliases = {2: 0}
    return pl.pallas_call(
        functools.partial(place_kernel, block_at),
        grid_spec=pltpu.PrefetchScalarGridSpec(
            num_scalar_prefetch=1,
            grid=(columns // unit,),
            in_specs=in_specs,
            out_specs=pl.BlockSpec((rows, unit), lambda g, place: (0, block_at(g, place))),
        ),
        out_shape=jax.ShapeDtypeStruct(shape, f32),
        input_output_aliases=aliases,
        cost_estimate=pl.CostEstimate(
            flops=0, bytes_accessed=6 * rows * columns, transcendentals=0
        ),
    )(*operands)


def body(
    inputs,
    attention_gain,
    qkv_weight,
    query_gain,
    key_gain,
    out_weight,
    mlp_gain,
    gate_up_weight,
    down_weight,
    cotangent,
):
    rows, width = inputs.shape
    fsdp_count = lax.axis_size("fsdp")
    cell_count = lax.axis_size("ctx") // CELL
    pair = 2 if fsdp_count % 2 == 0 else 1
    pair_count = fsdp_count // pair
    fsdp_here = lax.axis_index("fsdp")
    ctx_here = lax.axis_index("ctx")
    head = ctx_here % CELL
    cell = ctx_here // CELL
    in_pair = fsdp_here % pair
    pair_here = fsdp_here // pair
    weight_rows = qkv_weight.shape[0]
    query_width = HEADS * HEAD_DIM
    key_width = KV_HEADS * HEAD_DIM
    hidden_width = gate_up_weight.shape[1] // 2
    unit = hidden_width // (fsdp_count * CELL)
    place = jnp.stack([fsdp_here, cell]).astype(jnp.int32)

    def block(values, index, size, axis=0):
        return lax.dynamic_slice_in_dim(values, index * size, size, axis)

    def put(whole, part, index, axis=0):
        return lax.dynamic_update_slice_in_dim(whole, part, index * part.shape[axis], axis)

    def peer(distance):
        return jnp.bitwise_xor(head, distance)

    def cell_rows(shards):
        whole = blank((CELL * shards[0].shape[0],) + shards[0].shape[1:], shards[0].dtype)
        for distance, shard in enumerate(shards):
            whole = put(whole, shard, peer(distance))
        return whole

    def cell_pieces(values, axis=0):
        size = values.shape[axis] // CELL
        return [block(values, peer(distance), size, axis) for distance in range(CELL)]

    def fsdp_gather(shard):
        whole = blank((fsdp_count * shard.shape[0],) + shard.shape[1:], shard.dtype)
        whole = put(whole, shard, fsdp_here)
        for step in range(1, fsdp_count):
            whole = put(whole, fsdp_send(shard, step), (fsdp_here - step) % fsdp_count)
        return whole

    def cell_sum(values):
        total = values.astype(f32)
        for step in range(1, cell_count):
            total = total + cell_send(values.astype(bf16), step).astype(f32)
        return total

    def fsdp_reduce(values, size):
        total = block(values, fsdp_here, size).astype(f32)
        for step in range(1, fsdp_count):
            piece = block(values, (fsdp_here + step) % fsdp_count, size).astype(bf16)
            total = total + fsdp_send(piece, step).astype(f32)
        return cell_sum(total)

    def cell_turn(values, split_axis, join_axis):
        groups = None
        if cell_count > 1:
            groups = [[c * CELL + i for i in range(CELL)] for c in range(cell_count)]
        return lax.all_to_all(
            values, "ctx", split_axis, join_axis, axis_index_groups=groups, tiled=True
        )

    blocks_here = cell * CELL + jnp.arange(CELL, dtype=jnp.int32)
    positions = (
        ((blocks_here * fsdp_count + fsdp_here) * rows)[:, None]
        + jnp.arange(rows, dtype=jnp.int32)[None, :]
    ).reshape(-1)
    cell_tokens = CELL * rows
    half_dim = HEAD_DIM // 2
    frequency = theta ** (-jnp.arange(half_dim, dtype=f32) * 2.0 / HEAD_DIM)
    angles = positions.astype(f32)[:, None] * frequency[None, :]
    cosine = jnp.cos(angles)[:, None, :]
    sine = jnp.sin(angles)[:, None, :]

    def rotate(values):
        lower = values[..., :half_dim]
        upper = values[..., half_dim:]
        return jnp.concatenate(
            [lower * cosine - upper * sine, upper * cosine + lower * sine], axis=-1
        )

    def attention_inputs(values, q_gain, k_gain):
        queries = values[:, :GROUP_WIDTH].reshape(cell_tokens, GROUP, HEAD_DIM)
        key_rows = values[:, GROUP_WIDTH : GROUP_WIDTH + HEAD_DIM].reshape(
            cell_tokens, 1, HEAD_DIM
        )
        return (
            rotate(rms_scale(queries, q_gain)).reshape(cell_tokens, GROUP_WIDTH),
            rotate(rms_scale(key_rows, k_gain)).reshape(cell_tokens, HEAD_DIM),
            values[:, GROUP_WIDTH + HEAD_DIM :],
        )

    source = inputs.astype(f32)
    normed_attn_own = rms_scale(source, attention_gain).astype(bf16)
    normed_attn = cell_rows(gather_cell(normed_attn_own))
    qkv_columns = fsdp_gather(
        jnp.concatenate(
            [
                block(qkv_weight[:, :query_width], head, GROUP_WIDTH, 1),
                block(qkv_weight[:, query_width : query_width + key_width], head, HEAD_DIM, 1),
                block(qkv_weight[:, query_width + key_width :], head, HEAD_DIM, 1),
            ],
            axis=1,
        )
    )
    out_columns = fsdp_gather(block(out_weight, head, width // CELL, 1))
    out_rows = cell_turn(out_columns, 0, 1)

    def owner_columns(owner):
        return jnp.concatenate(
            [
                lax.dynamic_slice_in_dim(
                    gate_up_weight,
                    side * hidden_width + ((p * pair + owner) * CELL + head) * unit,
                    unit,
                    1,
                )
                for side in range(2)
                for p in range(pair_count)
            ],
            axis=1,
        )

    unit_columns = [owner_columns((in_pair + j) % pair) for j in range(pair)]
    local_units = pair_count * unit
    gate_up_mine = blank((width, 2 * local_units), bf16)
    gate_up_mine = put(gate_up_mine, unit_columns[0], fsdp_here)
    for step in range(1, fsdp_count):
        gate_up_mine = put(
            gate_up_mine,
            fsdp_send(unit_columns[step % pair], step),
            (fsdp_here - step) % fsdp_count,
        )
    down_own = block(down_weight, head, unit)
    down_mine = put(blank((local_units, width), bf16), down_own, pair_here)
    for step in range(1, pair_count):
        down_mine = put(
            down_mine, fsdp_send(down_own, step * pair), (pair_here - step) % pair_count
        )

    qkv_rows = dot(normed_attn, qkv_columns)
    query_rot, key_rot, value_rows = attention_inputs(qkv_rows, query_gain, key_gain)
    query_low = query_rot.astype(bf16)
    kv_own = jnp.concatenate([key_rot, value_rows], axis=1).astype(bf16)
    kv_own = kv_own.reshape(CELL, 1, rows, 2 * HEAD_DIM)
    kv_cells = blank((CELL, fsdp_count, rows, 2 * HEAD_DIM), bf16)
    kv_cells = put(kv_cells, kv_own, fsdp_here, 1)
    for step in range(1, fsdp_count):
        kv_cells = put(
            kv_cells, fsdp_send(kv_own, step), (fsdp_here - step) % fsdp_count, 1
        )
    chunk = fsdp_count * rows
    kv_cells = kv_cells.reshape(CELL * chunk, 2 * HEAD_DIM)
    if cell_count > 1:
        kv_all = put(
            blank((cell_count * CELL * chunk, 2 * HEAD_DIM), bf16), kv_cells, cell
        )
        for step in range(1, cell_count):
            kv_all = put(kv_all, cell_send(kv_cells, step), (cell - step) % cell_count)
    else:
        kv_all = kv_cells
    attended, log_total = attention(place, query_low, kv_all, rows, chunk)
    attended_low = attended.astype(bf16)
    out_partial = dot(attended_low, out_rows).astype(bf16)
    hidden_mid = source + reduce_cell(cell_pieces(out_partial))
    normed_mlp_own = rms_scale(hidden_mid, mlp_gain).astype(bf16)

    def pair_parts(own):
        shards = [own] + [pair_send(own, -j, pair) for j in range(1, pair)]
        return [cell_rows(gather_cell(shard)) for shard in shards]

    def pair_reduce(partials):
        total = None
        for j in reversed(range(pair)):
            summed = reduce_cell(cell_pieces(partials[j]))
            if j:
                summed = pair_send(summed.astype(bf16), j, pair).astype(f32)
            total = summed if total is None else total + summed
        return total

    cotangent_parts = pair_parts(cotangent)
    normed_parts = pair_parts(normed_mlp_own)
    gate_weight = gate_up_mine[:, :local_units]
    up_weight = gate_up_mine[:, local_units:]
    branch_partials, grad_partials, active_parts, gate_grads = [], [], [], []
    for j in range(pair):
        gate = dot(normed_parts[j], gate_weight)
        up = dot(normed_parts[j], up_weight)
        logistic = jax.nn.sigmoid(gate)
        active_low = (gate * logistic * up).astype(bf16)
        act_grad = dot(cotangent_parts[j], down_mine, NT)
        gate_part = act_grad * up * (logistic * (1.0 + gate * (1.0 - logistic)))
        up_part = act_grad * (gate * logistic)
        gate_grad = jnp.concatenate([gate_part.astype(bf16), up_part.astype(bf16)], axis=1)
        grad_partials.append(dot(gate_grad, gate_up_mine, NT).astype(bf16))
        branch_partials.append(dot(active_low, down_mine).astype(bf16))
        active_parts.append(active_low)
        gate_grads.append(gate_grad)
    normed_grad = pair_reduce(grad_partials)
    mid_part, mlp_gain_grad = jax.vjp(rms_scale, hidden_mid, mlp_gain)[1](normed_grad)
    hidden_grad = cotangent.astype(f32) + mid_part
    branch_grad = cell_rows(gather_cell(hidden_grad.astype(bf16)))

    down_partial = sum(dot(active_parts[j], cotangent_parts[j], TN) for j in range(pair))
    gate_up_partial = sum(dot(normed_parts[j], gate_grads[j], TN) for j in range(pair))
    gate_up_partial = gate_up_partial.astype(bf16)

    out_grad = dot(branch_grad, out_rows, NT).astype(bf16)
    query_grad, kv_grad = attention_grad(
        place, query_low, out_grad, attended, log_total, kv_all, rows, chunk
    )
    kv_grad = kv_grad.astype(bf16)
    if cell_count > 1:
        kv_grad_cell = block(kv_grad, cell, CELL * chunk).astype(f32)
        for step in range(1, cell_count):
            piece = block(kv_grad, (cell + step) % cell_count, CELL * chunk)
            kv_grad_cell = kv_grad_cell + cell_send(piece, step).astype(f32)
        kv_grad = kv_grad_cell.astype(bf16)
    kv_grad = kv_grad.reshape(CELL, fsdp_count, rows, 2 * HEAD_DIM)
    kv_total = block(kv_grad, fsdp_here, 1, 1).astype(f32)
    for step in range(1, fsdp_count):
        piece = block(kv_grad, (fsdp_here + step) % fsdp_count, 1, 1)
        kv_total = kv_total + fsdp_send(piece, step).astype(f32)
    kv_total = kv_total.reshape(cell_tokens, 2 * HEAD_DIM)
    pull_back = jax.vjp(attention_inputs, qkv_rows, query_gain, key_gain)[1]
    qkv_grad, query_gain_grad, key_gain_grad = pull_back(
        (query_grad, kv_total[:, :HEAD_DIM], kv_total[:, HEAD_DIM:])
    )
    qkv_grad_low = qkv_grad.astype(bf16)
    attn_partial = dot(qkv_grad_low, qkv_columns, NT).astype(bf16)
    attn_normed_grad = reduce_cell(cell_pieces(attn_partial))
    source_part, attention_gain_grad = jax.vjp(rms_scale, source, attention_gain)[1](
        attn_normed_grad
    )
    grad_inputs = (hidden_grad + source_part).astype(bf16)
    gain_sums = lax.psum(
        (attention_gain_grad, query_gain_grad, key_gain_grad, mlp_gain_grad), ("ctx", "fsdp")
    )

    outputs = (hidden_mid + pair_reduce(branch_partials)).astype(bf16)

    down_total = block(down_partial, pair_here, unit)
    for step in range(1, pair_count):
        piece = block(down_partial, (pair_here + step) % pair_count, unit).astype(bf16)
        down_total = down_total + fsdp_send(piece, step * pair).astype(f32)
    down_total = cell_sum(down_total).astype(bf16)
    grad_down = blank((CELL * unit, width), f32)
    for distance, shard in enumerate(gather_cell(down_total)):
        grad_down = put(grad_down, shard.astype(f32), peer(distance))

    pair_rows = pair * weight_rows
    gate_up_total = block(gate_up_partial, pair_here, pair_rows).astype(f32)
    for step in range(1, pair_count):
        piece = block(gate_up_partial, (pair_here + step) % pair_count, pair_rows)
        gate_up_total = gate_up_total + fsdp_send(piece, step * pair).astype(f32)
    gate_up_total = cell_sum(gate_up_total).astype(bf16)
    grad_gate_up = None
    for j in range(pair):
        part = block(gate_up_total, (in_pair + j) % pair, weight_rows)
        if j:
            part = pair_send(part, j, pair)
        owner = (in_pair - j) % pair
        for distance, shard in enumerate(gather_cell(part)):
            grad_gate_up = place_columns(
                grad_gate_up,
                gate_up_weight.shape,
                shard,
                unit,
                jnp.stack([owner, peer(distance)]).astype(jnp.int32),
                lambda g, at: (
                    (g // pair_count) * (hidden_width // unit)
                    + ((g % pair_count) * pair + at[0]) * CELL
                    + at[1]
                ),
            )

    out_partial_grad = dot(attended_low, branch_grad, TN).astype(bf16)
    out_total = fsdp_reduce(cell_turn(out_partial_grad, 1, 0), weight_rows).astype(bf16)
    grad_out = blank((weight_rows, width), f32)
    for distance, shard in enumerate(gather_cell(out_total)):
        grad_out = put(grad_out, shard.astype(f32), peer(distance), 1)

    qkv_partial = dot(normed_attn, qkv_grad_low, TN).astype(bf16)
    qkv_total = fsdp_reduce(qkv_partial, weight_rows).astype(bf16)
    stacked = cell_rows([shard[None] for shard in gather_cell(qkv_total)])
    side = stacked.transpose(1, 0, 2)
    grad_qkv = jnp.concatenate(
        [
            side[:, :, :GROUP_WIDTH].reshape(weight_rows, query_width),
            side[:, :, GROUP_WIDTH : GROUP_WIDTH + HEAD_DIM].reshape(weight_rows, key_width),
            side[:, :, GROUP_WIDTH + HEAD_DIM :].reshape(weight_rows, key_width),
        ],
        axis=1,
    ).astype(f32)

    return (
        outputs,
        grad_inputs,
        gain_sums[0],
        grad_qkv,
        gain_sums[1],
        gain_sums[2],
        grad_out,
        gain_sums[3],
        grad_gate_up,
        grad_down,
    )


def solution(mesh):
    return jax.shard_map(
        body,
        mesh=mesh,
        in_specs=(
            P(("ctx", "fsdp"), None),
            P(),
            P("fsdp", None),
            P(),
            P(),
            P("fsdp", None),
            P(),
            P("fsdp", None),
            P("fsdp", None),
            P(("ctx", "fsdp"), None),
        ),
        out_specs=(
            P(("ctx", "fsdp"), None),
            P(("ctx", "fsdp"), None),
            P(),
            P("fsdp", None),
            P(),
            P(),
            P("fsdp", None),
            P(),
            P("fsdp", None),
            P("fsdp", None),
        ),
        check_vma=False,
    )
```

time: 4970 us -> 1090 us (0.22)
  waiting for transfers between devices: 4530 us -> 411 us
  starting transfers between devices: 0.98 us -> 179 us
  matrix products: 233 us -> 85.8 us
  Pallas kernels: 0 us -> 128 us
  local copies, waits for them, and re-layouts: 45.3 us -> 137 us
    all_gather x6 -> x0, waiting for transfers between devices: 2020 us -> none  [the longest x4 1970 us: weights_forward(): lax.all_gather(shard, 'fsdp', axis=0, tiled=True)]
    unnamed x17 -> x0, waiting for transfers between devices: 1660 us -> none
    reduce_scatter x6 -> x0, waiting for transfers between devices: 550 us -> none  [the longest x2 305 us: weights_backward(): lax.psum_scatter(lax.dot_general(saved, gradient, (((0,), (0,)), ((), ())...]
    ppermute x0 -> x165, waiting for transfers between devices: none -> 411 us  [the longest x24 214 us: fsdp_send(): lax.ppermute(values, 'fsdp', [(i, (i + step) % count) for i in range(coun...]
    psum x1 -> x0, waiting for transfers between devices: 303 us -> none  [body(): lax.psum(grad_qkv.astype(jnp.bfloat16), 'ctx').astype(jnp.float32)]
    ppermute x0 -> x165, starting transfers between devices: none -> 171 us  [the longest x136 81.9 us: xor_send(): lax.ppermute(values, 'ctx', [(i, i ^ distance) for i in range(count)])]
    dot_general x19 -> x20, matrix products: 233 us -> 85.8 us  [dot(): return lax.dot_general(left, right, dims, preferred_element_type=f32)]
    pallas_call x0 -> x32, Pallas kernels: none -> 128 us  [the longest x16 68.7 us: place_columns(): pl.pallas_call(functools.partial(place_kernel, block_at), grid_spec=pltpu...]
  transfers between devices with their start and end apart: 15 -> 167, of which waited for: 15 -> 42; matrix products, arithmetic and copies ran while one was open for 3% -> 28% of each run, Pallas kernels for 0% -> 11%
where the time goes in v1:
time: 1090 us; the launch traced here: 1080 us
  waiting for transfers between devices  411 us (38%)
  starting transfers between devices  179 us (16%)
  local copies, waits for them, and re-layouts  137 us (13%)
  Pallas kernels  128 us (12%)
  other arithmetic  91.9 us (8%)
  matrix products  85.8 us (8%)
  blocking collectives  43.1 us (4%)
    ppermute x24, waiting for transfers between devices, fsdp_send(): lax.ppermute(values, 'fsdp', [(i, (i + step) % count) for i in range(coun...  214 us
    ppermute x136, waiting for transfers between devices, xor_send(): lax.ppermute(values, 'ctx', [(i, i ^ distance) for i in range(count)])  154 us
    dot_general x20, matrix products, dot(): return lax.dot_general(left, right, dims, preferred_element_type=f32)  85.8 us
    ppermute x136, starting transfers between devices, xor_send(): lax.ppermute(values, 'ctx', [(i, i ^ distance) for i in range(count)])  81.9 us
    ppermute x24, starting transfers between devices, fsdp_send(): lax.ppermute(values, 'fsdp', [(i, (i + step) % count) for i in range(coun...  72.4 us
    pallas_call x16, Pallas kernels, place_columns(): pl.pallas_call(functools.partial(place_kernel, block_at), grid_spec=pltpu...  68.7 us
    dynamic_update_slice x67, local copies, waits for them, and re-layouts, put(): lax.dynamic_update_slice_in_dim(whole, part, index * part.shape[axis], axis)  47.5 us
    psum x1, blocking collectives, body(): lax.psum((attention_gain_grad, query_gain_grad, key_gain_grad, mlp_gain_g...  43.1 us
  transfers between devices with their start and end apart: 167, of which 42 were waited for; matrix products, arithmetic and copies ran while one was open for 28% of the time, Pallas kernels for 11%

profile of v1, /device:TPU:0, one launch (start us, length us, event | category | flops | bytes accessed | tf_op | source)
XLA Modules:
  0.0 1080.9 jit_solution(6699348430211101315)
XLA Ops:
  38.0 14.1 %collective-permute-done.15 = bf16[512,256]{1,0:T(8,128)(2,1)} collective-permute-done((bf16[512,256]{1,0:T(8,128)(2,1)}, bf16[512,256]{1,0:T(8,128)(2,1)}, u32[]{:S(2)}, u32[]{:S(2)}) %collective-permute-start.15) | collective-permute-done | bytes 262176 | tf_op jit(solution)/shard_map/ppermute | solution.py:50
  73.3 11.2 %collective-permute-start.63 = (bf16[128,2048]{1,0:T(8,128)(2,1)S(1)}, bf16[128,2048]{1,0:T(8,128)(2,1)S(1)}, u32[]{:S(2)}, u32[]{:S(2)}) collective-permute-start(bf16[128,2048]{1,0:T(8,128)(2,1)S(1)} %copy-done.18), channel_id=1, source_target_pairs={{0,1},{1,0},{2,3},{3,2},{4,5},{5,4},{6,7},{7,6},{8,9},{9,8},{10,11... | collective-permute-start | bytes 1572872 | tf_op jit(solution)/shard_map/ppermute | solution.py:55
  87.3 12.7 %collective-permute-start.34 = (bf16[512,1024]{1,0:T(8,128)(2,1)S(1)}, bf16[512,1024]{1,0:T(8,128)(2,1)S(1)}, u32[]{:S(2)}, u32[]{:S(2)}) collective-permute-start(bf16[512,1024]{1,0:T(8,128)(2,1)S(1)} %copy-done.64), channel_id=1, source_target_pairs={{0,1},{1,2},{2,3},{3,0},{4,5},{5,6},{6,7},{7,4},{8,9},{9,10},{10,1... | collective-permute-start | bytes 3145736 | tf_op jit(solution)/shard_map/ppermute | solution.py:50
  132.4 37.9 %collective-permute-done.35 = bf16[512,1024]{1,0:T(8,128)(2,1)S(1)} collective-permute-done((bf16[512,1024]{1,0:T(8,128)(2,1)S(1)}, bf16[512,1024]{1,0:T(8,128)(2,1)S(1)}, u32[]{:S(2)}, u32[]{:S(2)}) %collective-permute-start.35) | collective-permute-done | bytes 1048608 | tf_op jit(solution)/shard_map/ppermute | solution.py:50
  183.6 31.5 %collective-permute-done.37 = bf16[256,2048]{1,0:T(8,128)(2,1)S(1)} collective-permute-done((bf16[256,2048]{1,0:T(8,128)(2,1)S(1)}, bf16[256,2048]{1,0:T(8,128)(2,1)S(1)}, u32[]{:S(2)}, u32[]{:S(2)}) %collective-permute-start.37) | collective-permute-done | bytes 1048608 | tf_op jit(solution)/shard_map/ppermute | solution.py:50
  226.1 24.2 %collective-permute-start.11 = (bf16[8,1,128,128]{3,2,1,0:T(8,128)(2,1)}, bf16[8,1,128,128]{3,2,1,0:T(8,128)(2,1)}, u32[]{:S(2)}, u32[]{:S(2)}) collective-permute-start(bf16[8,1,128,128]{3,2,1,0:T(8,128)(2,1)} %get-tuple-element.57), channel_id=1, source_target_pairs={{0,1},{1,2},{2,3},{3,0},{4,5},{5,6},{6,7},{7,4},{8,9},{9,10},{10,1... | collective-permute-start | bytes 786440 | tf_op jit(solution)/shard_map/ppermute | solution.py:50
  261.0 10.0 collective-permute-done.12
  272.0 21.9 %shard_map.180 = (f32[1024,256]{1,0:T(8,128)S(1)}, f32[8,1,512]{2,1,0:T(1,128)S(1)}) custom-call(s32[2]{0:T(128)S(1)} %pad_add_fusion.2.place_ref, bf16[1024,256]{1,0:T(8,128)(2,1)S(1)} %copy.46.q_ref, bf16[4096,128]{1,0:T(8,128)(2,1)S(1)} %bitcast.101), custom_call_target="tpu_custom_call" | custom-call | flops 17179869184 | bytes 8388608 | tf_op jit(solution)/shard_map/pallas_call | solution.py:164
  318.6 8.0 collective-permute-done.24
  354.5 11.1 %collective-permute-done.29 = bf16[128,2048]{1,0:T(8,128)(2,1)S(1)} collective-permute-done((bf16[128,2048]{1,0:T(8,128)(2,1)S(1)}, bf16[128,2048]{1,0:T(8,128)(2,1)S(1)}, u32[]{:S(2)}, u32[]{:S(2)}) %collective-permute-start.29) | collective-permute-done | bytes 524320 | tf_op jit(solution)/shard_map/ppermute | solution.py:40
  377.4 6.4 convolution_convert_fusion.4
  398.9 6.2 multiply_convert_fusion.3
  405.2 7.5 convolution_convert_fusion.5
  412.6 8.5 fusion.10
  442.0 7.8 add_convert_fusion
  461.8 5.8 collective-permute-done.61
  469.1 6.2 collective-permute-done.58
  501.9 10.8 collective-permute-done.79
  516.3 57.7 %collective-permute-done.156 = bf16[256,2048]{1,0:T(8,128)(2,1)S(1)} collective-permute-done((bf16[256,2048]{1,0:T(8,128)(2,1)S(1)}, bf16[256,2048]{1,0:T(8,128)(2,1)S(1)}, u32[]{:S(2)}, u32[]{:S(2)}) %collective-permute-start.156) | collective-permute-done | bytes 1048608 | tf_op jit(solution)/shard_map/ppermute | solution.py:50
  579.2 7.6 collective-permute-done.96
  589.0 40.6 %collective-permute-done.80 = bf16[128,2048]{1,0:T(8,128)(2,1)S(1)} collective-permute-done((bf16[128,2048]{1,0:T(8,128)(2,1)S(1)}, bf16[128,2048]{1,0:T(8,128)(2,1)S(1)}, u32[]{:S(2)}, u32[]{:S(2)}) %collective-permute-start.80) | collective-permute-done | bytes 524320 | tf_op jit(solution)/shard_map/ppermute | solution.py:55
  661.7 25.6 %collective-permute-done.102 = bf16[64,2048]{1,0:T(8,128)(2,1)S(1)} collective-permute-done((bf16[64,2048]{1,0:T(8,128)(2,1)S(1)}, bf16[64,2048]{1,0:T(8,128)(2,1)S(1)}, u32[]{:S(2)}, u32[]{:S(2)}) %collective-permute-start.102) | collective-permute-done | bytes 262176 | tf_op jit(solution)/shard_map/ppermute | solution.py:40
  731.5 37.9 %shard_map.189 = (f32[1024,256]{1,0:T(8,128)}, f32[4096,128]{1,0:T(8,128)}) custom-call(s32[2]{0:T(128)} %copy-done.5, bf16[1024,256]{1,0:T(8,128)(2,1)} %copy-done.4, bf16[1024,256]{1,0:T(8,128)(2,1)} %convolution_convert_fusion.8.grad_ref, f32[1024,256]{1,0:T(8,128)} %copy-done, f32[8,1,512]{2,1,0:T(1,128)} %copy-done.6, bf16[4096,128]{1,0:T(8,128)(2,1)} %bitcast.102), custom_call_target="tpu_custom_call" | custom-call | flops 42949672960 | bytes 8388608 | tf_op jit(solution)/shard_map/pallas_call | solution.py:233
  794.9 8.4 collective-permute-done.106
  822.7 8.6 collective-permute-done.118
  835.5 18.1 %collective-permute-done.117 = bf16[512,384]{1,0:T(8,128)(2,1)S(1)} collective-permute-done((bf16[512,384]{1,0:T(8,128)(2,1)S(1)}, bf16[512,384]{1,0:T(8,128)(2,1)S(1)}, u32[]{:S(2)}, u32[]{:S(2)}) %collective-permute-start.117) | collective-permute-done | bytes 393248 | tf_op jit(solution)/shard_map/ppermute | solution.py:50
  854.5 12.0 %collective-permute-done.116 = bf16[512,384]{1,0:T(8,128)(2,1)S(1)} collective-permute-done((bf16[512,384]{1,0:T(8,128)(2,1)S(1)}, bf16[512,384]{1,0:T(8,128)(2,1)S(1)}, u32[]{:S(2)}, u32[]{:S(2)}) %collective-permute-start.116) | collective-permute-done | bytes 393248 | tf_op jit(solution)/shard_map/ppermute | solution.py:50
  897.2 10.4 collective-permute-done.111
  912.1 12.8 %collective-permute-done.128 = bf16[512,256]{1,0:T(8,128)(2,1)S(1)} collective-permute-done((bf16[512,256]{1,0:T(8,128)(2,1)}, bf16[512,256]{1,0:T(8,128)(2,1)S(1)}, u32[]{:S(2)}, u32[]{:S(2)}) %collective-permute-start.128) | collective-permute-done | bytes 262176 | tf_op jit(solution)/shard_map/ppermute | solution.py:50
  934.8 13.0 %collective-permute-done.131 = bf16[512,256]{1,0:T(8,128)(2,1)S(1)} collective-permute-done((bf16[512,256]{1,0:T(8,128)(2,1)S(1)}, bf16[512,256]{1,0:T(8,128)(2,1)S(1)}, u32[]{:S(2)}, u32[]{:S(2)}) %collective-permute-start.131) | collective-permute-done | bytes 262176 | tf_op jit(solution)/shard_map/ppermute | solution.py:40
  982.4 43.1 %all-reduce.7 = (f32[2048]{0:T(1024)}, f32[64]{0:T(128)}, f32[64]{0:T(128)}, f32[2048]{0:T(1024)}) all-reduce(f32[2048]{0:T(1024)} %get-tuple-element.32, f32[64]{0:T(128)} %get-tuple-element.34, f32[64]{0:T(128)} %get-tuple-element.30, f32[2048]{0:T(1024)} %get-tuple-element.28), channel_id=1, replica_groups=mesh['ctx'=8,'fsdp'=4] {'ctx','fsdp'}, use_global_device_ids=true, to_apply=%region_9.10 | all-reduce | flops 4224 | bytes 33792 | tf_op jit(solution)/shard_map/psum | solution.py:540
  1046.7 6.6 copy.56
  (854 shorter events, 532.6 us)
Async XLA Ops:
  3.8 57.5 %collective-permute-start.8 = (bf16[512,384]{1,0:T(8,128)(2,1)}, bf16[512,384]{1,0:T(8,128)(2,1)}, u32[]{:S(2)}, u32[]{:S(2)}) collective-permute-start(bf16[512,384]{1,0:T(8,128)(2,1)} %get-tuple-element.59), channel_id=1, source_target_pairs={{0,1},{1,2},{2,3},{3,0},{4,5},{5,6},{6,7},{7,4},{8,9},{9,10},{10,1... | collective-permute-start | bytes 1179656 | tf_op jit(solution)/shard_map/ppermute | solution.py:50
  6.8 56.9 %collective-permute-start.9 = (bf16[512,384]{1,0:T(8,128)(2,1)}, bf16[512,384]{1,0:T(8,128)(2,1)}, u32[]{:S(2)}, u32[]{:S(2)}) collective-permute-start(bf16[512,384]{1,0:T(8,128)(2,1)} %get-tuple-element.59), channel_id=1, source_target_pairs={{0,2},{1,3},{2,0},{3,1},{4,6},{5,7},{6,4},{7,5},{8,10},{9,11},{10,... | collective-permute-start | bytes 1179656 | tf_op jit(solution)/shard_map/ppermute | solution.py:50
  57.0 237.6 %all-to-all-start = ((bf16[8,256,256]{1,2,0:T(8,128)(2,1)}), bf16[8,256,256]{1,2,0:T(8,128)(2,1)}, u32[]{:S(2)}, u32[]{:S(2)}) async-start(bf16[8,256,256]{1,2,0:T(8,128)(2,1)} %copy.47), calls=%async_computation | async-start | bytes 2097152 | tf_op jit(solution)/shard_map/all_to_all | solution.py:363
  100.0 70.3 %collective-permute-start.35 = (bf16[512,1024]{1,0:T(8,128)(2,1)S(1)}, bf16[512,1024]{1,0:T(8,128)(2,1)S(1)}, u32[]{:S(2)}, u32[]{:S(2)}) collective-permute-start(bf16[512,1024]{1,0:T(8,128)(2,1)S(1)} %copy-done.65), channel_id=1, source_target_pairs={{0,2},{1,3},{2,0},{3,1},{4,6},{5,7},{6,4},{7,5},{8,10},{9,11},{10,... | collective-permute-start | bytes 3145736 | tf_op jit(solution)/shard_map/ppermute | solution.py:50
  120.6 54.6 %collective-permute-start.85 = (bf16[128,2048]{1,0:T(8,128)(2,1)S(1)}, bf16[128,2048]{1,0:T(8,128)(2,1)S(1)}, u32[]{:S(2)}, u32[]{:S(2)}) collective-permute-start(bf16[128,2048]{1,0:T(8,128)(2,1)S(1)} %collective-permute-done.84), channel_id=1, source_target_pairs={{0,4},{4,0},{8,12},{12,8},{16,20},{20,16},{24,28},{28,24},{1,5},{5... | collective-permute-start | bytes 1572872 | tf_op jit(solution)/shard_map/ppermute | solution.py:40
  121.3 52.0 %collective-permute-start.65 = (bf16[128,2048]{1,0:T(8,128)(2,1)S(1)}, bf16[128,2048]{1,0:T(8,128)(2,1)}, u32[]{:S(2)}, u32[]{:S(2)}) collective-permute-start(bf16[128,2048]{1,0:T(8,128)(2,1)S(1)} %collective-permute-done.63), channel_id=1, source_target_pairs={{0,8},{4,12},{8,0},{12,4},{16,24},{20,28},{24,16},{28,20},{1,9},{5... | collective-permute-start | bytes 1572872 | tf_op jit(solution)/shard_map/ppermute | solution.py:40
  126.9 53.8 %collective-permute-start.36 = (bf16[512,1024]{1,0:T(8,128)(2,1)S(1)}, bf16[512,1024]{1,0:T(8,128)(2,1)S(1)}, u32[]{:S(2)}, u32[]{:S(2)}) collective-permute-start(bf16[512,1024]{1,0:T(8,128)(2,1)S(1)} %copy-done.64), channel_id=1, source_target_pairs={{0,3},{1,0},{2,1},{3,2},{4,7},{5,4},{6,5},{7,6},{8,11},{9,8},{10,9... | collective-permute-start | bytes 3145736 | tf_op jit(solution)/shard_map/ppermute | solution.py:50
  175.2 50.9 %collective-permute-start.88 = (bf16[128,2048]{1,0:T(8,128)(2,1)}, bf16[128,2048]{1,0:T(8,128)(2,1)}, u32[]{:S(2)}, u32[]{:S(2)}) collective-permute-start(bf16[128,2048]{1,0:T(8,128)(2,1)} %constant_dynamic-update-slice_fusion.8), channel_id=1, source_target_pairs={{0,4},{4,0},{8,12},{12,8},{16,20},{20,16},{24,28},{28,24},{1,5},{5... | collective-permute-start | bytes 1572872 | tf_op jit(solution)/shard_map/ppermute | solution.py:40
  178.3 74.1 %collective-permute-start.69 = (bf16[64,2048]{1,0:T(8,128)(2,1)}, bf16[64,2048]{1,0:T(8,128)(2,1)}, u32[]{:S(2)}, u32[]{:S(2)}) collective-permute-start(bf16[64,2048]{1,0:T(8,128)(2,1)} %slice.336), channel_id=1, source_target_pairs={{0,8},{4,12},{8,0},{12,4},{16,24},{20,28},{24,16},{28,20},{1,9},{5... | collective-permute-start | bytes 786440 | tf_op jit(solution)/shard_map/ppermute | solution.py:40
  180.7 75.6 %collective-permute-start.70 = (bf16[64,2048]{1,0:T(8,128)(2,1)}, bf16[64,2048]{1,0:T(8,128)(2,1)}, u32[]{:S(2)}, u32[]{:S(2)}) collective-permute-start(bf16[64,2048]{1,0:T(8,128)(2,1)} %slice.337), channel_id=1, source_target_pairs={{0,16},{4,20},{8,24},{12,28},{16,0},{20,4},{24,8},{28,12},{1,17},{... | collective-permute-start | bytes 786440 | tf_op jit(solution)/shard_map/ppermute | solution.py:40
  215.2 89.2 %collective-permute-start.66 = (bf16[128,2048]{1,0:T(8,128)(2,1)}, bf16[128,2048]{1,0:T(8,128)(2,1)}, u32[]{:S(2)}, u32[]{:S(2)}) collective-permute-start(bf16[128,2048]{1,0:T(8,128)(2,1)} %collective-permute-done.65), channel_id=1, source_target_pairs={{0,4},{4,0},{8,12},{12,8},{16,20},{20,16},{24,28},{28,24},{1,5},{5... | collective-permute-start | bytes 1572872 | tf_op jit(solution)/shard_map/ppermute | solution.py:40
  215.3 102.0 %collective-permute-start.68 = (bf16[128,2048]{1,0:T(8,128)(2,1)}, bf16[128,2048]{1,0:T(8,128)(2,1)}, u32[]{:S(2)}, u32[]{:S(2)}) collective-permute-start(bf16[128,2048]{1,0:T(8,128)(2,1)} %collective-permute-done.67), channel_id=1, source_target_pairs={{0,4},{4,0},{8,12},{12,8},{16,20},{20,16},{24,28},{28,24},{1,5},{5... | collective-permute-start | bytes 1572872 | tf_op jit(solution)/shard_map/ppermute | solution.py:40
  478.5 95.5 %collective-permute-start.156 = (bf16[256,2048]{1,0:T(8,128)(2,1)S(1)}, bf16[256,2048]{1,0:T(8,128)(2,1)S(1)}, u32[]{:S(2)}, u32[]{:S(2)}) collective-permute-start(bf16[256,2048]{1,0:T(8,128)(2,1)S(1)} %dynamic-slice_convert_fusion), channel_id=1, source_target_pairs={{0,2},{1,3},{2,0},{3,1},{4,6},{5,7},{6,4},{7,5},{8,10},{9,11},{10,... | collective-permute-start | bytes 3145736 | tf_op jit(solution)/shard_map/ppermute | solution.py:50
  500.3 74.3 %collective-permute-start.45 = (bf16[128,2048]{1,0:T(8,128)(2,1)S(1)}, bf16[128,2048]{1,0:T(8,128)(2,1)S(1)}, u32[]{:S(2)}, u32[]{:S(2)}) collective-permute-start(bf16[128,2048]{1,0:T(8,128)(2,1)S(1)} %pad_maximum_fusion.12), channel_id=1, source_target_pairs={{0,16},{4,20},{8,24},{12,28},{16,0},{20,4},{24,8},{28,12},{1,17},{... | collective-permute-start | bytes 1572872 | tf_op jit(solution)/shard_map/ppermute | solution.py:40
  512.7 63.4 %collective-permute-start.42 = (bf16[128,2048]{1,0:T(8,128)(2,1)S(1)}, bf16[128,2048]{1,0:T(8,128)(2,1)S(1)}, u32[]{:S(2)}, u32[]{:S(2)}) collective-permute-start(bf16[128,2048]{1,0:T(8,128)(2,1)S(1)} %pad_maximum_fusion.11), channel_id=1, source_target_pairs={{0,8},{4,12},{8,0},{12,4},{16,24},{20,28},{24,16},{28,20},{1,9},{5... | collective-permute-start | bytes 1572872 | tf_op jit(solution)/shard_map/ppermute | solution.py:40
  515.2 64.1 %collective-permute-start.89 = (bf16[128,2048]{1,0:T(8,128)(2,1)S(1)}, bf16[128,2048]{1,0:T(8,128)(2,1)S(1)}, u32[]{:S(2)}, u32[]{:S(2)}) collective-permute-start(bf16[128,2048]{1,0:T(8,128)(2,1)S(1)} %copy-done.76), channel_id=1, source_target_pairs={{0,4},{4,0},{8,12},{12,8},{16,20},{20,16},{24,28},{28,24},{1,5},{5... | collective-permute-start | bytes 1572872 | tf_op jit(solution)/shard_map/ppermute | solution.py:40
  515.5 120.4 %collective-permute-start.138 = (bf16[1024,1024]{1,0:T(8,128)(2,1)S(1)}, bf16[1024,1024]{1,0:T(8,128)(2,1)S(1)}, u32[]{:S(2)}, u32[]{:S(2)}) collective-permute-start(bf16[1024,1024]{1,0:T(8,128)(2,1)S(1)} %constant_dynamic-slice_fusion.2), channel_id=1, source_target_pairs={{0,2},{1,3},{2,0},{3,1},{4,6},{5,7},{6,4},{7,5},{8,10},{9,11},{10,... | collective-permute-start | bytes 6291464 | tf_op jit(solution)/shard_map/ppermute | solution.py:50
  576.1 53.5 %collective-permute-start.80 = (bf16[128,2048]{1,0:T(8,128)(2,1)S(1)}, bf16[128,2048]{1,0:T(8,128)(2,1)S(1)}, u32[]{:S(2)}, u32[]{:S(2)}) collective-permute-start(bf16[128,2048]{1,0:T(8,128)(2,1)S(1)} %add_convert_fusion.12), channel_id=1, source_target_pairs={{0,1},{1,0},{2,3},{3,2},{4,5},{5,4},{6,7},{7,6},{8,9},{9,8},{10,11... | collective-permute-start | bytes 1572872 | tf_op jit(solution)/shard_map/ppermute | solution.py:55
  579.2 59.4 %collective-permute-start.157 = (bf16[256,2048]{1,0:T(8,128)(2,1)S(1)}, bf16[256,2048]{1,0:T(8,128)(2,1)S(1)}, u32[]{:S(2)}, u32[]{:S(2)}) collective-permute-start(bf16[256,2048]{1,0:T(8,128)(2,1)S(1)} %get-tuple-element.41), channel_id=1, source_target_pairs={{0,4},{4,0},{8,12},{12,8},{16,20},{20,16},{24,28},{28,24},{1,5},{5... | collective-permute-start | bytes 3145736 | tf_op jit(solution)/shard_map/ppermute | solution.py:40
  586.9 54.8 %collective-permute-start.158 = (bf16[256,2048]{1,0:T(8,128)(2,1)S(1)}, bf16[256,2048]{1,0:T(8,128)(2,1)S(1)}, u32[]{:S(2)}, u32[]{:S(2)}) collective-permute-start(bf16[256,2048]{1,0:T(8,128)(2,1)S(1)} %get-tuple-element.41), channel_id=1, source_target_pairs={{0,8},{4,12},{8,0},{12,4},{16,24},{20,28},{24,16},{28,20},{1,9},{5... | collective-permute-start | bytes 3145736 | tf_op jit(solution)/shard_map/ppermute | solution.py:40
  638.6 63.3 %collective-permute-start.148 = (bf16[512,1024]{1,0:T(8,128)(2,1)S(1)}, bf16[512,1024]{1,0:T(8,128)(2,1)}, u32[]{:S(2)}, u32[]{:S(2)}) collective-permute-start(bf16[512,1024]{1,0:T(8,128)(2,1)S(1)} %get-tuple-element.124.shard_ref), channel_id=1, source_target_pairs={{0,16},{4,20},{8,24},{12,28},{16,0},{20,4},{24,8},{28,12},{1,17},{... | collective-permute-start | bytes 3145736 | tf_op jit(solution)/shard_map/ppermute | solution.py:40
  651.0 52.8 %collective-permute-start.150 = (bf16[512,1024]{1,0:T(8,128)(2,1)}, bf16[512,1024]{1,0:T(8,128)(2,1)}, u32[]{:S(2)}, u32[]{:S(2)}) collective-permute-start(bf16[512,1024]{1,0:T(8,128)(2,1)} %copy-done.21), channel_id=1, source_target_pairs={{0,8},{4,12},{8,0},{12,4},{16,24},{20,28},{24,16},{28,20},{1,9},{5... | collective-permute-start | bytes 3145736 | tf_op jit(solution)/shard_map/ppermute | solution.py:40
  699.1 92.4 %collective-permute-start.139 = (bf16[512,1024]{1,0:T(8,128)(2,1)}, bf16[512,1024]{1,0:T(8,128)(2,1)}, u32[]{:S(2)}, u32[]{:S(2)}) collective-permute-start(bf16[512,1024]{1,0:T(8,128)(2,1)} %get-tuple-element.125), channel_id=1, source_target_pairs={{0,1},{1,0},{2,3},{3,2},{4,5},{5,4},{6,7},{7,6},{8,9},{9,8},{10,11... | collective-permute-start | bytes 3145736 | tf_op jit(solution)/shard_map/ppermute | solution.py:55
  707.1 111.6 %collective-permute-start.164 = (bf16[256,2048]{1,0:T(8,128)(2,1)}, bf16[256,2048]{1,0:T(8,128)(2,1)}, u32[]{:S(2)}, u32[]{:S(2)}) collective-permute-start(bf16[256,2048]{1,0:T(8,128)(2,1)} %constant_dynamic-update-slice_fusion.20), channel_id=1, source_target_pairs={{0,4},{4,0},{8,12},{12,8},{16,20},{20,16},{24,28},{28,24},{1,5},{5... | collective-permute-start | bytes 3145736 | tf_op jit(solution)/shard_map/ppermute | solution.py:40
  783.4 85.2 %all-to-all-start.1 = ((bf16[256,8,256]{2,0,1:T(8,128)(2,1)}), bf16[256,8,256]{2,0,1:T(8,128)(2,1)}, u32[]{:S(2)}, u32[]{:S(2)}) async-start(bf16[256,8,256]{2,0,1:T(8,128)(2,1)} %bitcast.110), calls=%async_computation.1 | async-start | bytes 2097152 | tf_op jit(solution)/shard_map/all_to_all | solution.py:363
  803.3 85.0 %collective-permute-start.140 = (bf16[512,1024]{1,0:T(8,128)(2,1)}, bf16[512,1024]{1,0:T(8,128)(2,1)}, u32[]{:S(2)}, u32[]{:S(2)}) collective-permute-start(bf16[512,1024]{1,0:T(8,128)(2,1)} %collective-permute-done.139.shard_ref), channel_id=1, source_target_pairs={{0,16},{4,20},{8,24},{12,28},{16,0},{20,4},{24,8},{28,12},{1,17},{... | collective-permute-start | bytes 3145736 | tf_op jit(solution)/shard_map/ppermute | solution.py:40
  831.3 59.7 %collective-permute-start.142 = (bf16[512,1024]{1,0:T(8,128)(2,1)}, bf16[512,1024]{1,0:T(8,128)(2,1)}, u32[]{:S(2)}, u32[]{:S(2)}) collective-permute-start(bf16[512,1024]{1,0:T(8,128)(2,1)} %collective-permute-done.139.shard_ref), channel_id=1, source_target_pairs={{0,8},{4,12},{8,0},{12,4},{16,24},{20,28},{24,16},{28,20},{1,9},{5... | collective-permute-start | bytes 3145736 | tf_op jit(solution)/shard_map/ppermute | solution.py:40
  870.7 61.8 %collective-permute-start.147 = (bf16[512,1024]{1,0:T(8,128)(2,1)}, bf16[512,1024]{1,0:T(8,128)(2,1)}, u32[]{:S(2)}, u32[]{:S(2)}) collective-permute-start(bf16[512,1024]{1,0:T(8,128)(2,1)} %collective-permute-done.139.shard_ref), channel_id=1, source_target_pairs={{0,4},{4,0},{8,12},{12,8},{16,20},{20,16},{24,28},{28,24},{1,5},{5... | collective-permute-start | bytes 3145736 | tf_op jit(solution)/shard_map/ppermute | solution.py:40
  973.9 54.3 %collective-permute-start.55 = (bf16[128,2048]{1,0:T(8,128)(2,1)}, bf16[128,2048]{1,0:T(8,128)(2,1)}, u32[]{:S(2)}, u32[]{:S(2)}) collective-permute-start(bf16[128,2048]{1,0:T(8,128)(2,1)} %get-tuple-element.99), channel_id=1, source_target_pairs={{0,4},{4,0},{8,12},{12,8},{16,20},{20,16},{24,28},{28,24},{1,5},{5... | collective-permute-start | bytes 1572872 | tf_op jit(solution)/shard_map/ppermute | solution.py:40
  976.0 52.8 %collective-permute-start.62 = (bf16[128,2048]{1,0:T(8,128)(2,1)}, bf16[128,2048]{1,0:T(8,128)(2,1)}, u32[]{:S(2)}, u32[]{:S(2)}) collective-permute-start(bf16[128,2048]{1,0:T(8,128)(2,1)} %pad_maximum_fusion.14), channel_id=1, source_target_pairs={{0,16},{4,20},{8,24},{12,28},{16,0},{20,4},{24,8},{28,12},{1,17},{... | collective-permute-start | bytes 1572872 | tf_op jit(solution)/shard_map/ppermute | solution.py:40
  977.0 52.0 %collective-permute-start.59 = (bf16[128,2048]{1,0:T(8,128)(2,1)}, bf16[128,2048]{1,0:T(8,128)(2,1)}, u32[]{:S(2)}, u32[]{:S(2)}) collective-permute-start(bf16[128,2048]{1,0:T(8,128)(2,1)} %pad_maximum_fusion.13), channel_id=1, source_target_pairs={{0,8},{4,12},{8,0},{12,4},{16,24},{20,28},{24,16},{28,20},{1,9},{5... | collective-permute-start | bytes 1572872 | tf_op jit(solution)/shard_map/ppermute | solution.py:40
  977.7 51.7 %collective-permute-start.46 = (bf16[128,2048]{1,0:T(8,128)(2,1)}, bf16[128,2048]{1,0:T(8,128)(2,1)}, u32[]{:S(2)}, u32[]{:S(2)}) collective-permute-start(bf16[128,2048]{1,0:T(8,128)(2,1)} %add_convert_fusion.22), channel_id=1, source_target_pairs={{0,1},{1,0},{2,3},{3,2},{4,5},{5,4},{6,7},{7,6},{8,9},{9,8},{10,11... | collective-permute-start | bytes 1572872 | tf_op jit(solution)/shard_map/ppermute | solution.py:55
  (250 other events, 6198.7 us)

commit v2 on v1

v2 whole, which is shorter than its diff:
```python
import functools

import jax
import jax.numpy as jnp
from jax import lax
from jax.experimental import pallas as pl
from jax.experimental.pallas import tpu as pltpu
from jax.sharding import PartitionSpec as P

HEADS = 32
KV_HEADS = 8
HEAD_DIM = 64
GROUP = HEADS // KV_HEADS
GROUP_WIDTH = GROUP * HEAD_DIM

epsilon = 1e-05
theta = 1000000.0
score_scale = HEAD_DIM ** (-0.5)

f32 = jnp.float32
bf16 = jnp.bfloat16

CELL = KV_HEADS

NN = (((1,), (0,)), ((), ()))
NT = (((1,), (1,)), ((), ()))
TN = (((0,), (0,)), ((), ()))


def dot(left, right, dims=NN):
    return lax.dot_general(left, right, dims, preferred_element_type=f32)


def rms_scale(values, gain):
    return values * lax.rsqrt(jnp.mean(values * values, axis=-1, keepdims=True) + epsilon) * gain


def xor_send(values, distance):
    count = lax.axis_size("ctx")
    return lax.ppermute(values, "ctx", [(i, i ^ distance) for i in range(count)])


def cell_send(values, step):
    count = lax.axis_size("ctx")
    return lax.ppermute(values, "ctx", [(i, (i + step * CELL) % count) for i in range(count)])


def fsdp_send(values, step):
    count = lax.axis_size("fsdp")
    return lax.ppermute(values, "fsdp", [(i, (i + step) % count) for i in range(count)])


def pair_send(values, step, pair):
    count = lax.axis_size("fsdp")
    return lax.ppermute(
        values, "fsdp", [(i, i // pair * pair + (i % pair + step) % pair) for i in range(count)]
    )


def fsdp_relay(shard):
    count = lax.axis_size("fsdp")
    return [shard] + [fsdp_send(shard, step) for step in range(1, count)]


def fsdp_collect(piece_for):
    count = lax.axis_size("fsdp")
    total = piece_for(0).astype(f32)
    for step in range(1, count):
        total = total + fsdp_send(piece_for(step), step).astype(f32)
    return total


def round_send(values, odd_round):
    count = lax.axis_size("ctx")
    pairs = []
    for i in range(count):
        pairs.append((i, i ^ (2 if i % 2 == odd_round else 4)))
    return lax.ppermute(values, "ctx", pairs)


def add_low(left, right):
    return (left.astype(f32) + right.astype(f32)).astype(bf16)


def after(values, event):
    return lax.optimization_barrier((values, event))[0]


class Steps:
    def __init__(self):
        self.event = None
        self.jobs = []

    def begin(self, values):
        return values if self.event is None else after(values, self.event)

    def run(self, parts, spare=0):
        jobs, self.jobs = self.jobs[:spare], self.jobs[spare:]
        results = [function(self.begin(values)) for function, values in parts]
        results += [start(self.begin) for start, _ in jobs]
        results = lax.optimization_barrier(results)
        for (_, finish), value in zip(jobs, results[len(parts) :]):
            finish(value)
        self.event = results[0]
        return results[: len(parts)]

    def drain(self, done):
        while self.jobs and not done():
            self.run([(lambda v: v, self.event)], 2)


def first_round(values):
    return round_send(values, 0)


def second_round(values):
    return round_send(values, 1)


def twin_send(values):
    return xor_send(values, 1)


def rows_joined(*parts):
    return jnp.concatenate(parts, axis=0)


def gather_cell(shard):
    two = rows_joined(shard, first_round(shard))
    mine = rows_joined(two, second_round(two))
    return mine, twin_send(mine)


def reduce_first(mine, from_twin):
    half = mine.shape[0] // 2
    total = add_low(mine, from_twin)
    return total[:half], total[half:]


def reduce_second(kept, received):
    half = kept.shape[0] // 2
    total = add_low(kept, received)
    return total[:half], total[half:]


def reduce_cell(mine, other):
    kept, sent = reduce_first(mine, twin_send(other))
    kept, sent = reduce_second(kept, second_round(sent))
    return kept.astype(f32) + first_round(sent).astype(f32)


def sum_everywhere(values):
    for axis in ("ctx", "fsdp"):
        count = lax.axis_size(axis)
        if count & (count - 1):
            values = lax.psum(values, axis)
            continue
        distance = 1
        while distance < count:
            values = values + lax.ppermute(
                values, axis, [(i, i ^ distance) for i in range(count)]
            )
            distance *= 2
    return values


def blank(shape, dtype):
    return pl.pallas_call(
        lambda ref: None,
        out_specs=pl.BlockSpec(memory_space=pl.ANY),
        out_shape=jax.ShapeDtypeStruct(shape, dtype),
        cost_estimate=pl.CostEstimate(flops=0, bytes_accessed=0, transcendentals=0),
    )()


def cost(flops, moved, transcendentals=0):
    return pl.CostEstimate(
        flops=int(flops), bytes_accessed=int(moved), transcendentals=int(transcendentals)
    )


def own(i, place):
    slot = i % 4
    other = i // 4
    swapped = (place[2] + other) % 2
    return slot // 2 * (4 - 2 * swapped) + slot % 2 * (2 + 2 * swapped) + other


def token_block(i, place):
    return jnp.bitwise_xor(own(i, place), place[2])


def even_block(i):
    return jnp.minimum(i, 3)


def odd_block(i):
    return jnp.maximum(i - 4, 0)


def swap_halves(values):
    lane = lax.broadcasted_iota(jnp.int32, values.shape, 1) % HEAD_DIM
    return jnp.where(
        lane < HEAD_DIM // 2,
        pltpu.roll(values, values.shape[1] - HEAD_DIM // 2, 1),
        pltpu.roll(values, HEAD_DIM // 2, 1),
    )


def head_mean(values):
    first = lax.broadcasted_iota(jnp.int32, values.shape, 1) < HEAD_DIM
    low = jnp.sum(jnp.where(first, values, 0.0), axis=1, keepdims=True)
    high = jnp.sum(jnp.where(first, 0.0, values), axis=1, keepdims=True)
    return jnp.where(first, low, high) * (1.0 / HEAD_DIM)


def project_kernel(fsdp_count, place_ref, even_ref, odd_ref, angle_ref, gain_ref, *refs):
    weight_refs, (rows_ref, q_ref, kv_ref) = refs[:fsdp_count], refs[fsdp_count:]
    depth = weight_refs[0].shape[0]

    def project(left_ref):
        total = None
        for step in range(fsdp_count):
            owner = lax.rem(place_ref[0] - step + fsdp_count, fsdp_count)
            left = left_ref[:, pl.ds(pl.multiple_of(owner * depth, depth), depth)]
            term = dot(left, weight_refs[step][...])
            total = term if total is None else total + term
        rows_ref[...] = total

    @pl.when(pl.program_id(0) < 4)
    def _():
        project(even_ref)

    @pl.when(pl.program_id(0) >= 4)
    def _():
        project(odd_ref)

    cosine = angle_ref[:, : 2 * HEAD_DIM]
    sine = angle_ref[:, 2 * HEAD_DIM :]
    wide = 2 * HEAD_DIM
    for group in range(GROUP_WIDTH // wide + 1):
        values = rows_ref[:, group * wide : (group + 1) * wide]
        last = group == GROUP_WIDTH // wide
        normed = values * lax.rsqrt(head_mean(values * values) + epsilon)
        normed = normed * gain_ref[int(last) : int(last) + 1, :]
        turned = normed * cosine + swap_halves(normed) * sine
        if last:
            lane = lax.broadcasted_iota(jnp.int32, values.shape, 1)
            kv_ref[...] = jnp.where(lane < HEAD_DIM, turned, values).astype(bf16)
        else:
            q_ref[:, group * wide : (group + 1) * wide] = turned.astype(bf16)


def project(place, even, odd, angles, gains, weights, rows):
    count = CELL
    fsdp_count = len(weights)
    width = even.shape[1]
    columns = weights[0].shape[1]
    return pl.pallas_call(
        functools.partial(project_kernel, fsdp_count),
        grid_spec=pltpu.PrefetchScalarGridSpec(
            num_scalar_prefetch=1,
            grid=(count,),
            in_specs=[
                pl.BlockSpec((rows, width), lambda i, place: (even_block(i), 0)),
                pl.BlockSpec((rows, width), lambda i, place: (odd_block(i), 0)),
                pl.BlockSpec((rows, 4 * HEAD_DIM), lambda i, place: (token_block(i, place), 0)),
                pl.BlockSpec((8, 2 * HEAD_DIM), lambda i, place: (0, 0)),
            ]
            + [pl.BlockSpec(w.shape, lambda i, place: (0, 0)) for w in weights],
            out_specs=[
                pl.BlockSpec((rows, columns), lambda i, place: (token_block(i, place), 0)),
                pl.BlockSpec((rows, GROUP_WIDTH), lambda i, place: (token_block(i, place), 0)),
                pl.BlockSpec((rows, 2 * HEAD_DIM), lambda i, place: (token_block(i, place), 0)),
            ],
        ),
        out_shape=[
            jax.ShapeDtypeStruct((count * rows, columns), f32),
            jax.ShapeDtypeStruct((count * rows, GROUP_WIDTH), bf16),
            jax.ShapeDtypeStruct((count * rows, 2 * HEAD_DIM), bf16),
        ],
        compiler_params=pltpu.CompilerParams(vmem_limit_bytes=40 * 1024 * 1024),
        cost_estimate=cost(2 * count * rows * width * columns, 8e6),
    )(place, even, odd, angles, gains, *weights)


def project_grad_kernel(
    fsdp_count,
    place_ref,
    even_ref,
    odd_ref,
    angle_ref,
    gain_ref,
    rows_ref,
    q_even_ref,
    q_odd_ref,
    kv_ref,
    *refs,
):
    weight_refs = refs[:fsdp_count]
    (grad_even_ref, grad_odd_ref, part_even_ref, part_odd_ref, head_gain_ref, gain_grad_ref) = refs[
        fsdp_count:
    ]
    depth = weight_refs[0].shape[0]
    step_here = pl.program_id(0)

    @pl.when(step_here == 0)
    def _():
        head_gain_ref[...] = jnp.zeros_like(head_gain_ref)
        gain_grad_ref[...] = jnp.zeros_like(gain_grad_ref)

    cosine = angle_ref[:, : 2 * HEAD_DIM]
    sine = angle_ref[:, 2 * HEAD_DIM :]
    wide = 2 * HEAD_DIM
    pieces = []
    for group in range(GROUP_WIDTH // wide + 1):
        last = group == GROUP_WIDTH // wide
        values = rows_ref[:, group * wide : (group + 1) * wide]
        at = pl.ds(group * wide, wide)
        if last:
            grad = kv_ref[...]
        else:
            grad = jnp.where(step_here < 4, q_even_ref[:, at], q_odd_ref[:, at])
        scale = lax.rsqrt(head_mean(values * values) + epsilon)
        gain = gain_ref[int(last) : int(last) + 1, :]
        unturned = grad * cosine + swap_halves(grad * sine)
        head_gain_ref[int(last) : int(last) + 1, :] += jnp.sum(
            unturned * values * scale, axis=0, keepdims=True
        )
        scaled = unturned * gain
        piece = scale * scaled - values * (scale * scale * scale) * head_mean(scaled * values)
        if last:
            lane = lax.broadcasted_iota(jnp.int32, values.shape, 1)
            piece = jnp.where(lane < HEAD_DIM, piece, grad)
        pieces.append(piece.astype(bf16))
    low = jnp.concatenate(pieces, axis=1)

    def finish(normed_ref, grad_out_ref, part_ref):
        grad_out_ref[...] = low
        for step in range(fsdp_count):
            owner = lax.rem(place_ref[0] - step + fsdp_count, fsdp_count)
            at = pl.ds(pl.multiple_of(owner * depth, depth), depth)
            part = dot(low, weight_refs[step][...], NT)
            part_ref[:, at] = part.astype(bf16)
            gain_grad_ref[0:1, at] += jnp.sum(
                part * normed_ref[:, at].astype(f32), axis=0, keepdims=True
            )

    @pl.when(step_here < 4)
    def _():
        finish(even_ref, grad_even_ref, part_even_ref)

    @pl.when(step_here >= 4)
    def _():
        finish(odd_ref, grad_odd_ref, part_odd_ref)


def project_grad(place, even, odd, angles, gains, qkv_rows, query_grad, kv_grad, weights, rows):
    count = CELL
    fsdp_count = len(weights)
    width = even.shape[1]
    columns = weights[0].shape[1]

    def by_token(size):
        return pl.BlockSpec((rows, size), lambda i, place: (token_block(i, place), 0))

    def halves(size):
        return [
            pl.BlockSpec((rows, size), lambda i, place: (even_block(i), 0)),
            pl.BlockSpec((rows, size), lambda i, place: (odd_block(i), 0)),
        ]

    return pl.pallas_call(
        functools.partial(project_grad_kernel, fsdp_count),
        grid_spec=pltpu.PrefetchScalarGridSpec(
            num_scalar_prefetch=1,
            grid=(count,),
            in_specs=halves(width)
            + [
                by_token(4 * HEAD_DIM),
                pl.BlockSpec((8, 2 * HEAD_DIM), lambda i, place: (0, 0)),
                by_token(columns),
                *halves(GROUP_WIDTH),
                by_token(2 * HEAD_DIM),
            ]
            + [pl.BlockSpec(w.shape, lambda i, place: (0, 0)) for w in weights],
            out_specs=halves(columns)
            + halves(width)
            + [
                pl.BlockSpec((8, 2 * HEAD_DIM), lambda i, place: (0, 0)),
                pl.BlockSpec((8, width), lambda i, place: (0, 0)),
            ],
        ),
        out_shape=[
            jax.ShapeDtypeStruct((4 * rows, columns), bf16),
            jax.ShapeDtypeStruct((4 * rows, columns), bf16),
            jax.ShapeDtypeStruct((4 * rows, width), bf16),
            jax.ShapeDtypeStruct((4 * rows, width), bf16),
            jax.ShapeDtypeStruct((8, 2 * HEAD_DIM), f32),
            jax.ShapeDtypeStruct((8, width), f32),
        ],
        compiler_params=pltpu.CompilerParams(vmem_limit_bytes=40 * 1024 * 1024),
        cost_estimate=cost(2 * count * rows * width * columns, 12e6),
    )(place, even, odd, angles, gains, qkv_rows, *query_grad, kv_grad, *weights)


def stack_heads(block):
    return jnp.concatenate(
        [block[:, i * HEAD_DIM : (i + 1) * HEAD_DIM] for i in range(GROUP)], axis=0
    )


def unstack_heads(turned, rows):
    return jnp.concatenate([turned[:, i * rows : (i + 1) * rows].T for i in range(GROUP)], axis=1)


def fill_turned(place_ref, kv_ref, turned_ref, chunk):
    @pl.when(pl.program_id(0) == 0)
    def _():
        def turn(n, _):
            start = pl.multiple_of(n * chunk, chunk)
            turned_ref[:, pl.ds(start, chunk)] = kv_ref[pl.ds(start, chunk), :].T
            return 0

        lax.fori_loop(0, (place_ref[1] + 1) * CELL, turn, 0)


def visible_keys(place_ref, chunk, rows):
    key_at = lax.broadcasted_iota(jnp.int32, (chunk, GROUP * rows), 0)
    row_at = lax.broadcasted_iota(jnp.int32, (chunk, GROUP * rows), 1) % rows
    return key_at <= row_at + place_ref[0] * rows


def attention_kernel(
    chunk, place_ref, q_ref, kv_ref, even_ref, odd_ref, log_ref, turned_ref
):
    rows = q_ref.shape[0]
    fill_turned(place_ref, kv_ref, turned_ref, chunk)
    queries = stack_heads(q_ref[...].astype(f32) * score_scale).astype(bf16)
    queries = jnp.concatenate([queries, jnp.zeros_like(queries)], axis=1)

    def step(n, running, masked):
        total, summed = running
        start = pl.multiple_of(n * chunk, chunk)
        weights = jnp.exp(dot(kv_ref[pl.ds(start, chunk), :], queries, NT))
        if masked:
            weights = jnp.where(visible_keys(place_ref, chunk, rows), weights, 0.0)
        return (
            total + jnp.sum(weights, axis=0, keepdims=True),
            summed + dot(turned_ref[:, pl.ds(start, chunk)], weights.astype(bf16)),
        )

    last = place_ref[1] * CELL + token_block(pl.program_id(0), place_ref)
    running = (
        jnp.zeros((1, GROUP * rows), f32),
        jnp.zeros((2 * HEAD_DIM, GROUP * rows), f32),
    )
    running = lax.fori_loop(0, last, lambda n, r: step(n, r, False), running)
    total, summed = step(last, running, True)
    result = unstack_heads(summed[HEAD_DIM:] / total, rows).astype(bf16)

    @pl.when(pl.program_id(0) < 4)
    def _():
        even_ref[...] = result

    @pl.when(pl.program_id(0) >= 4)
    def _():
        odd_ref[...] = result

    log_ref[...] = jnp.log(total)[None]


def attention(place, queries, keys_values, rows, chunk):
    count = queries.shape[0] // rows
    keys = keys_values.shape[0]
    half = jax.ShapeDtypeStruct((4 * rows, GROUP_WIDTH), bf16)
    return pl.pallas_call(
        functools.partial(attention_kernel, chunk),
        grid_spec=pltpu.PrefetchScalarGridSpec(
            num_scalar_prefetch=1,
            grid=(count,),
            in_specs=[
                pl.BlockSpec((rows, GROUP_WIDTH), lambda i, place: (token_block(i, place), 0)),
                pl.BlockSpec((keys, 2 * HEAD_DIM), lambda i, place: (0, 0)),
            ],
            out_specs=[
                pl.BlockSpec((rows, GROUP_WIDTH), lambda i, place: (even_block(i), 0)),
                pl.BlockSpec((rows, GROUP_WIDTH), lambda i, place: (odd_block(i), 0)),
                pl.BlockSpec((1, 1, GROUP * rows), lambda i, place: (i, 0, 0)),
            ],
            scratch_shapes=[pltpu.VMEM((2 * HEAD_DIM, keys), bf16)],
        ),
        out_shape=[half, half, jax.ShapeDtypeStruct((count, 1, GROUP * rows), f32)],
        compiler_params=pltpu.CompilerParams(vmem_limit_bytes=40 * 1024 * 1024),
        cost_estimate=cost(16e9, 8e6, 1e7),
    )(place, queries, keys_values)


def attention_grad_kernel(
    chunk,
    other,
    place_ref,
    q_ref,
    branch_ref,
    out_ref,
    log_ref,
    weight_ref,
    kv_ref,
    *refs,
):
    q_grad_ref, kv_grad_ref, turned_ref = refs[-3:]
    rows = q_ref.shape[0]
    fill_turned(place_ref, kv_ref, turned_ref, chunk)

    @pl.when(pl.program_id(0) == 0)
    def _():
        kv_grad_ref[...] = refs[0][...] if other else jnp.zeros_like(kv_grad_ref)

    queries = stack_heads(q_ref[...].astype(f32) * score_scale).astype(bf16)
    queries = jnp.concatenate([queries, jnp.zeros_like(queries)], axis=1)
    out_grad = dot(branch_ref[...], weight_ref[...], NT).astype(bf16)
    grads = stack_heads(out_grad)
    attended = stack_heads(out_ref[...]).astype(f32)
    row_delta = jnp.sum((grads.astype(f32) * attended).T, axis=0, keepdims=True)
    grads = jnp.concatenate([jnp.zeros_like(grads), grads], axis=1)
    log_total = log_ref[0]

    def step(n, summed, masked):
        start = pl.multiple_of(n * chunk, chunk)
        block = kv_ref[pl.ds(start, chunk), :]
        weights = jnp.exp(dot(block, queries, NT) - log_total)
        if masked:
            weights = jnp.where(visible_keys(place_ref, chunk, rows), weights, 0.0)
        score_grad = (weights * (dot(block, grads, NT) - row_delta)).astype(bf16)
        kv_grad_ref[pl.ds(start, chunk), :] += dot(score_grad, queries) + dot(
            weights.astype(bf16), grads
        )
        return summed + dot(turned_ref[:, pl.ds(start, chunk)], score_grad)

    last = place_ref[1] * CELL + token_block(pl.program_id(0) + 4 * other, place_ref)
    summed = jnp.zeros((2 * HEAD_DIM, GROUP * rows), f32)
    summed = lax.fori_loop(0, last, lambda n, r: step(n, r, False), summed)
    summed = step(last, summed, True)
    q_grad_ref[...] = unstack_heads(summed[:HEAD_DIM] * score_scale, rows)


def attention_grad(
    place, queries, branch, attended, log_total, weight, keys_values, rows, chunk, other, kv_grad=None
):
    keys = keys_values.shape[0]
    width = weight.shape[1]
    whole_spec = pl.BlockSpec((keys, 2 * HEAD_DIM), lambda i, place: (0, 0))
    added = [] if kv_grad is None else [kv_grad]
    return pl.pallas_call(
        functools.partial(attention_grad_kernel, chunk, other),
        grid_spec=pltpu.PrefetchScalarGridSpec(
            num_scalar_prefetch=1,
            grid=(4,),
            in_specs=[
                pl.BlockSpec(
                    (rows, GROUP_WIDTH), lambda i, place: (token_block(i + 4 * other, place), 0)
                ),
                pl.BlockSpec((rows, width), lambda i, place: (i, 0)),
                pl.BlockSpec((rows, GROUP_WIDTH), lambda i, place: (i, 0)),
                pl.BlockSpec((1, 1, GROUP * rows), lambda i, place: (i + 4 * other, 0, 0)),
                pl.BlockSpec(weight.shape, lambda i, place: (0, 0)),
                whole_spec,
            ]
            + [whole_spec] * len(added),
            out_specs=[
                pl.BlockSpec((rows, GROUP_WIDTH), lambda i, place: (i, 0)),
                whole_spec,
            ],
            scratch_shapes=[pltpu.VMEM((2 * HEAD_DIM, keys), bf16)],
        ),
        out_shape=[
            jax.ShapeDtypeStruct((4 * rows, GROUP_WIDTH), f32),
            jax.ShapeDtypeStruct(keys_values.shape, f32),
        ],
        compiler_params=pltpu.CompilerParams(vmem_limit_bytes=48 * 1024 * 1024),
        cost_estimate=cost(18e9, 12e6, 5e6),
    )(place, queries, branch, attended, log_total, weight, keys_values, *added)


def feed_kernel(
    normed_ref, outer_ref, weight_ref, down_ref, active_ref, gate_grad_ref, part_ref, branch_ref
):
    units = active_ref.shape[1]
    both = dot(normed_ref[...], weight_ref[...])
    gate = both[:, :units]
    up = both[:, units:]
    act_grad = dot(outer_ref[...], down_ref[...], NT)
    logistic = 1.0 / (1.0 + jnp.exp(-gate))
    silu = gate * logistic
    active_ref[...] = (silu * up).astype(bf16)
    gate_part = act_grad * up * (logistic * (1.0 + gate * (1.0 - logistic)))
    gate_grad_ref[:, :units] = gate_part.astype(bf16)
    gate_grad_ref[:, units:] = (act_grad * silu).astype(bf16)
    part_ref[...] = dot(gate_grad_ref[...], weight_ref[...], NT).astype(bf16)
    branch_ref[...] = dot(active_ref[...], down_ref[...]).astype(bf16)


def feed(normed, outer, weight, down):
    tokens, width = normed.shape
    columns = weight.shape[1]
    rows = 256 if tokens % 256 == 0 else tokens

    def by_row(size):
        return pl.BlockSpec((rows, size), lambda i: (i, 0))

    def low(size):
        return jax.ShapeDtypeStruct((tokens, size), bf16)

    return pl.pallas_call(
        feed_kernel,
        grid=(tokens // rows,),
        in_specs=[
            by_row(width),
            by_row(width),
            pl.BlockSpec(weight.shape, lambda i: (0, 0)),
            pl.BlockSpec(down.shape, lambda i: (0, 0)),
        ],
        out_specs=[by_row(columns // 2), by_row(columns), by_row(width), by_row(width)],
        out_shape=[low(columns // 2), low(columns), low(width), low(width)],
        compiler_params=pltpu.CompilerParams(vmem_limit_bytes=48 * 1024 * 1024),
        cost_estimate=cost(6 * tokens * width * columns, 16e6, tokens * columns),
    )(normed, outer, weight, down)


def weight_grad_kernel(count, place_ref, *refs):
    total = None
    for left_ref, right_ref in zip(refs[:count], refs[count : 2 * count]):
        term = dot(left_ref[...], right_ref[...], TN)
        total = term if total is None else total + term
    refs[-1][...] = total.astype(bf16)


def weight_grad(lefts, rights, first, size, column, columns):
    tokens = lefts[0].shape[0]
    tile = min(512, size)
    tiles = size // tile
    place = jnp.stack([first * tiles]).astype(jnp.int32)
    return pl.pallas_call(
        functools.partial(weight_grad_kernel, len(lefts)),
        grid_spec=pltpu.PrefetchScalarGridSpec(
            num_scalar_prefetch=1,
            grid=(tiles,),
            in_specs=[pl.BlockSpec((tokens, tile), lambda i, at: (0, at[0] + i))] * len(lefts)
            + [pl.BlockSpec((tokens, columns), lambda i, at: (0, column))] * len(rights),
            out_specs=pl.BlockSpec((tile, columns), lambda i, at: (i, 0)),
        ),
        out_shape=jax.ShapeDtypeStruct((size, columns), bf16),
        compiler_params=pltpu.CompilerParams(vmem_limit_bytes=48 * 1024 * 1024),
        cost_estimate=cost(2 * len(lefts) * tokens * size * columns, 12e6),
    )(place, *lefts, *rights)


def place_kernel(place_ref, shard_ref, *refs):
    refs[-1][...] = shard_ref[...].astype(f32)


def place_blocks(whole, shape, source, block, grid, place, from_block, to_block):
    in_specs = [pl.BlockSpec(block, from_block)]
    operands = [place, source]
    aliases = {}
    if whole is not None:
        in_specs.append(pl.BlockSpec(memory_space=pl.ANY))
        operands.append(whole)
        aliases = {2: 0}
    return pl.pallas_call(
        place_kernel,
        grid_spec=pltpu.PrefetchScalarGridSpec(
            num_scalar_prefetch=1,
            grid=grid,
            in_specs=in_specs,
            out_specs=pl.BlockSpec(block, to_block),
        ),
        out_shape=jax.ShapeDtypeStruct(shape, f32),
        input_output_aliases=aliases,
        compiler_params=pltpu.CompilerParams(vmem_limit_bytes=24 * 1024 * 1024),
        cost_estimate=cost(0, 6 * source.size),
    )(*operands)


def place_columns(halves, unit, place):
    whole = None
    rows = halves[0].shape[0] // 4
    for odd, half in enumerate(halves):
        whole = place_blocks(
            whole,
            (rows, CELL * unit),
            half,
            (rows, unit),
            (4,),
            place,
            lambda i, at: (i, 0),
            lambda i, at, odd=odd: (0, token_block(4 * odd + i, at)),
        )
    return whole


def place_rows(halves, place):
    whole = None
    rows, columns = halves[0].shape[0] // 4, halves[0].shape[1]
    for odd, half in enumerate(halves):
        whole = place_blocks(
            whole,
            (CELL * rows, columns),
            half,
            (rows, columns),
            (4,),
            place,
            lambda i, at: (i, 0),
            lambda i, at, odd=odd: (token_block(4 * odd + i, at), 0),
        )
    return whole


def place_heads_kernel(place_ref, even_ref, odd_ref, out_ref):
    query_width = HEADS * HEAD_DIM
    key_width = KV_HEADS * HEAD_DIM
    even = even_ref[...].astype(f32)
    odd = odd_ref[...].astype(f32)
    first = lax.rem(place_ref[2], 2) == 0
    low = jnp.where(first, even, odd)
    high = jnp.where(first, odd, even)
    twins = token_block(pl.program_id(0), place_ref) // 2

    def at(start, size):
        return pl.ds(pl.multiple_of(start + twins * size, 128), size)

    out_ref[:, at(0, 2 * GROUP_WIDTH)] = jnp.concatenate(
        [low[:, :GROUP_WIDTH], high[:, :GROUP_WIDTH]], axis=1
    )
    middle = GROUP_WIDTH + HEAD_DIM
    out_ref[:, at(query_width, 2 * HEAD_DIM)] = jnp.concatenate(
        [low[:, GROUP_WIDTH:middle], high[:, GROUP_WIDTH:middle]], axis=1
    )
    out_ref[:, at(query_width + key_width, 2 * HEAD_DIM)] = jnp.concatenate(
        [low[:, middle:], high[:, middle:]], axis=1
    )


def place_heads(halves, place):
    rows, columns = halves[0].shape[0] // 4, halves[0].shape[1]
    shape = (rows, CELL * columns)
    return pl.pallas_call(
        place_heads_kernel,
        grid_spec=pltpu.PrefetchScalarGridSpec(
            num_scalar_prefetch=1,
            grid=(4,),
            in_specs=[
                pl.BlockSpec((rows, columns), lambda i, at: (i, 0)),
                pl.BlockSpec((rows, columns), lambda i, at: (i % 2 * 2 + i // 2, 0)),
            ],
            out_specs=pl.BlockSpec(shape, lambda i, at: (0, 0)),
        ),
        out_shape=jax.ShapeDtypeStruct(shape, f32),
        compiler_params=pltpu.CompilerParams(vmem_limit_bytes=32 * 1024 * 1024),
        cost_estimate=cost(0, 6 * rows * CELL * columns),
    )(place, *halves)


def body(
    inputs,
    attention_gain,
    qkv_weight,
    query_gain,
    key_gain,
    out_weight,
    mlp_gain,
    gate_up_weight,
    down_weight,
    cotangent,
):
    rows, width = inputs.shape
    fsdp_count = lax.axis_size("fsdp")
    cell_count = lax.axis_size("ctx") // CELL
    pair = 2 if fsdp_count % 2 == 0 else 1
    pair_count = fsdp_count // pair
    fsdp_here = lax.axis_index("fsdp")
    ctx_here = lax.axis_index("ctx")
    head = ctx_here % CELL
    cell = ctx_here // CELL
    in_pair = fsdp_here % pair
    pair_here = fsdp_here // pair
    weight_rows = qkv_weight.shape[0]
    query_width = HEADS * HEAD_DIM
    key_width = KV_HEADS * HEAD_DIM
    hidden_width = gate_up_weight.shape[1] // 2
    unit = hidden_width // (fsdp_count * CELL)
    place = jnp.stack([fsdp_here, cell, head, in_pair]).astype(jnp.int32)

    def block(values, index, size, axis=0):
        return lax.dynamic_slice_in_dim(values, index * size, size, axis)

    def put(whole, part, index, axis=0):
        return lax.dynamic_update_slice_in_dim(whole, part, index * part.shape[axis], axis)

    def cell_sum(values):
        total = values.astype(f32)
        for step in range(1, cell_count):
            total = total + cell_send(values.astype(bf16), step).astype(f32)
        return total

    def cell_turn(values, split_axis, join_axis):
        groups = None
        if cell_count > 1:
            groups = [[c * CELL + i for i in range(CELL)] for c in range(cell_count)]
        return lax.all_to_all(
            values, "ctx", split_axis, join_axis, axis_index_groups=groups, tiled=True
        )

    blocks_here = cell * CELL + jnp.arange(CELL, dtype=jnp.int32)
    positions = (
        ((blocks_here * fsdp_count + fsdp_here) * rows)[:, None]
        + jnp.arange(rows, dtype=jnp.int32)[None, :]
    ).reshape(-1)
    cell_tokens = CELL * rows
    half_dim = HEAD_DIM // 2
    frequency = theta ** (-jnp.arange(half_dim, dtype=f32) * 2.0 / HEAD_DIM)

    def angle_table(here):
        turns = here.astype(f32)[:, None] * frequency[None, :]
        cosine = jnp.cos(turns)
        sine = jnp.sin(turns)
        return jnp.concatenate([cosine] * 4 + [-sine, sine] * 2, axis=1)

    gains = jnp.concatenate(
        [
            jnp.tile(query_gain, 2)[None, :],
            jnp.concatenate([key_gain, jnp.ones_like(key_gain)])[None, :],
            jnp.zeros((6, 2 * HEAD_DIM), f32),
        ],
        axis=0,
    )

    source = inputs.astype(f32)
    normed_attn_own = rms_scale(source, attention_gain).astype(bf16)
    def head_columns(start):
        both = lax.dynamic_slice_in_dim(
            qkv_weight, start + head // 2 * (2 * HEAD_DIM), 2 * HEAD_DIM, 1
        )
        return jnp.where(head % 2 == 0, both[:, :HEAD_DIM], both[:, HEAD_DIM:])

    qkv_own = jnp.concatenate(
        [
            block(qkv_weight, head, GROUP_WIDTH, 1),
            head_columns(query_width),
            head_columns(query_width + key_width),
        ],
        axis=1,
    )
    out_own = block(out_weight, head, width // CELL, 1)
    local_units = pair_count * unit
    pair_rows = pair * weight_rows

    def owner_columns(weight, owner):
        return jnp.concatenate(
            [
                lax.dynamic_slice_in_dim(
                    weight,
                    side * hidden_width + ((p * pair + owner) * CELL + head) * unit,
                    unit,
                    1,
                )
                for side in range(2)
                for p in range(pair_count)
            ],
            axis=1,
        )

    down_own = block(down_weight, head, unit)
    steps = Steps()
    sends = [functools.partial(fsdp_send, step=k) for k in range(fsdp_count)]

    class Buffer:
        def __init__(self, shape):
            self.value = blank(shape, bf16)

        def write(self, part, row, axis=0):
            self.value = lax.dynamic_update_slice_in_dim(self.value, part, row, axis)

    gate_up_pair = Buffer((pair_rows, 2 * local_units))
    gate_up_mine = Buffer((width, 2 * local_units))
    down_mine = Buffer((local_units, width))
    down_mine.write(down_own, pair_here * unit)
    pair_jobs, down_jobs, gate_up_jobs = [], [], []

    def part_of(values, n, count):
        size = values.shape[0] // count
        return lax.slice_in_dim(values, n * size, (n + 1) * size)

    for j in range(1, pair):
        for n in range(2):
            size = weight_rows // 2
            pair_jobs.append(
                (
                    lambda begin, n=n, j=j: pair_send(begin(part_of(owned[j], n, 2)), j, pair),
                    lambda got, n=n, j=j, size=size: gate_up_pair.write(
                        got, (in_pair - j) % pair * weight_rows + n * size
                    ),
                )
            )
    for step in range(1, pair_count):
        for n in range(4):
            size = unit // 4
            down_jobs.append(
                (
                    lambda begin, n=n, step=step: fsdp_send(
                        begin(part_of(down_own, n, 4)), step * pair
                    ),
                    lambda got, n=n, step=step, size=size: down_mine.write(
                        got, (pair_here - step) % pair_count * unit + n * size
                    ),
                )
            )
        for n in range(8):
            size = pair_rows // 8
            gate_up_jobs.append(
                (
                    lambda begin, n=n, step=step: fsdp_send(
                        begin(part_of(gate_up_pair.value, n, 8)), step * pair
                    ),
                    lambda got, n=n, step=step, size=size: gate_up_mine.write(
                        got, (pair_here - step) % pair_count * pair_rows + n * size
                    ),
                )
            )

    last = max(fsdp_count - 1, 3)
    got = steps.run(
        [(first_round, normed_attn_own), (angle_table, positions)]
        + [(send, qkv_own) for send in sends[1:2]]
    )
    angles = got[1]
    qkv_pieces = [qkv_own] + got[2:]
    two = rows_joined(normed_attn_own, got[0])
    got = steps.run(
        [
            (second_round, two),
            (
                lambda v: [owner_columns(v, (in_pair + j) % pair) for j in range(pair)],
                gate_up_weight,
            ),
        ]
        + [(send, qkv_own) for send in sends[2:last]]
    )
    owned = got[1]
    gate_up_pair.write(owned[0], in_pair * weight_rows)
    qkv_pieces += got[2:]
    mine = rows_joined(two, got[0])
    got = steps.run([(twin_send, mine)] + [(send, qkv_own) for send in sends[last:]])
    qkv_pieces += got[1:]
    normed_attn = [mine, got[0]]

    projected, outer_got, *out_got = steps.run(
        [
            (lambda v: project(place, *v, angles, gains, qkv_pieces, rows), normed_attn),
            (first_round, cotangent),
        ]
        + [(send, out_own) for send in sends[1::2]]
    )
    qkv_rows, query_low, kv_own = projected
    outer_two = rows_joined(cotangent, outer_got)
    kv_own = kv_own.reshape(CELL, 1, rows, 2 * HEAD_DIM)
    got = steps.run(
        [(send, kv_own) for send in sends[1:]]
        + [(second_round, outer_two)]
        + [(send, out_own) for send in sends[2::2]]
    )
    kv_pieces, got = [kv_own] + got[: fsdp_count - 1], got[fsdp_count - 1 :]
    outer_mine = rows_joined(outer_two, got[0])
    out_pieces = [out_own] + [None] * (fsdp_count - 1)
    out_pieces[1::2] = out_got
    out_pieces[2::2] = got[1:]
    kv_cells = blank((CELL, fsdp_count, rows, 2 * HEAD_DIM), bf16)
    out_columns = blank((width, width // CELL), bf16)
    for k in range(fsdp_count):
        kv_cells = put(kv_cells, kv_pieces[k], (fsdp_here - k) % fsdp_count, 1)
        out_columns = put(out_columns, out_pieces[k], (fsdp_here - k) % fsdp_count)
    chunk = fsdp_count * rows
    kv_all = kv_cells.reshape(CELL * chunk, 2 * HEAD_DIM)
    if cell_count > 1:
        kv_cells = kv_all
        kv_all = put(
            blank((cell_count * CELL * chunk, 2 * HEAD_DIM), bf16), kv_cells, cell
        )
        for step in range(1, cell_count):
            kv_all = put(kv_all, cell_send(kv_cells, step), (cell - step) % cell_count)

    steps.jobs = pair_jobs[:1] + down_jobs[:2]
    attended, out_rows, outer_other = steps.run(
        [
            (lambda v: attention(place, *v, rows, chunk), (query_low, kv_all)),
            (lambda v: cell_turn(v, 0, 1), out_columns),
            (twin_send, outer_mine),
        ],
        3,
    )
    *attended, log_total = attended
    outer_parts = [[outer_mine, outer_other]]
    steps.jobs = pair_jobs[1:] + down_jobs[2:] + gate_up_jobs
    terms = [dot(half, out_rows).astype(bf16) for half in attended]
    got = steps.run([(twin_send, terms[1])], 1)
    kept, sent = reduce_first(terms[0], got[0])
    got = steps.run(
        [(second_round, sent)]
        + [(lambda v, j=j: pair_send(v, -j, pair), cotangent) for j in range(1, pair)],
        2,
    )
    outer_next = got[1:]
    kept, sent = reduce_second(kept, got[0])
    got = steps.run([(first_round, sent)] + [(first_round, shard) for shard in outer_next], 1)
    outer_twos = [rows_joined(shard, g) for shard, g in zip(outer_next, got[1:])]
    hidden_mid = source + kept.astype(f32) + got[0].astype(f32)
    normed_own = rms_scale(hidden_mid, mlp_gain).astype(bf16)

    got = steps.run(
        [(first_round, normed_own)]
        + [(lambda v, j=j: pair_send(v, -j, pair), normed_own) for j in range(1, pair)]
        + [(second_round, v) for v in outer_twos],
        1,
    )
    two = rows_joined(normed_own, got[0])
    normed_next = got[1:pair]
    outer_mines = [rows_joined(v, g) for v, g in zip(outer_twos, got[pair:])]
    got = steps.run([(second_round, two)] + [(twin_send, v) for v in outer_mines], 2)
    mine = rows_joined(two, got[0])
    outer_parts += [[a, b] for a, b in zip(outer_mines, got[1:])]
    got = steps.run([(twin_send, mine)] + [(first_round, v) for v in normed_next], 1)
    normed_parts = [[mine, got[0]]]
    twos = [rows_joined(v, g) for v, g in zip(normed_next, got[1:])]
    if twos:
        got = steps.run([(second_round, v) for v in twos], 2)
        mines = [rows_joined(v, g) for v, g in zip(twos, got)]
        got = steps.run([(twin_send, v) for v in mines], 1)
        normed_parts += [[a, b] for a, b in zip(mines, got)]
    while steps.jobs:
        steps.run([(lambda v: v, normed_parts[-1][1])], 2)
    gate_up_mine.write(gate_up_pair.value, pair_here * pair_rows)
    gate_up_all, down_all = gate_up_mine.value, down_mine.value

    def feed_half(values):
        return feed(*values, gate_up_all, down_all)

    order = [(j, side) for j in reversed(range(pair)) for side in (1, 0)]
    results = {}
    waiting = []
    sums = {}

    def advance():
        return [(function, values) for function, values, _ in waiting]

    def settle(got):
        nonlocal waiting
        ongoing, waiting = waiting, []
        for (_, _, then), value in zip(ongoing, got):
            then(value)

    def reduce_start(j, mine, other):
        def ended(kept):
            def end(value):
                sums[j] = kept.astype(f32) + value.astype(f32)
                if j:
                    waiting.append(
                        (
                            lambda v: pair_send(v, j, pair),
                            sums[j].astype(bf16),
                            lambda value: sums.__setitem__(j, value.astype(f32)),
                        )
                    )

            return end

        def second(kept):
            def end(value):
                now, sent = reduce_second(kept, value)
                waiting.append((first_round, sent, ended(now)))

            return end

        def end(value):
            now, sent = reduce_first(mine(), value)
            waiting.append((second_round, sent, second(now)))

        waiting.append((twin_send, other, end))

    for j, side in order:
        ready = (normed_parts[j][side], outer_parts[j][side])
        result, *got = steps.run([(feed_half, ready)] + advance())
        results[j, side] = result
        settle(got)
        if side:
            reduce_start(j, lambda j=j: results[j, 0][2], result[2])
    keys = [(j, side) for j in range(pair) for side in range(2)]
    normed_flat = [normed_parts[j][side] for j, side in keys]
    outer_flat = [outer_parts[j][side] for j, side in keys]

    class PairTotal:
        def __init__(self, rows_of, operands, count=4):
            self.rows_of, self.operands, self.count = rows_of, operands, count
            self.pieces, self.got, self.left = None, [], count * (pair_count - 1)
            self.jobs = [
                (functools.partial(self.start, step, n), self.got.append)
                for step in range(1, pair_count)
                for n in range(count)
            ]

        def others(self):
            return (
                lambda v: [
                    self.rows_of(v, (pair_here + step) % pair_count) for step in range(1, pair_count)
                ],
                self.operands,
            )

        def own(self):
            return (lambda v: self.rows_of(v, pair_here), self.operands)

        def start(self, step, n, begin):
            if self.pieces is None:
                function, operands = self.others()
                self.pieces = function(operands)
            return fsdp_send(begin(part_of(self.pieces[step - 1], n, self.count)), step * pair)

        def complete(self):
            return len(self.got) == self.left

        def total(self, mine):
            steps.drain(self.complete)
            rows_here = [part_of(mine, n, self.count).astype(f32) for n in range(self.count)]
            for k, value in enumerate(self.got):
                rows_here[k % self.count] += value.astype(f32)
            return cell_sum(rows_joined(*rows_here)).astype(bf16)

    def side_total(side):
        return PairTotal(
            lambda v, p: weight_grad(*v, p, pair_rows, side, local_units),
            (normed_flat, [results[k][1] for k in keys]),
        )

    gate, up = side_total(0), side_total(1)
    down = PairTotal(
        lambda v, p: weight_grad(*v, p, unit, 0, width),
        ([results[k][0] for k in keys], outer_flat),
    )

    def shares_sent(total):
        return [
            pair_send(block(total, (in_pair + j) % pair, weight_rows), j, pair)
            for j in range(1, pair)
        ]

    def shares(total, got):
        return jnp.concatenate([block(total, in_pair, weight_rows)] + got, axis=1)

    branch_terms = [tuple(results[j, side][3] for side in range(2)) for j in range(pair)]
    branch_twins = []
    steps.jobs = gate.jobs + up.jobs + down.jobs
    gate_mine = None
    while waiting:
        parts = advance()
        count = len(parts)
        extra = []
        if len(branch_twins) < pair:
            extra.append((twin_send, branch_terms[pair - 1 - len(branch_twins)][1]))
        if gate.pieces is not None and gate_mine is None:
            extra.append(gate.own())
        got = steps.run(parts + extra, 1)
        settle(got[:count])
        got = got[count:]
        if len(branch_twins) < pair:
            branch_twins.append(got.pop(0))
        if got:
            gate_mine = got[0]
    normed_grad = sum(sums[j] for j in range(pair))
    mid_part, mlp_gain_grad = jax.vjp(rms_scale, hidden_mid, mlp_gain)[1](normed_grad)
    hidden_grad = cotangent.astype(f32) + mid_part
    branch_own = hidden_grad.astype(bf16)
    got = steps.run([(first_round, branch_own), up.others()], 1)
    up.pieces = got[1]
    two = rows_joined(branch_own, got[0])
    got = steps.run([(second_round, two), up.own()], 1)
    up_mine = got[1]
    mine = rows_joined(two, got[0])
    if gate_mine is None:
        gate_mine = gate.own()[0](gate.operands)
    gate_total = gate.total(gate_mine)
    branch_twins = branch_twins[::-1]
    branch_kept, branch_sent = map(
        list,
        zip(*[reduce_first(terms[0], value) for terms, value in zip(branch_terms, branch_twins)]),
    )
    got = steps.run(
        [
            (twin_send, mine),
            (second_round, branch_sent[-1]),
            (shares_sent, gate_total),
            down.others(),
        ],
        1,
    )
    branch_grad = [mine, got[0]]
    branch_kept[-1], branch_sent[-1] = reduce_second(branch_kept[-1], got[1])
    gate_share = shares(gate_total, got[2])
    down.pieces = got[3]

    def attention_half(other, kv_grad=None):
        return lambda v: attention_grad(
            place, query_low, v, attended[other], log_total, out_rows, kv_all, rows, chunk, other, kv_grad
        )

    (query_grad_mine, kv_grad), gate_got, *got = steps.run(
        [(attention_half(0), branch_grad[0]), (first_round, gate_share)]
        + [(second_round, sent) for sent in branch_sent[:-1]],
        2,
    )
    gate_two = rows_joined(gate_share, gate_got)
    for j, value in enumerate(got):
        branch_kept[j], branch_sent[j] = reduce_second(branch_kept[j], value)
    (query_grad_other, kv_grad), gate_got = steps.run(
        [(attention_half(1, kv_grad), branch_grad[1]), (second_round, gate_two)], 2
    )
    gate_half = rows_joined(gate_two, gate_got)
    query_grad = (query_grad_mine, query_grad_other)
    kv_grad = kv_grad.astype(bf16)
    if cell_count > 1:
        kv_grad_cell = block(kv_grad, cell, CELL * chunk).astype(f32)
        for step in range(1, cell_count):
            piece = block(kv_grad, (cell + step) % cell_count, CELL * chunk)
            kv_grad_cell = kv_grad_cell + cell_send(piece, step).astype(f32)
        kv_grad = kv_grad_cell.astype(bf16)
    kv_grad = kv_grad.reshape(CELL, fsdp_count, rows, 2 * HEAD_DIM)

    def kv_piece(k):
        return block(kv_grad, (fsdp_here + k) % fsdp_count, 1, 1)

    def fsdp_piece(values, k):
        return block(values, (fsdp_here + k) % fsdp_count, weight_rows)

    up_total = up.total(up_mine)
    got = steps.run(
        [(sends[k], kv_piece(k)) for k in range(1, fsdp_count)]
        + [(first_round, sent) for sent in branch_sent]
        + [
            (shares_sent, up_total),
            (
                lambda v: sum(dot(half, branch, TN) for half, branch in zip(*v)).astype(bf16),
                (attended, branch_grad),
            ),
        ]
    )
    kv_total = kv_piece(0).astype(f32)
    for value in got[: fsdp_count - 1]:
        kv_total = kv_total + value.astype(f32)
    kv_total = kv_total.reshape(cell_tokens, 2 * HEAD_DIM)
    branch_sums = [
        kept.astype(f32) + value.astype(f32)
        for kept, value in zip(branch_kept, got[fsdp_count - 1 :])
    ]
    outputs = hidden_mid + branch_sums[0]
    up_got, out_partial = got[-2:]
    up_share = shares(up_total, up_got)

    projected, gate_got, up_got, *branch_got = steps.run(
        [
            (
                lambda v: project_grad(
                    place, *normed_attn, angles, gains, qkv_rows, query_grad, v, qkv_pieces, rows
                ),
                kv_total,
            ),
            (twin_send, gate_half),
            (first_round, up_share),
        ]
        + [
            (lambda v, j=j: pair_send(v, j, pair), value.astype(bf16))
            for j, value in enumerate(branch_sums[1:], 1)
        ],
        1,
    )
    *qkv_grad, attn_mine, attn_other, head_gain_grad, attention_gain_grad = projected
    for value in branch_got:
        outputs = outputs + value.astype(f32)
    outputs = outputs.astype(bf16)
    gate_halves = (gate_half, gate_got)
    up_two = rows_joined(up_share, up_got)

    def gather_place(side, odd, half, whole):
        return place_blocks(
            whole,
            gate_up_weight.shape,
            half,
            (weight_rows, unit),
            (4, pair * pair_count),
            place,
            lambda i, g, at: (i, g),
            lambda i, g, at: (
                0,
                side * (hidden_width // unit)
                + ((g % pair_count) * pair + (at[3] - g // pair_count + pair) % pair) * CELL
                + token_block(4 * odd + i, at),
            ),
        )

    got = steps.run(
        [
            (twin_send, attn_other),
            (second_round, up_two),
            (down.own()),
            (lambda v: gather_place(0, 0, v, None), gate_halves[0]),
            (
                lambda v: sum(dot(half, grad, TN) for half, grad in zip(*v)).astype(bf16),
                (normed_attn, qkv_grad),
            ),
        ],
        2,
    )
    kept, sent = reduce_first(attn_mine, got[0])
    up_half = rows_joined(up_two, got[1])
    down_own_rows, grad_gate_up, qkv_partial = got[2:]
    gains_here = jnp.concatenate(
        [
            attention_gain_grad[0] / attention_gain,
            mlp_gain_grad,
            head_gain_grad[0],
            head_gain_grad[1],
        ]
    ).reshape(-1, 2 * HEAD_DIM)
    got = steps.run(
        [
            (second_round, sent),
            (lambda v: cell_turn(v, 1, 0), out_partial),
            (twin_send, up_half),
            (lambda v: gather_place(0, 1, *v), (gate_halves[1], grad_gate_up)),
        ],
        1,
    )
    kept, sent = reduce_second(kept, got[0])
    out_partial = got[1]
    up_halves = (up_half, got[2])
    grad_gate_up = got[3]
    down_share = down.total(down_own_rows)
    got = steps.run(
        [
            (first_round, sent),
            (first_round, down_share),
            (lambda v: gather_place(1, 0, *v), (up_halves[0], grad_gate_up)),
        ]
        + [(sends[k], fsdp_piece(out_partial, k)) for k in range(1, fsdp_count)]
    )
    attn_normed_grad = kept.astype(f32) + got[0].astype(f32)
    down_two = rows_joined(down_share, got[1])
    grad_gate_up = got[2]
    out_total = fsdp_piece(out_partial, 0).astype(f32)
    for value in got[3:]:
        out_total = out_total + value.astype(f32)
    out_share = cell_sum(out_total).astype(bf16)
    got = steps.run(
        [
            (second_round, down_two),
            (first_round, out_share),
            (lambda v: gather_place(1, 1, *v), (up_halves[1], grad_gate_up)),
        ]
        + [(sends[k], fsdp_piece(qkv_partial, k)) for k in range(1, fsdp_count)]
    )
    down_half = rows_joined(down_two, got[0])
    out_two = rows_joined(out_share, got[1])
    grad_gate_up = got[2]
    qkv_total = fsdp_piece(qkv_partial, 0).astype(f32)
    for value in got[3:]:
        qkv_total = qkv_total + value.astype(f32)
    qkv_share = cell_sum(qkv_total).astype(bf16)
    got = steps.run(
        [
            (twin_send, down_half),
            (second_round, out_two),
            (first_round, qkv_share),
            (sum_everywhere, gains_here),
            (
                lambda v: jax.vjp(lambda u: rms_scale(u, attention_gain), source)[1](v)[0],
                attn_normed_grad,
            ),
        ]
    )
    grad_down_halves = (down_half, got[0])
    out_half = rows_joined(out_two, got[1])
    qkv_two = rows_joined(qkv_share, got[2])
    gain_sums = got[3].reshape(-1)
    grad_inputs = (hidden_grad + got[4]).astype(bf16)
    got = steps.run(
        [
            (twin_send, out_half),
            (second_round, qkv_two),
            (lambda v: place_rows(v, place), grad_down_halves),
        ]
    )
    out_halves = (out_half, got[0])
    qkv_half = rows_joined(qkv_two, got[1])
    grad_down = got[2]
    got = steps.run(
        [
            (twin_send, qkv_half),
            (lambda v: place_columns(v, width // CELL, place), out_halves),
        ]
    )
    grad_out = got[1]
    grad_qkv = place_heads([qkv_half, got[0]], place)
    attention_gain_sum, mlp_gain_sum = gain_sums[:width], gain_sums[width : 2 * width]
    head_sums = gain_sums[2 * width :].reshape(4, HEAD_DIM)

    gain_sums = (
        attention_gain_sum,
        head_sums[0] + head_sums[1],
        head_sums[2],
        mlp_gain_sum,
    )

    return (
        outputs,
        grad_inputs,
        gain_sums[0],
        grad_qkv,
        gain_sums[1],
        gain_sums[2],
        grad_out,
        gain_sums[3],
        grad_gate_up,
        grad_down,
    )


def solution(mesh):
    return jax.shard_map(
        body,
        mesh=mesh,
        in_specs=(
            P(("ctx", "fsdp"), None),
            P(),
            P("fsdp", None),
            P(),
            P(),
            P("fsdp", None),
            P(),
            P("fsdp", None),
            P("fsdp", None),
            P(("ctx", "fsdp"), None),
        ),
        out_specs=(
            P(("ctx", "fsdp"), None),
            P(("ctx", "fsdp"), None),
            P(),
            P("fsdp", None),
            P(),
            P(),
            P("fsdp", None),
            P(),
            P("fsdp", None),
            P("fsdp", None),
        ),
        check_vma=False,
    )
```

time: 1090 us -> 831 us (0.76)
  waiting for transfers between devices: 411 us -> 300 us
  Pallas kernels: 128 us -> 222 us
  matrix products: 85.8 us -> 12.6 us
  starting transfers between devices: 179 us -> 111 us
  blocking collectives: 43.1 us -> 0 us
  local copies, waits for them, and re-layouts: 137 us -> 98.1 us
  other arithmetic: 91.9 us -> 74.9 us
    ppermute x136 -> x17, waiting for transfers between devices: 154 us -> 0.04 us  [xor_send(): lax.ppermute(values, 'ctx', [(i, i ^ distance) for i in range(count)])]
    pallas_call x17 -> x23, Pallas kernels: 107 us -> 201 us  [the longest x8 54.2 us: place_blocks(): pl.pallas_call(place_kernel, grid_spec=pltpu.PrefetchScalarGridSpec(num_s...]
    ppermute x136 -> x17, starting transfers between devices: 81.9 us -> 1.5 us  [xor_send(): lax.ppermute(values, 'ctx', [(i, i ^ distance) for i in range(count)])]
    dot_general x20 -> x6, matrix products: 85.8 us -> 12.6 us  [dot(): return lax.dot_general(left, right, dims, preferred_element_type=f32)]
    psum x1 -> x0, blocking collectives: 43.1 us -> none  [body(): lax.psum((attention_gain_grad, query_gain_grad, key_gain_grad, mlp_gain_g...]
    dynamic_update_slice x67 -> x8, local copies, waits for them, and re-layouts: 47.5 us -> 4.85 us  [put(): lax.dynamic_update_slice_in_dim(whole, part, index * part.shape[axis], axis)]
    ppermute x0 -> x39, starting transfers between devices: none -> 42.1 us  [the longest x34 38.6 us: round_send(): return lax.ppermute(values, 'ctx', pairs)]
    ppermute x24 -> x42, waiting for transfers between devices: 214 us -> 254 us  [fsdp_send(): lax.ppermute(values, 'fsdp', [(i, (i + step) % count) for i in range(coun...]
  transfers between devices with their start and end apart: 167 -> 108, of which waited for: 42 -> 39; matrix products, arithmetic and copies ran while one was open for 28% -> 13% of each run, Pallas kernels for 11% -> 25%
where the time goes in v2:
time: 831 us; the launch traced here: 822 us
  waiting for transfers between devices  300 us (36%)
  Pallas kernels  222 us (27%)
  starting transfers between devices  111 us (13%)
  local copies, waits for them, and re-layouts  98.1 us (12%)
  other arithmetic  74.9 us (9%)
  matrix products  12.6 us (2%)
    ppermute x42, waiting for transfers between devices, fsdp_send(): lax.ppermute(values, 'fsdp', [(i, (i + step) % count) for i in range(coun...  254 us
    ppermute x42, starting transfers between devices, fsdp_send(): lax.ppermute(values, 'fsdp', [(i, (i + step) % count) for i in range(coun...  54.2 us
    pallas_call x8, Pallas kernels, place_blocks(): pl.pallas_call(place_kernel, grid_spec=pltpu.PrefetchScalarGridSpec(num_s...  54.2 us
    unnamed x379, local copies, waits for them, and re-layouts  46.5 us
    pallas_call x4, Pallas kernels, feed(): pl.pallas_call(feed_kernel, grid=(tokens // rows,), in_specs=[by_row(widt...  45.4 us
    pallas_call x2, Pallas kernels, attention_grad(): pl.pallas_call(functools.partial(attention_grad_kernel, chunk, other), gr...  43.1 us
    ppermute x34, starting transfers between devices, round_send(): return lax.ppermute(values, 'ctx', pairs)  38.6 us
    concatenate x20, other arithmetic, rows_joined(): return jnp.concatenate(parts, axis=0)  29.5 us
  transfers between devices with their start and end apart: 108, of which 39 were waited for; matrix products, arithmetic and copies ran while one was open for 13% of the time, Pallas kernels for 25%

profile of v2, /device:TPU:0, one launch (start us, length us, event | category | flops | bytes accessed | tf_op | source)
XLA Modules:
  0.0 822.5 jit_solution(15206282414694004863)
XLA Ops:
  26.7 13.8 %collective-permute-done.3.refs_2_ = bf16[512,384]{1,0:T(8,128)(2,1)S(1)} collective-permute-done((bf16[512,384]{1,0:T(8,128)(2,1)S(1)}, bf16[512,384]{1,0:T(8,128)(2,1)S(1)}, u32[]{:S(2)}, u32[]{:S(2)}) %collective-permute-start.3) | collective-permute-done | bytes 393248 | tf_op jit(solution)/shard_map/ppermute | solution.py:50
  46.6 8.0 collective-permute-done.5.refs_3_
  61.4 9.7 %shard_map.177 = (f32[1024,384]{1,0:T(8,128)S(1)}, bf16[1024,256]{1,0:T(8,128)(2,1)S(1)}, bf16[1024,128]{1,0:T(8,128)(2,1)S(1)}) custom-call(s32[4]{0:T(128)S(1)} %pad_add_fusion.place_ref, bf16[512,2048]{1,0:T(8,128)(2,1)S(1)} %pad_maximum_fusion.2.even_ref, bf16[512,2048]{1,0:T(8,128)(2,1)} %collective-permute-done.4.odd_ref, ...), custom_call_target="tpu_custom_call" | custom-call | flops 1610612736 | bytes 8000000 | tf_op jit(solution)/shard_map/pallas_call | solution.py:259
  85.3 28.9 %collective-permute-done.13 = bf16[512,256]{1,0:T(8,128)(2,1)S(1)} collective-permute-done((bf16[512,256]{1,0:T(8,128)(2,1)S(1)}, bf16[512,256]{1,0:T(8,128)(2,1)S(1)}, u32[]{:S(2)}, u32[]{:S(2)}) %collective-permute-start.13) | collective-permute-done | bytes 262176 | tf_op jit(solution)/shard_map/ppermute | solution.py:50
  128.2 21.4 %shard_map.179 = (bf16[512,256]{1,0:T(8,128)(2,1)S(1)}, bf16[512,256]{1,0:T(8,128)(2,1)S(1)}, f32[8,1,512]{2,1,0:T(1,128)S(1)}) custom-call(s32[4]{0:T(128)S(1)} %pad_add_fusion.place_ref, bf16[1024,256]{1,0:T(8,128)(2,1)S(1)} %copy-done.64, bf16[4096,128]{1,0:T(8,128)(2,1)S(1)} %bitcast.67), custom_call_target="tpu_custom_call" | custom-call | flops 16000000000 | bytes 8000000 | tf_op jit(solution)/shard_map/pallas_call | solution.py:477
  156.5 12.0 %collective-permute-done.19 = bf16[256,1024]{1,0:T(8,128)(2,1)S(1)} collective-permute-done((bf16[256,1024]{1,0:T(8,128)(2,1)S(1)}, bf16[256,1024]{1,0:T(8,128)(2,1)S(1)}, u32[]{:S(2)}, u32[]{:S(2)}) %collective-permute-start.19) | collective-permute-done | bytes 524320 | tf_op jit(solution)/shard_map/ppermute | solution.py:55
  183.4 10.3 %collective-permute-done.22 = bf16[64,2048]{1,0:T(8,128)(2,1)S(1)} collective-permute-done((bf16[64,2048]{1,0:T(8,128)(2,1)}, bf16[64,2048]{1,0:T(8,128)(2,1)S(1)}, u32[]{:S(2)}, u32[]{:S(2)}) %collective-permute-start.22) | collective-permute-done | bytes 262176 | tf_op jit(solution)/shard_map/ppermute | solution.py:50
  206.0 11.8 %collective-permute-done.26 = bf16[128,1024]{1,0:T(8,128)(2,1)S(1)} collective-permute-done((bf16[128,1024]{1,0:T(8,128)(2,1)S(1)}, bf16[128,1024]{1,0:T(8,128)(2,1)S(1)}, u32[]{:S(2)}, u32[]{:S(2)}) %collective-permute-start.26) | collective-permute-done | bytes 262176 | tf_op jit(solution)/shard_map/ppermute | solution.py:50
  222.7 14.9 %collective-permute-done.30 = bf16[128,1024]{1,0:T(8,128)(2,1)S(1)} collective-permute-done((bf16[128,1024]{1,0:T(8,128)(2,1)S(1)}, bf16[128,1024]{1,0:T(8,128)(2,1)S(1)}, u32[]{:S(2)}, u32[]{:S(2)}) %collective-permute-start.30) | collective-permute-done | bytes 262176 | tf_op jit(solution)/shard_map/ppermute | solution.py:50
  243.4 17.8 %collective-permute-done.34 = bf16[128,1024]{1,0:T(8,128)(2,1)S(1)} collective-permute-done((bf16[128,1024]{1,0:T(8,128)(2,1)S(1)}, bf16[128,1024]{1,0:T(8,128)(2,1)S(1)}, u32[]{:S(2)}, u32[]{:S(2)}) %collective-permute-start.34) | collective-permute-done | bytes 262176 | tf_op jit(solution)/shard_map/ppermute | solution.py:50
  268.4 12.5 %collective-permute-done.37 = bf16[128,1024]{1,0:T(8,128)(2,1)S(1)} collective-permute-done((bf16[128,1024]{1,0:T(8,128)(2,1)S(1)}, bf16[128,1024]{1,0:T(8,128)(2,1)S(1)}, u32[]{:S(2)}, u32[]{:S(2)}) %collective-permute-start.37) | collective-permute-done | bytes 262176 | tf_op jit(solution)/shard_map/ppermute | solution.py:50
  287.3 14.4 %collective-permute-done.40 = bf16[128,1024]{1,0:T(8,128)(2,1)S(1)} collective-permute-done((bf16[128,1024]{1,0:T(8,128)(2,1)S(1)}, bf16[128,1024]{1,0:T(8,128)(2,1)S(1)}, u32[]{:S(2)}, u32[]{:S(2)}) %collective-permute-start.40) | collective-permute-done | bytes 262176 | tf_op jit(solution)/shard_map/ppermute | solution.py:50
  316.2 14.3 %collective-permute-done.42 = bf16[128,1024]{1,0:T(8,128)(2,1)S(1)} collective-permute-done((bf16[128,1024]{1,0:T(8,128)(2,1)S(1)}, bf16[128,1024]{1,0:T(8,128)(2,1)S(1)}, u32[]{:S(2)}, u32[]{:S(2)}) %collective-permute-start.42) | collective-permute-done | bytes 262176 | tf_op jit(solution)/shard_map/ppermute | solution.py:50
  332.8 11.7 %shard_map.184 = (bf16[512,512]{1,0:T(8,128)(2,1)S(1)}, bf16[512,1024]{1,0:T(8,128)(2,1)S(1)}, bf16[512,2048]{1,0:T(8,128)(2,1)S(1)}, bf16[512,2048]{1,0:T(8,128)(2,1)}) custom-call(bf16[512,2048]{1,0:T(8,128)(2,1)} %collective-permute-done.41.normed_ref.refs_3_, bf16[512,2048]{1,0:T(8,128)(2,1)} %collective-permute-done.32.outer_ref.refs_7_, ...), custom_call_target="tpu_custom_call" | custom-call | flops 6442450944 | bytes 16000000 | tf_op jit(solution)/shard_map/pallas_call | solution.py:614
  345.4 11.2 %shard_map.185 = (bf16[512,512]{1,0:T(8,128)(2,1)S(1)}, bf16[512,1024]{1,0:T(8,128)(2,1)S(1)}, bf16[512,2048]{1,0:T(8,128)(2,1)S(1)}, bf16[512,2048]{1,0:T(8,128)(2,1)S(1)}) custom-call(bf16[512,2048]{1,0:T(8,128)(2,1)} %constant_dynamic-update-slice_fusion.6.normed_ref.refs_2_, bf16[512,2048]{1,0:T(8,128)(2,1)} %copy-done.79, ...), custom_call_target="tpu_custom_call" | custom-call | flops 6442450944 | bytes 16000000 | tf_op jit(solution)/shard_map/pallas_call | solution.py:614
  360.3 11.7 %shard_map.186 = (bf16[512,512]{1,0:T(8,128)(2,1)S(1)}, bf16[512,1024]{1,0:T(8,128)(2,1)S(1)}, bf16[512,2048]{1,0:T(8,128)(2,1)S(1)}, bf16[512,2048]{1,0:T(8,128)(2,1)}) custom-call(bf16[512,2048]{1,0:T(8,128)(2,1)} %collective-permute-done.35.normed_ref.refs_1_, bf16[512,2048]{1,0:T(8,128)(2,1)} %collective-permute-done.14.outer_ref.refs_5_, ...), custom_call_target="tpu_custom_call" | custom-call | flops 6442450944 | bytes 16000000 | tf_op jit(solution)/shard_map/pallas_call | solution.py:614
  375.7 10.9 %shard_map.187 = (bf16[512,512]{1,0:T(8,128)(2,1)S(1)}, bf16[512,1024]{1,0:T(8,128)(2,1)S(1)}, bf16[512,2048]{1,0:T(8,128)(2,1)S(1)}, bf16[512,2048]{1,0:T(8,128)(2,1)S(1)}) custom-call(bf16[512,2048]{1,0:T(8,128)(2,1)} %copy-done.69, bf16[512,2048]{1,0:T(8,128)(2,1)} %constant_dynamic-update-slice_fusion.outer_ref.refs_4_, bf16[2048,1024]{1,0:T(8,128)(2,1)} %copy-done.102, ...), custom_call_target="tpu_custom_call" | custom-call | flops 6442450944 | bytes 16000000 | tf_op jit(solution)/shard_map/pallas_call | solution.py:614
  405.3 12.7 %collective-permute-done.50 = bf16[256,512]{1,0:T(8,128)(2,1)S(1)} collective-permute-done((bf16[256,512]{1,0:T(8,128)(2,1)S(1)}, bf16[256,512]{1,0:T(8,128)(2,1)S(1)}, u32[]{:S(2)}, u32[]{:S(2)}) %collective-permute-start.50) | collective-permute-done | bytes 262176 | tf_op jit(solution)/shard_map/ppermute | solution.py:50
  447.9 8.3 %collective-permute-done.55 = bf16[256,512]{1,0:T(8,128)(2,1)S(1)} collective-permute-done((bf16[256,512]{1,0:T(8,128)(2,1)S(1)}, bf16[256,512]{1,0:T(8,128)(2,1)S(1)}, u32[]{:S(2)}, u32[]{:S(2)}) %collective-permute-start.55) | collective-permute-done | bytes 262176 | tf_op jit(solution)/shard_map/ppermute | solution.py:50
  498.1 7.9 collective-permute-done.61
  514.7 19.6 %shard_map.193 = (f32[512,256]{1,0:T(8,128)S(1)}, f32[4096,128]{1,0:T(8,128)S(1)}) custom-call(s32[4]{0:T(128)S(1)} %pad_add_fusion.place_ref, bf16[1024,256]{1,0:T(8,128)(2,1)S(1)} %copy-done.65, bf16[512,2048]{1,0:T(8,128)(2,1)} %pad_maximum_fusion.4.branch_ref, bf16[512,256]{1,0:T(8,128)(2,1)S(1)} %copy-done.54, f32[8,1,512]{2,1,0:T(1,128)S(1)} %copy-done.68, ...), custom_call_target="tpu_custom_call" | custom-call | flops 17999998976 | bytes 12000000 | tf_op jit(solution)/shard_map/pallas_call | solution.py:554
  544.6 23.5 %shard_map.194 = (f32[512,256]{1,0:T(8,128)S(1)}, f32[4096,128]{1,0:T(8,128)S(1)}) custom-call(s32[4]{0:T(128)S(1)} %pad_add_fusion.place_ref, bf16[1024,256]{1,0:T(8,128)(2,1)S(1)} %copy-done.65, bf16[512,2048]{1,0:T(8,128)(2,1)} %collective-permute-done.58.branch_ref, bf16[512,256]{1,0:T(8,128)(2,1)S(1)} %copy-done.57, f32[8,1,512]{2,1,0:T(1,128)S(1)} %copy-done.68, ...), custom_call_target="tpu_custom_call" | custom-call | flops 17999998976 | bytes 12000000 | tf_op jit(solution)/shard_map/pallas_call | solution.py:554
  585.1 11.0 %collective-permute-done.71 = bf16[8,1,128,128]{3,2,0,1:T(8,128)(2,1)S(1)} collective-permute-done((bf16[8,1,128,128]{3,2,0,1:T(8,128)(2,1)S(1)}, bf16[8,1,128,128]{3,2,0,1:T(8,128)(2,1)S(1)}, u32[]{:S(2)}, u32[]{:S(2)}) %collective-permute-start.71) | collective-permute-done | bytes 262176 | tf_op jit(solution)/shard_map/ppermute | solution.py:50
  609.0 13.3 %shard_map.195 = (bf16[512,384]{1,0:T(8,128)(2,1)S(1)}, bf16[512,384]{1,0:T(8,128)(2,1)S(1)}, bf16[512,2048]{1,0:T(8,128)(2,1)S(1)}, bf16[512,2048]{1,0:T(8,128)...) custom-call(s32[4]{0:T(128)S(1)} %pad_add_fusion.place_ref, bf16[512,2048]{1,0:T(8,128)(2,1)S(1)} %pad_maximum_fusion.2.even_ref, ...), custom_call_target="tpu_custom_call" | custom-call | flops 1610612736 | bytes 12000000 | tf_op jit(solution)/shard_map/pallas_call | solution.py:373
  640.5 7.8 shard_map.197.refs_0_
  657.7 7.3 pad_maximum_fusion.1.shard_ref
  678.4 7.8 shard_map.198.refs_0_
  688.4 9.1 %collective-permute-done.83 = bf16[256,2048]{1,0:T(8,128)(2,1)} collective-permute-done((bf16[256,2048]{1,0:T(8,128)(2,1)}, bf16[256,2048]{1,0:T(8,128)(2,1)}, u32[]{:S(2)}, u32[]{:S(2)}) %collective-permute-start.83) | collective-permute-done | bytes 1048608 | tf_op jit(solution)/shard_map/ppermute | solution.py:78
  706.5 11.5 %shard_map.199.refs_0_ = f32[512,16384]{1,0:T(8,128)} custom-call(s32[4]{0:T(128)S(1)} %pad_add_fusion.place_ref, bf16[2048,1024]{1,0:T(8,128)(2,1)} %pad_maximum_fusion.1.shard_ref, f32[512,16384]{1,0:T(8,128)} %shard_map.198.refs_0_), custom_call_target="tpu_custom_call", output_to_operand_aliasing={{}: (2, {})} | custom-call | bytes 12582912 | tf_op jit(solution)/shard_map/pallas_call | solution.py:670
  717.9 7.9 collective-permute-done.88
  735.3 11.4 %shard_map.200 = f32[512,16384]{1,0:T(8,128)} custom-call(s32[4]{0:T(128)S(1)} %pad_add_fusion.place_ref, bf16[2048,1024]{1,0:T(8,128)(2,1)} %collective-permute-done.84.shard_ref, f32[512,16384]{1,0:T(8,128)} %shard_map.199.refs_0_), custom_call_target="tpu_custom_call", output_to_operand_aliasing={{}: (2, {})} | custom-call | bytes 12582912 | tf_op jit(solution)/shard_map/pallas_call | solution.py:670
  746.8 17.6 %collective-permute-done.93 = bf16[512,384]{1,0:T(8,128)(2,1)S(1)} collective-permute-done((bf16[512,384]{1,0:T(8,128)(2,1)S(1)}, bf16[512,384]{1,0:T(8,128)(2,1)S(1)}, u32[]{:S(2)}, u32[]{:S(2)}) %collective-permute-start.93) | collective-permute-done | bytes 393248 | tf_op jit(solution)/shard_map/ppermute | solution.py:50
  (744 shorter events, 407.2 us)
Async XLA Ops:
  72.7 41.6 %collective-permute-start.12 = (bf16[256,2048]{1,0:T(8,128)(2,1)S(1)}, bf16[256,2048]{1,0:T(8,128)(2,1)S(1)}, u32[]{:S(2)}, u32[]{:S(2)}) collective-permute-start(bf16[256,2048]{1,0:T(8,128)(2,1)S(1)} %pad_maximum_fusion.11), channel_id=1, source_target_pairs={{0,16},{4,12},{8,24},{12,4},{16,0},{20,28},{24,8},{28,20},{1,17},{... | collective-permute-start | bytes 3145736 | tf_op jit(solution)/shard_map/ppermute | solution.py:78
  78.4 35.8 %collective-permute-start.10 = (bf16[8,1,128,128]{3,2,1,0:T(8,128)(2,1)S(1)}, bf16[8,1,128,128]{3,2,1,0:T(8,128)(2,1)S(1)}, u32[]{:S(2)}, u32[]{:S(2)}) collective-permute-start(bf16[8,1,128,128]{3,2,1,0:T(8,128)(2,1)S(1)} %bitcast.70), channel_id=1, source_target_pairs={{0,2},{1,3},{2,0},{3,1},{4,6},{5,7},{6,4},{7,5},{8,10},{9,11},{10,... | collective-permute-start | bytes 786440 | tf_op jit(solution)/shard_map/ppermute | solution.py:50
  78.8 35.5 %collective-permute-start.11 = (bf16[8,1,128,128]{3,2,1,0:T(8,128)(2,1)S(1)}, bf16[8,1,128,128]{3,2,1,0:T(8,128)(2,1)S(1)}, u32[]{:S(2)}, u32[]{:S(2)}) collective-permute-start(bf16[8,1,128,128]{3,2,1,0:T(8,128)(2,1)S(1)} %bitcast.71), channel_id=1, source_target_pairs={{0,3},{1,0},{2,1},{3,2},{4,7},{5,4},{6,5},{7,6},{8,11},{9,8},{10,9... | collective-permute-start | bytes 786440 | tf_op jit(solution)/shard_map/ppermute | solution.py:50
  80.5 33.8 %collective-permute-start.9 = (bf16[8,1,128,128]{3,2,1,0:T(8,128)(2,1)S(1)}, bf16[8,1,128,128]{3,2,1,0:T(8,128)(2,1)S(1)}, u32[]{:S(2)}, u32[]{:S(2)}) collective-permute-start(bf16[8,1,128,128]{3,2,1,0:T(8,128)(2,1)S(1)} %bitcast.72), channel_id=1, source_target_pairs={{0,1},{1,2},{2,3},{3,0},{4,5},{5,6},{6,7},{7,4},{8,9},{9,10},{10,1... | collective-permute-start | bytes 786440 | tf_op jit(solution)/shard_map/ppermute | solution.py:50
  80.8 33.5 %collective-permute-start.13 = (bf16[512,256]{1,0:T(8,128)(2,1)S(1)}, bf16[512,256]{1,0:T(8,128)(2,1)S(1)}, u32[]{:S(2)}, u32[]{:S(2)}) collective-permute-start(bf16[512,256]{1,0:T(8,128)(2,1)S(1)} %copy-done.156), channel_id=1, source_target_pairs={{0,2},{1,3},{2,0},{3,1},{4,6},{5,7},{6,4},{7,5},{8,10},{9,11},{10,... | collective-permute-start | bytes 786440 | tf_op jit(solution)/shard_map/ppermute | solution.py:50
  115.5 37.6 %collective-permute-start.14 = (bf16[512,2048]{1,0:T(8,128)(2,1)}, bf16[512,2048]{1,0:T(8,128)(2,1)}, u32[]{:S(2)}, u32[]{:S(2)}) collective-permute-start(bf16[512,2048]{1,0:T(8,128)(2,1)} %constant_dynamic-update-slice_fusion.outer_ref.refs_4_), channel_id=1, source_target_pairs={{0,4},{4,0},{8,12},{12,8},{16,20},{20,16},{24,28},{28,24},{1,5},{5... | collective-permute-start | bytes 6291464 | tf_op jit(solution)/shard_map/ppermute | solution.py:40
  115.5 37.6 %collective-permute-start.15 = (bf16[256,1024]{1,0:T(8,128)(2,1)}, bf16[256,1024]{1,0:T(8,128)(2,1)}, u32[]{:S(2)}, u32[]{:S(2)}) collective-permute-start(bf16[256,1024]{1,0:T(8,128)(2,1)} %get-tuple-element.406), channel_id=1, source_target_pairs={{0,1},{1,0},{2,3},{3,2},{4,5},{5,4},{6,7},{7,6},{8,9},{9,8},{10,11... | collective-permute-start | bytes 1572872 | tf_op jit(solution)/shard_map/ppermute | solution.py:55
  116.7 35.0 %all-to-all-start = ((bf16[8,256,256]{2,1,0:T(8,128)(2,1)}), bf16[8,256,256]{2,1,0:T(8,128)(2,1)}, u32[]{:S(2)}, u32[]{:S(2)}) async-start(bf16[8,256,256]{2,1,0:T(8,128)(2,1)} %bitcast.77), calls=%async_computation | async-start | bytes 2097152 | tf_op jit(solution)/shard_map/all_to_all | solution.py:810
  124.2 28.9 %collective-permute-start.16 = (bf16[64,2048]{1,0:T(8,128)(2,1)}, bf16[64,2048]{1,0:T(8,128)(2,1)}, u32[]{:S(2)}, u32[]{:S(2)}) collective-permute-start(bf16[64,2048]{1,0:T(8,128)(2,1)} %get-tuple-element.407), channel_id=1, source_target_pairs={{0,2},{1,3},{2,0},{3,1},{4,6},{5,7},{6,4},{7,5},{8,10},{9,11},{10,... | collective-permute-start | bytes 786440 | tf_op jit(solution)/shard_map/ppermute | solution.py:50
  126.3 26.8 %collective-permute-start.17 = (bf16[64,2048]{1,0:T(8,128)(2,1)}, bf16[64,2048]{1,0:T(8,128)(2,1)}, u32[]{:S(2)}, u32[]{:S(2)}) collective-permute-start(bf16[64,2048]{1,0:T(8,128)(2,1)} %get-tuple-element.408), channel_id=1, source_target_pairs={{0,2},{1,3},{2,0},{3,1},{4,6},{5,7},{6,4},{7,5},{8,10},{9,11},{10,... | collective-permute-start | bytes 786440 | tf_op jit(solution)/shard_map/ppermute | solution.py:50
  171.8 29.2 %collective-permute-start.20 = (bf16[256,2048]{1,0:T(8,128)(2,1)}, bf16[256,2048]{1,0:T(8,128)(2,1)}, u32[]{:S(2)}, u32[]{:S(2)}) collective-permute-start(bf16[256,2048]{1,0:T(8,128)(2,1)} %slice.310), channel_id=1, source_target_pairs={{0,16},{4,12},{8,24},{12,4},{16,0},{20,28},{24,8},{28,20},{1,17},{... | collective-permute-start | bytes 3145736 | tf_op jit(solution)/shard_map/ppermute | solution.py:78
  173.8 26.5 %collective-permute-start.21 = (bf16[128,2048]{1,0:T(8,128)(2,1)S(1)}, bf16[128,2048]{1,0:T(8,128)(2,1)S(1)}, u32[]{:S(2)}, u32[]{:S(2)}) collective-permute-start(bf16[128,2048]{1,0:T(8,128)(2,1)S(1)} %copy-done.91), channel_id=1, source_target_pairs={{0,1},{1,0},{2,3},{3,2},{4,5},{5,4},{6,7},{7,6},{8,9},{9,8},{10,11... | collective-permute-start | bytes 1572872 | tf_op jit(solution)/shard_map/ppermute | solution.py:55
  239.8 27.6 %collective-permute-start.32 = (bf16[512,2048]{1,0:T(8,128)(2,1)S(1)}, bf16[512,2048]{1,0:T(8,128)(2,1)}, u32[]{:S(2)}, u32[]{:S(2)}) collective-permute-start(bf16[512,2048]{1,0:T(8,128)(2,1)S(1)} %constant_dynamic-update-slice_fusion.3.outer_ref.refs_6_), channel_id=1, source_target_pairs={{0,4},{4,0},{8,12},{12,8},{16,20},{20,16},{24,28},{28,24},{1,5},{5... | collective-permute-start | bytes 6291464 | tf_op jit(solution)/shard_map/ppermute | solution.py:40
  240.0 26.8 %collective-permute-start.31 = (bf16[256,2048]{1,0:T(8,128)(2,1)S(1)}, bf16[256,2048]{1,0:T(8,128)(2,1)S(1)}, u32[]{:S(2)}, u32[]{:S(2)}) collective-permute-start(bf16[256,2048]{1,0:T(8,128)(2,1)S(1)} %pad_maximum_fusion.13), channel_id=1, source_target_pairs={{0,16},{4,12},{8,24},{12,4},{16,0},{20,28},{24,8},{28,20},{1,17},{... | collective-permute-start | bytes 3145736 | tf_op jit(solution)/shard_map/ppermute | solution.py:78
  392.6 25.5 %collective-permute-start.49 = (bf16[512,2048]{1,0:T(8,128)(2,1)}, bf16[512,2048]{1,0:T(8,128)(2,1)}, u32[]{:S(2)}, u32[]{:S(2)}) collective-permute-start(bf16[512,2048]{1,0:T(8,128)(2,1)} %get-tuple-element.513), channel_id=1, source_target_pairs={{0,4},{4,0},{8,12},{12,8},{16,20},{20,16},{24,28},{28,24},{1,5},{5... | collective-permute-start | bytes 6291464 | tf_op jit(solution)/shard_map/ppermute | solution.py:40
  475.4 32.8 %collective-permute-start.58 = (bf16[512,2048]{1,0:T(8,128)(2,1)}, bf16[512,2048]{1,0:T(8,128)(2,1)}, u32[]{:S(2)}, u32[]{:S(2)}) collective-permute-start(bf16[512,2048]{1,0:T(8,128)(2,1)} %pad_maximum_fusion.4.branch_ref), channel_id=1, source_target_pairs={{0,4},{4,0},{8,12},{12,8},{16,20},{20,16},{24,28},{28,24},{1,5},{5... | collective-permute-start | bytes 6291464 | tf_op jit(solution)/shard_map/ppermute | solution.py:40
  508.1 29.9 %collective-permute-start.65 = (bf16[256,512]{1,0:T(8,128)(2,1)S(1)}, bf16[256,512]{1,0:T(8,128)(2,1)S(1)}, u32[]{:S(2)}, u32[]{:S(2)}) collective-permute-start(bf16[256,512]{1,0:T(8,128)(2,1)S(1)} %get-tuple-element.579), channel_id=1, source_target_pairs={{0,2},{1,3},{2,0},{3,1},{4,6},{5,7},{6,4},{7,5},{8,10},{9,11},{10,... | collective-permute-start | bytes 786440 | tf_op jit(solution)/shard_map/ppermute | solution.py:50
  509.4 28.7 %collective-permute-start.64 = (bf16[256,512]{1,0:T(8,128)(2,1)S(1)}, bf16[256,512]{1,0:T(8,128)(2,1)S(1)}, u32[]{:S(2)}, u32[]{:S(2)}) collective-permute-start(bf16[256,512]{1,0:T(8,128)(2,1)S(1)} %get-tuple-element.578), channel_id=1, source_target_pairs={{0,2},{1,3},{2,0},{3,1},{4,6},{5,7},{6,4},{7,5},{8,10},{9,11},{10,... | collective-permute-start | bytes 786440 | tf_op jit(solution)/shard_map/ppermute | solution.py:50
  511.1 26.9 %collective-permute-start.63 = (bf16[256,2048]{1,0:T(8,128)(2,1)}, bf16[256,2048]{1,0:T(8,128)(2,1)}, u32[]{:S(2)}, u32[]{:S(2)}) collective-permute-start(bf16[256,2048]{1,0:T(8,128)(2,1)} %slice.335), channel_id=1, source_target_pairs={{0,16},{4,12},{8,24},{12,4},{16,0},{20,28},{24,8},{28,20},{1,17},{... | collective-permute-start | bytes 3145736 | tf_op jit(solution)/shard_map/ppermute | solution.py:78
  538.1 32.0 %collective-permute-start.68 = (bf16[64,2048]{1,0:T(8,128)(2,1)}, bf16[64,2048]{1,0:T(8,128)(2,1)S(1)}, u32[]{:S(2)}, u32[]{:S(2)}) collective-permute-start(bf16[64,2048]{1,0:T(8,128)(2,1)} %get-tuple-element.590), channel_id=1, source_target_pairs={{0,2},{1,3},{2,0},{3,1},{4,6},{5,7},{6,4},{7,5},{8,10},{9,11},{10,... | collective-permute-start | bytes 786440 | tf_op jit(solution)/shard_map/ppermute | solution.py:50
  539.4 30.7 %collective-permute-start.67 = (bf16[256,512]{1,0:T(8,128)(2,1)}, bf16[256,512]{1,0:T(8,128)(2,1)S(1)}, u32[]{:S(2)}, u32[]{:S(2)}) collective-permute-start(bf16[256,512]{1,0:T(8,128)(2,1)} %get-tuple-element.588), channel_id=1, source_target_pairs={{0,2},{1,3},{2,0},{3,1},{4,6},{5,7},{6,4},{7,5},{8,10},{9,11},{10,... | collective-permute-start | bytes 786440 | tf_op jit(solution)/shard_map/ppermute | solution.py:50
  543.9 26.4 %collective-permute-start.66 = (bf16[1024,1024]{1,0:T(8,128)(2,1)}, bf16[1024,1024]{1,0:T(8,128)(2,1)}, u32[]{:S(2)}, u32[]{:S(2)}) collective-permute-start(bf16[1024,1024]{1,0:T(8,128)(2,1)} %pad_maximum_fusion.5), channel_id=1, source_target_pairs={{0,16},{4,12},{8,24},{12,4},{16,0},{20,28},{24,8},{28,20},{1,17},{... | collective-permute-start | bytes 6291464 | tf_op jit(solution)/shard_map/ppermute | solution.py:78
  571.9 32.3 %collective-permute-start.74 = (bf16[512,512]{1,0:T(8,128)(2,1)S(1)}, bf16[512,512]{1,0:T(8,128)(2,1)S(1)}, u32[]{:S(2)}, u32[]{:S(2)}) collective-permute-start(bf16[512,512]{1,0:T(8,128)(2,1)S(1)} %constant_dynamic-slice_fusion.10), channel_id=1, source_target_pairs={{0,1},{1,0},{2,3},{3,2},{4,5},{5,4},{6,7},{7,6},{8,9},{9,8},{10,11... | collective-permute-start | bytes 1572872 | tf_op jit(solution)/shard_map/ppermute | solution.py:55
  572.6 31.6 %collective-permute-start.73 = (bf16[128,2048]{1,0:T(8,128)(2,1)S(1)}, bf16[128,2048]{1,0:T(8,128)(2,1)S(1)}, u32[]{:S(2)}, u32[]{:S(2)}) collective-permute-start(bf16[128,2048]{1,0:T(8,128)(2,1)S(1)} %slice.339), channel_id=1, source_target_pairs={{0,8},{4,20},{8,0},{12,28},{16,24},{20,4},{24,16},{28,12},{1,9},{5... | collective-permute-start | bytes 1572872 | tf_op jit(solution)/shard_map/ppermute | solution.py:78
  573.8 30.5 %collective-permute-start.72 = (bf16[128,2048]{1,0:T(8,128)(2,1)S(1)}, bf16[128,2048]{1,0:T(8,128)(2,1)S(1)}, u32[]{:S(2)}, u32[]{:S(2)}) collective-permute-start(bf16[128,2048]{1,0:T(8,128)(2,1)S(1)} %slice.337), channel_id=1, source_target_pairs={{0,8},{4,20},{8,0},{12,28},{16,24},{20,4},{24,16},{28,12},{1,9},{5... | collective-permute-start | bytes 1572872 | tf_op jit(solution)/shard_map/ppermute | solution.py:78
  630.7 27.0 %collective-permute-start.80 = (bf16[1024,1024]{1,0:T(8,128)(2,1)}, bf16[1024,1024]{1,0:T(8,128)(2,1)}, u32[]{:S(2)}, u32[]{:S(2)}) collective-permute-start(bf16[1024,1024]{1,0:T(8,128)(2,1)} %pad_maximum_fusion.6), channel_id=1, source_target_pairs={{0,16},{4,12},{8,24},{12,4},{16,0},{20,28},{24,8},{28,20},{1,17},{... | collective-permute-start | bytes 6291464 | tf_op jit(solution)/shard_map/ppermute | solution.py:78
  632.1 25.5 %collective-permute-start.79 = (bf16[512,2048]{1,0:T(8,128)(2,1)}, bf16[512,2048]{1,0:T(8,128)(2,1)S(1)}, u32[]{:S(2)}, u32[]{:S(2)}) collective-permute-start(bf16[512,2048]{1,0:T(8,128)(2,1)} %get-tuple-element.634), channel_id=1, source_target_pairs={{0,4},{4,0},{8,12},{12,8},{16,20},{20,16},{24,28},{28,24},{1,5},{5... | collective-permute-start | bytes 6291464 | tf_op jit(solution)/shard_map/ppermute | solution.py:40
  665.0 32.5 %collective-permute-start.84 = (bf16[2048,1024]{1,0:T(8,128)(2,1)}, bf16[2048,1024]{1,0:T(8,128)(2,1)}, u32[]{:S(2)}, u32[]{:S(2)}) collective-permute-start(bf16[2048,1024]{1,0:T(8,128)(2,1)} %pad_maximum_fusion.1.shard_ref), channel_id=1, source_target_pairs={{0,4},{4,0},{8,12},{12,8},{16,20},{20,16},{24,28},{28,24},{1,5},{5... | collective-permute-start | bytes 12582920 | tf_op jit(solution)/shard_map/ppermute | solution.py:40
  697.6 28.3 %collective-permute-start.86 = (bf16[256,2048]{1,0:T(8,128)(2,1)S(1)}, bf16[256,2048]{1,0:T(8,128)(2,1)S(1)}, u32[]{:S(2)}, u32[]{:S(2)}) collective-permute-start(bf16[256,2048]{1,0:T(8,128)(2,1)S(1)} %pad_maximum_fusion.20), channel_id=1, source_target_pairs={{0,8},{4,20},{8,0},{12,28},{16,24},{20,4},{24,16},{28,12},{1,9},{5... | collective-permute-start | bytes 3145736 | tf_op jit(solution)/shard_map/ppermute | solution.py:78
  727.0 37.3 %collective-permute-start.90 = (bf16[512,2048]{1,0:T(8,128)(2,1)S(1)}, bf16[512,2048]{1,0:T(8,128)(2,1)S(1)}, u32[]{:S(2)}, u32[]{:S(2)}) collective-permute-start(bf16[512,2048]{1,0:T(8,128)(2,1)S(1)} %get-tuple-element.679), channel_id=1, source_target_pairs={{0,16},{4,12},{8,24},{12,4},{16,0},{20,28},{24,8},{28,20},{1,17},{... | collective-permute-start | bytes 6291464 | tf_op jit(solution)/shard_map/ppermute | solution.py:78
  728.5 35.8 %collective-permute-start.93 = (bf16[512,384]{1,0:T(8,128)(2,1)S(1)}, bf16[512,384]{1,0:T(8,128)(2,1)S(1)}, u32[]{:S(2)}, u32[]{:S(2)}) collective-permute-start(bf16[512,384]{1,0:T(8,128)(2,1)S(1)} %get-tuple-element.690), channel_id=1, source_target_pairs={{0,2},{1,3},{2,0},{3,1},{4,6},{5,7},{6,4},{7,5},{8,10},{9,11},{10,... | collective-permute-start | bytes 1179656 | tf_op jit(solution)/shard_map/ppermute | solution.py:50
  731.5 32.8 %collective-permute-start.92 = (bf16[512,384]{1,0:T(8,128)(2,1)S(1)}, bf16[512,384]{1,0:T(8,128)(2,1)S(1)}, u32[]{:S(2)}, u32[]{:S(2)}) collective-permute-start(bf16[512,384]{1,0:T(8,128)(2,1)S(1)} %get-tuple-element.689), channel_id=1, source_target_pairs={{0,1},{1,2},{2,3},{3,0},{4,5},{5,6},{6,7},{7,4},{8,9},{9,10},{10,1... | collective-permute-start | bytes 1179656 | tf_op jit(solution)/shard_map/ppermute | solution.py:50
  (260 other events, 2490.2 us)

commit v3 on v2

--- a/solution.py
+++ b/solution.py
@@ -121,47 +121,106 @@
     return xor_send(values, 1)
 
 
+def join_kernel(place_ref, *refs):
+    for n, ref in enumerate(refs[:-1]):
+
+        @pl.when(pl.program_id(0) == n)
+        def _(ref=ref):
+            refs[-1][...] = ref[...]
+
+
+def join(parts, places=None):
+    shape, dtype = parts[0].shape, parts[0].dtype
+    if places is None:
+        places = list(range(len(parts)))
+    size = parts[0].size * 2
+    return pl.pallas_call(
+        join_kernel,
+        grid_spec=pltpu.PrefetchScalarGridSpec(
+            num_scalar_prefetch=1,
+            grid=(len(parts),),
+            in_specs=[pl.BlockSpec(shape, lambda i, at: (0, 0))] * len(parts),
+            out_specs=pl.BlockSpec(shape, lambda i, at: (at[i], 0)),
+        ),
+        out_shape=jax.ShapeDtypeStruct((len(parts) * shape[0], shape[1]), dtype),
+        compiler_params=pltpu.CompilerParams(
+            vmem_limit_bytes=(2 * len(parts) + 2) * size + 4 * 1024 * 1024
+        ),
+        cost_estimate=cost(0, 2 * size * len(parts)),
+    )(jnp.stack([jnp.asarray(p, jnp.int32) for p in places]), *parts)
+
+
 def rows_joined(*parts):
-    return jnp.concatenate(parts, axis=0)
-
-
-def gather_cell(shard):
-    two = rows_joined(shard, first_round(shard))
-    mine = rows_joined(two, second_round(two))
-    return mine, twin_send(mine)
+    return join(parts)
+
+
+def add_kernel(left_ref, right_ref, first_ref, second_ref):
+    total = (left_ref[...].astype(f32) + right_ref[...].astype(f32)).astype(bf16)
+
+    @pl.when(pl.program_id(0) == 0)
+    def _():
+        first_ref[...] = total
+
+    @pl.when(pl.program_id(0) == 1)
+    def _():
+        second_ref[...] = total
+
+
+def add_halves(left, right):
+    rows, columns = left.shape
+    half = jax.ShapeDtypeStruct((rows // 2, columns), bf16)
+    in_spec = pl.BlockSpec((rows // 2, columns), lambda i: (i, 0))
+    out_spec = pl.BlockSpec((rows // 2, columns), lambda i: (0, 0))
+    return pl.pallas_call(
+        add_kernel,
+        grid=(2,),
+        in_specs=[in_spec] * 2,
+        out_specs=[out_spec] * 2,
+        out_shape=[half, half],
+        compiler_params=pltpu.CompilerParams(vmem_limit_bytes=20 * 1024 * 1024),
+        cost_estimate=cost(left.size, 6 * left.size),
+    )(left, right)
 
 
 def reduce_first(mine, from_twin):
-    half = mine.shape[0] // 2
-    total = add_low(mine, from_twin)
-    return total[:half], total[half:]
+    return add_halves(mine, from_twin)
 
 
 def reduce_second(kept, received):
-    half = kept.shape[0] // 2
-    total = add_low(kept, received)
-    return total[:half], total[half:]
-
-
-def reduce_cell(mine, other):
-    kept, sent = reduce_first(mine, twin_send(other))
-    kept, sent = reduce_second(kept, second_round(sent))
-    return kept.astype(f32) + first_round(sent).astype(f32)
-
-
-def sum_everywhere(values):
-    for axis in ("ctx", "fsdp"):
-        count = lax.axis_size(axis)
-        if count & (count - 1):
-            values = lax.psum(values, axis)
-            continue
-        distance = 1
-        while distance < count:
-            values = values + lax.ppermute(
-                values, axis, [(i, i ^ distance) for i in range(count)]
-            )
-            distance *= 2
-    return values
+    return add_halves(kept, received)
+
+
+class SumEverywhere:
+    def __init__(self, values):
+        self.total = values
+        self.rounds = []
+        for axis in ("ctx", "fsdp"):
+            count = lax.axis_size(axis)
+            if count & (count - 1):
+                self.rounds.append(functools.partial(self.whole, axis))
+                continue
+            distance = 1
+            while distance < count:
+                self.rounds.append(functools.partial(self.exchange, axis, count, distance))
+                distance *= 2
+
+    def exchange(self, axis, count, distance, values):
+        return lax.ppermute(values, axis, [(i, i ^ distance) for i in range(count)])
+
+    def whole(self, axis, values):
+        return lax.psum(values, axis) - values
+
+    def part(self):
+        return (self.rounds.pop(0), self.total)
+
+    def add(self, got):
+        self.total = self.total + got
+
+    def finish(self):
+        while self.rounds:
+            function, values = self.part()
+            self.add(function(values))
+        return self.total
 
 
 def blank(shape, dtype):
@@ -171,6 +230,10 @@
         out_shape=jax.ShapeDtypeStruct(shape, dtype),
         cost_estimate=pl.CostEstimate(flops=0, bytes_accessed=0, transcendentals=0),
     )()
+
+
+def vmem(mebibytes, keys=0):
+    return pltpu.CompilerParams(vmem_limit_bytes=mebibytes * 1024 * 1024 + keys * 2560)
 
 
 def cost(flops, moved, transcendentals=0):
@@ -279,7 +342,7 @@
             jax.ShapeDtypeStruct((count * rows, GROUP_WIDTH), bf16),
             jax.ShapeDtypeStruct((count * rows, 2 * HEAD_DIM), bf16),
         ],
-        compiler_params=pltpu.CompilerParams(vmem_limit_bytes=40 * 1024 * 1024),
+        compiler_params=vmem(20),
         cost_estimate=cost(2 * count * rows * width * columns, 8e6),
     )(place, even, odd, angles, gains, *weights)
 
@@ -399,7 +462,7 @@
             jax.ShapeDtypeStruct((8, 2 * HEAD_DIM), f32),
             jax.ShapeDtypeStruct((8, width), f32),
         ],
-        compiler_params=pltpu.CompilerParams(vmem_limit_bytes=40 * 1024 * 1024),
+        compiler_params=vmem(48),
         cost_estimate=cost(2 * count * rows * width * columns, 12e6),
     )(place, even, odd, angles, gains, qkv_rows, *query_grad, kv_grad, *weights)
 
@@ -426,9 +489,11 @@
 
 
 def visible_keys(place_ref, chunk, rows):
-    key_at = lax.broadcasted_iota(jnp.int32, (chunk, GROUP * rows), 0)
+    key_row = lax.broadcasted_iota(jnp.int32, (chunk, GROUP * rows), 0)
     row_at = lax.broadcasted_iota(jnp.int32, (chunk, GROUP * rows), 1) % rows
-    return key_at <= row_at + place_ref[0] * rows
+    count = chunk // rows
+    owner = (place_ref[0] - key_row // rows + count) % count
+    return owner * rows + key_row % rows <= row_at + place_ref[0] * rows
 
 
 def attention_kernel(
@@ -491,7 +556,7 @@
             scratch_shapes=[pltpu.VMEM((2 * HEAD_DIM, keys), bf16)],
         ),
         out_shape=[half, half, jax.ShapeDtypeStruct((count, 1, GROUP * rows), f32)],
-        compiler_params=pltpu.CompilerParams(vmem_limit_bytes=40 * 1024 * 1024),
+        compiler_params=vmem(12, keys),
         cost_estimate=cost(16e9, 8e6, 1e7),
     )(place, queries, keys_values)
 
@@ -577,7 +642,7 @@
             jax.ShapeDtypeStruct((4 * rows, GROUP_WIDTH), f32),
             jax.ShapeDtypeStruct(keys_values.shape, f32),
         ],
-        compiler_params=pltpu.CompilerParams(vmem_limit_bytes=48 * 1024 * 1024),
+        compiler_params=vmem(18, keys),
         cost_estimate=cost(18e9, 12e6, 5e6),
     )(place, queries, branch, attended, log_total, weight, keys_values, *added)
 
@@ -622,7 +687,7 @@
         ],
         out_specs=[by_row(columns // 2), by_row(columns), by_row(width), by_row(width)],
         out_shape=[low(columns // 2), low(columns), low(width), low(width)],
-        compiler_params=pltpu.CompilerParams(vmem_limit_bytes=48 * 1024 * 1024),
+        compiler_params=vmem(36),
         cost_estimate=cost(6 * tokens * width * columns, 16e6, tokens * columns),
     )(normed, outer, weight, down)
 
@@ -632,27 +697,36 @@
     for left_ref, right_ref in zip(refs[:count], refs[count : 2 * count]):
         term = dot(left_ref[...], right_ref[...], TN)
         total = term if total is None else total + term
-    refs[-1][...] = total.astype(bf16)
-
-
-def weight_grad(lefts, rights, first, size, column, columns):
+    for n, ref in enumerate(refs[2 * count :]):
+
+        @pl.when(pl.program_id(0) == n)
+        def _(ref=ref):
+            ref[...] = total.astype(bf16)
+
+
+def weight_grad(lefts, rights, first, size, column, columns, count):
     tokens = lefts[0].shape[0]
-    tile = min(512, size)
-    tiles = size // tile
-    place = jnp.stack([first * tiles]).astype(jnp.int32)
-    return pl.pallas_call(
+    tile = size // count
+    place = jnp.stack([first * count]).astype(jnp.int32)
+    if tile % 128:
+        tile, place = size, jnp.stack([first]).astype(jnp.int32)
+    parts = size // tile
+    made = pl.pallas_call(
         functools.partial(weight_grad_kernel, len(lefts)),
         grid_spec=pltpu.PrefetchScalarGridSpec(
             num_scalar_prefetch=1,
-            grid=(tiles,),
+            grid=(parts,),
             in_specs=[pl.BlockSpec((tokens, tile), lambda i, at: (0, at[0] + i))] * len(lefts)
             + [pl.BlockSpec((tokens, columns), lambda i, at: (0, column))] * len(rights),
-            out_specs=pl.BlockSpec((tile, columns), lambda i, at: (i, 0)),
+            out_specs=[pl.BlockSpec((tile, columns), lambda i, at: (0, 0))] * parts,
         ),
-        out_shape=jax.ShapeDtypeStruct((size, columns), bf16),
-        compiler_params=pltpu.CompilerParams(vmem_limit_bytes=48 * 1024 * 1024),
+        out_shape=[jax.ShapeDtypeStruct((tile, columns), bf16)] * parts,
+        compiler_params=vmem(36),
         cost_estimate=cost(2 * len(lefts) * tokens * size * columns, 12e6),
     )(place, *lefts, *rights)
+    if parts == count:
+        return list(made)
+    return [lax.slice_in_dim(made[0], n * size // count, (n + 1) * size // count) for n in range(count)]
 
 
 def place_kernel(place_ref, shard_ref, *refs):
@@ -677,7 +751,54 @@
         ),
         out_shape=jax.ShapeDtypeStruct(shape, f32),
         input_output_aliases=aliases,
-        compiler_params=pltpu.CompilerParams(vmem_limit_bytes=24 * 1024 * 1024),
+        compiler_params=vmem(16),
+        cost_estimate=cost(0, 6 * source.size),
+    )(*operands)
+
+
+def place_units_kernel(block_at, unit, columns, place_ref, source_ref, *refs):
+    out_ref, wide_ref, sems = refs[-3:]
+    rows = wide_ref.shape[1]
+    copies = []
+    for n in range(wide_ref.shape[0]):
+        slot, column = n // columns, n % columns
+        wide_ref[n] = source_ref[
+            slot * rows : (slot + 1) * rows, column * unit : (column + 1) * unit
+        ].astype(f32)
+        start = pl.multiple_of(block_at(slot, column, place_ref) * unit, unit)
+        copies.append(
+            pltpu.make_async_copy(wide_ref.at[n], out_ref.at[:, pl.ds(start, unit)], sems.at[n])
+        )
+        copies[-1].start()
+    for copy in copies:
+        copy.wait()
+
+
+def place_units(whole, shape, source, rows, unit, place, block_at):
+    slots, columns = source.shape[0] // rows, source.shape[1] // unit
+    count = slots * columns
+    in_specs = [pl.BlockSpec(source.shape, lambda i, at: (0, 0))]
+    operands = [place, source]
+    aliases = {}
+    if whole is not None:
+        in_specs.append(pl.BlockSpec(memory_space=pl.ANY))
+        operands.append(whole)
+        aliases = {2: 0}
+    return pl.pallas_call(
+        functools.partial(place_units_kernel, block_at, unit, columns),
+        grid_spec=pltpu.PrefetchScalarGridSpec(
+            num_scalar_prefetch=1,
+            grid=(1,),
+            in_specs=in_specs,
+            out_specs=pl.BlockSpec(memory_space=pl.ANY),
+            scratch_shapes=[
+                pltpu.VMEM((count, rows, unit), f32),
+                pltpu.SemaphoreType.DMA((count,)),
+            ],
+        ),
+        out_shape=jax.ShapeDtypeStruct(shape, f32),
+        input_output_aliases=aliases,
+        compiler_params=vmem(16),
         cost_estimate=cost(0, 6 * source.size),
     )(*operands)
 
@@ -699,19 +820,19 @@
     return whole
 
 
-def place_rows(halves, place):
+def place_rows(quarters, place):
     whole = None
-    rows, columns = halves[0].shape[0] // 4, halves[0].shape[1]
-    for odd, half in enumerate(halves):
+    rows, columns = quarters[0].shape[0] // 2, quarters[0].shape[1]
+    for n, quarter in enumerate(quarters):
         whole = place_blocks(
             whole,
             (CELL * rows, columns),
-            half,
+            quarter,
             (rows, columns),
-            (4,),
+            (2,),
             place,
             lambda i, at: (i, 0),
-            lambda i, at, odd=odd: (token_block(4 * odd + i, at), 0),
+            lambda i, at, n=n: (token_block(2 * n + i, at), 0),
         )
     return whole
 
@@ -756,7 +877,7 @@
             out_specs=pl.BlockSpec(shape, lambda i, at: (0, 0)),
         ),
         out_shape=jax.ShapeDtypeStruct(shape, f32),
-        compiler_params=pltpu.CompilerParams(vmem_limit_bytes=32 * 1024 * 1024),
+        compiler_params=vmem(28),
         cost_estimate=cost(0, 6 * rows * CELL * columns),
     )(place, *halves)
 
@@ -870,63 +991,54 @@
             axis=1,
         )
 
-    down_own = block(down_weight, head, unit)
     steps = Steps()
     sends = [functools.partial(fsdp_send, step=k) for k in range(fsdp_count)]
 
-    class Buffer:
-        def __init__(self, shape):
-            self.value = blank(shape, bf16)
-
-        def write(self, part, row, axis=0):
-            self.value = lax.dynamic_update_slice_in_dim(self.value, part, row, axis)
-
-    gate_up_pair = Buffer((pair_rows, 2 * local_units))
-    gate_up_mine = Buffer((width, 2 * local_units))
-    down_mine = Buffer((local_units, width))
-    down_mine.write(down_own, pair_here * unit)
-    pair_jobs, down_jobs, gate_up_jobs = [], [], []
-
-    def part_of(values, n, count):
-        size = values.shape[0] // count
-        return lax.slice_in_dim(values, n * size, (n + 1) * size)
-
-    for j in range(1, pair):
-        for n in range(2):
-            size = weight_rows // 2
-            pair_jobs.append(
-                (
-                    lambda begin, n=n, j=j: pair_send(begin(part_of(owned[j], n, 2)), j, pair),
-                    lambda got, n=n, j=j, size=size: gate_up_pair.write(
-                        got, (in_pair - j) % pair * weight_rows + n * size
-                    ),
-                )
-            )
-    for step in range(1, pair_count):
-        for n in range(4):
-            size = unit // 4
-            down_jobs.append(
-                (
-                    lambda begin, n=n, step=step: fsdp_send(
-                        begin(part_of(down_own, n, 4)), step * pair
-                    ),
-                    lambda got, n=n, step=step, size=size: down_mine.write(
-                        got, (pair_here - step) % pair_count * unit + n * size
-                    ),
-                )
-            )
-        for n in range(8):
-            size = pair_rows // 8
-            gate_up_jobs.append(
-                (
-                    lambda begin, n=n, step=step: fsdp_send(
-                        begin(part_of(gate_up_pair.value, n, 8)), step * pair
-                    ),
-                    lambda got, n=n, step=step, size=size: gate_up_mine.write(
-                        got, (pair_here - step) % pair_count * pair_rows + n * size
-                    ),
-                )
-            )
+    pair_jobs, down_jobs, own_jobs, mate_jobs = [], [], [], []
+    gate_up_parts, down_parts = [], []
+
+    def half_columns(weight, owner, n):
+        size = weight_rows // 2
+        return owner_columns(lax.slice_in_dim(weight, n * size, (n + 1) * size), owner)
+
+    def cross_job(read, step, row):
+        return (
+            lambda begin: fsdp_send(begin(read()), step * pair),
+            lambda got: gate_up_parts.append((got, (fsdp_here - step * pair) % fsdp_count, row)),
+        )
+
+    mates = {}
+
+    def mate_job(j, n):
+        def finish(got):
+            mates[j, n] = got
+            gate_up_parts.append((got, pair_here * pair + (in_pair - j) % pair, n))
+
+        return (lambda begin: pair_send(begin(owned[j, n]), j, pair), finish)
+
+    def mate_cross_job(j, n, step):
+        def finish(got):
+            layer = (pair_here - step) % pair_count * pair + (in_pair - j) % pair
+            gate_up_parts.append((got, layer, n))
+
+        return (lambda begin: fsdp_send(begin(mates[j, n]), step * pair), finish)
+
+    def down_job(step, n):
+        return (
+            lambda begin: fsdp_send(begin(down_pieces[n]), step * pair),
+            lambda got: down_parts.append((got, (pair_here - step) % pair_count, n)),
+        )
+
+    for n in range(2):
+        for j in range(1, pair):
+            pair_jobs.append(mate_job(j, n))
+        for step in range(1, pair_count):
+            own_jobs.append(cross_job(lambda n=n: owned[0, n], step, n))
+            for j in range(1, pair):
+                mate_jobs.append(mate_cross_job(j, n, step))
+    for n in range(4):
+        for step in range(1, pair_count):
+            down_jobs.append(down_job(step, n))
 
     last = max(fsdp_count - 1, 3)
     got = steps.run(
@@ -940,45 +1052,70 @@
         [
             (second_round, two),
             (
-                lambda v: [owner_columns(v, (in_pair + j) % pair) for j in range(pair)],
-                gate_up_weight,
+                lambda v: (
+                    {
+                        (j, n): half_columns(v[0], (in_pair + j) % pair, n)
+                        for j in range(pair)
+                        for n in range(2)
+                    },
+                    [
+                        lax.dynamic_slice_in_dim(
+                            v[1], head * unit + n * (unit // 4), unit // 4
+                        )
+                        for n in range(4)
+                    ],
+                ),
+                (gate_up_weight, down_weight),
             ),
         ]
         + [(send, qkv_own) for send in sends[2:last]]
     )
-    owned = got[1]
-    gate_up_pair.write(owned[0], in_pair * weight_rows)
+    owned, down_pieces = got[1]
+    for n in range(2):
+        gate_up_parts.append((owned[0, n], fsdp_here, n))
+    for n in range(4):
+        down_parts.append((down_pieces[n], pair_here, n))
     qkv_pieces += got[2:]
     mine = rows_joined(two, got[0])
     got = steps.run([(twin_send, mine)] + [(send, qkv_own) for send in sends[last:]])
     qkv_pieces += got[1:]
     normed_attn = [mine, got[0]]
 
+    queue = [pair_jobs, pair_jobs, own_jobs, down_jobs, own_jobs, down_jobs, down_jobs]
+    for jobs in queue + [mate_jobs, down_jobs, mate_jobs]:
+        if jobs:
+            steps.jobs.append(jobs.pop(0))
+    steps.jobs += pair_jobs + down_jobs + own_jobs + mate_jobs
+
     projected, outer_got, *out_got = steps.run(
         [
             (lambda v: project(place, *v, angles, gains, qkv_pieces, rows), normed_attn),
             (first_round, cotangent),
         ]
-        + [(send, out_own) for send in sends[1::2]]
+        + [(send, out_own) for send in sends[1:]],
+        1,
     )
     qkv_rows, query_low, kv_own = projected
     outer_two = rows_joined(cotangent, outer_got)
     kv_own = kv_own.reshape(CELL, 1, rows, 2 * HEAD_DIM)
-    got = steps.run(
-        [(send, kv_own) for send in sends[1:]]
-        + [(second_round, outer_two)]
-        + [(send, out_own) for send in sends[2::2]]
-    )
-    kv_pieces, got = [kv_own] + got[: fsdp_count - 1], got[fsdp_count - 1 :]
-    outer_mine = rows_joined(outer_two, got[0])
-    out_pieces = [out_own] + [None] * (fsdp_count - 1)
-    out_pieces[1::2] = out_got
-    out_pieces[2::2] = got[1:]
-    kv_cells = blank((CELL, fsdp_count, rows, 2 * HEAD_DIM), bf16)
-    out_columns = blank((width, width // CELL), bf16)
-    for k in range(fsdp_count):
-        kv_cells = put(kv_cells, kv_pieces[k], (fsdp_here - k) % fsdp_count, 1)
-        out_columns = put(out_columns, out_pieces[k], (fsdp_here - k) % fsdp_count)
+    out_columns = join([out_own] + out_got, [(fsdp_here - k) % fsdp_count for k in range(fsdp_count)])
+
+    def send_then_turn(split_axis, join_axis):
+        def act(v):
+            got = sends[1](v[0])
+            return got, cell_turn(after(v[1], got), split_axis, join_axis)
+
+        return act
+
+    (kv_next, out_rows), *got = steps.run(
+        [(send_then_turn(0, 1), (kv_own, out_columns))]
+        + [(send, kv_own) for send in sends[2:]]
+        + [(second_round, outer_two)],
+        1,
+    )
+    kv_pieces = [kv_own, kv_next] + got[:-1]
+    outer_mine = rows_joined(outer_two, got[-1])
+    kv_cells = jnp.concatenate(kv_pieces, axis=1)
     chunk = fsdp_count * rows
     kv_all = kv_cells.reshape(CELL * chunk, 2 * HEAD_DIM)
     if cell_count > 1:
@@ -989,25 +1126,22 @@
         for step in range(1, cell_count):
             kv_all = put(kv_all, cell_send(kv_cells, step), (cell - step) % cell_count)
 
-    steps.jobs = pair_jobs[:1] + down_jobs[:2]
-    attended, out_rows, outer_other = steps.run(
+    attended, outer_other = steps.run(
         [
             (lambda v: attention(place, *v, rows, chunk), (query_low, kv_all)),
-            (lambda v: cell_turn(v, 0, 1), out_columns),
             (twin_send, outer_mine),
         ],
-        3,
+        1,
     )
     *attended, log_total = attended
     outer_parts = [[outer_mine, outer_other]]
-    steps.jobs = pair_jobs[1:] + down_jobs[2:] + gate_up_jobs
     terms = [dot(half, out_rows).astype(bf16) for half in attended]
     got = steps.run([(twin_send, terms[1])], 1)
     kept, sent = reduce_first(terms[0], got[0])
     got = steps.run(
         [(second_round, sent)]
         + [(lambda v, j=j: pair_send(v, -j, pair), cotangent) for j in range(1, pair)],
-        2,
+        1,
     )
     outer_next = got[1:]
     kept, sent = reduce_second(kept, got[0])
@@ -1025,21 +1159,26 @@
     two = rows_joined(normed_own, got[0])
     normed_next = got[1:pair]
     outer_mines = [rows_joined(v, g) for v, g in zip(outer_twos, got[pair:])]
-    got = steps.run([(second_round, two)] + [(twin_send, v) for v in outer_mines], 2)
+    got = steps.run(
+        [(second_round, two)]
+        + [(first_round, v) for v in normed_next]
+        + [(twin_send, v) for v in outer_mines],
+        1,
+    )
     mine = rows_joined(two, got[0])
-    outer_parts += [[a, b] for a, b in zip(outer_mines, got[1:])]
-    got = steps.run([(twin_send, mine)] + [(first_round, v) for v in normed_next], 1)
+    twos = [rows_joined(v, g) for v, g in zip(normed_next, got[1:])]
+    outer_parts += [[a, b] for a, b in zip(outer_mines, got[1 + len(twos) :])]
+    got = steps.run([(twin_send, mine)] + [(second_round, v) for v in twos], 1)
     normed_parts = [[mine, got[0]]]
-    twos = [rows_joined(v, g) for v, g in zip(normed_next, got[1:])]
-    if twos:
-        got = steps.run([(second_round, v) for v in twos], 2)
-        mines = [rows_joined(v, g) for v, g in zip(twos, got)]
+    mines = [rows_joined(v, g) for v, g in zip(twos, got[1:])]
+    if mines:
         got = steps.run([(twin_send, v) for v in mines], 1)
         normed_parts += [[a, b] for a, b in zip(mines, got)]
-    while steps.jobs:
-        steps.run([(lambda v: v, normed_parts[-1][1])], 2)
-    gate_up_mine.write(gate_up_pair.value, pair_here * pair_rows)
-    gate_up_all, down_all = gate_up_mine.value, down_mine.value
+    steps.drain(lambda: False)
+    gate_up_all = join(
+        [part for part, _, _ in gate_up_parts], [layer * 2 + n for _, layer, n in gate_up_parts]
+    )
+    down_all = join([part for part, _, _ in down_parts], [p * 4 + n for _, p, n in down_parts])
 
     def feed_half(values):
         return feed(*values, gate_up_all, down_all)
@@ -1122,27 +1261,27 @@
             if self.pieces is None:
                 function, operands = self.others()
                 self.pieces = function(operands)
-            return fsdp_send(begin(part_of(self.pieces[step - 1], n, self.count)), step * pair)
+            return fsdp_send(begin(self.pieces[step - 1][n]), step * pair)
 
         def complete(self):
             return len(self.got) == self.left
 
         def total(self, mine):
             steps.drain(self.complete)
-            rows_here = [part_of(mine, n, self.count).astype(f32) for n in range(self.count)]
+            rows_here = [part.astype(f32) for part in mine]
             for k, value in enumerate(self.got):
                 rows_here[k % self.count] += value.astype(f32)
-            return cell_sum(rows_joined(*rows_here)).astype(bf16)
+            return join([cell_sum(part).astype(bf16) for part in rows_here])
 
     def side_total(side):
         return PairTotal(
-            lambda v, p: weight_grad(*v, p, pair_rows, side, local_units),
+            lambda v, p: weight_grad(*v, p, pair_rows, side, local_units, 4),
             (normed_flat, [results[k][1] for k in keys]),
         )
 
     gate, up = side_total(0), side_total(1)
     down = PairTotal(
-        lambda v, p: weight_grad(*v, p, unit, 0, width),
+        lambda v, p: weight_grad(*v, p, unit, 0, width, 4),
         ([results[k][0] for k in keys], outer_flat),
     )
 
@@ -1158,53 +1297,54 @@
     branch_terms = [tuple(results[j, side][3] for side in range(2)) for j in range(pair)]
     branch_twins = []
     steps.jobs = gate.jobs + up.jobs + down.jobs
-    gate_mine = None
-    while waiting:
+    kernels = [gate.others(), gate.own()]
+    made = []
+    while waiting or len(branch_twins) < pair:
         parts = advance()
         count = len(parts)
         extra = []
         if len(branch_twins) < pair:
             extra.append((twin_send, branch_terms[pair - 1 - len(branch_twins)][1]))
-        if gate.pieces is not None and gate_mine is None:
-            extra.append(gate.own())
-        got = steps.run(parts + extra, 1)
+        if kernels:
+            extra.append(kernels.pop(0))
+        got = steps.run(parts + extra, 1 if made else 0)
         settle(got[:count])
         got = got[count:]
         if len(branch_twins) < pair:
             branch_twins.append(got.pop(0))
         if got:
-            gate_mine = got[0]
+            made.append(got[0])
+            gate.pieces = made[0]
     normed_grad = sum(sums[j] for j in range(pair))
     mid_part, mlp_gain_grad = jax.vjp(rms_scale, hidden_mid, mlp_gain)[1](normed_grad)
     hidden_grad = cotangent.astype(f32) + mid_part
     branch_own = hidden_grad.astype(bf16)
-    got = steps.run([(first_round, branch_own), up.others()], 1)
+    branch_twins = branch_twins[::-1]
+    got = steps.run(
+        [
+            (first_round, branch_own),
+            up.others(),
+            (
+                lambda v: [reduce_first(mine, value) for mine, value in v],
+                [(terms[0], value) for terms, value in zip(branch_terms, branch_twins)],
+            ),
+        ]
+        + kernels,
+        1,
+    )
+    made += got[3:]
+    gate_mine = made[1]
     up.pieces = got[1]
+    branch_kept, branch_sent = map(list, zip(*got[2]))
     two = rows_joined(branch_own, got[0])
     got = steps.run([(second_round, two), up.own()], 1)
     up_mine = got[1]
     mine = rows_joined(two, got[0])
-    if gate_mine is None:
-        gate_mine = gate.own()[0](gate.operands)
-    gate_total = gate.total(gate_mine)
-    branch_twins = branch_twins[::-1]
-    branch_kept, branch_sent = map(
-        list,
-        zip(*[reduce_first(terms[0], value) for terms, value in zip(branch_terms, branch_twins)]),
-    )
-    got = steps.run(
-        [
-            (twin_send, mine),
-            (second_round, branch_sent[-1]),
-            (shares_sent, gate_total),
-            down.others(),
-        ],
-        1,
-    )
+    got = steps.run([(twin_send, mine), (second_round, branch_sent[-1]), down.others()], 1)
     branch_grad = [mine, got[0]]
     branch_kept[-1], branch_sent[-1] = reduce_second(branch_kept[-1], got[1])
-    gate_share = shares(gate_total, got[2])
-    down.pieces = got[3]
+    down.pieces = got[2]
+    gate_total = gate.total(gate_mine)
 
     def attention_half(other, kv_grad=None):
         return lambda v: attention_grad(
@@ -1212,17 +1352,31 @@
         )
 
     (query_grad_mine, kv_grad), gate_got, *got = steps.run(
-        [(attention_half(0), branch_grad[0]), (first_round, gate_share)]
+        [
+            (attention_half(0), branch_grad[0]),
+            (shares_sent, gate_total),
+            (
+                lambda v: sum(dot(half, branch, TN) for half, branch in zip(*v)).astype(bf16),
+                (attended, branch_grad),
+            ),
+        ]
         + [(second_round, sent) for sent in branch_sent[:-1]],
         2,
     )
-    gate_two = rows_joined(gate_share, gate_got)
+    out_partial, *got = got
+    gate_share = shares(gate_total, gate_got)
     for j, value in enumerate(got):
         branch_kept[j], branch_sent[j] = reduce_second(branch_kept[j], value)
-    (query_grad_other, kv_grad), gate_got = steps.run(
-        [(attention_half(1, kv_grad), branch_grad[1]), (second_round, gate_two)], 2
-    )
-    gate_half = rows_joined(gate_two, gate_got)
+    (query_grad_other, kv_grad), gate_got, *branch_got = steps.run(
+        [(attention_half(1, kv_grad), branch_grad[1]), (first_round, gate_share)]
+        + [(first_round, sent) for sent in branch_sent],
+        2,
+    )
+    gate_two = rows_joined(gate_share, gate_got)
+    branch_sums = [
+        kept.astype(f32) + value.astype(f32) for kept, value in zip(branch_kept, branch_got)
+    ]
+    outputs = hidden_mid + branch_sums[0]
     query_grad = (query_grad_mine, query_grad_other)
     kv_grad = kv_grad.astype(bf16)
     if cell_count > 1:
@@ -1234,36 +1388,31 @@
     kv_grad = kv_grad.reshape(CELL, fsdp_count, rows, 2 * HEAD_DIM)
 
     def kv_piece(k):
-        return block(kv_grad, (fsdp_here + k) % fsdp_count, 1, 1)
+        at = -k % fsdp_count
+        return lax.slice_in_dim(kv_grad, at, at + 1, axis=1)
 
     def fsdp_piece(values, k):
         return block(values, (fsdp_here + k) % fsdp_count, weight_rows)
 
     up_total = up.total(up_mine)
-    got = steps.run(
-        [(sends[k], kv_piece(k)) for k in range(1, fsdp_count)]
-        + [(first_round, sent) for sent in branch_sent]
-        + [
-            (shares_sent, up_total),
-            (
-                lambda v: sum(dot(half, branch, TN) for half, branch in zip(*v)).astype(bf16),
-                (attended, branch_grad),
-            ),
-        ]
-    )
-    kv_total = kv_piece(0).astype(f32)
-    for value in got[: fsdp_count - 1]:
+
+    def send_then_share(v):
+        got = sends[1](v[0])
+        return got, shares_sent(after(v[1], got))
+
+    (kv_next, up_got), *got = steps.run(
+        [(send_then_share, (kv_piece(1), up_total))]
+        + [(sends[k], kv_piece(k)) for k in range(2, fsdp_count)]
+        + [(second_round, gate_two)]
+    )
+    kv_total = kv_piece(0).astype(f32) + kv_next.astype(f32)
+    for value in got[:-1]:
         kv_total = kv_total + value.astype(f32)
     kv_total = kv_total.reshape(cell_tokens, 2 * HEAD_DIM)
-    branch_sums = [
-        kept.astype(f32) + value.astype(f32)
-        for kept, value in zip(branch_kept, got[fsdp_count - 1 :])
-    ]
-    outputs = hidden_mid + branch_sums[0]
-    up_got, out_partial = got[-2:]
+    gate_got = got[-1]
     up_share = shares(up_total, up_got)
 
-    projected, gate_got, up_got, *branch_got = steps.run(
+    projected, gate_two_twin, up_got, out_partial, *branch_got = steps.run(
         [
             (
                 lambda v: project_grad(
@@ -1271,142 +1420,174 @@
                 ),
                 kv_total,
             ),
-            (twin_send, gate_half),
+            (twin_send, gate_two),
             (first_round, up_share),
+            (lambda v: cell_turn(v, 1, 0), out_partial),
         ]
         + [
             (lambda v, j=j: pair_send(v, j, pair), value.astype(bf16))
             for j, value in enumerate(branch_sums[1:], 1)
         ],
-        1,
+        2,
     )
     *qkv_grad, attn_mine, attn_other, head_gain_grad, attention_gain_grad = projected
-    for value in branch_got:
-        outputs = outputs + value.astype(f32)
-    outputs = outputs.astype(bf16)
-    gate_halves = (gate_half, gate_got)
     up_two = rows_joined(up_share, up_got)
-
-    def gather_place(side, odd, half, whole):
-        return place_blocks(
-            whole,
-            gate_up_weight.shape,
-            half,
-            (weight_rows, unit),
-            (4, pair * pair_count),
-            place,
-            lambda i, g, at: (i, g),
-            lambda i, g, at: (
-                0,
-                side * (hidden_width // unit)
-                + ((g % pair_count) * pair + (at[3] - g // pair_count + pair) % pair) * CELL
-                + token_block(4 * odd + i, at),
-            ),
-        )
-
-    got = steps.run(
-        [
-            (twin_send, attn_other),
-            (second_round, up_two),
-            (down.own()),
-            (lambda v: gather_place(0, 0, v, None), gate_halves[0]),
-            (
-                lambda v: sum(dot(half, grad, TN) for half, grad in zip(*v)).astype(bf16),
-                (normed_attn, qkv_grad),
-            ),
-        ],
-        2,
-    )
-    kept, sent = reduce_first(attn_mine, got[0])
-    up_half = rows_joined(up_two, got[1])
-    down_own_rows, grad_gate_up, qkv_partial = got[2:]
-    gains_here = jnp.concatenate(
+    gains_here = SumEverywhere(jnp.concatenate(
         [
             attention_gain_grad[0] / attention_gain,
             mlp_gain_grad,
             head_gain_grad[0],
             head_gain_grad[1],
         ]
-    ).reshape(-1, 2 * HEAD_DIM)
+    ).reshape(-1, 2 * HEAD_DIM))
+
+    def gather_place(side, slot, part, whole):
+        return place_units(
+            whole,
+            gate_up_weight.shape,
+            part,
+            weight_rows,
+            unit,
+            place,
+            lambda i, g, at: (
+                side * (hidden_width // unit)
+                + ((g % pair_count) * pair + (at[3] - g // pair_count + pair) % pair) * CELL
+                + token_block(slot + i, at)
+            ),
+        )
+
+    def placing(side, parts):
+        def place_all(v):
+            whole, arrays = v
+            for (slot, _), array in zip(parts, arrays):
+                whole = gather_place(side, slot, array, whole)
+            return whole
+
+        return place_all, (grad_gate_up, [part for _, part in parts])
+
+    def fsdp_sum(values, got):
+        total = fsdp_piece(values, 0).astype(f32)
+        for value in got:
+            total = total + value.astype(f32)
+        return cell_sum(total).astype(bf16)
+
+    def sent_pieces(values, distances):
+        return [(sends[k], fsdp_piece(values, k)) for k in distances]
+
+    odd_steps, even_steps = range(1, fsdp_count, 2), range(2, fsdp_count, 2)
+    grad_gate_up = None
+    got = steps.run(
+        [
+            (twin_send, attn_other),
+            (second_round, up_two),
+            (
+                lambda v: sum(dot(half, grad, TN) for half, grad in zip(*v)).astype(bf16),
+                (normed_attn, qkv_grad),
+            ),
+            down.own(),
+            (lambda v: gather_place(0, 0, v, None), gate_two),
+            gains_here.part(),
+        ],
+        2,
+    )
+    kept, sent = reduce_first(attn_mine, got[0])
+    up_got = got[1]
+    qkv_partial, down_own_rows, grad_gate_up, gain_got = got[2:]
+    gains_here.add(gain_got)
+    down_share = down.total(down_own_rows)
     got = steps.run(
         [
             (second_round, sent),
-            (lambda v: cell_turn(v, 1, 0), out_partial),
-            (twin_send, up_half),
-            (lambda v: gather_place(0, 1, *v), (gate_halves[1], grad_gate_up)),
-        ],
-        1,
+            (first_round, down_share),
+            (twin_send, gate_got),
+            placing(0, [(4, gate_two_twin), (2, gate_got)]),
+        ]
+        + sent_pieces(qkv_partial, odd_steps)
     )
     kept, sent = reduce_second(kept, got[0])
-    out_partial = got[1]
-    up_halves = (up_half, got[2])
+    down_two = rows_joined(down_share, got[1])
+    gate_got_twin = got[2]
     grad_gate_up = got[3]
-    down_share = down.total(down_own_rows)
+    qkv_got = got[4:]
     got = steps.run(
         [
             (first_round, sent),
-            (first_round, down_share),
-            (lambda v: gather_place(1, 0, *v), (up_halves[0], grad_gate_up)),
+            (second_round, down_two),
+            placing(0, [(6, gate_got_twin)]),
         ]
-        + [(sends[k], fsdp_piece(out_partial, k)) for k in range(1, fsdp_count)]
+        + sent_pieces(qkv_partial, even_steps)
+        + sent_pieces(out_partial, odd_steps)
     )
     attn_normed_grad = kept.astype(f32) + got[0].astype(f32)
-    down_two = rows_joined(down_share, got[1])
+    down_got = got[1]
     grad_gate_up = got[2]
-    out_total = fsdp_piece(out_partial, 0).astype(f32)
-    for value in got[3:]:
-        out_total = out_total + value.astype(f32)
-    out_share = cell_sum(out_total).astype(bf16)
+    qkv_share = fsdp_sum(qkv_partial, qkv_got + got[3 : 3 + len(even_steps)])
+    out_got = got[3 + len(even_steps) :]
     got = steps.run(
         [
-            (second_round, down_two),
-            (first_round, out_share),
-            (lambda v: gather_place(1, 1, *v), (up_halves[1], grad_gate_up)),
+            (first_round, qkv_share),
+            (twin_send, up_two),
+            (twin_send, up_got),
+            placing(1, [(0, up_two), (2, up_got)]),
+            gains_here.part(),
         ]
-        + [(sends[k], fsdp_piece(qkv_partial, k)) for k in range(1, fsdp_count)]
-    )
-    down_half = rows_joined(down_two, got[0])
-    out_two = rows_joined(out_share, got[1])
-    grad_gate_up = got[2]
-    qkv_total = fsdp_piece(qkv_partial, 0).astype(f32)
-    for value in got[3:]:
-        qkv_total = qkv_total + value.astype(f32)
-    qkv_share = cell_sum(qkv_total).astype(bf16)
+        + sent_pieces(out_partial, even_steps)
+    )
+    qkv_two = rows_joined(qkv_share, got[0])
+    up_two_twin, up_got_twin, grad_gate_up = got[1:4]
+    gains_here.add(got[4])
+    out_share = fsdp_sum(out_partial, out_got + got[5:])
     got = steps.run(
         [
-            (twin_send, down_half),
-            (second_round, out_two),
-            (first_round, qkv_share),
-            (sum_everywhere, gains_here),
+            (second_round, qkv_two),
+            (first_round, out_share),
+            (twin_send, down_two),
+            (twin_send, down_got),
+            placing(1, [(4, up_two_twin), (6, up_got_twin)]),
             (
-                lambda v: jax.vjp(lambda u: rms_scale(u, attention_gain), source)[1](v)[0],
-                attn_normed_grad,
+                lambda v: (
+                    v[1] + jax.vjp(lambda u: rms_scale(u, attention_gain), source)[1](v[0])[0]
+                ).astype(bf16),
+                (attn_normed_grad, hidden_grad),
+            ),
+            gains_here.part(),
+            (
+                lambda v: sum([g.astype(f32) for g in v[1:]], v[0]).astype(bf16),
+                [outputs] + branch_got,
             ),
         ]
     )
-    grad_down_halves = (down_half, got[0])
-    out_half = rows_joined(out_two, got[1])
-    qkv_two = rows_joined(qkv_share, got[2])
-    gain_sums = got[3].reshape(-1)
-    grad_inputs = (hidden_grad + got[4]).astype(bf16)
+    qkv_half = rows_joined(qkv_two, got[0])
+    out_two = rows_joined(out_share, got[1])
+    down_two_twin, down_got_twin, grad_gate_up, grad_inputs, gain_got, outputs = got[2:]
+    gains_here.add(gain_got)
     got = steps.run(
         [
-            (twin_send, out_half),
-            (second_round, qkv_two),
-            (lambda v: place_rows(v, place), grad_down_halves),
+            gains_here.part(),
+            (second_round, out_two),
+            (twin_send, qkv_half),
+            (
+                lambda v: place_rows(v, place),
+                [down_two, down_got, down_two_twin, down_got_twin],
+            ),
         ]
     )
-    out_halves = (out_half, got[0])
-    qkv_half = rows_joined(qkv_two, got[1])
+    gains_here.add(got[0])
+    got = got[1:]
+    out_half = rows_joined(out_two, got[0])
     grad_down = got[2]
     got = steps.run(
         [
-            (twin_send, qkv_half),
-            (lambda v: place_columns(v, width // CELL, place), out_halves),
+            gains_here.part(),
+            (twin_send, out_half),
+            (lambda v: place_heads(v, place), (qkv_half, got[1])),
         ]
     )
-    grad_out = got[1]
-    grad_qkv = place_heads([qkv_half, got[0]], place)
+    gains_here.add(got[0])
+    gain_sums = gains_here.finish().reshape(-1)
+    got = got[1:]
+    grad_qkv = got[1]
+    grad_out = place_columns((out_half, got[0]), width // CELL, place)
     attention_gain_sum, mlp_gain_sum = gain_sums[:width], gain_sums[width : 2 * width]
     head_sums = gain_sums[2 * width :].reshape(4, HEAD_DIM)
 

time: 831 us -> 762 us (0.917)
  other arithmetic: 74.9 us -> 34.7 us
  waiting for transfers between devices: 300 us -> 268 us
  local copies, waits for them, and re-layouts: 98.1 us -> 75.4 us
  Pallas kernels: 222 us -> 243 us
    pallas_call x5 -> x45, Pallas kernels: 0.01 us -> 76.6 us  [the longest x8 31.2 us: place_units(): pl.pallas_call(functools.partial(place_units_kernel, block_at, unit, colu...]
    pallas_call x8 -> x6, Pallas kernels: 54.2 us -> 16 us  [place_blocks(): pl.pallas_call(place_kernel, grid_spec=pltpu.PrefetchScalarGridSpec(num_s...]
    ppermute x42 -> x38, waiting for transfers between devices: 254 us -> 221 us  [fsdp_send(): lax.ppermute(values, 'fsdp', [(i, (i + step) % count) for i in range(coun...]
    concatenate x20 -> x1, other arithmetic: 29.5 us -> 2.09 us  [body(): kv_cells = jnp.concatenate(kv_pieces, axis=1)]
    dynamic_update_slice x25 -> x0, local copies, waits for them, and re-layouts: 17.7 us -> none  [the longest x17 12.8 us: write(): self.value = lax.dynamic_update_slice_in_dim(self.value, part, row, axis)]
    convert_element_type x15 -> x16, other arithmetic: 26.2 us -> 10.6 us  [the longest x12 4.75 us: total(): return join([cell_sum(part).astype(bf16) for part in rows_here])]
    ppermute x5, waiting for transfers between devices: 14.6 us -> 0.01 us  [exchange(): return lax.ppermute(values, axis, [(i, i ^ distance) for i in range(count)])]
    pallas_call x4, Pallas kernels: 45.4 us -> 33.7 us  [feed(): pl.pallas_call(feed_kernel, grid=(tokens // rows,), in_specs=[by_row(widt...]
  transfers between devices with their start and end apart: 108 -> 107, of which waited for: 39 -> 38; matrix products, arithmetic and copies ran while one was open for 13% -> 8% of each run, Pallas kernels for 25% -> 27%
where the time goes in v3:
time: 762 us; the launch traced here: 755 us
  waiting for transfers between devices  268 us (35%)
  Pallas kernels  243 us (32%)
  starting transfers between devices  116 us (15%)
  local copies, waits for them, and re-layouts  75.4 us (10%)
  other arithmetic  34.7 us (5%)
  matrix products  13.4 us (2%)
    ppermute x38, waiting for transfers between devices, fsdp_send(): lax.ppermute(values, 'fsdp', [(i, (i + step) % count) for i in range(coun...  221 us
    ppermute x38, starting transfers between devices, fsdp_send(): lax.ppermute(values, 'fsdp', [(i, (i + step) % count) for i in range(coun...  56.8 us
    unnamed x405, local copies, waits for them, and re-layouts  51.3 us
    pallas_call x2, Pallas kernels, attention_grad(): pl.pallas_call(functools.partial(attention_grad_kernel, chunk, other), gr...  42.3 us
    ppermute x34, starting transfers between devices, round_send(): return lax.ppermute(values, 'ctx', pairs)  41.1 us
    pallas_call x4, Pallas kernels, feed(): pl.pallas_call(feed_kernel, grid=(tokens // rows,), in_specs=[by_row(widt...  33.7 us
    pallas_call x8, Pallas kernels, place_units(): pl.pallas_call(functools.partial(place_units_kernel, block_at, unit, colu...  31.2 us
    pallas_call x25, Pallas kernels, join(): pl.pallas_call(join_kernel, grid_spec=pltpu.PrefetchScalarGridSpec(num_sc...  30 us
  transfers between devices with their start and end apart: 107, of which 38 were waited for; matrix products, arithmetic and copies ran while one was open for 8% of the time, Pallas kernels for 27%

profile of v3, /device:TPU:0, one launch (start us, length us, event | category | flops | bytes accessed | tf_op | source)
XLA Modules:
  0.0 754.7 jit_solution(9163843467229923795)
XLA Ops:
  23.2 6.7 fusion.16
  41.5 9.5 %collective-permute-done.5.refs_3_ = bf16[512,384]{1,0:T(8,128)(2,1)} collective-permute-done((bf16[512,384]{1,0:T(8,128)(2,1)S(1)}, bf16[512,384]{1,0:T(8,128)(2,1)}, u32[]{:S(2)}, u32[]{:S(2)}) %collective-permute-start.5) | collective-permute-done | bytes 393248 | tf_op jit(solution)/shard_map/ppermute | solution.py:50
  59.6 10.1 %shard_map.179 = (f32[1024,384]{1,0:T(8,128)S(1)}, bf16[1024,256]{1,0:T(8,128)(2,1)S(1)}, bf16[1024,128]{1,0:T(8,128)(2,1)S(1)}) custom-call(s32[4]{0:T(128)S(1)} %pad_add_fusion.place_ref, bf16[512,2048]{1,0:T(8,128)(2,1)} %shard_map.178.even_ref, bf16[512,2048]{1,0:T(8,128)(2,1)} %collective-permute-done.4.odd_ref, f32[1024,256]{1,0:T(8,128)S(1)} %concatenate.36.angle_ref, ...), custom_call_target="tpu_custom_call" | custom-call | flops 1610612736 | bytes 8000000 | tf_op jit(solution)/shard_map/pallas_call | solution.py:322
  70.5 6.4 collective-permute-done.9.refs_3_
  76.9 7.3 collective-permute-done.7.refs_1_
  88.5 7.7 %collective-permute-done.11 = bf16[8,1,128,128]{3,2,1,0:T(8,128)(2,1)} collective-permute-done((bf16[8,1,128,128]{3,2,1,0:T(8,128)(2,1)S(1)}, bf16[8,1,128,128]{3,2,1,0:T(8,128)(2,1)}, u32[]{:S(2)}, u32[]{:S(2)}) %collective-permute-start.11) | collective-permute-done | bytes 262176 | tf_op jit(solution)/shard_map/ppermute | solution.py:50
  104.3 11.7 %all-to-all-done = bf16[8,256,256]{2,1,0:T(8,128)(2,1)} async-done(((bf16[8,256,256]{2,1,0:T(8,128)(2,1)}), bf16[8,256,256]{2,1,0:T(8,128)(2,1)}, u32[]{:S(2)}, u32[]{:S(2)}) %all-to-all-start) | async-done | bytes 1048608 | tf_op jit(solution)/shard_map/all_to_all | solution.py:931
  117.3 8.9 %collective-permute-done.13 = bf16[8,1,128,128]{3,2,1,0:T(8,128)(2,1)S(1)} collective-permute-done((bf16[8,1,128,128]{3,2,1,0:T(8,128)(2,1)S(1)}, bf16[8,1,128,128]{3,2,1,0:T(8,128)(2,1)S(1)}, u32[]{:S(2)}, u32[]{:S(2)}) %collective-permute-start.13) | collective-permute-done | bytes 262176 | tf_op jit(solution)/shard_map/ppermute | solution.py:50
  130.7 22.3 %shard_map.182 = (bf16[512,256]{1,0:T(8,128)(2,1)S(1)}, bf16[512,256]{1,0:T(8,128)(2,1)S(1)}, f32[8,1,512]{2,1,0:T(1,128)S(1)}) custom-call(s32[4]{0:T(128)S(1)} %pad_add_fusion.place_ref, bf16[1024,256]{1,0:T(8,128)(2,1)S(1)} %copy-done.140, bf16[4096,128]{1,0:T(8,128)(2,1)S(1)} %bitcast.97), custom_call_target="tpu_custom_call" | custom-call | flops 16000000000 | bytes 8000000 | tf_op jit(solution)/shard_map/pallas_call | solution.py:542
  157.2 11.0 %collective-permute-done.19.refs_4_ = bf16[64,2048]{1,0:T(8,128)(2,1)S(1)} collective-permute-done((bf16[64,2048]{1,0:T(8,128)(2,1)S(1)}, bf16[64,2048]{1,0:T(8,128)(2,1)S(1)}, u32[]{:S(2)}, u32[]{:S(2)}) %collective-permute-start.19) | collective-permute-done | bytes 262176 | tf_op jit(solution)/shard_map/ppermute | solution.py:50
  174.3 21.3 %collective-permute-done.21.refs_0_ = bf16[128,2048]{1,0:T(8,128)(2,1)S(1)} collective-permute-done((bf16[128,2048]{1,0:T(8,128)(2,1)S(1)}, bf16[128,2048]{1,0:T(8,128)(2,1)S(1)}, u32[]{:S(2)}, u32[]{:S(2)}) %collective-permute-start.21) | collective-permute-done | bytes 524320 | tf_op jit(solution)/shard_map/ppermute | solution.py:55
  199.9 13.2 %collective-permute-done.25.refs_5_ = bf16[64,2048]{1,0:T(8,128)(2,1)S(1)} collective-permute-done((bf16[64,2048]{1,0:T(8,128)(2,1)S(1)}, bf16[64,2048]{1,0:T(8,128)(2,1)S(1)}, u32[]{:S(2)}, u32[]{:S(2)}) %collective-permute-start.25) | collective-permute-done | bytes 262176 | tf_op jit(solution)/shard_map/ppermute | solution.py:50
  218.6 14.1 %collective-permute-done.29.refs_6_ = bf16[64,2048]{1,0:T(8,128)(2,1)S(1)} collective-permute-done((bf16[64,2048]{1,0:T(8,128)(2,1)S(1)}, bf16[64,2048]{1,0:T(8,128)(2,1)S(1)}, u32[]{:S(2)}, u32[]{:S(2)}) %collective-permute-start.29) | collective-permute-done | bytes 262176 | tf_op jit(solution)/shard_map/ppermute | solution.py:50
  239.6 23.6 %collective-permute-done.33.refs_6_ = bf16[256,1024]{1,0:T(8,128)(2,1)S(1)} collective-permute-done((bf16[256,1024]{1,0:T(8,128)(2,1)S(1)}, bf16[256,1024]{1,0:T(8,128)(2,1)S(1)}, u32[]{:S(2)}, u32[]{:S(2)}) %collective-permute-start.33) | collective-permute-done | bytes 524320 | tf_op jit(solution)/shard_map/ppermute | solution.py:50
  267.7 13.7 %collective-permute-done.36.refs_7_ = bf16[64,2048]{1,0:T(8,128)(2,1)S(1)} collective-permute-done((bf16[64,2048]{1,0:T(8,128)(2,1)S(1)}, bf16[64,2048]{1,0:T(8,128)(2,1)S(1)}, u32[]{:S(2)}, u32[]{:S(2)}) %collective-permute-start.36) | collective-permute-done | bytes 262176 | tf_op jit(solution)/shard_map/ppermute | solution.py:50
  294.4 17.4 %collective-permute-done.38.refs_7_ = bf16[256,1024]{1,0:T(8,128)(2,1)} collective-permute-done((bf16[256,1024]{1,0:T(8,128)(2,1)}, bf16[256,1024]{1,0:T(8,128)(2,1)}, u32[]{:S(2)}, u32[]{:S(2)}) %collective-permute-start.38) | collective-permute-done | bytes 524320 | tf_op jit(solution)/shard_map/ppermute | solution.py:50
  314.2 9.6 %shard_map.194 = (bf16[512,512]{1,0:T(8,128)(2,1)S(1)}, bf16[512,1024]{1,0:T(8,128)(2,1)S(1)}, bf16[512,2048]{1,0:T(8,128)(2,1)S(1)}, bf16[512,2048]{1,0:T(8,128)(2,1)}) custom-call(bf16[512,2048]{1,0:T(8,128)(2,1)} %collective-permute-done.37.normed_ref.refs_3_, bf16[512,2048]{1,0:T(8,128)(2,1)S(1)} %copy-done.29, ...), custom_call_target="tpu_custom_call" | custom-call | flops 6442450944 | bytes 16000000 | tf_op jit(solution)/shard_map/pallas_call | solution.py:679
  324.7 8.8 %shard_map.195 = (bf16[512,512]{1,0:T(8,128)(2,1)S(1)}, bf16[512,1024]{1,0:T(8,128)(2,1)S(1)}, bf16[512,2048]{1,0:T(8,128)(2,1)S(1)}, bf16[512,2048]{1,0:T(8,128)(2,1)S(1)}) custom-call(bf16[512,2048]{1,0:T(8,128)(2,1)} %shard_map.191.normed_ref.refs_2_, bf16[512,2048]{1,0:T(8,128)(2,1)S(1)} %copy-done.9, bf16[2048,1024]{1,0:T(8,128)(2,1)S(1)} %shard_map.192.weight_ref, ...), custom_call_target="tpu_custom_call" | custom-call | flops 6442450944 | bytes 16000000 | tf_op jit(solution)/shard_map/pallas_call | solution.py:679
  338.3 8.0 %shard_map.196 = (bf16[512,512]{1,0:T(8,128)(2,1)S(1)}, bf16[512,1024]{1,0:T(8,128)(2,1)S(1)}, bf16[512,2048]{1,0:T(8,128)(2,1)}, bf16[512,2048]{1,0:T(8,128)(2,1)S(1)}) custom-call(bf16[512,2048]{1,0:T(8,128)(2,1)S(1)} %copy-done.3, bf16[512,2048]{1,0:T(8,128)(2,1)S(1)} %copy-done.25, bf16[2048,1024]{1,0:T(8,128)(2,1)S(1)} %shard_map.192.weight_ref, ...), custom_call_target="tpu_custom_call" | custom-call | flops 6442450944 | bytes 16000000 | tf_op jit(solution)/shard_map/pallas_call | solution.py:679
  353.2 7.2 shard_map.198
  389.1 9.6 %collective-permute-done.48 = bf16[256,512]{1,0:T(8,128)(2,1)S(1)} collective-permute-done((bf16[256,512]{1,0:T(8,128)(2,1)S(1)}, bf16[256,512]{1,0:T(8,128)(2,1)S(1)}, u32[]{:S(2)}, u32[]{:S(2)}) %collective-permute-start.48) | collective-permute-done | bytes 262176 | tf_op jit(solution)/shard_map/ppermute | solution.py:50
  426.4 7.8 %collective-permute-done.52 = bf16[256,512]{1,0:T(8,128)(2,1)S(1)} collective-permute-done((bf16[256,512]{1,0:T(8,128)(2,1)S(1)}, bf16[256,512]{1,0:T(8,128)(2,1)S(1)}, u32[]{:S(2)}, u32[]{:S(2)}) %collective-permute-start.52) | collective-permute-done | bytes 262176 | tf_op jit(solution)/shard_map/ppermute | solution.py:50
  459.7 19.6 %shard_map.211 = (f32[512,256]{1,0:T(8,128)S(1)}, f32[4096,128]{1,0:T(8,128)S(1)}) custom-call(s32[4]{0:T(128)S(1)} %pad_add_fusion.place_ref, bf16[1024,256]{1,0:T(8,128)(2,1)S(1)} %copy-done.141, bf16[512,2048]{1,0:T(8,128)(2,1)} %shard_map.209.branch_ref, bf16[512,256]{1,0:T(8,128)(2,1)S(1)} %copy-done.83, f32[8,1,512]{2,1,0:T(1,128)S(1)} %copy-done.152, ...), custom_call_target="tpu_custom_call" | custom-call | flops 17999998976 | bytes 12000000 | tf_op jit(solution)/shard_map/pallas_call | solution.py:619
  492.3 22.6 %shard_map.213 = (f32[512,256]{1,0:T(8,128)S(1)}, f32[4096,128]{1,0:T(8,128)S(1)}) custom-call(s32[4]{0:T(128)S(1)} %pad_add_fusion.place_ref, bf16[1024,256]{1,0:T(8,128)(2,1)S(1)} %copy-done.141, bf16[512,2048]{1,0:T(8,128)(2,1)} %collective-permute-done.53.branch_ref, bf16[512,256]{1,0:T(8,128)(2,1)S(1)} %copy-done.85, f32[8,1,512]{2,1,0:T(1,128)S(1)} %copy-done.152, ...), custom_call_target="tpu_custom_call" | custom-call | flops 17999998976 | bytes 12000000 | tf_op jit(solution)/shard_map/pallas_call | solution.py:619
  523.1 7.4 collective-permute-done.65
  534.9 13.7 %collective-permute-done.67 = bf16[8,1,128,128]{3,2,0,1:T(8,128)(2,1)S(1)} collective-permute-done((bf16[8,1,128,128]{3,2,0,1:T(8,128)(2,1)S(1)}, bf16[8,1,128,128]{3,2,0,1:T(8,128)(2,1)S(1)}, u32[]{:S(2)}, u32[]{:S(2)}) %collective-permute-start.67) | collective-permute-done | bytes 262176 | tf_op jit(solution)/shard_map/ppermute | solution.py:50
  548.6 5.3 collective-permute-done.68
  568.5 13.9 %shard_map.218 = (bf16[512,384]{1,0:T(8,128)(2,1)S(1)}, bf16[512,384]{1,0:T(8,128)(2,1)S(1)}, bf16[512,2048]{1,0:T(8,128)(2,1)}, bf16[512,2048]{1,0:T(8,128)(2,1...) custom-call(s32[4]{0:T(128)S(1)} %pad_add_fusion.place_ref, bf16[512,2048]{1,0:T(8,128)(2,1)} %shard_map.178.even_ref, ...), custom_call_target="tpu_custom_call" | custom-call | flops 1610612736 | bytes 12000000 | tf_op jit(solution)/shard_map/pallas_call | solution.py:436
  584.5 6.4 collective-permute-done.74
  644.7 5.6 collective-permute-done.84
  669.7 7.3 collective-permute-done.88
  676.9 7.9 %collective-permute-done.89 = bf16[512,256]{1,0:T(8,128)(2,1)S(1)} collective-permute-done((bf16[512,256]{1,0:T(8,128)(2,1)S(1)}, bf16[512,256]{1,0:T(8,128)(2,1)S(1)}, u32[]{:S(2)}, u32[]{:S(2)}) %collective-permute-start.89) | collective-permute-done | bytes 262176 | tf_op jit(solution)/shard_map/ppermute | solution.py:50
  (767 shorter events, 385.3 us)
Async XLA Ops:
  50.9 33.3 %collective-permute-start.6 = (bf16[128,2048]{1,0:T(8,128)(2,1)}, bf16[128,2048]{1,0:T(8,128)(2,1)S(1)}, u32[]{:S(2)}, u32[]{:S(2)}) collective-permute-start(bf16[128,2048]{1,0:T(8,128)(2,1)} %refs_0_.1), channel_id=1, source_target_pairs={{0,8},{4,20},{8,0},{12,28},{16,24},{20,4},{24,16},{28,12},{1,9},{5... | collective-permute-start | bytes 1572872 | tf_op jit(solution)/shard_map/ppermute | solution.py:78
  52.1 32.9 %collective-permute-start.10 = (bf16[256,1024]{1,0:T(8,128)(2,1)}, bf16[256,1024]{1,0:T(8,128)(2,1)S(1)}, u32[]{:S(2)}, u32[]{:S(2)}) collective-permute-start(bf16[256,1024]{1,0:T(8,128)(2,1)} %pad_maximum_fusion.5), channel_id=1, source_target_pairs={{0,1},{1,0},{2,3},{3,2},{4,5},{5,4},{6,7},{7,6},{8,9},{9,8},{10,11... | collective-permute-start | bytes 1572872 | tf_op jit(solution)/shard_map/ppermute | solution.py:55
  56.6 27.7 %collective-permute-start.7 = (bf16[512,256]{1,0:T(8,128)(2,1)}, bf16[512,256]{1,0:T(8,128)(2,1)S(1)}, u32[]{:S(2)}, u32[]{:S(2)}) collective-permute-start(bf16[512,256]{1,0:T(8,128)(2,1)} %constant_dynamic-slice_fusion.10.refs_0_), channel_id=1, source_target_pairs={{0,1},{1,2},{2,3},{3,0},{4,5},{5,6},{6,7},{7,4},{8,9},{9,10},{10,1... | collective-permute-start | bytes 786440 | tf_op jit(solution)/shard_map/ppermute | solution.py:50
  87.9 38.3 %collective-permute-start.14 = (bf16[256,2048]{1,0:T(8,128)(2,1)S(1)}, bf16[256,2048]{1,0:T(8,128)(2,1)S(1)}, u32[]{:S(2)}, u32[]{:S(2)}) collective-permute-start(bf16[256,2048]{1,0:T(8,128)(2,1)S(1)} %shard_map.181.refs_0_), channel_id=1, source_target_pairs={{0,16},{4,12},{8,24},{12,4},{16,0},{20,28},{24,8},{28,20},{1,17},{... | collective-permute-start | bytes 3145736 | tf_op jit(solution)/shard_map/ppermute | solution.py:78
  100.5 25.7 %collective-permute-start.15 = (bf16[256,1024]{1,0:T(8,128)(2,1)}, bf16[256,1024]{1,0:T(8,128)(2,1)}, u32[]{:S(2)}, u32[]{:S(2)}) collective-permute-start(bf16[256,1024]{1,0:T(8,128)(2,1)} %pad_maximum_fusion.6), channel_id=1, source_target_pairs={{0,1},{1,0},{2,3},{3,2},{4,5},{5,4},{6,7},{7,6},{8,9},{9,8},{10,11... | collective-permute-start | bytes 1572872 | tf_op jit(solution)/shard_map/ppermute | solution.py:55
  100.6 25.6 %collective-permute-start.13 = (bf16[8,1,128,128]{3,2,1,0:T(8,128)(2,1)S(1)}, bf16[8,1,128,128]{3,2,1,0:T(8,128)(2,1)S(1)}, u32[]{:S(2)}, u32[]{:S(2)}) collective-permute-start(bf16[8,1,128,128]{3,2,1,0:T(8,128)(2,1)S(1)} %bitcast.101), channel_id=1, source_target_pairs={{0,3},{1,0},{2,1},{3,2},{4,7},{5,4},{6,5},{7,6},{8,11},{9,8},{10,9... | collective-permute-start | bytes 786440 | tf_op jit(solution)/shard_map/ppermute | solution.py:50
  127.7 26.9 %collective-permute-start.16 = (bf16[512,2048]{1,0:T(8,128)(2,1)S(1)}, bf16[512,2048]{1,0:T(8,128)(2,1)S(1)}, u32[]{:S(2)}, u32[]{:S(2)}) collective-permute-start(bf16[512,2048]{1,0:T(8,128)(2,1)S(1)} %shard_map.183.outer_ref.refs_4_), channel_id=1, source_target_pairs={{0,4},{4,0},{8,12},{12,8},{16,20},{20,16},{24,28},{28,24},{1,5},{5... | collective-permute-start | bytes 6291464 | tf_op jit(solution)/shard_map/ppermute | solution.py:40
  169.4 27.5 %collective-permute-start.20 = (bf16[256,2048]{1,0:T(8,128)(2,1)S(1)}, bf16[256,2048]{1,0:T(8,128)(2,1)S(1)}, u32[]{:S(2)}, u32[]{:S(2)}) collective-permute-start(bf16[256,2048]{1,0:T(8,128)(2,1)S(1)} %get-tuple-element.525), channel_id=1, source_target_pairs={{0,16},{4,12},{8,24},{12,4},{16,0},{20,28},{24,8},{28,20},{1,17},{... | collective-permute-start | bytes 3145736 | tf_op jit(solution)/shard_map/ppermute | solution.py:78
  171.1 25.8 %collective-permute-start.22 = (bf16[256,1024]{1,0:T(8,128)(2,1)S(1)}, bf16[256,1024]{1,0:T(8,128)(2,1)S(1)}, u32[]{:S(2)}, u32[]{:S(2)}) collective-permute-start(bf16[256,1024]{1,0:T(8,128)(2,1)S(1)} %copy-done.50), channel_id=1, source_target_pairs={{0,2},{1,3},{2,0},{3,1},{4,6},{5,7},{6,4},{7,5},{8,10},{9,11},{10,... | collective-permute-start | bytes 1572872 | tf_op jit(solution)/shard_map/ppermute | solution.py:50
  235.7 28.4 %collective-permute-start.32 = (bf16[512,2048]{1,0:T(8,128)(2,1)S(1)}, bf16[512,2048]{1,0:T(8,128)(2,1)S(1)}, u32[]{:S(2)}, u32[]{:S(2)}) collective-permute-start(bf16[512,2048]{1,0:T(8,128)(2,1)S(1)} %shard_map.188.outer_ref.refs_6_), channel_id=1, source_target_pairs={{0,4},{4,0},{8,12},{12,8},{16,20},{20,16},{24,28},{28,24},{1,5},{5... | collective-permute-start | bytes 6291464 | tf_op jit(solution)/shard_map/ppermute | solution.py:40
  236.4 27.7 %collective-permute-start.30 = (bf16[256,2048]{1,0:T(8,128)(2,1)S(1)}, bf16[256,2048]{1,0:T(8,128)(2,1)S(1)}, u32[]{:S(2)}, u32[]{:S(2)}) collective-permute-start(bf16[256,2048]{1,0:T(8,128)(2,1)S(1)} %shard_map.187.refs_0_), channel_id=1, source_target_pairs={{0,16},{4,12},{8,24},{12,4},{16,0},{20,28},{24,8},{28,20},{1,17},{... | collective-permute-start | bytes 3145736 | tf_op jit(solution)/shard_map/ppermute | solution.py:78
  285.5 26.3 %collective-permute-start.37 = (bf16[512,2048]{1,0:T(8,128)(2,1)}, bf16[512,2048]{1,0:T(8,128)(2,1)}, u32[]{:S(2)}, u32[]{:S(2)}) collective-permute-start(bf16[512,2048]{1,0:T(8,128)(2,1)} %shard_map.191.normed_ref.refs_2_), channel_id=1, source_target_pairs={{0,4},{4,0},{8,12},{12,8},{16,20},{20,16},{24,28},{28,24},{1,5},{5... | collective-permute-start | bytes 6291464 | tf_op jit(solution)/shard_map/ppermute | solution.py:40
  285.5 26.2 %collective-permute-start.38 = (bf16[256,1024]{1,0:T(8,128)(2,1)}, bf16[256,1024]{1,0:T(8,128)(2,1)}, u32[]{:S(2)}, u32[]{:S(2)}) collective-permute-start(bf16[256,1024]{1,0:T(8,128)(2,1)} %collective-permute-done.15.refs_3_), channel_id=1, source_target_pairs={{0,2},{1,3},{2,0},{3,1},{4,6},{5,7},{6,4},{7,5},{8,10},{9,11},{10,... | collective-permute-start | bytes 1572872 | tf_op jit(solution)/shard_map/ppermute | solution.py:50
  455.6 29.8 %collective-permute-start.58 = (bf16[256,512]{1,0:T(8,128)(2,1)S(1)}, bf16[256,512]{1,0:T(8,128)(2,1)S(1)}, u32[]{:S(2)}, u32[]{:S(2)}) collective-permute-start(bf16[256,512]{1,0:T(8,128)(2,1)S(1)} %copy-done.150), channel_id=1, source_target_pairs={{0,2},{1,3},{2,0},{3,1},{4,6},{5,7},{6,4},{7,5},{8,10},{9,11},{10,... | collective-permute-start | bytes 786440 | tf_op jit(solution)/shard_map/ppermute | solution.py:50
  455.6 29.7 %collective-permute-start.59 = (bf16[256,512]{1,0:T(8,128)(2,1)S(1)}, bf16[256,512]{1,0:T(8,128)(2,1)S(1)}, u32[]{:S(2)}, u32[]{:S(2)}) collective-permute-start(bf16[256,512]{1,0:T(8,128)(2,1)S(1)} %copy-done.148), channel_id=1, source_target_pairs={{0,2},{1,3},{2,0},{3,1},{4,6},{5,7},{6,4},{7,5},{8,10},{9,11},{10,... | collective-permute-start | bytes 786440 | tf_op jit(solution)/shard_map/ppermute | solution.py:50
  458.6 26.8 %collective-permute-start.56 = (bf16[512,512]{1,0:T(8,128)(2,1)S(1)}, bf16[512,512]{1,0:T(8,128)(2,1)S(1)}, u32[]{:S(2)}, u32[]{:S(2)}) collective-permute-start(bf16[512,512]{1,0:T(8,128)(2,1)S(1)} %constant_dynamic-slice_fusion.9), channel_id=1, source_target_pairs={{0,1},{1,0},{2,3},{3,2},{4,5},{5,4},{6,7},{7,6},{8,9},{9,8},{10,11... | collective-permute-start | bytes 1572872 | tf_op jit(solution)/shard_map/ppermute | solution.py:55
  458.7 26.7 %collective-permute-start.57 = (bf16[256,2048]{1,0:T(8,128)(2,1)S(1)}, bf16[256,2048]{1,0:T(8,128)(2,1)S(1)}, u32[]{:S(2)}, u32[]{:S(2)}) collective-permute-start(bf16[256,2048]{1,0:T(8,128)(2,1)S(1)} %copy-done.137), channel_id=1, source_target_pairs={{0,16},{4,12},{8,24},{12,4},{16,0},{20,28},{24,8},{28,20},{1,17},{... | collective-permute-start | bytes 3145736 | tf_op jit(solution)/shard_map/ppermute | solution.py:78
  486.3 28.7 %collective-permute-start.63 = (bf16[256,512]{1,0:T(8,128)(2,1)S(1)}, bf16[256,512]{1,0:T(8,128)(2,1)S(1)}, u32[]{:S(2)}, u32[]{:S(2)}) collective-permute-start(bf16[256,512]{1,0:T(8,128)(2,1)S(1)} %copy-done.145), channel_id=1, source_target_pairs={{0,2},{1,3},{2,0},{3,1},{4,6},{5,7},{6,4},{7,5},{8,10},{9,11},{10,... | collective-permute-start | bytes 786440 | tf_op jit(solution)/shard_map/ppermute | solution.py:50
  488.8 26.2 %collective-permute-start.64 = (bf16[256,512]{1,0:T(8,128)(2,1)S(1)}, bf16[256,512]{1,0:T(8,128)(2,1)S(1)}, u32[]{:S(2)}, u32[]{:S(2)}) collective-permute-start(bf16[256,512]{1,0:T(8,128)(2,1)S(1)} %copy-done.143), channel_id=1, source_target_pairs={{0,2},{1,3},{2,0},{3,1},{4,6},{5,7},{6,4},{7,5},{8,10},{9,11},{10,... | collective-permute-start | bytes 786440 | tf_op jit(solution)/shard_map/ppermute | solution.py:50
  489.3 25.8 %collective-permute-start.62 = (bf16[128,2048]{1,0:T(8,128)(2,1)S(1)}, bf16[128,2048]{1,0:T(8,128)(2,1)S(1)}, u32[]{:S(2)}, u32[]{:S(2)}) collective-permute-start(bf16[128,2048]{1,0:T(8,128)(2,1)S(1)} %get-tuple-element.751), channel_id=1, source_target_pairs={{0,8},{4,20},{8,0},{12,28},{16,24},{20,4},{24,16},{28,12},{1,9},{5... | collective-permute-start | bytes 1572872 | tf_op jit(solution)/shard_map/ppermute | solution.py:78
  517.9 36.0 %collective-permute-start.69 = (bf16[1024,1024]{1,0:T(8,128)(2,1)}, bf16[1024,1024]{1,0:T(8,128)(2,1)S(1)}, u32[]{:S(2)}, u32[]{:S(2)}) collective-permute-start(bf16[1024,1024]{1,0:T(8,128)(2,1)} %shard_map.217.source_ref), channel_id=1, source_target_pairs={{0,16},{4,12},{8,24},{12,4},{16,0},{20,28},{24,8},{28,20},{1,17},{... | collective-permute-start | bytes 6291464 | tf_op jit(solution)/shard_map/ppermute | solution.py:78
  553.9 37.0 %collective-permute-start.70 = (bf16[1024,1024]{1,0:T(8,128)(2,1)}, bf16[1024,1024]{1,0:T(8,128)(2,1)}, u32[]{:S(2)}, u32[]{:S(2)}) collective-permute-start(bf16[1024,1024]{1,0:T(8,128)(2,1)} %shard_map.217.source_ref), channel_id=1, source_target_pairs={{0,4},{4,0},{8,12},{12,8},{16,20},{20,16},{24,28},{28,24},{1,5},{5... | collective-permute-start | bytes 6291464 | tf_op jit(solution)/shard_map/ppermute | solution.py:40
  554.8 36.2 %collective-permute-start.71 = (bf16[512,1024]{1,0:T(8,128)(2,1)S(1)}, bf16[512,1024]{1,0:T(8,128)(2,1)}, u32[]{:S(2)}, u32[]{:S(2)}) collective-permute-start(bf16[512,1024]{1,0:T(8,128)(2,1)S(1)} %pad_maximum_fusion.2.refs_0_), channel_id=1, source_target_pairs={{0,8},{4,20},{8,0},{12,28},{16,24},{20,4},{24,16},{28,12},{1,9},{5... | collective-permute-start | bytes 3145736 | tf_op jit(solution)/shard_map/ppermute | solution.py:78
  558.0 32.9 %all-to-all-start.1 = ((bf16[256,8,256]{2,0,1:T(8,128)(2,1)}), bf16[256,8,256]{2,0,1:T(8,128)(2,1)}, u32[]{:S(2)}, u32[]{:S(2)}) async-start(bf16[256,8,256]{2,0,1:T(8,128)(2,1)} %bitcast.106), calls=%async_computation.1 | async-start | bytes 2097152 | tf_op jit(solution)/shard_map/all_to_all | solution.py:931
  564.1 26.9 %collective-permute-start.72 = (bf16[128,2048]{1,0:T(8,128)(2,1)S(1)}, bf16[128,2048]{1,0:T(8,128)(2,1)}, u32[]{:S(2)}, u32[]{:S(2)}) collective-permute-start(bf16[128,2048]{1,0:T(8,128)(2,1)S(1)} %add_convert_fusion.2), channel_id=1, source_target_pairs={{0,1},{1,0},{2,3},{3,2},{4,5},{5,4},{6,7},{7,6},{8,9},{9,8},{10,11... | collective-permute-start | bytes 1572872 | tf_op jit(solution)/shard_map/ppermute | solution.py:55
  593.3 28.9 %collective-permute-start.75 = (bf16[512,2048]{1,0:T(8,128)(2,1)}, bf16[512,2048]{1,0:T(8,128)(2,1)S(1)}, u32[]{:S(2)}, u32[]{:S(2)}) collective-permute-start(bf16[512,2048]{1,0:T(8,128)(2,1)} %get-tuple-element.801), channel_id=1, source_target_pairs={{0,4},{4,0},{8,12},{12,8},{16,20},{20,16},{24,28},{28,24},{1,5},{5... | collective-permute-start | bytes 6291464 | tf_op jit(solution)/shard_map/ppermute | solution.py:40
  593.4 28.9 %collective-permute-start.76 = (bf16[1024,1024]{1,0:T(8,128)(2,1)S(1)}, bf16[1024,1024]{1,0:T(8,128)(2,1)}, u32[]{:S(2)}, u32[]{:S(2)}) collective-permute-start(bf16[1024,1024]{1,0:T(8,128)(2,1)S(1)} %shard_map.219.source_ref), channel_id=1, source_target_pairs={{0,16},{4,12},{8,24},{12,4},{16,0},{20,28},{24,8},{28,20},{1,17},{... | collective-permute-start | bytes 6291464 | tf_op jit(solution)/shard_map/ppermute | solution.py:78
  596.3 25.9 %collective-permute-start.79 = (bf16[64,2048]{1,0:T(8,128)(2,1)}, bf16[64,2048]{1,0:T(8,128)(2,1)S(1)}, u32[]{:S(2)}, u32[]{:S(2)}) collective-permute-start(bf16[64,2048]{1,0:T(8,128)(2,1)} %get-tuple-element.821), channel_id=1, source_target_pairs={{0,2},{1,3},{2,0},{3,1},{4,6},{5,7},{6,4},{7,5},{8,10},{9,11},{10,... | collective-permute-start | bytes 786440 | tf_op jit(solution)/shard_map/ppermute | solution.py:50
  622.3 30.9 %collective-permute-start.82 = (bf16[1024,1024]{1,0:T(8,128)(2,1)S(1)}, bf16[1024,1024]{1,0:T(8,128)(2,1)}, u32[]{:S(2)}, u32[]{:S(2)}) collective-permute-start(bf16[1024,1024]{1,0:T(8,128)(2,1)S(1)} %copy-done.35), channel_id=1, source_target_pairs={{0,4},{4,0},{8,12},{12,8},{16,20},{20,16},{24,28},{28,24},{1,5},{5... | collective-permute-start | bytes 6291464 | tf_op jit(solution)/shard_map/ppermute | solution.py:40
  627.5 25.6 %collective-permute-start.81 = (bf16[256,2048]{1,0:T(8,128)(2,1)S(1)}, bf16[256,2048]{1,0:T(8,128)(2,1)}, u32[]{:S(2)}, u32[]{:S(2)}) collective-permute-start(bf16[256,2048]{1,0:T(8,128)(2,1)S(1)} %shard_map.223.refs_0_), channel_id=1, source_target_pairs={{0,8},{4,20},{8,0},{12,28},{16,24},{20,4},{24,16},{28,12},{1,9},{5... | collective-permute-start | bytes 3145736 | tf_op jit(solution)/shard_map/ppermute | solution.py:78
  655.1 31.7 %collective-permute-start.86 = (bf16[512,2048]{1,0:T(8,128)(2,1)S(1)}, bf16[512,2048]{1,0:T(8,128)(2,1)S(1)}, u32[]{:S(2)}, u32[]{:S(2)}) collective-permute-start(bf16[512,2048]{1,0:T(8,128)(2,1)S(1)} %shard_map.227.shard_ref), channel_id=1, source_target_pairs={{0,16},{4,12},{8,24},{12,4},{16,0},{20,28},{24,8},{28,20},{1,17},{... | collective-permute-start | bytes 6291464 | tf_op jit(solution)/shard_map/ppermute | solution.py:78
  658.2 26.6 %collective-permute-start.85 = (bf16[128,2048]{1,0:T(8,128)(2,1)S(1)}, bf16[128,2048]{1,0:T(8,128)(2,1)S(1)}, u32[]{:S(2)}, u32[]{:S(2)}) collective-permute-start(bf16[128,2048]{1,0:T(8,128)(2,1)S(1)} %get-tuple-element.849), channel_id=1, source_target_pairs={{0,8},{4,20},{8,0},{12,28},{16,24},{20,4},{24,16},{28,12},{1,9},{5... | collective-permute-start | bytes 1572872 | tf_op jit(solution)/shard_map/ppermute | solution.py:78
  (277 other events, 2642.9 us)

commit v4 on v3

--- a/solution.py
+++ b/solution.py
@@ -96,13 +96,13 @@
 
     def run(self, parts, spare=0):
         jobs, self.jobs = self.jobs[:spare], self.jobs[spare:]
+        early = [start(self.begin) for start, _ in jobs]
         results = [function(self.begin(values)) for function, values in parts]
-        results += [start(self.begin) for start, _ in jobs]
-        results = lax.optimization_barrier(results)
-        for (_, finish), value in zip(jobs, results[len(parts) :]):
+        early, results = lax.optimization_barrier((early, results))
+        for (_, finish), value in zip(jobs, early):
             finish(value)
         self.event = results[0]
-        return results[: len(parts)]
+        return results
 
     def drain(self, done):
         while self.jobs and not done():
@@ -729,31 +729,43 @@
     return [lax.slice_in_dim(made[0], n * size // count, (n + 1) * size // count) for n in range(count)]
 
 
-def place_kernel(place_ref, shard_ref, *refs):
-    refs[-1][...] = shard_ref[...].astype(f32)
-
-
-def place_blocks(whole, shape, source, block, grid, place, from_block, to_block):
-    in_specs = [pl.BlockSpec(block, from_block)]
-    operands = [place, source]
-    aliases = {}
-    if whole is not None:
-        in_specs.append(pl.BlockSpec(memory_space=pl.ANY))
-        operands.append(whole)
-        aliases = {2: 0}
+def norm_grad_kernel(hidden_ref, outer_ref, gain_ref, *refs):
+    terms, (low_ref, grad_ref, gain_grad_ref) = refs[:-3], refs[-3:]
+    normed_grad = terms[0][...]
+    for term in terms[1:]:
+        normed_grad = normed_grad + term[...]
+    hidden = hidden_ref[...]
+    scale = lax.rsqrt(jnp.mean(hidden * hidden, axis=1, keepdims=True) + epsilon)
+    scaled = normed_grad * gain_ref[...]
+    along = jnp.mean(scaled * hidden, axis=1, keepdims=True)
+    grad = outer_ref[...].astype(f32) + scale * scaled - hidden * (scale * scale * scale * along)
+    grad_ref[...] = grad
+    low_ref[...] = grad.astype(bf16)
+
+    @pl.when(pl.program_id(0) == 0)
+    def _():
+        gain_grad_ref[...] = jnp.zeros_like(gain_grad_ref)
+
+    gain_grad_ref[0:1, :] += jnp.sum(normed_grad * hidden * scale, axis=0, keepdims=True)
+
+
+def norm_grad(hidden, outer, gain, terms):
+    tokens, width = hidden.shape
+    rows = tokens // 4
+    by_row = pl.BlockSpec((rows, width), lambda i: (i, 0))
     return pl.pallas_call(
-        place_kernel,
-        grid_spec=pltpu.PrefetchScalarGridSpec(
-            num_scalar_prefetch=1,
-            grid=grid,
-            in_specs=in_specs,
-            out_specs=pl.BlockSpec(block, to_block),
-        ),
-        out_shape=jax.ShapeDtypeStruct(shape, f32),
-        input_output_aliases=aliases,
+        norm_grad_kernel,
+        grid=(4,),
+        in_specs=[by_row, by_row, pl.BlockSpec((1, width), lambda i: (0, 0))] + [by_row] * len(terms),
+        out_specs=[by_row, by_row, pl.BlockSpec((8, width), lambda i: (0, 0))],
+        out_shape=[
+            jax.ShapeDtypeStruct((tokens, width), bf16),
+            jax.ShapeDtypeStruct((tokens, width), f32),
+            jax.ShapeDtypeStruct((8, width), f32),
+        ],
         compiler_params=vmem(16),
-        cost_estimate=cost(0, 6 * source.size),
-    )(*operands)
+        cost_estimate=cost(20 * tokens * width, 5e6),
+    )(hidden, outer, gain[None, :], *terms)
 
 
 def place_units_kernel(block_at, unit, columns, place_ref, source_ref, *refs):
@@ -807,33 +819,56 @@
     whole = None
     rows = halves[0].shape[0] // 4
     for odd, half in enumerate(halves):
-        whole = place_blocks(
+        whole = place_units(
             whole,
             (rows, CELL * unit),
             half,
-            (rows, unit),
-            (4,),
+            rows,
+            unit,
             place,
-            lambda i, at: (i, 0),
-            lambda i, at, odd=odd: (0, token_block(4 * odd + i, at)),
+            lambda slot, column, at, odd=odd: token_block(4 * odd + slot, at),
         )
     return whole
+
+
+def place_rows_kernel(slot, place_ref, source_ref, *refs):
+    out_ref, wide_ref, sems = refs[-3:]
+    rows = wide_ref.shape[1]
+    copies = []
+    for n in range(wide_ref.shape[0]):
+        wide_ref[n] = source_ref[n * rows : (n + 1) * rows].astype(f32)
+        start = pl.multiple_of(token_block(slot + n, place_ref) * rows, rows)
+        copies.append(
+            pltpu.make_async_copy(wide_ref.at[n], out_ref.at[pl.ds(start, rows)], sems.at[n])
+        )
+        copies[-1].start()
+    for copy in copies:
+        copy.wait()
 
 
 def place_rows(quarters, place):
     whole = None
     rows, columns = quarters[0].shape[0] // 2, quarters[0].shape[1]
     for n, quarter in enumerate(quarters):
-        whole = place_blocks(
-            whole,
-            (CELL * rows, columns),
-            quarter,
-            (rows, columns),
-            (2,),
-            place,
-            lambda i, at: (i, 0),
-            lambda i, at, n=n: (token_block(2 * n + i, at), 0),
-        )
+        extra = [] if whole is None else [whole]
+        whole = pl.pallas_call(
+            functools.partial(place_rows_kernel, 2 * n),
+            grid_spec=pltpu.PrefetchScalarGridSpec(
+                num_scalar_prefetch=1,
+                grid=(1,),
+                in_specs=[pl.BlockSpec(quarter.shape, lambda i, at: (0, 0))]
+                + [pl.BlockSpec(memory_space=pl.ANY)] * len(extra),
+                out_specs=pl.BlockSpec(memory_space=pl.ANY),
+                scratch_shapes=[
+                    pltpu.VMEM((2, rows, columns), f32),
+                    pltpu.SemaphoreType.DMA((2,)),
+                ],
+            ),
+            out_shape=jax.ShapeDtypeStruct((CELL * rows, columns), f32),
+            input_output_aliases={2: 0} if extra else {},
+            compiler_params=vmem(16),
+            cost_estimate=cost(0, 6 * quarter.size),
+        )(place, quarter, *extra)
     return whole
 
 
@@ -1126,48 +1161,38 @@
         for step in range(1, cell_count):
             kv_all = put(kv_all, cell_send(kv_cells, step), (cell - step) % cell_count)
 
-    attended, outer_other = steps.run(
+    attended, outer_other, *outer_next = steps.run(
         [
             (lambda v: attention(place, *v, rows, chunk), (query_low, kv_all)),
             (twin_send, outer_mine),
-        ],
+        ]
+        + [(lambda v, j=j: pair_send(v, -j, pair), cotangent) for j in range(1, pair)],
         1,
     )
     *attended, log_total = attended
     outer_parts = [[outer_mine, outer_other]]
     terms = [dot(half, out_rows).astype(bf16) for half in attended]
-    got = steps.run([(twin_send, terms[1])], 1)
+    got = steps.run([(twin_send, terms[1])] + [(first_round, shard) for shard in outer_next], 1)
+    outer_twos = [rows_joined(shard, g) for shard, g in zip(outer_next, got[1:])]
     kept, sent = reduce_first(terms[0], got[0])
-    got = steps.run(
-        [(second_round, sent)]
-        + [(lambda v, j=j: pair_send(v, -j, pair), cotangent) for j in range(1, pair)],
-        1,
-    )
-    outer_next = got[1:]
+    got = steps.run([(second_round, sent)] + [(second_round, v) for v in outer_twos], 1)
+    outer_mines = [rows_joined(v, g) for v, g in zip(outer_twos, got[1:])]
     kept, sent = reduce_second(kept, got[0])
-    got = steps.run([(first_round, sent)] + [(first_round, shard) for shard in outer_next], 1)
-    outer_twos = [rows_joined(shard, g) for shard, g in zip(outer_next, got[1:])]
+    got = steps.run([(first_round, sent)] + [(twin_send, v) for v in outer_mines], 1)
+    outer_parts += [[a, b] for a, b in zip(outer_mines, got[1:])]
     hidden_mid = source + kept.astype(f32) + got[0].astype(f32)
     normed_own = rms_scale(hidden_mid, mlp_gain).astype(bf16)
 
     got = steps.run(
         [(first_round, normed_own)]
-        + [(lambda v, j=j: pair_send(v, -j, pair), normed_own) for j in range(1, pair)]
-        + [(second_round, v) for v in outer_twos],
+        + [(lambda v, j=j: pair_send(v, -j, pair), normed_own) for j in range(1, pair)],
         1,
     )
     two = rows_joined(normed_own, got[0])
-    normed_next = got[1:pair]
-    outer_mines = [rows_joined(v, g) for v, g in zip(outer_twos, got[pair:])]
-    got = steps.run(
-        [(second_round, two)]
-        + [(first_round, v) for v in normed_next]
-        + [(twin_send, v) for v in outer_mines],
-        1,
-    )
+    normed_next = got[1:]
+    got = steps.run([(second_round, two)] + [(first_round, v) for v in normed_next], 1)
     mine = rows_joined(two, got[0])
     twos = [rows_joined(v, g) for v, g in zip(normed_next, got[1:])]
-    outer_parts += [[a, b] for a, b in zip(outer_mines, got[1 + len(twos) :])]
     got = steps.run([(twin_send, mine)] + [(second_round, v) for v in twos], 1)
     normed_parts = [[mine, got[0]]]
     mines = [rows_joined(v, g) for v, g in zip(twos, got[1:])]
@@ -1237,7 +1262,7 @@
     outer_flat = [outer_parts[j][side] for j, side in keys]
 
     class PairTotal:
-        def __init__(self, rows_of, operands, count=4):
+        def __init__(self, rows_of, operands, count):
             self.rows_of, self.operands, self.count = rows_of, operands, count
             self.pieces, self.got, self.left = None, [], count * (pair_count - 1)
             self.jobs = [
@@ -1273,16 +1298,18 @@
                 rows_here[k % self.count] += value.astype(f32)
             return join([cell_sum(part).astype(bf16) for part in rows_here])
 
-    def side_total(side):
+    def side_total(side, count):
         return PairTotal(
-            lambda v, p: weight_grad(*v, p, pair_rows, side, local_units, 4),
+            lambda v, p: weight_grad(*v, p, pair_rows, side, local_units, count),
             (normed_flat, [results[k][1] for k in keys]),
+            count,
         )
 
-    gate, up = side_total(0), side_total(1)
+    gate, up = side_total(0, 4), side_total(1, 2)
     down = PairTotal(
-        lambda v, p: weight_grad(*v, p, unit, 0, width, 4),
+        lambda v, p: weight_grad(*v, p, unit, 0, width, 2),
         ([results[k][0] for k in keys], outer_flat),
+        2,
     )
 
     def shares_sent(total):
@@ -1315,10 +1342,10 @@
         if got:
             made.append(got[0])
             gate.pieces = made[0]
-    normed_grad = sum(sums[j] for j in range(pair))
-    mid_part, mlp_gain_grad = jax.vjp(rms_scale, hidden_mid, mlp_gain)[1](normed_grad)
-    hidden_grad = cotangent.astype(f32) + mid_part
-    branch_own = hidden_grad.astype(bf16)
+    branch_own, hidden_grad, mlp_gain_grad = norm_grad(
+        hidden_mid, cotangent, mlp_gain, [sums[j] for j in range(pair)]
+    )
+    mlp_gain_grad = mlp_gain_grad[0]
     branch_twins = branch_twins[::-1]
     got = steps.run(
         [
@@ -1355,22 +1382,17 @@
         [
             (attention_half(0), branch_grad[0]),
             (shares_sent, gate_total),
-            (
-                lambda v: sum(dot(half, branch, TN) for half, branch in zip(*v)).astype(bf16),
-                (attended, branch_grad),
-            ),
         ]
         + [(second_round, sent) for sent in branch_sent[:-1]],
-        2,
-    )
-    out_partial, *got = got
+        1,
+    )
     gate_share = shares(gate_total, gate_got)
     for j, value in enumerate(got):
         branch_kept[j], branch_sent[j] = reduce_second(branch_kept[j], value)
     (query_grad_other, kv_grad), gate_got, *branch_got = steps.run(
         [(attention_half(1, kv_grad), branch_grad[1]), (first_round, gate_share)]
         + [(first_round, sent) for sent in branch_sent],
-        2,
+        1,
     )
     gate_two = rows_joined(gate_share, gate_got)
     branch_sums = [
@@ -1403,8 +1425,15 @@
     (kv_next, up_got), *got = steps.run(
         [(send_then_share, (kv_piece(1), up_total))]
         + [(sends[k], kv_piece(k)) for k in range(2, fsdp_count)]
-        + [(second_round, gate_two)]
-    )
+        + [
+            (second_round, gate_two),
+            (
+                lambda v: sum(dot(half, branch, TN) for half, branch in zip(*v)).astype(bf16),
+                (attended, branch_grad),
+            ),
+        ]
+    )
+    out_partial = got.pop()
     kv_total = kv_piece(0).astype(f32) + kv_next.astype(f32)
     for value in got[:-1]:
         kv_total = kv_total + value.astype(f32)
@@ -1428,7 +1457,7 @@
             (lambda v, j=j: pair_send(v, j, pair), value.astype(bf16))
             for j, value in enumerate(branch_sums[1:], 1)
         ],
-        2,
+        1,
     )
     *qkv_grad, attn_mine, attn_other, head_gain_grad, attention_gain_grad = projected
     up_two = rows_joined(up_share, up_got)
@@ -1488,7 +1517,7 @@
             (lambda v: gather_place(0, 0, v, None), gate_two),
             gains_here.part(),
         ],
-        2,
+        1,
     )
     kept, sent = reduce_first(attn_mine, got[0])
     up_got = got[1]

time: 762 us -> 752 us (0.987)
    ppermute x8, waiting for transfers between devices: 26.3 us -> 13.4 us  [pair_send(): lax.ppermute(values, 'fsdp', [(i, i // pair * pair + (i % pair + step) %...]
    ppermute x38 -> x34, starting transfers between devices: 56.8 us -> 46.8 us  [fsdp_send(): lax.ppermute(values, 'fsdp', [(i, (i + step) % count) for i in range(coun...]
    ppermute x8, starting transfers between devices: 0.43 us -> 9.72 us  [pair_send(): lax.ppermute(values, 'fsdp', [(i, i // pair * pair + (i % pair + step) %...]
    ppermute x38 -> x34, waiting for transfers between devices: 221 us -> 229 us  [fsdp_send(): lax.ppermute(values, 'fsdp', [(i, (i + step) % count) for i in range(coun...]
    unnamed x405 -> x411, local copies, waits for them, and re-layouts: 51.3 us -> 46.6 us
    pallas_call x8 -> x10, Pallas kernels: 31.2 us -> 35.1 us  [place_units(): pl.pallas_call(functools.partial(place_units_kernel, block_at, unit, colu...]
    pallas_call x6 -> x5, Pallas kernels: 16 us -> 13.1 us  [the longest x4 10.8 us: place_rows(): pl.pallas_call(functools.partial(place_rows_kernel, 2 * n), grid_spec=plt...]
  transfers between devices with their start and end apart: 107 -> 103, of which waited for: 38 -> 39; matrix products, arithmetic and copies ran while one was open for 8% -> 9% of each run, Pallas kernels for 27% -> 28%
where the time goes in v4:
time: 752 us; the launch traced here: 745 us
  waiting for transfers between devices  263 us (35%)
  Pallas kernels  248 us (33%)
  starting transfers between devices  115 us (15%)
  local copies, waits for them, and re-layouts  71.6 us (10%)
  other arithmetic  30.5 us (4%)
  matrix products  13.2 us (2%)
    ppermute x34, waiting for transfers between devices, fsdp_send(): lax.ppermute(values, 'fsdp', [(i, (i + step) % count) for i in range(coun...  229 us
    ppermute x34, starting transfers between devices, fsdp_send(): lax.ppermute(values, 'fsdp', [(i, (i + step) % count) for i in range(coun...  46.8 us
    unnamed x411, local copies, waits for them, and re-layouts  46.6 us
    pallas_call x2, Pallas kernels, attention_grad(): pl.pallas_call(functools.partial(attention_grad_kernel, chunk, other), gr...  42 us
    ppermute x34, starting transfers between devices, round_send(): return lax.ppermute(values, 'ctx', pairs)  41.1 us
    pallas_call x10, Pallas kernels, place_units(): pl.pallas_call(functools.partial(place_units_kernel, block_at, unit, colu...  35.1 us
    pallas_call x4, Pallas kernels, feed(): pl.pallas_call(feed_kernel, grid=(tokens // rows,), in_specs=[by_row(widt...  32.8 us
    pallas_call x25, Pallas kernels, join(): pl.pallas_call(join_kernel, grid_spec=pltpu.PrefetchScalarGridSpec(num_sc...  31 us
  transfers between devices with their start and end apart: 103, of which 39 were waited for; matrix products, arithmetic and copies ran while one was open for 9% of the time, Pallas kernels for 28%

profile of v4, /device:TPU:0, one launch (start us, length us, event | category | flops | bytes accessed | tf_op | source)
XLA Modules:
  0.0 744.8 jit_solution(13183663986255412208)
XLA Ops:
  23.2 6.7 fusion.12
  41.5 9.5 %collective-permute-done.5.refs_3_ = bf16[512,384]{1,0:T(8,128)(2,1)} collective-permute-done((bf16[512,384]{1,0:T(8,128)(2,1)S(1)}, bf16[512,384]{1,0:T(8,128)(2,1)}, u32[]{:S(2)}, u32[]{:S(2)}) %collective-permute-start.5) | collective-permute-done | bytes 393248 | tf_op jit(solution)/shard_map/ppermute | solution.py:50
  59.6 10.1 %shard_map.179 = (f32[1024,384]{1,0:T(8,128)S(1)}, bf16[1024,256]{1,0:T(8,128)(2,1)S(1)}, bf16[1024,128]{1,0:T(8,128)(2,1)S(1)}) custom-call(s32[4]{0:T(128)S(1)} %pad_add_fusion.place_ref, bf16[512,2048]{1,0:T(8,128)(2,1)} %shard_map.178.even_ref, bf16[512,2048]{1,0:T(8,128)(2,1)} %collective-permute-done.4.odd_ref, f32[1024,256]{1,0:T(8,128)S(1)} %concatenate.36.angle_ref, ...), custom_call_target="tpu_custom_call" | custom-call | flops 1610612736 | bytes 8000000 | tf_op jit(solution)/shard_map/pallas_call | solution.py:322
  75.9 7.1 collective-permute-done.8.refs_1_
  88.3 7.0 collective-permute-done.12
  103.4 11.7 %all-to-all-done = bf16[8,256,256]{2,1,0:T(8,128)(2,1)} async-done(((bf16[8,256,256]{2,1,0:T(8,128)(2,1)}), bf16[8,256,256]{2,1,0:T(8,128)(2,1)}, u32[]{:S(2)}, u32[]{:S(2)}) %all-to-all-start) | async-done | bytes 1048608 | tf_op jit(solution)/shard_map/all_to_all | solution.py:966
  116.4 8.9 %collective-permute-done.14 = bf16[8,1,128,128]{3,2,1,0:T(8,128)(2,1)S(1)} collective-permute-done((bf16[8,1,128,128]{3,2,1,0:T(8,128)(2,1)S(1)}, bf16[8,1,128,128]{3,2,1,0:T(8,128)(2,1)S(1)}, u32[]{:S(2)}, u32[]{:S(2)}) %collective-permute-start.14) | collective-permute-done | bytes 262176 | tf_op jit(solution)/shard_map/ppermute | solution.py:50
  129.8 22.3 %shard_map.182 = (bf16[512,256]{1,0:T(8,128)(2,1)S(1)}, bf16[512,256]{1,0:T(8,128)(2,1)S(1)}, f32[8,1,512]{2,1,0:T(1,128)S(1)}) custom-call(s32[4]{0:T(128)S(1)} %pad_add_fusion.place_ref, bf16[1024,256]{1,0:T(8,128)(2,1)S(1)} %copy-done.152, bf16[4096,128]{1,0:T(8,128)(2,1)S(1)} %bitcast.99), custom_call_target="tpu_custom_call" | custom-call | flops 16000000000 | bytes 8000000 | tf_op jit(solution)/shard_map/pallas_call | solution.py:542
  157.8 13.6 %collective-permute-done.19.refs_4_ = bf16[64,2048]{1,0:T(8,128)(2,1)S(1)} collective-permute-done((bf16[64,2048]{1,0:T(8,128)(2,1)S(1)}, bf16[64,2048]{1,0:T(8,128)(2,1)S(1)}, u32[]{:S(2)}, u32[]{:S(2)}) %collective-permute-start.19) | collective-permute-done | bytes 262176 | tf_op jit(solution)/shard_map/ppermute | solution.py:50
  176.0 24.2 %collective-permute-done.22.refs_5_ = bf16[256,1024]{1,0:T(8,128)(2,1)S(1)} collective-permute-done((bf16[256,1024]{1,0:T(8,128)(2,1)S(1)}, bf16[256,1024]{1,0:T(8,128)(2,1)S(1)}, u32[]{:S(2)}, u32[]{:S(2)}) %collective-permute-start.22) | collective-permute-done | bytes 524320 | tf_op jit(solution)/shard_map/ppermute | solution.py:50
  203.0 14.0 %collective-permute-done.25.refs_5_ = bf16[64,2048]{1,0:T(8,128)(2,1)S(1)} collective-permute-done((bf16[64,2048]{1,0:T(8,128)(2,1)S(1)}, bf16[64,2048]{1,0:T(8,128)(2,1)S(1)}, u32[]{:S(2)}, u32[]{:S(2)}) %collective-permute-start.25) | collective-permute-done | bytes 262176 | tf_op jit(solution)/shard_map/ppermute | solution.py:50
  222.0 13.8 %collective-permute-done.28.refs_6_ = bf16[64,2048]{1,0:T(8,128)(2,1)S(1)} collective-permute-done((bf16[64,2048]{1,0:T(8,128)(2,1)S(1)}, bf16[64,2048]{1,0:T(8,128)(2,1)S(1)}, u32[]{:S(2)}, u32[]{:S(2)}) %collective-permute-start.28) | collective-permute-done | bytes 262176 | tf_op jit(solution)/shard_map/ppermute | solution.py:50
  243.2 21.9 %collective-permute-done.31.refs_6_ = bf16[256,1024]{1,0:T(8,128)(2,1)S(1)} collective-permute-done((bf16[256,1024]{1,0:T(8,128)(2,1)S(1)}, bf16[256,1024]{1,0:T(8,128)(2,1)S(1)}, u32[]{:S(2)}, u32[]{:S(2)}) %collective-permute-start.31) | collective-permute-done | bytes 524320 | tf_op jit(solution)/shard_map/ppermute | solution.py:50
  267.9 13.0 %collective-permute-done.34.refs_7_ = bf16[64,2048]{1,0:T(8,128)(2,1)S(1)} collective-permute-done((bf16[64,2048]{1,0:T(8,128)(2,1)S(1)}, bf16[64,2048]{1,0:T(8,128)(2,1)S(1)}, u32[]{:S(2)}, u32[]{:S(2)}) %collective-permute-start.34) | collective-permute-done | bytes 262176 | tf_op jit(solution)/shard_map/ppermute | solution.py:50
  295.5 16.0 %collective-permute-done.37.refs_7_ = bf16[256,1024]{1,0:T(8,128)(2,1)} collective-permute-done((bf16[256,1024]{1,0:T(8,128)(2,1)}, bf16[256,1024]{1,0:T(8,128)(2,1)}, u32[]{:S(2)}, u32[]{:S(2)}) %collective-permute-start.37) | collective-permute-done | bytes 524320 | tf_op jit(solution)/shard_map/ppermute | solution.py:50
  314.0 9.6 %shard_map.194 = (bf16[512,512]{1,0:T(8,128)(2,1)S(1)}, bf16[512,1024]{1,0:T(8,128)(2,1)S(1)}, bf16[512,2048]{1,0:T(8,128)(2,1)S(1)}, bf16[512,2048]{1,0:T(8,128)(2,1)}) custom-call(bf16[512,2048]{1,0:T(8,128)(2,1)} %collective-permute-done.38.normed_ref.refs_3_, bf16[512,2048]{1,0:T(8,128)(2,1)S(1)} %copy-done.36, ...), custom_call_target="tpu_custom_call" | custom-call | flops 6442450944 | bytes 16000000 | tf_op jit(solution)/shard_map/pallas_call | solution.py:679
  324.4 8.8 %shard_map.195 = (bf16[512,512]{1,0:T(8,128)(2,1)S(1)}, bf16[512,1024]{1,0:T(8,128)(2,1)S(1)}, bf16[512,2048]{1,0:T(8,128)(2,1)S(1)}, bf16[512,2048]{1,0:T(8,128)(2,1)S(1)}) custom-call(bf16[512,2048]{1,0:T(8,128)(2,1)} %shard_map.191.normed_ref.refs_2_, bf16[512,2048]{1,0:T(8,128)(2,1)S(1)} %copy-done.10, bf16[2048,1024]{1,0:T(8,128)(2,1)S(1)} %shard_map.192.weight_ref, ...), custom_call_target="tpu_custom_call" | custom-call | flops 6442450944 | bytes 16000000 | tf_op jit(solution)/shard_map/pallas_call | solution.py:679
  337.4 7.2 shard_map.197
  352.8 7.2 shard_map.199
  371.3 5.8 shard_map.201
  388.9 8.8 %collective-permute-done.46 = bf16[256,512]{1,0:T(8,128)(2,1)S(1)} collective-permute-done((bf16[256,512]{1,0:T(8,128)(2,1)S(1)}, bf16[256,512]{1,0:T(8,128)(2,1)S(1)}, u32[]{:S(2)}, u32[]{:S(2)}) %collective-permute-start.46) | collective-permute-done | bytes 262176 | tf_op jit(solution)/shard_map/ppermute | solution.py:50
  428.1 7.2 collective-permute-done.51
  460.5 19.4 %shard_map.212 = (f32[512,256]{1,0:T(8,128)S(1)}, f32[4096,128]{1,0:T(8,128)S(1)}) custom-call(s32[4]{0:T(128)S(1)} %pad_add_fusion.place_ref, bf16[1024,256]{1,0:T(8,128)(2,1)S(1)} %copy-done.153, bf16[512,2048]{1,0:T(8,128)(2,1)} %shard_map.210.branch_ref, bf16[512,256]{1,0:T(8,128)(2,1)S(1)} %copy-done.94, f32[8,1,512]{2,1,0:T(1,128)S(1)} %copy-done.165, ...), custom_call_target="tpu_custom_call" | custom-call | flops 17999998976 | bytes 12000000 | tf_op jit(solution)/shard_map/pallas_call | solution.py:619
  488.0 22.6 %shard_map.214 = (f32[512,256]{1,0:T(8,128)S(1)}, f32[4096,128]{1,0:T(8,128)S(1)}) custom-call(s32[4]{0:T(128)S(1)} %pad_add_fusion.place_ref, bf16[1024,256]{1,0:T(8,128)(2,1)S(1)} %copy-done.153, bf16[512,2048]{1,0:T(8,128)(2,1)} %collective-permute-done.54.branch_ref, bf16[512,256]{1,0:T(8,128)(2,1)S(1)} %copy-done.96, f32[8,1,512]{2,1,0:T(1,128)S(1)} %copy-done.165, ...), custom_call_target="tpu_custom_call" | custom-call | flops 17999998976 | bytes 12000000 | tf_op jit(solution)/shard_map/pallas_call | solution.py:619
  520.5 5.9 collective-permute-done.63
  526.4 8.8 %collective-permute-start.64 = (bf16[512,512]{1,0:T(8,128)(2,1)S(1)}, bf16[512,512]{1,0:T(8,128)(2,1)S(1)}, u32[]{:S(2)}, u32[]{:S(2)}) collective-permute-start(bf16[512,512]{1,0:T(8,128)(2,1)S(1)} %constant_dynamic-slice_fusion.7), channel_id=1, source_target_pairs={{0,1},{1,0},{2,3},{3,2},{4,5},{5,4},{6,7},{7,6},{8,9},{9,8},{10,11... | collective-permute-start | bytes 1572872 | tf_op jit(solution)/shard_map/ppermute | solution.py:55
  540.0 7.9 %collective-permute-done.64 = bf16[512,512]{1,0:T(8,128)(2,1)S(1)} collective-permute-done((bf16[512,512]{1,0:T(8,128)(2,1)S(1)}, bf16[512,512]{1,0:T(8,128)(2,1)S(1)}, u32[]{:S(2)}, u32[]{:S(2)}) %collective-permute-start.64) | collective-permute-done | bytes 524320 | tf_op jit(solution)/shard_map/ppermute | solution.py:55
  558.8 13.9 %shard_map.219 = (bf16[512,384]{1,0:T(8,128)(2,1)S(1)}, bf16[512,384]{1,0:T(8,128)(2,1)S(1)}, bf16[512,2048]{1,0:T(8,128)(2,1)}, bf16[512,2048]{1,0:T(8,128)(2,1...) custom-call(s32[4]{0:T(128)S(1)} %pad_add_fusion.place_ref, bf16[512,2048]{1,0:T(8,128)(2,1)} %shard_map.178.even_ref, ...), custom_call_target="tpu_custom_call" | custom-call | flops 1610612736 | bytes 12000000 | tf_op jit(solution)/shard_map/pallas_call | solution.py:436
  574.8 7.6 %collective-permute-done.68 = bf16[128,2048]{1,0:T(8,128)(2,1)} collective-permute-done((bf16[128,2048]{1,0:T(8,128)(2,1)}, bf16[128,2048]{1,0:T(8,128)(2,1)}, u32[]{:S(2)}, u32[]{:S(2)}) %collective-permute-start.68) | collective-permute-done | bytes 524320 | tf_op jit(solution)/shard_map/ppermute | solution.py:50
  603.7 10.7 %collective-permute-done.72 = bf16[128,2048]{1,0:T(8,128)(2,1)S(1)} collective-permute-done((bf16[128,2048]{1,0:T(8,128)(2,1)S(1)}, bf16[128,2048]{1,0:T(8,128)(2,1)S(1)}, u32[]{:S(2)}, u32[]{:S(2)}) %collective-permute-start.72) | collective-permute-done | bytes 524320 | tf_op jit(solution)/shard_map/ppermute | solution.py:50
  661.2 7.2 collective-permute-done.84
  668.3 7.9 %collective-permute-done.85 = bf16[512,256]{1,0:T(8,128)(2,1)S(1)} collective-permute-done((bf16[512,256]{1,0:T(8,128)(2,1)S(1)}, bf16[512,256]{1,0:T(8,128)(2,1)S(1)}, u32[]{:S(2)}, u32[]{:S(2)}) %collective-permute-start.85) | collective-permute-done | bytes 262176 | tf_op jit(solution)/shard_map/ppermute | solution.py:50
  (760 shorter events, 374.7 us)
Async XLA Ops:
  50.9 32.1 %collective-permute-start.6 = (bf16[256,1024]{1,0:T(8,128)(2,1)}, bf16[256,1024]{1,0:T(8,128)(2,1)S(1)}, u32[]{:S(2)}, u32[]{:S(2)}) collective-permute-start(bf16[256,1024]{1,0:T(8,128)(2,1)} %pad_maximum_fusion.5), channel_id=1, source_target_pairs={{0,1},{1,0},{2,3},{3,2},{4,5},{5,4},{6,7},{7,6},{8,9},{9,8},{10,11... | collective-permute-start | bytes 1572872 | tf_op jit(solution)/shard_map/ppermute | solution.py:55
  50.9 32.1 %collective-permute-start.7 = (bf16[128,2048]{1,0:T(8,128)(2,1)}, bf16[128,2048]{1,0:T(8,128)(2,1)S(1)}, u32[]{:S(2)}, u32[]{:S(2)}) collective-permute-start(bf16[128,2048]{1,0:T(8,128)(2,1)} %outer_ref.1), channel_id=1, source_target_pairs={{0,8},{4,20},{8,0},{12,28},{16,24},{20,4},{24,16},{28,12},{1,9},{5... | collective-permute-start | bytes 1572872 | tf_op jit(solution)/shard_map/ppermute | solution.py:78
  56.6 26.5 %collective-permute-start.8 = (bf16[512,256]{1,0:T(8,128)(2,1)}, bf16[512,256]{1,0:T(8,128)(2,1)S(1)}, u32[]{:S(2)}, u32[]{:S(2)}) collective-permute-start(bf16[512,256]{1,0:T(8,128)(2,1)} %constant_dynamic-slice_fusion.10.refs_0_), channel_id=1, source_target_pairs={{0,1},{1,2},{2,3},{3,0},{4,5},{5,6},{6,7},{7,4},{8,9},{9,10},{10,1... | collective-permute-start | bytes 786440 | tf_op jit(solution)/shard_map/ppermute | solution.py:50
  86.7 38.6 %collective-permute-start.15 = (bf16[256,2048]{1,0:T(8,128)(2,1)S(1)}, bf16[256,2048]{1,0:T(8,128)(2,1)S(1)}, u32[]{:S(2)}, u32[]{:S(2)}) collective-permute-start(bf16[256,2048]{1,0:T(8,128)(2,1)S(1)} %shard_map.181.refs_0_), channel_id=1, source_target_pairs={{0,16},{4,12},{8,24},{12,4},{16,0},{20,28},{24,8},{28,20},{1,17},{... | collective-permute-start | bytes 3145736 | tf_op jit(solution)/shard_map/ppermute | solution.py:78
  99.6 25.7 %collective-permute-start.11 = (bf16[256,1024]{1,0:T(8,128)(2,1)}, bf16[256,1024]{1,0:T(8,128)(2,1)}, u32[]{:S(2)}, u32[]{:S(2)}) collective-permute-start(bf16[256,1024]{1,0:T(8,128)(2,1)} %pad_maximum_fusion.6), channel_id=1, source_target_pairs={{0,1},{1,0},{2,3},{3,2},{4,5},{5,4},{6,7},{7,6},{8,9},{9,8},{10,11... | collective-permute-start | bytes 1572872 | tf_op jit(solution)/shard_map/ppermute | solution.py:55
  99.7 25.6 %collective-permute-start.14 = (bf16[8,1,128,128]{3,2,1,0:T(8,128)(2,1)S(1)}, bf16[8,1,128,128]{3,2,1,0:T(8,128)(2,1)S(1)}, u32[]{:S(2)}, u32[]{:S(2)}) collective-permute-start(bf16[8,1,128,128]{3,2,1,0:T(8,128)(2,1)S(1)} %bitcast.103), channel_id=1, source_target_pairs={{0,3},{1,0},{2,1},{3,2},{4,7},{5,4},{6,5},{7,6},{8,11},{9,8},{10,9... | collective-permute-start | bytes 786440 | tf_op jit(solution)/shard_map/ppermute | solution.py:50
  100.0 25.3 %collective-permute-start.13 = (bf16[8,1,128,128]{3,2,1,0:T(8,128)(2,1)S(1)}, bf16[8,1,128,128]{3,2,1,0:T(8,128)(2,1)}, u32[]{:S(2)}, u32[]{:S(2)}) collective-permute-start(bf16[8,1,128,128]{3,2,1,0:T(8,128)(2,1)S(1)} %bitcast.104), channel_id=1, source_target_pairs={{0,2},{1,3},{2,0},{3,1},{4,6},{5,7},{6,4},{7,5},{8,10},{9,11},{10,... | collective-permute-start | bytes 786440 | tf_op jit(solution)/shard_map/ppermute | solution.py:50
  126.8 27.6 %collective-permute-start.17 = (bf16[512,2048]{1,0:T(8,128)(2,1)S(1)}, bf16[512,2048]{1,0:T(8,128)(2,1)S(1)}, u32[]{:S(2)}, u32[]{:S(2)}) collective-permute-start(bf16[512,2048]{1,0:T(8,128)(2,1)S(1)} %shard_map.183.outer_ref.refs_4_), channel_id=1, source_target_pairs={{0,4},{4,0},{8,12},{12,8},{16,20},{20,16},{24,28},{28,24},{1,5},{5... | collective-permute-start | bytes 6291464 | tf_op jit(solution)/shard_map/ppermute | solution.py:40
  173.9 26.3 %collective-permute-start.24 = (bf16[256,2048]{1,0:T(8,128)(2,1)S(1)}, bf16[256,2048]{1,0:T(8,128)(2,1)S(1)}, u32[]{:S(2)}, u32[]{:S(2)}) collective-permute-start(bf16[256,2048]{1,0:T(8,128)(2,1)S(1)} %shard_map.185.refs_0_), channel_id=1, source_target_pairs={{0,16},{4,12},{8,24},{12,4},{16,0},{20,28},{24,8},{28,20},{1,17},{... | collective-permute-start | bytes 3145736 | tf_op jit(solution)/shard_map/ppermute | solution.py:78
  174.5 25.7 %collective-permute-start.23 = (bf16[256,2048]{1,0:T(8,128)(2,1)S(1)}, bf16[256,2048]{1,0:T(8,128)(2,1)S(1)}, u32[]{:S(2)}, u32[]{:S(2)}) collective-permute-start(bf16[256,2048]{1,0:T(8,128)(2,1)S(1)} %get-tuple-element.518), channel_id=1, source_target_pairs={{0,16},{4,12},{8,24},{12,4},{16,0},{20,28},{24,8},{28,20},{1,17},{... | collective-permute-start | bytes 3145736 | tf_op jit(solution)/shard_map/ppermute | solution.py:78
  238.7 26.5 %collective-permute-start.32 = (bf16[256,2048]{1,0:T(8,128)(2,1)S(1)}, bf16[256,2048]{1,0:T(8,128)(2,1)S(1)}, u32[]{:S(2)}, u32[]{:S(2)}) collective-permute-start(bf16[256,2048]{1,0:T(8,128)(2,1)S(1)} %shard_map.188.refs_0_), channel_id=1, source_target_pairs={{0,16},{4,12},{8,24},{12,4},{16,0},{20,28},{24,8},{28,20},{1,17},{... | collective-permute-start | bytes 3145736 | tf_op jit(solution)/shard_map/ppermute | solution.py:78
  240.3 24.9 %collective-permute-start.31 = (bf16[256,1024]{1,0:T(8,128)(2,1)S(1)}, bf16[256,1024]{1,0:T(8,128)(2,1)S(1)}, u32[]{:S(2)}, u32[]{:S(2)}) collective-permute-start(bf16[256,1024]{1,0:T(8,128)(2,1)S(1)} %copy-done.98), channel_id=1, source_target_pairs={{0,2},{1,3},{2,0},{3,1},{4,6},{5,7},{6,4},{7,5},{8,10},{9,11},{10,... | collective-permute-start | bytes 1572872 | tf_op jit(solution)/shard_map/ppermute | solution.py:50
  284.9 26.6 %collective-permute-start.38 = (bf16[512,2048]{1,0:T(8,128)(2,1)}, bf16[512,2048]{1,0:T(8,128)(2,1)}, u32[]{:S(2)}, u32[]{:S(2)}) collective-permute-start(bf16[512,2048]{1,0:T(8,128)(2,1)} %shard_map.191.normed_ref.refs_2_), channel_id=1, source_target_pairs={{0,4},{4,0},{8,12},{12,8},{16,20},{20,16},{24,28},{28,24},{1,5},{5... | collective-permute-start | bytes 6291464 | tf_op jit(solution)/shard_map/ppermute | solution.py:40
  284.9 26.5 %collective-permute-start.37 = (bf16[256,1024]{1,0:T(8,128)(2,1)}, bf16[256,1024]{1,0:T(8,128)(2,1)}, u32[]{:S(2)}, u32[]{:S(2)}) collective-permute-start(bf16[256,1024]{1,0:T(8,128)(2,1)} %collective-permute-done.11.refs_3_), channel_id=1, source_target_pairs={{0,2},{1,3},{2,0},{3,1},{4,6},{5,7},{6,4},{7,5},{8,10},{9,11},{10,... | collective-permute-start | bytes 1572872 | tf_op jit(solution)/shard_map/ppermute | solution.py:50
  457.3 24.7 %collective-permute-start.57 = (bf16[512,512]{1,0:T(8,128)(2,1)S(1)}, bf16[512,512]{1,0:T(8,128)(2,1)S(1)}, u32[]{:S(2)}, u32[]{:S(2)}) collective-permute-start(bf16[512,512]{1,0:T(8,128)(2,1)S(1)} %constant_dynamic-slice_fusion.9), channel_id=1, source_target_pairs={{0,1},{1,0},{2,3},{3,2},{4,5},{5,4},{6,7},{7,6},{8,9},{9,8},{10,11... | collective-permute-start | bytes 1572872 | tf_op jit(solution)/shard_map/ppermute | solution.py:55
  457.4 25.4 %collective-permute-start.56 = (bf16[512,512]{1,0:T(8,128)(2,1)S(1)}, bf16[512,512]{1,0:T(8,128)(2,1)S(1)}, u32[]{:S(2)}, u32[]{:S(2)}) collective-permute-start(bf16[512,512]{1,0:T(8,128)(2,1)S(1)} %copy-done.160), channel_id=1, source_target_pairs={{0,2},{1,3},{2,0},{3,1},{4,6},{5,7},{6,4},{7,5},{8,10},{9,11},{10,... | collective-permute-start | bytes 1572872 | tf_op jit(solution)/shard_map/ppermute | solution.py:50
  483.9 26.8 %collective-permute-start.59 = (bf16[512,512]{1,0:T(8,128)(2,1)S(1)}, bf16[512,512]{1,0:T(8,128)(2,1)S(1)}, u32[]{:S(2)}, u32[]{:S(2)}) collective-permute-start(bf16[512,512]{1,0:T(8,128)(2,1)S(1)} %copy-done.158), channel_id=1, source_target_pairs={{0,2},{1,3},{2,0},{3,1},{4,6},{5,7},{6,4},{7,5},{8,10},{9,11},{10,... | collective-permute-start | bytes 1572872 | tf_op jit(solution)/shard_map/ppermute | solution.py:50
  484.8 25.8 %collective-permute-start.62 = (bf16[128,2048]{1,0:T(8,128)(2,1)S(1)}, bf16[128,2048]{1,0:T(8,128)(2,1)S(1)}, u32[]{:S(2)}, u32[]{:S(2)}) collective-permute-start(bf16[128,2048]{1,0:T(8,128)(2,1)S(1)} %get-tuple-element.735), channel_id=1, source_target_pairs={{0,8},{4,20},{8,0},{12,28},{16,24},{20,4},{24,16},{28,12},{1,9},{5... | collective-permute-start | bytes 1572872 | tf_op jit(solution)/shard_map/ppermute | solution.py:78
  512.9 35.0 %collective-permute-start.67 = (bf16[1024,1024]{1,0:T(8,128)(2,1)}, bf16[1024,1024]{1,0:T(8,128)(2,1)S(1)}, u32[]{:S(2)}, u32[]{:S(2)}) collective-permute-start(bf16[1024,1024]{1,0:T(8,128)(2,1)} %shard_map.218.source_ref), channel_id=1, source_target_pairs={{0,16},{4,12},{8,24},{12,4},{16,0},{20,28},{24,8},{28,20},{1,17},{... | collective-permute-start | bytes 6291464 | tf_op jit(solution)/shard_map/ppermute | solution.py:78
  547.9 34.5 %collective-permute-start.69 = (bf16[1024,1024]{1,0:T(8,128)(2,1)}, bf16[1024,1024]{1,0:T(8,128)(2,1)}, u32[]{:S(2)}, u32[]{:S(2)}) collective-permute-start(bf16[1024,1024]{1,0:T(8,128)(2,1)} %shard_map.218.source_ref), channel_id=1, source_target_pairs={{0,4},{4,0},{8,12},{12,8},{16,20},{20,16},{24,28},{28,24},{1,5},{5... | collective-permute-start | bytes 6291464 | tf_op jit(solution)/shard_map/ppermute | solution.py:40
  548.1 34.3 %collective-permute-start.70 = (bf16[512,1024]{1,0:T(8,128)(2,1)S(1)}, bf16[512,1024]{1,0:T(8,128)(2,1)}, u32[]{:S(2)}, u32[]{:S(2)}) collective-permute-start(bf16[512,1024]{1,0:T(8,128)(2,1)S(1)} %pad_maximum_fusion.2.refs_0_), channel_id=1, source_target_pairs={{0,8},{4,20},{8,0},{12,28},{16,24},{20,4},{24,16},{28,12},{1,9},{5... | collective-permute-start | bytes 3145736 | tf_op jit(solution)/shard_map/ppermute | solution.py:78
  550.2 32.2 %all-to-all-start.1 = ((bf16[256,8,256]{2,0,1:T(8,128)(2,1)}), bf16[256,8,256]{2,0,1:T(8,128)(2,1)}, u32[]{:S(2)}, u32[]{:S(2)}) async-start(bf16[256,8,256]{2,0,1:T(8,128)(2,1)} %bitcast.109), calls=%async_computation.1 | async-start | bytes 2097152 | tf_op jit(solution)/shard_map/all_to_all | solution.py:966
  556.0 26.4 %collective-permute-start.68 = (bf16[128,2048]{1,0:T(8,128)(2,1)}, bf16[128,2048]{1,0:T(8,128)(2,1)}, u32[]{:S(2)}, u32[]{:S(2)}) collective-permute-start(bf16[128,2048]{1,0:T(8,128)(2,1)} %copy-done.156), channel_id=1, source_target_pairs={{0,2},{1,3},{2,0},{3,1},{4,6},{5,7},{6,4},{7,5},{8,10},{9,11},{10,... | collective-permute-start | bytes 1572872 | tf_op jit(solution)/shard_map/ppermute | solution.py:50
  556.7 25.7 %collective-permute-start.71 = (bf16[128,2048]{1,0:T(8,128)(2,1)S(1)}, bf16[128,2048]{1,0:T(8,128)(2,1)}, u32[]{:S(2)}, u32[]{:S(2)}) collective-permute-start(bf16[128,2048]{1,0:T(8,128)(2,1)S(1)} %add_convert_fusion.4), channel_id=1, source_target_pairs={{0,1},{1,0},{2,3},{3,2},{4,5},{5,4},{6,7},{7,6},{8,9},{9,8},{10,11... | collective-permute-start | bytes 1572872 | tf_op jit(solution)/shard_map/ppermute | solution.py:55
  584.7 29.7 %collective-permute-start.73 = (bf16[512,2048]{1,0:T(8,128)(2,1)S(1)}, bf16[512,2048]{1,0:T(8,128)(2,1)S(1)}, u32[]{:S(2)}, u32[]{:S(2)}) collective-permute-start(bf16[512,2048]{1,0:T(8,128)(2,1)S(1)} %copy-done.202), channel_id=1, source_target_pairs={{0,4},{4,0},{8,12},{12,8},{16,20},{20,16},{24,28},{28,24},{1,5},{5... | collective-permute-start | bytes 6291464 | tf_op jit(solution)/shard_map/ppermute | solution.py:40
  584.9 29.5 %collective-permute-start.74 = (bf16[1024,1024]{1,0:T(8,128)(2,1)S(1)}, bf16[1024,1024]{1,0:T(8,128)(2,1)}, u32[]{:S(2)}, u32[]{:S(2)}) collective-permute-start(bf16[1024,1024]{1,0:T(8,128)(2,1)S(1)} %shard_map.220.source_ref), channel_id=1, source_target_pairs={{0,16},{4,12},{8,24},{12,4},{16,0},{20,28},{24,8},{28,20},{1,17},{... | collective-permute-start | bytes 6291464 | tf_op jit(solution)/shard_map/ppermute | solution.py:78
  588.2 26.2 %collective-permute-start.72 = (bf16[128,2048]{1,0:T(8,128)(2,1)S(1)}, bf16[128,2048]{1,0:T(8,128)(2,1)S(1)}, u32[]{:S(2)}, u32[]{:S(2)}) collective-permute-start(bf16[128,2048]{1,0:T(8,128)(2,1)S(1)} %copy-done.155), channel_id=1, source_target_pairs={{0,2},{1,3},{2,0},{3,1},{4,6},{5,7},{6,4},{7,5},{8,10},{9,11},{10,... | collective-permute-start | bytes 1572872 | tf_op jit(solution)/shard_map/ppermute | solution.py:50
  614.4 30.3 %collective-permute-start.78 = (bf16[1024,1024]{1,0:T(8,128)(2,1)S(1)}, bf16[1024,1024]{1,0:T(8,128)(2,1)}, u32[]{:S(2)}, u32[]{:S(2)}) collective-permute-start(bf16[1024,1024]{1,0:T(8,128)(2,1)S(1)} %copy-done.42), channel_id=1, source_target_pairs={{0,4},{4,0},{8,12},{12,8},{16,20},{20,16},{24,28},{28,24},{1,5},{5... | collective-permute-start | bytes 6291464 | tf_op jit(solution)/shard_map/ppermute | solution.py:40
  619.0 25.6 %collective-permute-start.77 = (bf16[256,2048]{1,0:T(8,128)(2,1)S(1)}, bf16[256,2048]{1,0:T(8,128)(2,1)}, u32[]{:S(2)}, u32[]{:S(2)}) collective-permute-start(bf16[256,2048]{1,0:T(8,128)(2,1)S(1)} %shard_map.224.refs_0_), channel_id=1, source_target_pairs={{0,8},{4,20},{8,0},{12,28},{16,24},{20,4},{24,16},{28,12},{1,9},{5... | collective-permute-start | bytes 3145736 | tf_op jit(solution)/shard_map/ppermute | solution.py:78
  646.7 31.7 %collective-permute-start.82 = (bf16[512,2048]{1,0:T(8,128)(2,1)S(1)}, bf16[512,2048]{1,0:T(8,128)(2,1)S(1)}, u32[]{:S(2)}, u32[]{:S(2)}) collective-permute-start(bf16[512,2048]{1,0:T(8,128)(2,1)S(1)} %shard_map.228.source_ref), channel_id=1, source_target_pairs={{0,16},{4,12},{8,24},{12,4},{16,0},{20,28},{24,8},{28,20},{1,17},{... | collective-permute-start | bytes 6291464 | tf_op jit(solution)/shard_map/ppermute | solution.py:78
  649.8 26.4 %collective-permute-start.81 = (bf16[128,2048]{1,0:T(8,128)(2,1)S(1)}, bf16[128,2048]{1,0:T(8,128)(2,1)S(1)}, u32[]{:S(2)}, u32[]{:S(2)}) collective-permute-start(bf16[128,2048]{1,0:T(8,128)(2,1)S(1)} %get-tuple-element.822), channel_id=1, source_target_pairs={{0,8},{4,20},{8,0},{12,28},{16,24},{20,4},{24,16},{28,12},{1,9},{5... | collective-permute-start | bytes 1572872 | tf_op jit(solution)/shard_map/ppermute | solution.py:78
  651.0 25.3 %collective-permute-start.83 = (bf16[512,384]{1,0:T(8,128)(2,1)S(1)}, bf16[512,384]{1,0:T(8,128)(2,1)S(1)}, u32[]{:S(2)}, u32[]{:S(2)}) collective-permute-start(bf16[512,384]{1,0:T(8,128)(2,1)S(1)} %get-tuple-element.829), channel_id=1, source_target_pairs={{0,2},{1,3},{2,0},{3,1},{4,6},{5,7},{6,4},{7,5},{8,10},{9,11},{10,... | collective-permute-start | bytes 1179656 | tf_op jit(solution)/shard_map/ppermute | solution.py:50
  (276 other events, 2508.4 us)

commit v5 on v4

--- a/solution.py
+++ b/solution.py
@@ -846,30 +846,27 @@
         copy.wait()
 
 
-def place_rows(quarters, place):
-    whole = None
-    rows, columns = quarters[0].shape[0] // 2, quarters[0].shape[1]
-    for n, quarter in enumerate(quarters):
-        extra = [] if whole is None else [whole]
-        whole = pl.pallas_call(
-            functools.partial(place_rows_kernel, 2 * n),
-            grid_spec=pltpu.PrefetchScalarGridSpec(
-                num_scalar_prefetch=1,
-                grid=(1,),
-                in_specs=[pl.BlockSpec(quarter.shape, lambda i, at: (0, 0))]
-                + [pl.BlockSpec(memory_space=pl.ANY)] * len(extra),
-                out_specs=pl.BlockSpec(memory_space=pl.ANY),
-                scratch_shapes=[
-                    pltpu.VMEM((2, rows, columns), f32),
-                    pltpu.SemaphoreType.DMA((2,)),
-                ],
-            ),
-            out_shape=jax.ShapeDtypeStruct((CELL * rows, columns), f32),
-            input_output_aliases={2: 0} if extra else {},
-            compiler_params=vmem(16),
-            cost_estimate=cost(0, 6 * quarter.size),
-        )(place, quarter, *extra)
-    return whole
+def place_rows(whole, slot, quarter, place):
+    rows, columns = quarter.shape[0] // 2, quarter.shape[1]
+    extra = [] if whole is None else [whole]
+    return pl.pallas_call(
+        functools.partial(place_rows_kernel, slot),
+        grid_spec=pltpu.PrefetchScalarGridSpec(
+            num_scalar_prefetch=1,
+            grid=(1,),
+            in_specs=[pl.BlockSpec(quarter.shape, lambda i, at: (0, 0))]
+            + [pl.BlockSpec(memory_space=pl.ANY)] * len(extra),
+            out_specs=pl.BlockSpec(memory_space=pl.ANY),
+            scratch_shapes=[
+                pltpu.VMEM((2, rows, columns), f32),
+                pltpu.SemaphoreType.DMA((2,)),
+            ],
+        ),
+        out_shape=jax.ShapeDtypeStruct((CELL * rows, columns), f32),
+        input_output_aliases={2: 0} if extra else {},
+        compiler_params=vmem(16),
+        cost_estimate=cost(0, 6 * quarter.size),
+    )(place, quarter, *extra)
 
 
 def place_heads_kernel(place_ref, even_ref, odd_ref, out_ref):
@@ -1011,14 +1008,17 @@
     local_units = pair_count * unit
     pair_rows = pair * weight_rows
 
-    def owner_columns(weight, owner):
+    def half_columns(weight, owner, n):
+        size = weight_rows // 2
         return jnp.concatenate(
             [
-                lax.dynamic_slice_in_dim(
+                lax.dynamic_slice(
                     weight,
-                    side * hidden_width + ((p * pair + owner) * CELL + head) * unit,
-                    unit,
-                    1,
+                    (
+                        n * size,
+                        side * hidden_width + ((p * pair + owner) * CELL + head) * unit,
+                    ),
+                    (size, unit),
                 )
                 for side in range(2)
                 for p in range(pair_count)
@@ -1031,10 +1031,6 @@
 
     pair_jobs, down_jobs, own_jobs, mate_jobs = [], [], [], []
     gate_up_parts, down_parts = [], []
-
-    def half_columns(weight, owner, n):
-        size = weight_rows // 2
-        return owner_columns(lax.slice_in_dim(weight, n * size, (n + 1) * size), owner)
 
     def cross_job(read, step, row):
         return (
@@ -1485,23 +1481,26 @@
             ),
         )
 
-    def placing(side, parts):
+    def placing(parts):
         def place_all(v):
             whole, arrays = v
-            for (slot, _), array in zip(parts, arrays):
+            for (side, slot, _), array in zip(parts, arrays):
                 whole = gather_place(side, slot, array, whole)
             return whole
 
-        return place_all, (grad_gate_up, [part for _, part in parts])
-
-    def fsdp_sum(values, got):
-        total = fsdp_piece(values, 0).astype(f32)
+        return place_all, (grad_gate_up, [part for _, _, part in parts])
+
+    def fsdp_sum(pieces, got):
+        total = pieces[0].astype(f32)
         for value in got:
             total = total + value.astype(f32)
         return cell_sum(total).astype(bf16)
 
-    def sent_pieces(values, distances):
-        return [(sends[k], fsdp_piece(values, k)) for k in distances]
+    def sent_pieces(pieces, distances):
+        return [(sends[k], pieces[k]) for k in distances]
+
+    def all_pieces(values):
+        return [fsdp_piece(values, k) for k in range(fsdp_count)]
 
     odd_steps, even_steps = range(1, fsdp_count, 2), range(2, fsdp_count, 2)
     grad_gate_up = None
@@ -1509,10 +1508,14 @@
         [
             (twin_send, attn_other),
             (second_round, up_two),
+            (twin_send, up_two),
             (
-                lambda v: sum(dot(half, grad, TN) for half, grad in zip(*v)).astype(bf16),
+                lambda v: all_pieces(
+                    sum(dot(half, grad, TN) for half, grad in zip(*v)).astype(bf16)
+                ),
                 (normed_attn, qkv_grad),
             ),
+            (all_pieces, out_partial),
             down.own(),
             (lambda v: gather_place(0, 0, v, None), gate_two),
             gains_here.part(),
@@ -1520,8 +1523,8 @@
         1,
     )
     kept, sent = reduce_first(attn_mine, got[0])
-    up_got = got[1]
-    qkv_partial, down_own_rows, grad_gate_up, gain_got = got[2:]
+    up_got, up_two_twin = got[1:3]
+    qkv_parts, out_parts, down_own_rows, grad_gate_up, gain_got = got[3:]
     gains_here.add(gain_got)
     down_share = down.total(down_own_rows)
     got = steps.run(
@@ -1529,9 +1532,9 @@
             (second_round, sent),
             (first_round, down_share),
             (twin_send, gate_got),
-            placing(0, [(4, gate_two_twin), (2, gate_got)]),
+            placing([(0, 4, gate_two_twin), (0, 2, gate_got), (1, 0, up_two)]),
         ]
-        + sent_pieces(qkv_partial, odd_steps)
+        + sent_pieces(qkv_parts, odd_steps)
     )
     kept, sent = reduce_second(kept, got[0])
     down_two = rows_joined(down_share, got[1])
@@ -1542,80 +1545,76 @@
         [
             (first_round, sent),
             (second_round, down_two),
-            placing(0, [(6, gate_got_twin)]),
+            placing([(0, 6, gate_got_twin), (1, 2, up_got), (1, 4, up_two_twin)]),
+            (
+                lambda v: sum([g.astype(f32) for g in v[1:]], v[0]).astype(bf16),
+                [outputs] + branch_got,
+            ),
         ]
-        + sent_pieces(qkv_partial, even_steps)
-        + sent_pieces(out_partial, odd_steps)
+        + sent_pieces(qkv_parts, even_steps)
+        + sent_pieces(out_parts, odd_steps)
     )
     attn_normed_grad = kept.astype(f32) + got[0].astype(f32)
     down_got = got[1]
     grad_gate_up = got[2]
-    qkv_share = fsdp_sum(qkv_partial, qkv_got + got[3 : 3 + len(even_steps)])
-    out_got = got[3 + len(even_steps) :]
+    outputs = got[3]
+    qkv_share = fsdp_sum(qkv_parts, qkv_got + got[4 : 4 + len(even_steps)])
+    out_got = got[4 + len(even_steps) :]
     got = steps.run(
         [
             (first_round, qkv_share),
-            (twin_send, up_two),
             (twin_send, up_got),
-            placing(1, [(0, up_two), (2, up_got)]),
+            (twin_send, down_two),
+            (lambda v: place_rows(place_rows(None, 0, v[0], place), 2, v[1], place), (down_two, down_got)),
             gains_here.part(),
-        ]
-        + sent_pieces(out_partial, even_steps)
-    )
-    qkv_two = rows_joined(qkv_share, got[0])
-    up_two_twin, up_got_twin, grad_gate_up = got[1:4]
-    gains_here.add(got[4])
-    out_share = fsdp_sum(out_partial, out_got + got[5:])
-    got = steps.run(
-        [
-            (second_round, qkv_two),
-            (first_round, out_share),
-            (twin_send, down_two),
-            (twin_send, down_got),
-            placing(1, [(4, up_two_twin), (6, up_got_twin)]),
             (
                 lambda v: (
                     v[1] + jax.vjp(lambda u: rms_scale(u, attention_gain), source)[1](v[0])[0]
                 ).astype(bf16),
                 (attn_normed_grad, hidden_grad),
             ),
+        ]
+        + sent_pieces(out_parts, even_steps)
+    )
+    qkv_two = rows_joined(qkv_share, got[0])
+    up_got_twin, down_two_twin, grad_down, gain_got, grad_inputs = got[1:6]
+    gains_here.add(gain_got)
+    out_share = fsdp_sum(out_parts, out_got + got[6:])
+    got = steps.run(
+        [
+            (second_round, qkv_two),
+            (first_round, out_share),
+            (twin_send, down_got),
+            placing([(1, 6, up_got_twin)]),
+            (lambda v: place_rows(v[0], 4, v[1], place), (grad_down, down_two_twin)),
             gains_here.part(),
-            (
-                lambda v: sum([g.astype(f32) for g in v[1:]], v[0]).astype(bf16),
-                [outputs] + branch_got,
-            ),
         ]
     )
     qkv_half = rows_joined(qkv_two, got[0])
     out_two = rows_joined(out_share, got[1])
-    down_two_twin, down_got_twin, grad_gate_up, grad_inputs, gain_got, outputs = got[2:]
+    down_got_twin, grad_gate_up, grad_down, gain_got = got[2:]
     gains_here.add(gain_got)
     got = steps.run(
         [
-            gains_here.part(),
             (second_round, out_two),
             (twin_send, qkv_half),
-            (
-                lambda v: place_rows(v, place),
-                [down_two, down_got, down_two_twin, down_got_twin],
-            ),
+            (lambda v: place_rows(v[0], 6, v[1], place), (grad_down, down_got_twin)),
+            gains_here.part(),
         ]
     )
-    gains_here.add(got[0])
-    got = got[1:]
     out_half = rows_joined(out_two, got[0])
-    grad_down = got[2]
+    qkv_other, grad_down, gain_got = got[1:]
+    gains_here.add(gain_got)
     got = steps.run(
         [
+            (twin_send, out_half),
             gains_here.part(),
-            (twin_send, out_half),
-            (lambda v: place_heads(v, place), (qkv_half, got[1])),
+            (lambda v: place_heads(v, place), (qkv_half, qkv_other)),
         ]
     )
-    gains_here.add(got[0])
+    gains_here.add(got[1])
     gain_sums = gains_here.finish().reshape(-1)
-    got = got[1:]
-    grad_qkv = got[1]
+    grad_qkv = got[2]
     grad_out = place_columns((out_half, got[0]), width // CELL, place)
     attention_gain_sum, mlp_gain_sum = gain_sums[:width], gain_sums[width : 2 * width]
     head_sums = gain_sums[2 * width :].reshape(4, HEAD_DIM)

time: 752 us -> 746 us (level)
  waiting for transfers between devices: 263 us -> 280 us
  starting transfers between devices: 115 us -> 102 us
    ppermute x34, waiting for transfers between devices: 9.29 us -> 22 us  [round_send(): return lax.ppermute(values, 'ctx', pairs)]
    unnamed x411 -> x363, local copies, waits for them, and re-layouts: 46.6 us -> 54.8 us
    ppermute x8, starting transfers between devices: 9.72 us -> 1.55 us  [pair_send(): lax.ppermute(values, 'fsdp', [(i, i // pair * pair + (i % pair + step) %...]
  transfers between devices with their start and end apart: 103 -> 103, of which waited for: 39 -> 42; matrix products, arithmetic and copies ran while one was open for 9% -> 6% of each run, Pallas kernels for 28% -> 28%
where the time goes in v5:
time: 746 us; the launch traced here: 739 us
  waiting for transfers between devices  280 us (38%)
  Pallas kernels  245 us (33%)
  starting transfers between devices  102 us (14%)
  local copies, waits for them, and re-layouts  73.6 us (10%)
  other arithmetic  23.9 us (3%)
  matrix products  9.86 us (1%)
    ppermute x34, waiting for transfers between devices, fsdp_send(): lax.ppermute(values, 'fsdp', [(i, (i + step) % count) for i in range(coun...  224 us
    unnamed x363, local copies, waits for them, and re-layouts  54.8 us
    ppermute x34, starting transfers between devices, fsdp_send(): lax.ppermute(values, 'fsdp', [(i, (i + step) % count) for i in range(coun...  46.8 us
    pallas_call x2, Pallas kernels, attention_grad(): pl.pallas_call(functools.partial(attention_grad_kernel, chunk, other), gr...  42 us
    ppermute x34, starting transfers between devices, round_send(): return lax.ppermute(values, 'ctx', pairs)  40.8 us
    pallas_call x4, Pallas kernels, feed(): pl.pallas_call(feed_kernel, grid=(tokens // rows,), in_specs=[by_row(widt...  32.9 us
    pallas_call x25, Pallas kernels, join(): pl.pallas_call(join_kernel, grid_spec=pltpu.PrefetchScalarGridSpec(num_sc...  32.3 us
    pallas_call x10, Pallas kernels, place_units(): pl.pallas_call(functools.partial(place_units_kernel, block_at, unit, colu...  31.4 us
  transfers between devices with their start and end apart: 103, of which 42 were waited for; matrix products, arithmetic and copies ran while one was open for 6% of the time, Pallas kernels for 28%

profile of v5, /device:TPU:0, one launch (start us, length us, event | category | flops | bytes accessed | tf_op | source)
XLA Modules:
  0.0 738.8 jit_solution(15122635887014095275)
XLA Ops:
  30.7 10.3 %collective-permute-done.3.refs_2_ = bf16[512,384]{1,0:T(8,128)(2,1)S(1)} collective-permute-done((bf16[512,384]{1,0:T(8,128)(2,1)S(1)}, bf16[512,384]{1,0:T(8,128)(2,1)S(1)}, u32[]{:S(2)}, u32[]{:S(2)}) %collective-permute-start.3) | collective-permute-done | bytes 393248 | tf_op jit(solution)/shard_map/ppermute | solution.py:50
  47.5 8.7 %collective-permute-done.5.refs_3_ = bf16[512,384]{1,0:T(8,128)(2,1)S(1)} collective-permute-done((bf16[512,384]{1,0:T(8,128)(2,1)S(1)}, bf16[512,384]{1,0:T(8,128)(2,1)S(1)}, u32[]{:S(2)}, u32[]{:S(2)}) %collective-permute-start.5) | collective-permute-done | bytes 393248 | tf_op jit(solution)/shard_map/ppermute | solution.py:50
  70.9 10.4 %shard_map.179 = (f32[1024,384]{1,0:T(8,128)S(1)}, bf16[1024,256]{1,0:T(8,128)(2,1)S(1)}, bf16[1024,128]{1,0:T(8,128)(2,1)}) custom-call(s32[4]{0:T(128)S(1)} %pad_add_fusion.place_ref, bf16[512,2048]{1,0:T(8,128)(2,1)S(1)} %copy-done.3, bf16[512,2048]{1,0:T(8,128)(2,1)S(1)} %copy-done.10, f32[1024,256]{1,0:T(8,128)S(1)} %concatenate.36.angle_ref, ...), custom_call_target="tpu_custom_call" | custom-call | flops 1610612736 | bytes 8000000 | tf_op jit(solution)/shard_map/pallas_call | solution.py:322
  81.3 7.7 %collective-permute-done.10.refs_3_ = bf16[512,256]{1,0:T(8,128)(2,1)S(1)} collective-permute-done((bf16[512,256]{1,0:T(8,128)(2,1)}, bf16[512,256]{1,0:T(8,128)(2,1)S(1)}, u32[]{:S(2)}, u32[]{:S(2)}) %collective-permute-start.10) | collective-permute-done | bytes 262176 | tf_op jit(solution)/shard_map/ppermute | solution.py:50
  108.8 13.0 %all-to-all-done = bf16[8,256,256]{2,1,0:T(8,128)(2,1)S(1)} async-done(((bf16[8,256,256]{2,1,0:T(8,128)(2,1)}), bf16[8,256,256]{2,1,0:T(8,128)(2,1)S(1)}, u32[]{:S(2)}, u32[]{:S(2)}) %all-to-all-start) | async-done | bytes 1048608 | tf_op jit(solution)/shard_map/all_to_all | solution.py:963
  124.1 5.8 collective-permute-done.14
  135.5 22.3 %shard_map.182 = (bf16[512,256]{1,0:T(8,128)(2,1)S(1)}, bf16[512,256]{1,0:T(8,128)(2,1)S(1)}, f32[8,1,512]{2,1,0:T(1,128)S(1)}) custom-call(s32[4]{0:T(128)S(1)} %pad_add_fusion.place_ref, bf16[1024,256]{1,0:T(8,128)(2,1)S(1)} %copy-done.143, bf16[4096,128]{1,0:T(8,128)(2,1)S(1)} %bitcast.99), custom_call_target="tpu_custom_call" | custom-call | flops 16000000000 | bytes 8000000 | tf_op jit(solution)/shard_map/pallas_call | solution.py:542
  162.7 13.7 %collective-permute-done.19.refs_4_ = bf16[64,2048]{1,0:T(8,128)(2,1)S(1)} collective-permute-done((bf16[64,2048]{1,0:T(8,128)(2,1)S(1)}, bf16[64,2048]{1,0:T(8,128)(2,1)S(1)}, u32[]{:S(2)}, u32[]{:S(2)}) %collective-permute-start.19) | collective-permute-done | bytes 262176 | tf_op jit(solution)/shard_map/ppermute | solution.py:50
  181.1 24.1 %collective-permute-done.22.refs_5_ = bf16[256,1024]{1,0:T(8,128)(2,1)S(1)} collective-permute-done((bf16[256,1024]{1,0:T(8,128)(2,1)S(1)}, bf16[256,1024]{1,0:T(8,128)(2,1)S(1)}, u32[]{:S(2)}, u32[]{:S(2)}) %collective-permute-start.22) | collective-permute-done | bytes 524320 | tf_op jit(solution)/shard_map/ppermute | solution.py:50
  208.0 13.8 %collective-permute-done.25.refs_5_ = bf16[64,2048]{1,0:T(8,128)(2,1)S(1)} collective-permute-done((bf16[64,2048]{1,0:T(8,128)(2,1)S(1)}, bf16[64,2048]{1,0:T(8,128)(2,1)S(1)}, u32[]{:S(2)}, u32[]{:S(2)}) %collective-permute-start.25) | collective-permute-done | bytes 262176 | tf_op jit(solution)/shard_map/ppermute | solution.py:50
  226.8 15.0 %collective-permute-done.28.refs_6_ = bf16[64,2048]{1,0:T(8,128)(2,1)S(1)} collective-permute-done((bf16[64,2048]{1,0:T(8,128)(2,1)S(1)}, bf16[64,2048]{1,0:T(8,128)(2,1)S(1)}, u32[]{:S(2)}, u32[]{:S(2)}) %collective-permute-start.28) | collective-permute-done | bytes 262176 | tf_op jit(solution)/shard_map/ppermute | solution.py:50
  248.0 12.0 %collective-permute-done.33.refs_1_ = bf16[128,2048]{1,0:T(8,128)(2,1)S(1)} collective-permute-done((bf16[128,2048]{1,0:T(8,128)(2,1)S(1)}, bf16[128,2048]{1,0:T(8,128)(2,1)S(1)}, u32[]{:S(2)}, u32[]{:S(2)}) %collective-permute-start.33) | collective-permute-done | bytes 524320 | tf_op jit(solution)/shard_map/ppermute | solution.py:78
  260.0 11.3 %collective-permute-done.31.refs_6_ = bf16[256,1024]{1,0:T(8,128)(2,1)S(1)} collective-permute-done((bf16[256,1024]{1,0:T(8,128)(2,1)}, bf16[256,1024]{1,0:T(8,128)(2,1)S(1)}, u32[]{:S(2)}, u32[]{:S(2)}) %collective-permute-start.31) | collective-permute-done | bytes 524320 | tf_op jit(solution)/shard_map/ppermute | solution.py:50
  275.3 12.7 %collective-permute-done.34.refs_7_ = bf16[64,2048]{1,0:T(8,128)(2,1)S(1)} collective-permute-done((bf16[64,2048]{1,0:T(8,128)(2,1)S(1)}, bf16[64,2048]{1,0:T(8,128)(2,1)S(1)}, u32[]{:S(2)}, u32[]{:S(2)}) %collective-permute-start.34) | collective-permute-done | bytes 262176 | tf_op jit(solution)/shard_map/ppermute | solution.py:50
  302.8 15.6 %collective-permute-done.37.refs_7_ = bf16[256,1024]{1,0:T(8,128)(2,1)} collective-permute-done((bf16[256,1024]{1,0:T(8,128)(2,1)}, bf16[256,1024]{1,0:T(8,128)(2,1)}, u32[]{:S(2)}, u32[]{:S(2)}) %collective-permute-start.37) | collective-permute-done | bytes 524320 | tf_op jit(solution)/shard_map/ppermute | solution.py:50
  321.1 9.6 %shard_map.194 = (bf16[512,512]{1,0:T(8,128)(2,1)S(1)}, bf16[512,1024]{1,0:T(8,128)(2,1)S(1)}, bf16[512,2048]{1,0:T(8,128)(2,1)S(1)}, bf16[512,2048]{1,0:T(8,128)(2,1)}) custom-call(bf16[512,2048]{1,0:T(8,128)(2,1)} %collective-permute-done.38.normed_ref.refs_3_, bf16[512,2048]{1,0:T(8,128)(2,1)S(1)} %copy-done.43, ...), custom_call_target="tpu_custom_call" | custom-call | flops 6442450944 | bytes 16000000 | tf_op jit(solution)/shard_map/pallas_call | solution.py:679
  331.6 8.8 %shard_map.195 = (bf16[512,512]{1,0:T(8,128)(2,1)S(1)}, bf16[512,1024]{1,0:T(8,128)(2,1)S(1)}, bf16[512,2048]{1,0:T(8,128)(2,1)S(1)}, bf16[512,2048]{1,0:T(8,128)(2,1)S(1)}) custom-call(bf16[512,2048]{1,0:T(8,128)(2,1)} %shard_map.191.normed_ref.refs_2_, bf16[512,2048]{1,0:T(8,128)(2,1)S(1)} %copy-done.17, bf16[2048,1024]{1,0:T(8,128)(2,1)S(1)} %shard_map.192.weight_ref, ...), custom_call_target="tpu_custom_call" | custom-call | flops 6442450944 | bytes 16000000 | tf_op jit(solution)/shard_map/pallas_call | solution.py:679
  344.8 7.2 shard_map.197
  360.1 7.2 shard_map.199
  378.7 5.8 shard_map.201
  396.3 8.7 %collective-permute-done.46 = bf16[256,512]{1,0:T(8,128)(2,1)S(1)} collective-permute-done((bf16[256,512]{1,0:T(8,128)(2,1)S(1)}, bf16[256,512]{1,0:T(8,128)(2,1)S(1)}, u32[]{:S(2)}, u32[]{:S(2)}) %collective-permute-start.46) | collective-permute-done | bytes 262176 | tf_op jit(solution)/shard_map/ppermute | solution.py:50
  435.1 7.2 collective-permute-done.51
  468.1 19.4 %shard_map.212 = (f32[512,256]{1,0:T(8,128)S(1)}, f32[4096,128]{1,0:T(8,128)S(1)}) custom-call(s32[4]{0:T(128)S(1)} %pad_add_fusion.place_ref, bf16[1024,256]{1,0:T(8,128)(2,1)S(1)} %copy-done.144, bf16[512,2048]{1,0:T(8,128)(2,1)} %shard_map.210.branch_ref, bf16[512,256]{1,0:T(8,128)(2,1)S(1)} %copy-done.96, f32[8,1,512]{2,1,0:T(1,128)S(1)} %copy-done.155, ...), custom_call_target="tpu_custom_call" | custom-call | flops 17999998976 | bytes 12000000 | tf_op jit(solution)/shard_map/pallas_call | solution.py:619
  494.9 22.5 %shard_map.214 = (f32[512,256]{1,0:T(8,128)S(1)}, f32[4096,128]{1,0:T(8,128)S(1)}) custom-call(s32[4]{0:T(128)S(1)} %pad_add_fusion.place_ref, bf16[1024,256]{1,0:T(8,128)(2,1)S(1)} %copy-done.144, bf16[512,2048]{1,0:T(8,128)(2,1)} %collective-permute-done.54.branch_ref, bf16[512,256]{1,0:T(8,128)(2,1)S(1)} %copy-done.98, f32[8,1,512]{2,1,0:T(1,128)S(1)} %copy-done.155, ...), custom_call_target="tpu_custom_call" | custom-call | flops 17999998976 | bytes 12000000 | tf_op jit(solution)/shard_map/pallas_call | solution.py:619
  528.2 7.3 collective-permute-done.63
  540.6 9.2 %collective-permute-done.65 = bf16[8,1,128,128]{3,2,0,1:T(8,128)(2,1)S(1)} collective-permute-done((bf16[8,1,128,128]{3,2,0,1:T(8,128)(2,1)S(1)}, bf16[8,1,128,128]{3,2,0,1:T(8,128)(2,1)S(1)}, u32[]{:S(2)}, u32[]{:S(2)}) %collective-permute-start.65) | collective-permute-done | bytes 262176 | tf_op jit(solution)/shard_map/ppermute | solution.py:50
  569.0 13.7 %shard_map.219 = (bf16[512,384]{1,0:T(8,128)(2,1)S(1)}, bf16[512,384]{1,0:T(8,128)(2,1)S(1)}, bf16[512,2048]{1,0:T(8,128)(2,1)}, bf16[512,2048]{1,0:T(8,128)(2,1...) custom-call(s32[4]{0:T(128)S(1)} %pad_add_fusion.place_ref, bf16[512,2048]{1,0:T(8,128)(2,1)} %copy-done.2, ...), custom_call_target="tpu_custom_call" | custom-call | flops 1610612736 | bytes 12000000 | tf_op jit(solution)/shard_map/pallas_call | solution.py:436
  613.3 12.0 %collective-permute-done.72 = bf16[128,2048]{1,0:T(8,128)(2,1)S(1)} collective-permute-done((bf16[128,2048]{1,0:T(8,128)(2,1)}, bf16[128,2048]{1,0:T(8,128)(2,1)S(1)}, u32[]{:S(2)}, u32[]{:S(2)}) %collective-permute-start.72) | collective-permute-done | bytes 524320 | tf_op jit(solution)/shard_map/ppermute | solution.py:50
  645.3 6.2 collective-permute-done.81
  671.8 13.9 %collective-permute-done.84 = bf16[512,384]{1,0:T(8,128)(2,1)S(1)} collective-permute-done((bf16[512,384]{1,0:T(8,128)(2,1)S(1)}, bf16[512,384]{1,0:T(8,128)(2,1)S(1)}, u32[]{:S(2)}, u32[]{:S(2)}) %collective-permute-start.84) | collective-permute-done | bytes 393248 | tf_op jit(solution)/shard_map/ppermute | solution.py:50
  695.6 5.5 collective-permute-done.91
  710.9 6.3 collective-permute-done.95
  (709 shorter events, 368.4 us)
Async XLA Ops:
  58.3 30.6 %collective-permute-start.6 = (bf16[256,1024]{1,0:T(8,128)(2,1)}, bf16[256,1024]{1,0:T(8,128)(2,1)}, u32[]{:S(2)}, u32[]{:S(2)}) collective-permute-start(bf16[256,1024]{1,0:T(8,128)(2,1)} %get-tuple-element.479), channel_id=1, source_target_pairs={{0,1},{1,0},{2,3},{3,2},{4,5},{5,4},{6,7},{7,6},{8,9},{9,8},{10,11... | collective-permute-start | bytes 1572872 | tf_op jit(solution)/shard_map/ppermute | solution.py:55
  58.3 30.6 %collective-permute-start.7 = (bf16[128,2048]{1,0:T(8,128)(2,1)}, bf16[128,2048]{1,0:T(8,128)(2,1)}, u32[]{:S(2)}, u32[]{:S(2)}) collective-permute-start(bf16[128,2048]{1,0:T(8,128)(2,1)} %outer_ref.1), channel_id=1, source_target_pairs={{0,8},{4,20},{8,0},{12,28},{16,24},{20,4},{24,16},{28,12},{1,9},{5... | collective-permute-start | bytes 1572872 | tf_op jit(solution)/shard_map/ppermute | solution.py:78
  59.5 29.5 %collective-permute-start.10 = (bf16[512,256]{1,0:T(8,128)(2,1)}, bf16[512,256]{1,0:T(8,128)(2,1)S(1)}, u32[]{:S(2)}, u32[]{:S(2)}) collective-permute-start(bf16[512,256]{1,0:T(8,128)(2,1)} %constant_dynamic-slice_fusion.12.refs_0_), channel_id=1, source_target_pairs={{0,3},{1,0},{2,1},{3,2},{4,7},{5,4},{6,5},{7,6},{8,11},{9,8},{10,9... | collective-permute-start | bytes 786440 | tf_op jit(solution)/shard_map/ppermute | solution.py:50
  63.0 25.9 %collective-permute-start.8 = (bf16[512,256]{1,0:T(8,128)(2,1)}, bf16[512,256]{1,0:T(8,128)(2,1)S(1)}, u32[]{:S(2)}, u32[]{:S(2)}) collective-permute-start(bf16[512,256]{1,0:T(8,128)(2,1)} %constant_dynamic-slice_fusion.12.refs_0_), channel_id=1, source_target_pairs={{0,1},{1,2},{2,3},{3,0},{4,5},{5,6},{6,7},{7,4},{8,9},{9,10},{10,1... | collective-permute-start | bytes 786440 | tf_op jit(solution)/shard_map/ppermute | solution.py:50
  63.0 25.9 %collective-permute-start.9 = (bf16[512,256]{1,0:T(8,128)(2,1)}, bf16[512,256]{1,0:T(8,128)(2,1)S(1)}, u32[]{:S(2)}, u32[]{:S(2)}) collective-permute-start(bf16[512,256]{1,0:T(8,128)(2,1)} %constant_dynamic-slice_fusion.12.refs_0_), channel_id=1, source_target_pairs={{0,2},{1,3},{2,0},{3,1},{4,6},{5,7},{6,4},{7,5},{8,10},{9,11},{10,... | collective-permute-start | bytes 786440 | tf_op jit(solution)/shard_map/ppermute | solution.py:50
  95.7 34.2 %collective-permute-start.15 = (bf16[256,2048]{1,0:T(8,128)(2,1)S(1)}, bf16[256,2048]{1,0:T(8,128)(2,1)S(1)}, u32[]{:S(2)}, u32[]{:S(2)}) collective-permute-start(bf16[256,2048]{1,0:T(8,128)(2,1)S(1)} %shard_map.181.refs_0_), channel_id=1, source_target_pairs={{0,16},{4,12},{8,24},{12,4},{16,0},{20,28},{24,8},{28,20},{1,17},{... | collective-permute-start | bytes 3145736 | tf_op jit(solution)/shard_map/ppermute | solution.py:78
  104.1 25.8 %collective-permute-start.11 = (bf16[256,1024]{1,0:T(8,128)(2,1)}, bf16[256,1024]{1,0:T(8,128)(2,1)}, u32[]{:S(2)}, u32[]{:S(2)}) collective-permute-start(bf16[256,1024]{1,0:T(8,128)(2,1)} %get-tuple-element.494), channel_id=1, source_target_pairs={{0,1},{1,0},{2,3},{3,2},{4,5},{5,4},{6,7},{7,6},{8,9},{9,8},{10,11... | collective-permute-start | bytes 1572872 | tf_op jit(solution)/shard_map/ppermute | solution.py:55
  130.7 28.3 %collective-permute-start.17 = (bf16[512,2048]{1,0:T(8,128)(2,1)S(1)}, bf16[512,2048]{1,0:T(8,128)(2,1)S(1)}, u32[]{:S(2)}, u32[]{:S(2)}) collective-permute-start(bf16[512,2048]{1,0:T(8,128)(2,1)S(1)} %shard_map.183.outer_ref.refs_4_), channel_id=1, source_target_pairs={{0,4},{4,0},{8,12},{12,8},{16,20},{20,16},{24,28},{28,24},{1,5},{5... | collective-permute-start | bytes 6291464 | tf_op jit(solution)/shard_map/ppermute | solution.py:40
  130.8 28.0 %collective-permute-start.18 = (bf16[128,2048]{1,0:T(8,128)(2,1)}, bf16[128,2048]{1,0:T(8,128)(2,1)S(1)}, u32[]{:S(2)}, u32[]{:S(2)}) collective-permute-start(bf16[128,2048]{1,0:T(8,128)(2,1)} %outer_ref.1), channel_id=1, source_target_pairs={{0,1},{1,0},{2,3},{3,2},{4,5},{5,4},{6,7},{7,6},{8,9},{9,8},{10,11... | collective-permute-start | bytes 1572872 | tf_op jit(solution)/shard_map/ppermute | solution.py:55
  133.0 26.0 %collective-permute-start.16 = (bf16[256,1024]{1,0:T(8,128)(2,1)S(1)}, bf16[256,1024]{1,0:T(8,128)(2,1)S(1)}, u32[]{:S(2)}, u32[]{:S(2)}) collective-permute-start(bf16[256,1024]{1,0:T(8,128)(2,1)S(1)} %copy-done.55), channel_id=1, source_target_pairs={{0,2},{1,3},{2,0},{3,1},{4,6},{5,7},{6,4},{7,5},{8,10},{9,11},{10,... | collective-permute-start | bytes 1572872 | tf_op jit(solution)/shard_map/ppermute | solution.py:50
  177.8 27.4 %collective-permute-start.24 = (bf16[256,2048]{1,0:T(8,128)(2,1)S(1)}, bf16[256,2048]{1,0:T(8,128)(2,1)S(1)}, u32[]{:S(2)}, u32[]{:S(2)}) collective-permute-start(bf16[256,2048]{1,0:T(8,128)(2,1)S(1)} %shard_map.185.refs_0_), channel_id=1, source_target_pairs={{0,16},{4,12},{8,24},{12,4},{16,0},{20,28},{24,8},{28,20},{1,17},{... | collective-permute-start | bytes 3145736 | tf_op jit(solution)/shard_map/ppermute | solution.py:78
  179.4 25.9 %collective-permute-start.23 = (bf16[256,2048]{1,0:T(8,128)(2,1)S(1)}, bf16[256,2048]{1,0:T(8,128)(2,1)S(1)}, u32[]{:S(2)}, u32[]{:S(2)}) collective-permute-start(bf16[256,2048]{1,0:T(8,128)(2,1)S(1)} %get-tuple-element.527), channel_id=1, source_target_pairs={{0,16},{4,12},{8,24},{12,4},{16,0},{20,28},{24,8},{28,20},{1,17},{... | collective-permute-start | bytes 3145736 | tf_op jit(solution)/shard_map/ppermute | solution.py:78
  244.7 27.4 %collective-permute-start.32 = (bf16[256,2048]{1,0:T(8,128)(2,1)S(1)}, bf16[256,2048]{1,0:T(8,128)(2,1)S(1)}, u32[]{:S(2)}, u32[]{:S(2)}) collective-permute-start(bf16[256,2048]{1,0:T(8,128)(2,1)S(1)} %shard_map.188.refs_0_), channel_id=1, source_target_pairs={{0,16},{4,12},{8,24},{12,4},{16,0},{20,28},{24,8},{28,20},{1,17},{... | collective-permute-start | bytes 3145736 | tf_op jit(solution)/shard_map/ppermute | solution.py:78
  292.1 26.4 %collective-permute-start.38 = (bf16[512,2048]{1,0:T(8,128)(2,1)}, bf16[512,2048]{1,0:T(8,128)(2,1)}, u32[]{:S(2)}, u32[]{:S(2)}) collective-permute-start(bf16[512,2048]{1,0:T(8,128)(2,1)} %shard_map.191.normed_ref.refs_2_), channel_id=1, source_target_pairs={{0,4},{4,0},{8,12},{12,8},{16,20},{20,16},{24,28},{28,24},{1,5},{5... | collective-permute-start | bytes 6291464 | tf_op jit(solution)/shard_map/ppermute | solution.py:40
  292.1 26.4 %collective-permute-start.37 = (bf16[256,1024]{1,0:T(8,128)(2,1)}, bf16[256,1024]{1,0:T(8,128)(2,1)}, u32[]{:S(2)}, u32[]{:S(2)}) collective-permute-start(bf16[256,1024]{1,0:T(8,128)(2,1)} %collective-permute-done.11.refs_3_), channel_id=1, source_target_pairs={{0,2},{1,3},{2,0},{3,1},{4,6},{5,7},{6,4},{7,5},{8,10},{9,11},{10,... | collective-permute-start | bytes 1572872 | tf_op jit(solution)/shard_map/ppermute | solution.py:50
  463.4 27.3 %collective-permute-start.58 = (bf16[256,2048]{1,0:T(8,128)(2,1)S(1)}, bf16[256,2048]{1,0:T(8,128)(2,1)S(1)}, u32[]{:S(2)}, u32[]{:S(2)}) collective-permute-start(bf16[256,2048]{1,0:T(8,128)(2,1)S(1)} %copy-done.141), channel_id=1, source_target_pairs={{0,16},{4,12},{8,24},{12,4},{16,0},{20,28},{24,8},{28,20},{1,17},{... | collective-permute-start | bytes 3145736 | tf_op jit(solution)/shard_map/ppermute | solution.py:78
  490.6 26.8 %collective-permute-start.62 = (bf16[128,2048]{1,0:T(8,128)(2,1)S(1)}, bf16[128,2048]{1,0:T(8,128)(2,1)S(1)}, u32[]{:S(2)}, u32[]{:S(2)}) collective-permute-start(bf16[128,2048]{1,0:T(8,128)(2,1)S(1)} %get-tuple-element.743), channel_id=1, source_target_pairs={{0,8},{4,20},{8,0},{12,28},{16,24},{20,4},{24,16},{28,12},{1,9},{5... | collective-permute-start | bytes 1572872 | tf_op jit(solution)/shard_map/ppermute | solution.py:78
  493.5 27.5 %collective-permute-start.60 = (bf16[512,1024]{1,0:T(8,128)(2,1)S(1)}, bf16[512,1024]{1,0:T(8,128)(2,1)S(1)}, u32[]{:S(2)}, u32[]{:S(2)}) collective-permute-start(bf16[512,1024]{1,0:T(8,128)(2,1)S(1)} %pad_maximum_fusion.1.refs_0_), channel_id=1, source_target_pairs={{0,8},{4,20},{8,0},{12,28},{16,24},{20,4},{24,16},{28,12},{1,9},{5... | collective-permute-start | bytes 3145736 | tf_op jit(solution)/shard_map/ppermute | solution.py:78
  494.6 26.5 %collective-permute-start.59 = (bf16[512,512]{1,0:T(8,128)(2,1)S(1)}, bf16[512,512]{1,0:T(8,128)(2,1)S(1)}, u32[]{:S(2)}, u32[]{:S(2)}) collective-permute-start(bf16[512,512]{1,0:T(8,128)(2,1)S(1)} %copy-done.148), channel_id=1, source_target_pairs={{0,2},{1,3},{2,0},{3,1},{4,6},{5,7},{6,4},{7,5},{8,10},{9,11},{10,... | collective-permute-start | bytes 1572872 | tf_op jit(solution)/shard_map/ppermute | solution.py:50
  521.9 33.3 %collective-permute-start.67 = (bf16[1024,1024]{1,0:T(8,128)(2,1)S(1)}, bf16[1024,1024]{1,0:T(8,128)(2,1)S(1)}, u32[]{:S(2)}, u32[]{:S(2)}) collective-permute-start(bf16[1024,1024]{1,0:T(8,128)(2,1)S(1)} %shard_map.218.source_ref), channel_id=1, source_target_pairs={{0,16},{4,12},{8,24},{12,4},{16,0},{20,28},{24,8},{28,20},{1,17},{... | collective-permute-start | bytes 6291464 | tf_op jit(solution)/shard_map/ppermute | solution.py:78
  555.2 36.3 %collective-permute-start.69 = (bf16[1024,1024]{1,0:T(8,128)(2,1)S(1)}, bf16[1024,1024]{1,0:T(8,128)(2,1)}, u32[]{:S(2)}, u32[]{:S(2)}) collective-permute-start(bf16[1024,1024]{1,0:T(8,128)(2,1)S(1)} %shard_map.218.source_ref), channel_id=1, source_target_pairs={{0,4},{4,0},{8,12},{12,8},{16,20},{20,16},{24,28},{28,24},{1,5},{5... | collective-permute-start | bytes 6291464 | tf_op jit(solution)/shard_map/ppermute | solution.py:40
  555.4 36.0 %collective-permute-start.70 = (bf16[512,1024]{1,0:T(8,128)(2,1)S(1)}, bf16[512,1024]{1,0:T(8,128)(2,1)}, u32[]{:S(2)}, u32[]{:S(2)}) collective-permute-start(bf16[512,1024]{1,0:T(8,128)(2,1)S(1)} %pad_maximum_fusion.2.refs_0_), channel_id=1, source_target_pairs={{0,8},{4,20},{8,0},{12,28},{16,24},{20,4},{24,16},{28,12},{1,9},{5... | collective-permute-start | bytes 3145736 | tf_op jit(solution)/shard_map/ppermute | solution.py:78
  557.3 34.1 %all-to-all-start.1 = ((bf16[256,8,256]{2,0,1:T(8,128)(2,1)}), bf16[256,8,256]{2,0,1:T(8,128)(2,1)}, u32[]{:S(2)}, u32[]{:S(2)}) async-start(bf16[256,8,256]{2,0,1:T(8,128)(2,1)} %bitcast.105), calls=%async_computation.1 | async-start | bytes 2097152 | tf_op jit(solution)/shard_map/all_to_all | solution.py:963
  563.5 27.9 %collective-permute-start.68 = (bf16[128,2048]{1,0:T(8,128)(2,1)}, bf16[128,2048]{1,0:T(8,128)(2,1)}, u32[]{:S(2)}, u32[]{:S(2)}) collective-permute-start(bf16[128,2048]{1,0:T(8,128)(2,1)} %copy-done.146), channel_id=1, source_target_pairs={{0,2},{1,3},{2,0},{3,1},{4,6},{5,7},{6,4},{7,5},{8,10},{9,11},{10,... | collective-permute-start | bytes 1572872 | tf_op jit(solution)/shard_map/ppermute | solution.py:50
  594.8 30.5 %collective-permute-start.74 = (bf16[1024,1024]{1,0:T(8,128)(2,1)}, bf16[1024,1024]{1,0:T(8,128)(2,1)}, u32[]{:S(2)}, u32[]{:S(2)}) collective-permute-start(bf16[1024,1024]{1,0:T(8,128)(2,1)} %shard_map.220.source_ref), channel_id=1, source_target_pairs={{0,16},{4,12},{8,24},{12,4},{16,0},{20,28},{24,8},{28,20},{1,17},{... | collective-permute-start | bytes 6291464 | tf_op jit(solution)/shard_map/ppermute | solution.py:78
  596.5 28.8 %collective-permute-start.75 = (bf16[1024,1024]{1,0:T(8,128)(2,1)}, bf16[1024,1024]{1,0:T(8,128)(2,1)}, u32[]{:S(2)}, u32[]{:S(2)}) collective-permute-start(bf16[1024,1024]{1,0:T(8,128)(2,1)} %shard_map.220.source_ref), channel_id=1, source_target_pairs={{0,4},{4,0},{8,12},{12,8},{16,20},{20,16},{24,28},{28,24},{1,5},{5... | collective-permute-start | bytes 6291464 | tf_op jit(solution)/shard_map/ppermute | solution.py:40
  596.5 28.8 %collective-permute-start.73 = (bf16[512,2048]{1,0:T(8,128)(2,1)}, bf16[512,2048]{1,0:T(8,128)(2,1)}, u32[]{:S(2)}, u32[]{:S(2)}) collective-permute-start(bf16[512,2048]{1,0:T(8,128)(2,1)} %get-tuple-element.788), channel_id=1, source_target_pairs={{0,4},{4,0},{8,12},{12,8},{16,20},{20,16},{24,28},{28,24},{1,5},{5... | collective-permute-start | bytes 6291464 | tf_op jit(solution)/shard_map/ppermute | solution.py:40
  598.8 26.5 %collective-permute-start.72 = (bf16[128,2048]{1,0:T(8,128)(2,1)}, bf16[128,2048]{1,0:T(8,128)(2,1)S(1)}, u32[]{:S(2)}, u32[]{:S(2)}) collective-permute-start(bf16[128,2048]{1,0:T(8,128)(2,1)} %copy-done.145), channel_id=1, source_target_pairs={{0,2},{1,3},{2,0},{3,1},{4,6},{5,7},{6,4},{7,5},{8,10},{9,11},{10,... | collective-permute-start | bytes 1572872 | tf_op jit(solution)/shard_map/ppermute | solution.py:50
  625.3 27.9 %collective-permute-start.79 = (bf16[1024,1024]{1,0:T(8,128)(2,1)S(1)}, bf16[1024,1024]{1,0:T(8,128)(2,1)S(1)}, u32[]{:S(2)}, u32[]{:S(2)}) collective-permute-start(bf16[1024,1024]{1,0:T(8,128)(2,1)S(1)} %copy-done.47), channel_id=1, source_target_pairs={{0,4},{4,0},{8,12},{12,8},{16,20},{20,16},{24,28},{28,24},{1,5},{5... | collective-permute-start | bytes 6291464 | tf_op jit(solution)/shard_map/ppermute | solution.py:40
  653.9 31.8 %collective-permute-start.83 = (bf16[512,2048]{1,0:T(8,128)(2,1)S(1)}, bf16[512,2048]{1,0:T(8,128)(2,1)S(1)}, u32[]{:S(2)}, u32[]{:S(2)}) collective-permute-start(bf16[512,2048]{1,0:T(8,128)(2,1)S(1)} %shard_map.229.source_ref), channel_id=1, source_target_pairs={{0,16},{4,12},{8,24},{12,4},{16,0},{20,28},{24,8},{28,20},{1,17},{... | collective-permute-start | bytes 6291464 | tf_op jit(solution)/shard_map/ppermute | solution.py:78
  654.9 30.9 %collective-permute-start.82 = (bf16[128,2048]{1,0:T(8,128)(2,1)S(1)}, bf16[128,2048]{1,0:T(8,128)(2,1)S(1)}, u32[]{:S(2)}, u32[]{:S(2)}) collective-permute-start(bf16[128,2048]{1,0:T(8,128)(2,1)S(1)} %get-tuple-element.833), channel_id=1, source_target_pairs={{0,8},{4,20},{8,0},{12,28},{16,24},{20,4},{24,16},{28,12},{1,9},{5... | collective-permute-start | bytes 1572872 | tf_op jit(solution)/shard_map/ppermute | solution.py:78
  659.1 26.6 %collective-permute-start.84 = (bf16[512,384]{1,0:T(8,128)(2,1)S(1)}, bf16[512,384]{1,0:T(8,128)(2,1)S(1)}, u32[]{:S(2)}, u32[]{:S(2)}) collective-permute-start(bf16[512,384]{1,0:T(8,128)(2,1)S(1)} %get-tuple-element.850), channel_id=1, source_target_pairs={{0,2},{1,3},{2,0},{3,1},{4,6},{5,7},{6,4},{7,5},{8,10},{9,11},{10,... | collective-permute-start | bytes 1179656 | tf_op jit(solution)/shard_map/ppermute | solution.py:50
  (252 other events, 2279.4 us)

commit v6 on v5

--- a/solution.py
+++ b/solution.py
@@ -1078,10 +1078,11 @@
     )
     angles = got[1]
     qkv_pieces = [qkv_own] + got[2:]
-    two = rows_joined(normed_attn_own, got[0])
+    from_first = got[0]
     got = steps.run(
         [
-            (second_round, two),
+            (second_round, normed_attn_own),
+            (second_round, from_first),
             (
                 lambda v: (
                     {
@@ -1101,13 +1102,13 @@
         ]
         + [(send, qkv_own) for send in sends[2:last]]
     )
-    owned, down_pieces = got[1]
+    owned, down_pieces = got[2]
     for n in range(2):
         gate_up_parts.append((owned[0, n], fsdp_here, n))
     for n in range(4):
         down_parts.append((down_pieces[n], pair_here, n))
-    qkv_pieces += got[2:]
-    mine = rows_joined(two, got[0])
+    qkv_pieces += got[3:]
+    mine = rows_joined(normed_attn_own, from_first, got[0], got[1])
     got = steps.run([(twin_send, mine)] + [(send, qkv_own) for send in sends[last:]])
     qkv_pieces += got[1:]
     normed_attn = [mine, got[0]]

time: 746 us -> 742 us (level)
    pallas_call x25 -> x24, Pallas kernels: 32.3 us -> 29.3 us  [join(): pl.pallas_call(join_kernel, grid_spec=pltpu.PrefetchScalarGridSpec(num_sc...]
    ppermute x34 -> x35, starting transfers between devices: 40.8 us -> 41.8 us  [round_send(): return lax.ppermute(values, 'ctx', pairs)]
    ppermute x34 -> x35, waiting for transfers between devices: 22 us -> 21.9 us  [round_send(): return lax.ppermute(values, 'ctx', pairs)]
  transfers between devices with their start and end apart: 103 -> 104, of which waited for: 42 -> 43; matrix products, arithmetic and copies ran while one was open for 6% -> 6% of each run, Pallas kernels for 28% -> 28%
where the time goes in v6:
time: 742 us; the launch traced here: 735 us
  waiting for transfers between devices  282 us (38%)
  Pallas kernels  243 us (33%)
  starting transfers between devices  99.9 us (13%)
  local copies, waits for them, and re-layouts  73.6 us (10%)
  other arithmetic  23.9 us (3%)
  matrix products  9.72 us (1%)
    ppermute x34, waiting for transfers between devices, fsdp_send(): lax.ppermute(values, 'fsdp', [(i, (i + step) % count) for i in range(coun...  226 us
    unnamed x363, local copies, waits for them, and re-layouts  54.8 us
    ppermute x34, starting transfers between devices, fsdp_send(): lax.ppermute(values, 'fsdp', [(i, (i + step) % count) for i in range(coun...  44.9 us
    pallas_call x2, Pallas kernels, attention_grad(): pl.pallas_call(functools.partial(attention_grad_kernel, chunk, other), gr...  42 us
    ppermute x35, starting transfers between devices, round_send(): return lax.ppermute(values, 'ctx', pairs)  41.8 us
    pallas_call x4, Pallas kernels, feed(): pl.pallas_call(feed_kernel, grid=(tokens // rows,), in_specs=[by_row(widt...  32.9 us
    pallas_call x10, Pallas kernels, place_units(): pl.pallas_call(functools.partial(place_units_kernel, block_at, unit, colu...  31.4 us
    pallas_call x24, Pallas kernels, join(): pl.pallas_call(join_kernel, grid_spec=pltpu.PrefetchScalarGridSpec(num_sc...  29.3 us
  transfers between devices with their start and end apart: 104, of which 43 were waited for; matrix products, arithmetic and copies ran while one was open for 6% of the time, Pallas kernels for 28%

profile of v6, /device:TPU:0, one launch (start us, length us, event | category | flops | bytes accessed | tf_op | source)
XLA Modules:
  0.0 735.0 jit_solution(10431401400760428152)
XLA Ops:
  28.5 8.8 %collective-permute-done.4.refs_2_ = bf16[512,384]{1,0:T(8,128)(2,1)S(1)} collective-permute-done((bf16[512,384]{1,0:T(8,128)(2,1)S(1)}, bf16[512,384]{1,0:T(8,128)(2,1)S(1)}, u32[]{:S(2)}, u32[]{:S(2)}) %collective-permute-start.4) | collective-permute-done | bytes 393248 | tf_op jit(solution)/shard_map/ppermute | solution.py:50
  43.5 8.8 %collective-permute-done.6.refs_3_ = bf16[512,384]{1,0:T(8,128)(2,1)S(1)} collective-permute-done((bf16[512,384]{1,0:T(8,128)(2,1)S(1)}, bf16[512,384]{1,0:T(8,128)(2,1)S(1)}, u32[]{:S(2)}, u32[]{:S(2)}) %collective-permute-start.6) | collective-permute-done | bytes 393248 | tf_op jit(solution)/shard_map/ppermute | solution.py:50
  67.7 10.4 %shard_map.178 = (f32[1024,384]{1,0:T(8,128)S(1)}, bf16[1024,256]{1,0:T(8,128)(2,1)S(1)}, bf16[1024,128]{1,0:T(8,128)(2,1)}) custom-call(s32[4]{0:T(128)S(1)} %pad_add_fusion.place_ref, bf16[512,2048]{1,0:T(8,128)(2,1)S(1)} %copy-done.3, bf16[512,2048]{1,0:T(8,128)(2,1)S(1)} %copy-done.10, f32[1024,256]{1,0:T(8,128)S(1)} %concatenate.36.angle_ref, ...), custom_call_target="tpu_custom_call" | custom-call | flops 1610612736 | bytes 8000000 | tf_op jit(solution)/shard_map/pallas_call | solution.py:322
  79.4 7.6 %collective-permute-done.9.refs_1_ = bf16[512,256]{1,0:T(8,128)(2,1)S(1)} collective-permute-done((bf16[512,256]{1,0:T(8,128)(2,1)}, bf16[512,256]{1,0:T(8,128)(2,1)S(1)}, u32[]{:S(2)}, u32[]{:S(2)}) %collective-permute-start.9) | collective-permute-done | bytes 262176 | tf_op jit(solution)/shard_map/ppermute | solution.py:50
  92.4 6.2 collective-permute-done.13
  106.8 10.7 %all-to-all-done = bf16[8,256,256]{2,1,0:T(8,128)(2,1)S(1)} async-done(((bf16[8,256,256]{2,1,0:T(8,128)(2,1)}), bf16[8,256,256]{2,1,0:T(8,128)(2,1)S(1)}, u32[]{:S(2)}, u32[]{:S(2)}) %all-to-all-start) | async-done | bytes 1048608 | tf_op jit(solution)/shard_map/all_to_all | solution.py:963
  120.5 7.6 %collective-permute-done.15 = bf16[8,1,128,128]{3,2,1,0:T(8,128)(2,1)} collective-permute-done((bf16[8,1,128,128]{3,2,1,0:T(8,128)(2,1)}, bf16[8,1,128,128]{3,2,1,0:T(8,128)(2,1)}, u32[]{:S(2)}, u32[]{:S(2)}) %collective-permute-start.15) | collective-permute-done | bytes 262176 | tf_op jit(solution)/shard_map/ppermute | solution.py:50
  133.0 22.3 %shard_map.181 = (bf16[512,256]{1,0:T(8,128)(2,1)S(1)}, bf16[512,256]{1,0:T(8,128)(2,1)S(1)}, f32[8,1,512]{2,1,0:T(1,128)S(1)}) custom-call(s32[4]{0:T(128)S(1)} %pad_add_fusion.place_ref, bf16[1024,256]{1,0:T(8,128)(2,1)S(1)} %copy-done.143, bf16[4096,128]{1,0:T(8,128)(2,1)S(1)} %bitcast.99), custom_call_target="tpu_custom_call" | custom-call | flops 16000000000 | bytes 8000000 | tf_op jit(solution)/shard_map/pallas_call | solution.py:542
  160.8 13.3 %collective-permute-done.20.refs_4_ = bf16[64,2048]{1,0:T(8,128)(2,1)S(1)} collective-permute-done((bf16[64,2048]{1,0:T(8,128)(2,1)S(1)}, bf16[64,2048]{1,0:T(8,128)(2,1)S(1)}, u32[]{:S(2)}, u32[]{:S(2)}) %collective-permute-start.20) | collective-permute-done | bytes 262176 | tf_op jit(solution)/shard_map/ppermute | solution.py:50
  178.8 24.5 %collective-permute-done.23.refs_5_ = bf16[256,1024]{1,0:T(8,128)(2,1)S(1)} collective-permute-done((bf16[256,1024]{1,0:T(8,128)(2,1)S(1)}, bf16[256,1024]{1,0:T(8,128)(2,1)S(1)}, u32[]{:S(2)}, u32[]{:S(2)}) %collective-permute-start.23) | collective-permute-done | bytes 524320 | tf_op jit(solution)/shard_map/ppermute | solution.py:50
  206.1 13.5 %collective-permute-done.26.refs_5_ = bf16[64,2048]{1,0:T(8,128)(2,1)S(1)} collective-permute-done((bf16[64,2048]{1,0:T(8,128)(2,1)S(1)}, bf16[64,2048]{1,0:T(8,128)(2,1)S(1)}, u32[]{:S(2)}, u32[]{:S(2)}) %collective-permute-start.26) | collective-permute-done | bytes 262176 | tf_op jit(solution)/shard_map/ppermute | solution.py:50
  224.9 14.7 %collective-permute-done.29.refs_6_ = bf16[64,2048]{1,0:T(8,128)(2,1)S(1)} collective-permute-done((bf16[64,2048]{1,0:T(8,128)(2,1)S(1)}, bf16[64,2048]{1,0:T(8,128)(2,1)S(1)}, u32[]{:S(2)}, u32[]{:S(2)}) %collective-permute-start.29) | collective-permute-done | bytes 262176 | tf_op jit(solution)/shard_map/ppermute | solution.py:50
  245.8 12.0 %collective-permute-done.34.refs_1_ = bf16[128,2048]{1,0:T(8,128)(2,1)S(1)} collective-permute-done((bf16[128,2048]{1,0:T(8,128)(2,1)S(1)}, bf16[128,2048]{1,0:T(8,128)(2,1)S(1)}, u32[]{:S(2)}, u32[]{:S(2)}) %collective-permute-start.34) | collective-permute-done | bytes 524320 | tf_op jit(solution)/shard_map/ppermute | solution.py:78
  257.8 11.5 %collective-permute-done.32.refs_6_ = bf16[256,1024]{1,0:T(8,128)(2,1)S(1)} collective-permute-done((bf16[256,1024]{1,0:T(8,128)(2,1)}, bf16[256,1024]{1,0:T(8,128)(2,1)S(1)}, u32[]{:S(2)}, u32[]{:S(2)}) %collective-permute-start.32) | collective-permute-done | bytes 524320 | tf_op jit(solution)/shard_map/ppermute | solution.py:50
  273.1 13.0 %collective-permute-done.35.refs_7_ = bf16[64,2048]{1,0:T(8,128)(2,1)S(1)} collective-permute-done((bf16[64,2048]{1,0:T(8,128)(2,1)S(1)}, bf16[64,2048]{1,0:T(8,128)(2,1)S(1)}, u32[]{:S(2)}, u32[]{:S(2)}) %collective-permute-start.35) | collective-permute-done | bytes 262176 | tf_op jit(solution)/shard_map/ppermute | solution.py:50
  300.8 15.6 %collective-permute-done.38.refs_7_ = bf16[256,1024]{1,0:T(8,128)(2,1)} collective-permute-done((bf16[256,1024]{1,0:T(8,128)(2,1)}, bf16[256,1024]{1,0:T(8,128)(2,1)}, u32[]{:S(2)}, u32[]{:S(2)}) %collective-permute-start.38) | collective-permute-done | bytes 524320 | tf_op jit(solution)/shard_map/ppermute | solution.py:50
  319.1 9.6 %shard_map.193 = (bf16[512,512]{1,0:T(8,128)(2,1)S(1)}, bf16[512,1024]{1,0:T(8,128)(2,1)S(1)}, bf16[512,2048]{1,0:T(8,128)(2,1)S(1)}, bf16[512,2048]{1,0:T(8,128)(2,1)}) custom-call(bf16[512,2048]{1,0:T(8,128)(2,1)} %collective-permute-done.39.normed_ref.refs_3_, bf16[512,2048]{1,0:T(8,128)(2,1)S(1)} %copy-done.43, ...), custom_call_target="tpu_custom_call" | custom-call | flops 6442450944 | bytes 16000000 | tf_op jit(solution)/shard_map/pallas_call | solution.py:679
  329.5 8.8 %shard_map.194 = (bf16[512,512]{1,0:T(8,128)(2,1)S(1)}, bf16[512,1024]{1,0:T(8,128)(2,1)S(1)}, bf16[512,2048]{1,0:T(8,128)(2,1)S(1)}, bf16[512,2048]{1,0:T(8,128)(2,1)S(1)}) custom-call(bf16[512,2048]{1,0:T(8,128)(2,1)} %shard_map.190.normed_ref.refs_2_, bf16[512,2048]{1,0:T(8,128)(2,1)S(1)} %copy-done.17, bf16[2048,1024]{1,0:T(8,128)(2,1)S(1)} %shard_map.191.weight_ref, ...), custom_call_target="tpu_custom_call" | custom-call | flops 6442450944 | bytes 16000000 | tf_op jit(solution)/shard_map/pallas_call | solution.py:679
  342.7 7.2 shard_map.196
  358.1 7.2 shard_map.198
  376.6 5.8 shard_map.200
  394.4 8.5 %collective-permute-done.47 = bf16[256,512]{1,0:T(8,128)(2,1)S(1)} collective-permute-done((bf16[256,512]{1,0:T(8,128)(2,1)S(1)}, bf16[256,512]{1,0:T(8,128)(2,1)S(1)}, u32[]{:S(2)}, u32[]{:S(2)}) %collective-permute-start.47) | collective-permute-done | bytes 262176 | tf_op jit(solution)/shard_map/ppermute | solution.py:50
  433.0 7.3 collective-permute-done.52
  466.0 19.4 %shard_map.211 = (f32[512,256]{1,0:T(8,128)S(1)}, f32[4096,128]{1,0:T(8,128)S(1)}) custom-call(s32[4]{0:T(128)S(1)} %pad_add_fusion.place_ref, bf16[1024,256]{1,0:T(8,128)(2,1)S(1)} %copy-done.144, bf16[512,2048]{1,0:T(8,128)(2,1)} %shard_map.209.branch_ref, bf16[512,256]{1,0:T(8,128)(2,1)S(1)} %copy-done.96, f32[8,1,512]{2,1,0:T(1,128)S(1)} %copy-done.155, ...), custom_call_target="tpu_custom_call" | custom-call | flops 17999998976 | bytes 12000000 | tf_op jit(solution)/shard_map/pallas_call | solution.py:619
  492.8 22.6 %shard_map.213 = (f32[512,256]{1,0:T(8,128)S(1)}, f32[4096,128]{1,0:T(8,128)S(1)}) custom-call(s32[4]{0:T(128)S(1)} %pad_add_fusion.place_ref, bf16[1024,256]{1,0:T(8,128)(2,1)S(1)} %copy-done.144, bf16[512,2048]{1,0:T(8,128)(2,1)} %collective-permute-done.55.branch_ref, bf16[512,256]{1,0:T(8,128)(2,1)S(1)} %copy-done.98, f32[8,1,512]{2,1,0:T(1,128)S(1)} %copy-done.155, ...), custom_call_target="tpu_custom_call" | custom-call | flops 17999998976 | bytes 12000000 | tf_op jit(solution)/shard_map/pallas_call | solution.py:619
  526.0 7.3 collective-permute-done.64
  538.3 9.4 %collective-permute-done.66 = bf16[8,1,128,128]{3,2,0,1:T(8,128)(2,1)S(1)} collective-permute-done((bf16[8,1,128,128]{3,2,0,1:T(8,128)(2,1)S(1)}, bf16[8,1,128,128]{3,2,0,1:T(8,128)(2,1)S(1)}, u32[]{:S(2)}, u32[]{:S(2)}) %collective-permute-start.66) | collective-permute-done | bytes 262176 | tf_op jit(solution)/shard_map/ppermute | solution.py:50
  566.0 13.7 %shard_map.218 = (bf16[512,384]{1,0:T(8,128)(2,1)S(1)}, bf16[512,384]{1,0:T(8,128)(2,1)S(1)}, bf16[512,2048]{1,0:T(8,128)(2,1)}, bf16[512,2048]{1,0:T(8,128)(2,1...) custom-call(s32[4]{0:T(128)S(1)} %pad_add_fusion.place_ref, bf16[512,2048]{1,0:T(8,128)(2,1)} %copy-done.2, ...), custom_call_target="tpu_custom_call" | custom-call | flops 1610612736 | bytes 12000000 | tf_op jit(solution)/shard_map/pallas_call | solution.py:436
  609.6 11.8 %collective-permute-done.73 = bf16[128,2048]{1,0:T(8,128)(2,1)S(1)} collective-permute-done((bf16[128,2048]{1,0:T(8,128)(2,1)}, bf16[128,2048]{1,0:T(8,128)(2,1)S(1)}, u32[]{:S(2)}, u32[]{:S(2)}) %collective-permute-start.73) | collective-permute-done | bytes 524320 | tf_op jit(solution)/shard_map/ppermute | solution.py:50
  641.3 6.2 collective-permute-done.82
  668.0 14.0 %collective-permute-done.85 = bf16[512,384]{1,0:T(8,128)(2,1)S(1)} collective-permute-done((bf16[512,384]{1,0:T(8,128)(2,1)S(1)}, bf16[512,384]{1,0:T(8,128)(2,1)S(1)}, u32[]{:S(2)}, u32[]{:S(2)}) %collective-permute-start.85) | collective-permute-done | bytes 393248 | tf_op jit(solution)/shard_map/ppermute | solution.py:50
  707.0 6.4 collective-permute-done.96
  (709 shorter events, 365.7 us)
Async XLA Ops:
  54.4 32.6 %collective-permute-start.7 = (bf16[256,1024]{1,0:T(8,128)(2,1)}, bf16[256,1024]{1,0:T(8,128)(2,1)}, u32[]{:S(2)}, u32[]{:S(2)}) collective-permute-start(bf16[256,1024]{1,0:T(8,128)(2,1)} %get-tuple-element.483), channel_id=1, source_target_pairs={{0,1},{1,0},{2,3},{3,2},{4,5},{5,4},{6,7},{7,6},{8,9},{9,8},{10,11... | collective-permute-start | bytes 1572872 | tf_op jit(solution)/shard_map/ppermute | solution.py:55
  54.4 32.6 %collective-permute-start.8 = (bf16[128,2048]{1,0:T(8,128)(2,1)}, bf16[128,2048]{1,0:T(8,128)(2,1)}, u32[]{:S(2)}, u32[]{:S(2)}) collective-permute-start(bf16[128,2048]{1,0:T(8,128)(2,1)} %outer_ref.1), channel_id=1, source_target_pairs={{0,8},{4,20},{8,0},{12,28},{16,24},{20,4},{24,16},{28,12},{1,9},{5... | collective-permute-start | bytes 1572872 | tf_op jit(solution)/shard_map/ppermute | solution.py:78
  60.5 26.5 %collective-permute-start.9 = (bf16[512,256]{1,0:T(8,128)(2,1)}, bf16[512,256]{1,0:T(8,128)(2,1)S(1)}, u32[]{:S(2)}, u32[]{:S(2)}) collective-permute-start(bf16[512,256]{1,0:T(8,128)(2,1)} %constant_dynamic-slice_fusion.12.refs_0_), channel_id=1, source_target_pairs={{0,1},{1,2},{2,3},{3,0},{4,5},{5,6},{6,7},{7,4},{8,9},{9,10},{10,1... | collective-permute-start | bytes 786440 | tf_op jit(solution)/shard_map/ppermute | solution.py:50
  91.0 37.0 %collective-permute-start.16 = (bf16[256,2048]{1,0:T(8,128)(2,1)S(1)}, bf16[256,2048]{1,0:T(8,128)(2,1)S(1)}, u32[]{:S(2)}, u32[]{:S(2)}) collective-permute-start(bf16[256,2048]{1,0:T(8,128)(2,1)S(1)} %shard_map.180.refs_0_), channel_id=1, source_target_pairs={{0,16},{4,12},{8,24},{12,4},{16,0},{20,28},{24,8},{28,20},{1,17},{... | collective-permute-start | bytes 3145736 | tf_op jit(solution)/shard_map/ppermute | solution.py:78
  102.2 25.9 %collective-permute-start.12 = (bf16[256,1024]{1,0:T(8,128)(2,1)}, bf16[256,1024]{1,0:T(8,128)(2,1)}, u32[]{:S(2)}, u32[]{:S(2)}) collective-permute-start(bf16[256,1024]{1,0:T(8,128)(2,1)} %get-tuple-element.498), channel_id=1, source_target_pairs={{0,1},{1,0},{2,3},{3,2},{4,5},{5,4},{6,7},{7,6},{8,9},{9,8},{10,11... | collective-permute-start | bytes 1572872 | tf_op jit(solution)/shard_map/ppermute | solution.py:55
  102.4 25.7 %collective-permute-start.15 = (bf16[8,1,128,128]{3,2,1,0:T(8,128)(2,1)}, bf16[8,1,128,128]{3,2,1,0:T(8,128)(2,1)}, u32[]{:S(2)}, u32[]{:S(2)}) collective-permute-start(bf16[8,1,128,128]{3,2,1,0:T(8,128)(2,1)} %bitcast.14), channel_id=1, source_target_pairs={{0,3},{1,0},{2,1},{3,2},{4,7},{5,4},{6,5},{7,6},{8,11},{9,8},{10,9... | collective-permute-start | bytes 786440 | tf_op jit(solution)/shard_map/ppermute | solution.py:50
  128.8 28.1 %collective-permute-start.18 = (bf16[512,2048]{1,0:T(8,128)(2,1)S(1)}, bf16[512,2048]{1,0:T(8,128)(2,1)S(1)}, u32[]{:S(2)}, u32[]{:S(2)}) collective-permute-start(bf16[512,2048]{1,0:T(8,128)(2,1)S(1)} %shard_map.182.outer_ref.refs_4_), channel_id=1, source_target_pairs={{0,4},{4,0},{8,12},{12,8},{16,20},{20,16},{24,28},{28,24},{1,5},{5... | collective-permute-start | bytes 6291464 | tf_op jit(solution)/shard_map/ppermute | solution.py:40
  128.9 27.4 %collective-permute-start.19 = (bf16[128,2048]{1,0:T(8,128)(2,1)}, bf16[128,2048]{1,0:T(8,128)(2,1)S(1)}, u32[]{:S(2)}, u32[]{:S(2)}) collective-permute-start(bf16[128,2048]{1,0:T(8,128)(2,1)} %outer_ref.1), channel_id=1, source_target_pairs={{0,1},{1,0},{2,3},{3,2},{4,5},{5,4},{6,7},{7,6},{8,9},{9,8},{10,11... | collective-permute-start | bytes 1572872 | tf_op jit(solution)/shard_map/ppermute | solution.py:55
  131.2 25.8 %collective-permute-start.17 = (bf16[256,1024]{1,0:T(8,128)(2,1)S(1)}, bf16[256,1024]{1,0:T(8,128)(2,1)S(1)}, u32[]{:S(2)}, u32[]{:S(2)}) collective-permute-start(bf16[256,1024]{1,0:T(8,128)(2,1)S(1)} %copy-done.55), channel_id=1, source_target_pairs={{0,2},{1,3},{2,0},{3,1},{4,6},{5,7},{6,4},{7,5},{8,10},{9,11},{10,... | collective-permute-start | bytes 1572872 | tf_op jit(solution)/shard_map/ppermute | solution.py:50
  175.5 27.8 %collective-permute-start.25 = (bf16[256,2048]{1,0:T(8,128)(2,1)S(1)}, bf16[256,2048]{1,0:T(8,128)(2,1)S(1)}, u32[]{:S(2)}, u32[]{:S(2)}) collective-permute-start(bf16[256,2048]{1,0:T(8,128)(2,1)S(1)} %shard_map.184.refs_0_), channel_id=1, source_target_pairs={{0,16},{4,12},{8,24},{12,4},{16,0},{20,28},{24,8},{28,20},{1,17},{... | collective-permute-start | bytes 3145736 | tf_op jit(solution)/shard_map/ppermute | solution.py:78
  177.0 26.3 %collective-permute-start.24 = (bf16[256,2048]{1,0:T(8,128)(2,1)S(1)}, bf16[256,2048]{1,0:T(8,128)(2,1)S(1)}, u32[]{:S(2)}, u32[]{:S(2)}) collective-permute-start(bf16[256,2048]{1,0:T(8,128)(2,1)S(1)} %get-tuple-element.531), channel_id=1, source_target_pairs={{0,16},{4,12},{8,24},{12,4},{16,0},{20,28},{24,8},{28,20},{1,17},{... | collective-permute-start | bytes 3145736 | tf_op jit(solution)/shard_map/ppermute | solution.py:78
  242.5 27.6 %collective-permute-start.33 = (bf16[256,2048]{1,0:T(8,128)(2,1)S(1)}, bf16[256,2048]{1,0:T(8,128)(2,1)S(1)}, u32[]{:S(2)}, u32[]{:S(2)}) collective-permute-start(bf16[256,2048]{1,0:T(8,128)(2,1)S(1)} %shard_map.187.refs_0_), channel_id=1, source_target_pairs={{0,16},{4,12},{8,24},{12,4},{16,0},{20,28},{24,8},{28,20},{1,17},{... | collective-permute-start | bytes 3145736 | tf_op jit(solution)/shard_map/ppermute | solution.py:78
  290.2 26.2 %collective-permute-start.39 = (bf16[512,2048]{1,0:T(8,128)(2,1)}, bf16[512,2048]{1,0:T(8,128)(2,1)}, u32[]{:S(2)}, u32[]{:S(2)}) collective-permute-start(bf16[512,2048]{1,0:T(8,128)(2,1)} %shard_map.190.normed_ref.refs_2_), channel_id=1, source_target_pairs={{0,4},{4,0},{8,12},{12,8},{16,20},{20,16},{24,28},{28,24},{1,5},{5... | collective-permute-start | bytes 6291464 | tf_op jit(solution)/shard_map/ppermute | solution.py:40
  290.2 26.2 %collective-permute-start.38 = (bf16[256,1024]{1,0:T(8,128)(2,1)}, bf16[256,1024]{1,0:T(8,128)(2,1)}, u32[]{:S(2)}, u32[]{:S(2)}) collective-permute-start(bf16[256,1024]{1,0:T(8,128)(2,1)} %collective-permute-done.12.refs_3_), channel_id=1, source_target_pairs={{0,2},{1,3},{2,0},{3,1},{4,6},{5,7},{6,4},{7,5},{8,10},{9,11},{10,... | collective-permute-start | bytes 1572872 | tf_op jit(solution)/shard_map/ppermute | solution.py:50
  461.4 26.9 %collective-permute-start.59 = (bf16[256,2048]{1,0:T(8,128)(2,1)S(1)}, bf16[256,2048]{1,0:T(8,128)(2,1)S(1)}, u32[]{:S(2)}, u32[]{:S(2)}) collective-permute-start(bf16[256,2048]{1,0:T(8,128)(2,1)S(1)} %copy-done.141), channel_id=1, source_target_pairs={{0,16},{4,12},{8,24},{12,4},{16,0},{20,28},{24,8},{28,20},{1,17},{... | collective-permute-start | bytes 3145736 | tf_op jit(solution)/shard_map/ppermute | solution.py:78
  488.4 27.0 %collective-permute-start.63 = (bf16[128,2048]{1,0:T(8,128)(2,1)S(1)}, bf16[128,2048]{1,0:T(8,128)(2,1)S(1)}, u32[]{:S(2)}, u32[]{:S(2)}) collective-permute-start(bf16[128,2048]{1,0:T(8,128)(2,1)S(1)} %get-tuple-element.747), channel_id=1, source_target_pairs={{0,8},{4,20},{8,0},{12,28},{16,24},{20,4},{24,16},{28,12},{1,9},{5... | collective-permute-start | bytes 1572872 | tf_op jit(solution)/shard_map/ppermute | solution.py:78
  491.2 27.7 %collective-permute-start.61 = (bf16[512,1024]{1,0:T(8,128)(2,1)S(1)}, bf16[512,1024]{1,0:T(8,128)(2,1)S(1)}, u32[]{:S(2)}, u32[]{:S(2)}) collective-permute-start(bf16[512,1024]{1,0:T(8,128)(2,1)S(1)} %pad_maximum_fusion.1.refs_0_), channel_id=1, source_target_pairs={{0,8},{4,20},{8,0},{12,28},{16,24},{20,4},{24,16},{28,12},{1,9},{5... | collective-permute-start | bytes 3145736 | tf_op jit(solution)/shard_map/ppermute | solution.py:78
  492.6 26.4 %collective-permute-start.60 = (bf16[512,512]{1,0:T(8,128)(2,1)S(1)}, bf16[512,512]{1,0:T(8,128)(2,1)S(1)}, u32[]{:S(2)}, u32[]{:S(2)}) collective-permute-start(bf16[512,512]{1,0:T(8,128)(2,1)S(1)} %copy-done.148), channel_id=1, source_target_pairs={{0,2},{1,3},{2,0},{3,1},{4,6},{5,7},{6,4},{7,5},{8,10},{9,11},{10,... | collective-permute-start | bytes 1572872 | tf_op jit(solution)/shard_map/ppermute | solution.py:50
  519.7 33.3 %collective-permute-start.68 = (bf16[1024,1024]{1,0:T(8,128)(2,1)S(1)}, bf16[1024,1024]{1,0:T(8,128)(2,1)S(1)}, u32[]{:S(2)}, u32[]{:S(2)}) collective-permute-start(bf16[1024,1024]{1,0:T(8,128)(2,1)S(1)} %shard_map.217.source_ref), channel_id=1, source_target_pairs={{0,16},{4,12},{8,24},{12,4},{16,0},{20,28},{24,8},{28,20},{1,17},{... | collective-permute-start | bytes 6291464 | tf_op jit(solution)/shard_map/ppermute | solution.py:78
  553.0 34.3 %collective-permute-start.70 = (bf16[1024,1024]{1,0:T(8,128)(2,1)S(1)}, bf16[1024,1024]{1,0:T(8,128)(2,1)}, u32[]{:S(2)}, u32[]{:S(2)}) collective-permute-start(bf16[1024,1024]{1,0:T(8,128)(2,1)S(1)} %shard_map.217.source_ref), channel_id=1, source_target_pairs={{0,4},{4,0},{8,12},{12,8},{16,20},{20,16},{24,28},{28,24},{1,5},{5... | collective-permute-start | bytes 6291464 | tf_op jit(solution)/shard_map/ppermute | solution.py:40
  553.3 34.0 %collective-permute-start.71 = (bf16[512,1024]{1,0:T(8,128)(2,1)S(1)}, bf16[512,1024]{1,0:T(8,128)(2,1)}, u32[]{:S(2)}, u32[]{:S(2)}) collective-permute-start(bf16[512,1024]{1,0:T(8,128)(2,1)S(1)} %pad_maximum_fusion.2.refs_0_), channel_id=1, source_target_pairs={{0,8},{4,20},{8,0},{12,28},{16,24},{20,4},{24,16},{28,12},{1,9},{5... | collective-permute-start | bytes 3145736 | tf_op jit(solution)/shard_map/ppermute | solution.py:78
  555.2 32.1 %all-to-all-start.1 = ((bf16[256,8,256]{2,0,1:T(8,128)(2,1)}), bf16[256,8,256]{2,0,1:T(8,128)(2,1)}, u32[]{:S(2)}, u32[]{:S(2)}) async-start(bf16[256,8,256]{2,0,1:T(8,128)(2,1)} %bitcast.105), calls=%async_computation.1 | async-start | bytes 2097152 | tf_op jit(solution)/shard_map/all_to_all | solution.py:963
  561.0 25.5 %collective-permute-start.72 = (bf16[128,2048]{1,0:T(8,128)(2,1)S(1)}, bf16[128,2048]{1,0:T(8,128)(2,1)S(1)}, u32[]{:S(2)}, u32[]{:S(2)}) collective-permute-start(bf16[128,2048]{1,0:T(8,128)(2,1)S(1)} %add_convert_fusion.4), channel_id=1, source_target_pairs={{0,1},{1,0},{2,3},{3,2},{4,5},{5,4},{6,7},{7,6},{8,9},{9,8},{10,11... | collective-permute-start | bytes 1572872 | tf_op jit(solution)/shard_map/ppermute | solution.py:55
  561.4 25.9 %collective-permute-start.69 = (bf16[128,2048]{1,0:T(8,128)(2,1)}, bf16[128,2048]{1,0:T(8,128)(2,1)}, u32[]{:S(2)}, u32[]{:S(2)}) collective-permute-start(bf16[128,2048]{1,0:T(8,128)(2,1)} %copy-done.146), channel_id=1, source_target_pairs={{0,2},{1,3},{2,0},{3,1},{4,6},{5,7},{6,4},{7,5},{8,10},{9,11},{10,... | collective-permute-start | bytes 1572872 | tf_op jit(solution)/shard_map/ppermute | solution.py:50
  590.6 30.7 %collective-permute-start.75 = (bf16[1024,1024]{1,0:T(8,128)(2,1)}, bf16[1024,1024]{1,0:T(8,128)(2,1)}, u32[]{:S(2)}, u32[]{:S(2)}) collective-permute-start(bf16[1024,1024]{1,0:T(8,128)(2,1)} %shard_map.219.source_ref), channel_id=1, source_target_pairs={{0,16},{4,12},{8,24},{12,4},{16,0},{20,28},{24,8},{28,20},{1,17},{... | collective-permute-start | bytes 6291464 | tf_op jit(solution)/shard_map/ppermute | solution.py:78
  592.3 29.0 %collective-permute-start.76 = (bf16[1024,1024]{1,0:T(8,128)(2,1)}, bf16[1024,1024]{1,0:T(8,128)(2,1)}, u32[]{:S(2)}, u32[]{:S(2)}) collective-permute-start(bf16[1024,1024]{1,0:T(8,128)(2,1)} %shard_map.219.source_ref), channel_id=1, source_target_pairs={{0,4},{4,0},{8,12},{12,8},{16,20},{20,16},{24,28},{28,24},{1,5},{5... | collective-permute-start | bytes 6291464 | tf_op jit(solution)/shard_map/ppermute | solution.py:40
  592.3 29.0 %collective-permute-start.74 = (bf16[512,2048]{1,0:T(8,128)(2,1)}, bf16[512,2048]{1,0:T(8,128)(2,1)}, u32[]{:S(2)}, u32[]{:S(2)}) collective-permute-start(bf16[512,2048]{1,0:T(8,128)(2,1)} %get-tuple-element.792), channel_id=1, source_target_pairs={{0,4},{4,0},{8,12},{12,8},{16,20},{20,16},{24,28},{28,24},{1,5},{5... | collective-permute-start | bytes 6291464 | tf_op jit(solution)/shard_map/ppermute | solution.py:40
  594.7 26.7 %collective-permute-start.73 = (bf16[128,2048]{1,0:T(8,128)(2,1)}, bf16[128,2048]{1,0:T(8,128)(2,1)S(1)}, u32[]{:S(2)}, u32[]{:S(2)}) collective-permute-start(bf16[128,2048]{1,0:T(8,128)(2,1)} %copy-done.145), channel_id=1, source_target_pairs={{0,2},{1,3},{2,0},{3,1},{4,6},{5,7},{6,4},{7,5},{8,10},{9,11},{10,... | collective-permute-start | bytes 1572872 | tf_op jit(solution)/shard_map/ppermute | solution.py:50
  621.4 27.9 %collective-permute-start.80 = (bf16[1024,1024]{1,0:T(8,128)(2,1)S(1)}, bf16[1024,1024]{1,0:T(8,128)(2,1)S(1)}, u32[]{:S(2)}, u32[]{:S(2)}) collective-permute-start(bf16[1024,1024]{1,0:T(8,128)(2,1)S(1)} %copy-done.47), channel_id=1, source_target_pairs={{0,4},{4,0},{8,12},{12,8},{16,20},{20,16},{24,28},{28,24},{1,5},{5... | collective-permute-start | bytes 6291464 | tf_op jit(solution)/shard_map/ppermute | solution.py:40
  650.0 31.9 %collective-permute-start.84 = (bf16[512,2048]{1,0:T(8,128)(2,1)S(1)}, bf16[512,2048]{1,0:T(8,128)(2,1)S(1)}, u32[]{:S(2)}, u32[]{:S(2)}) collective-permute-start(bf16[512,2048]{1,0:T(8,128)(2,1)S(1)} %shard_map.228.source_ref), channel_id=1, source_target_pairs={{0,16},{4,12},{8,24},{12,4},{16,0},{20,28},{24,8},{28,20},{1,17},{... | collective-permute-start | bytes 6291464 | tf_op jit(solution)/shard_map/ppermute | solution.py:78
  651.0 31.0 %collective-permute-start.83 = (bf16[128,2048]{1,0:T(8,128)(2,1)S(1)}, bf16[128,2048]{1,0:T(8,128)(2,1)S(1)}, u32[]{:S(2)}, u32[]{:S(2)}) collective-permute-start(bf16[128,2048]{1,0:T(8,128)(2,1)S(1)} %get-tuple-element.837), channel_id=1, source_target_pairs={{0,8},{4,20},{8,0},{12,28},{16,24},{20,4},{24,16},{28,12},{1,9},{5... | collective-permute-start | bytes 1572872 | tf_op jit(solution)/shard_map/ppermute | solution.py:78
  655.2 26.8 %collective-permute-start.85 = (bf16[512,384]{1,0:T(8,128)(2,1)S(1)}, bf16[512,384]{1,0:T(8,128)(2,1)S(1)}, u32[]{:S(2)}, u32[]{:S(2)}) collective-permute-start(bf16[512,384]{1,0:T(8,128)(2,1)S(1)} %get-tuple-element.854), channel_id=1, source_target_pairs={{0,2},{1,3},{2,0},{3,1},{4,6},{5,7},{6,4},{7,5},{8,10},{9,11},{10,... | collective-permute-start | bytes 1179656 | tf_op jit(solution)/shard_map/ppermute | solution.py:50
  (253 other events, 2271.9 us)
